TPU v7x, 32 devices: a whole 2x2x4 slice. The times are simulated.
32 devices in a mesh: stream: 4 (over y, core), dp: 8 (over z, x).
Axes of the slice: x: 2, y: 2, z: 4, core: 2. Of those that a mesh axis runs over, the one named last changes fastest.
Arguments:
- enc_input: bfloat16 [4096, 1024], P(('stream', 'dp')), may hold values from -6 to 6
- pred_input: bfloat16 [2, 4096, 1024], P(None, ('stream', 'dp')), may hold values from -6 to 6
- cotangent: bfloat16 [3, 4096, 1024], P(None, ('stream', 'dp')), may hold values from -6 to 6
- bucket_len: int32 [8], P('dp'), may hold values from 256 to 512, as said below
- pad_len: int32 [8, 2], P('dp'), may hold values from 0 to 63, as said below
- rel_table: int32 [512], replicated, may hold values from 0 to 31
- enc_qkv: bfloat16 [3, 1024, 1024], P(None, 'dp'), may hold values from -0.1875 to 0.1875
- enc_out: bfloat16 [1024, 1024], P('dp'), may hold values from -3 to 3
- enc_ffn_in: bfloat16 [1024, 4096], P('dp'), may hold values from -0.1875 to 0.1875
- enc_ffn_out: bfloat16 [4096, 1024], P('dp'), may hold values from -0.09375 to 0.09375
- enc_ffn_bias: bfloat16 [4096], P('dp'), may hold values from -3 to 3
- enc_bias: bfloat16 [4, 1024], P(None, 'dp'), may hold values from -2 to 2
- enc_gain: bfloat16 [2, 1024], P(None, 'dp'), may hold values from 0.5 to 1.5
- enc_shift: bfloat16 [2, 1024], P(None, 'dp'), may hold values from -2 to 2
- dec_qkv: bfloat16 [3, 1024, 1024], P(None, 'dp'), may hold values from -0.1875 to 0.1875
- dec_out: bfloat16 [1024, 1024], P('dp'), may hold values from -3 to 3
- dec_rel: bfloat16 [1024, 512], P('dp'), may hold values from -0.1875 to 0.1875
- dec_rel_bias: bfloat16 [512], P('dp'), may hold values from -3 to 3
- dec_ffn_in: bfloat16 [1024, 4096], P('dp'), may hold values from -0.1875 to 0.1875
- dec_ffn_out: bfloat16 [4096, 1024], P('dp'), may hold values from -0.09375 to 0.09375
- dec_ffn_bias: bfloat16 [4096], P('dp'), may hold values from -3 to 3
- dec_bias: bfloat16 [4, 1024], P(None, 'dp'), may hold values from -2 to 2
- dec_gain: bfloat16 [2, 1024], P(None, 'dp'), may hold values from 0.5 to 1.5
- dec_shift: bfloat16 [2, 1024], P(None, 'dp'), may hold values from -2 to 2
Outputs:
- dec_output: float32 [3, 4096, 1024], P(None, ('stream', 'dp'))
- enc_input_grad: float32 [4096, 1024], P(('stream', 'dp'))
- pred_input_grad: float32 [2, 4096, 1024], P(None, ('stream', 'dp'))
- enc_qkv_grad: float32 [3, 1024, 1024], P(None, 'dp')
- enc_out_grad: float32 [1024, 1024], P('dp')
- enc_ffn_in_grad: float32 [1024, 4096], P('dp')
- enc_ffn_out_grad: float32 [4096, 1024], P('dp')
- enc_ffn_bias_grad: float32 [4096], P('dp')
- enc_bias_grad: float32 [4, 1024], P(None, 'dp')
- enc_gain_grad: float32 [2, 1024], P(None, 'dp')
- enc_shift_grad: float32 [2, 1024], P(None, 'dp')
- dec_qkv_grad: float32 [3, 1024, 1024], P(None, 'dp')
- dec_out_grad: float32 [1024, 1024], P('dp')
- dec_rel_grad: float32 [1024, 512], P('dp')
- dec_rel_bias_grad: float32 [512], P('dp')
- dec_ffn_in_grad: float32 [1024, 4096], P('dp')
- dec_ffn_out_grad: float32 [4096, 1024], P('dp')
- dec_ffn_bias_grad: float32 [4096], P('dp')
- dec_bias_grad: float32 [4, 1024], P(None, 'dp')
- dec_gain_grad: float32 [2, 1024], P(None, 'dp')
- dec_shift_grad: float32 [2, 1024], P(None, 'dp')
Inputs may be any that keep to these rules, and one draw needn't show every extreme that they name: bucket_len[g] is 512 or 256, each in some group; data group g holds 512 // bucket_len[g] sequences of that length. pad_len[g, q] is below bucket_len[g] // 8; entries with q >= 512 // bucket_len[g] are unused.
All inputs are finite; a program needn't handle non-finite values.
Results may differ from a plain program's by a relative error of at most 0.03.
Values may be sent and summed in bfloat16 or wider, within the bound.
No kernel may reach another device: no remote copies, remote signals or barrier semaphores. Data moves between devices by JAX's collectives and lax.ppermute only.
A program may use at most 320 MiB of HBM per device.

v0:
```python
from functools import partial

import jax
import jax.numpy as jnp
from jax import lax
from jax.sharding import PartitionSpec as P

H = 16
NB = 32
HD = 64


EPSILON = 1e-05
MASKED = -1000000000.0
BFLOAT = jnp.bfloat16
SINGLE = jnp.float32


def normed(values, gain, shift):
    center = values - jnp.mean(values, axis=-1, keepdims=True)
    spread = jnp.mean(center * center, axis=-1, keepdims=True)
    return center * lax.rsqrt(spread + EPSILON) * gain + shift


def split_heads(values):
    return values.reshape(values.shape[0], H, values.shape[1] // H)


def product(rows_in, matrix):
    return jnp.dot(rows_in, matrix, preferred_element_type=SINGLE)


def project(rows_in, matrix, bias):
    return product(rows_in, matrix) + bias.astype(SINGLE)


def back_rows(grad_rows, matrix):
    return jnp.einsum("rf,df->rd", grad_rows, matrix, preferred_element_type=SINGLE)


def outer_sum(rows_in, grad_rows):
    return jnp.einsum("rd,rf->df", rows_in, grad_rows, preferred_element_type=SINGLE)


def column_sum(grad_rows):
    return jnp.sum(grad_rows.astype(SINGLE), axis=0)


def projections(rounded, weights):
    queries = project(rounded, weights[0][0], weights[5][0]).astype(BFLOAT)
    key_rows = product(rounded, weights[0][1]).astype(BFLOAT)
    val_rows = project(rounded, weights[0][2], weights[5][1]).astype(BFLOAT)
    return (queries, key_rows, val_rows)


def soft_weights(queries, key_all, allowed, extra, own):
    scale = (queries.shape[1] // H) ** (-0.5)
    scores = (
        jnp.einsum(
            "qhd,khd->hqk",
            split_heads(queries),
            split_heads(key_all),
            preferred_element_type=SINGLE,
        )
        * scale
    )
    if extra is not None:
        scores = scores + extra
    scores = jnp.where(allowed[None], scores, MASKED)
    top = jnp.max(scores, axis=2)
    if own is not None:
        top = jnp.maximum(top, own)
    expos = jnp.exp(scores - top[:, :, None])
    total = jnp.sum(expos, axis=2)
    if own is None:
        return (expos / total[:, :, None], None)
    own_expo = jnp.exp(own - top)
    total = total + own_expo
    return (expos / total[:, :, None], own_expo / total)


def context_of(probs, own_probs, val_all, val_own):
    context = jnp.einsum(
        "hqk,khd->qhd", probs.astype(BFLOAT), split_heads(val_all), preferred_element_type=SINGLE
    )
    if own_probs is not None:
        context = context + jnp.transpose(own_probs)[:, :, None] * split_heads(val_own).astype(
            SINGLE
        )
    return context.reshape(context.shape[0], -1)


def attention_back(context_grad, queries, key_all, val_all, key_own, val_own, probs, own_probs):
    scale = (queries.shape[1] // H) ** (-0.5)
    grad_heads = split_heads(context_grad)
    query_heads = split_heads(queries)
    prob_grad = jnp.einsum(
        "qhd,khd->hqk", grad_heads, split_heads(val_all), preferred_element_type=SINGLE
    )
    val_grad = jnp.einsum(
        "hqk,qhd->khd", probs.astype(BFLOAT), grad_heads, preferred_element_type=SINGLE
    ).reshape(val_all.shape)
    rowdot = jnp.sum(probs * prob_grad, axis=2)
    if own_probs is not None:
        own_prob_grad = jnp.transpose(
            jnp.sum(grad_heads.astype(SINGLE) * split_heads(val_own).astype(SINGLE), axis=2)
        )
        rowdot = rowdot + own_probs * own_prob_grad
    score_grad = (probs * (prob_grad - rowdot[:, :, None])).astype(BFLOAT)
    query_grad = (
        jnp.einsum("hqk,khd->qhd", score_grad, split_heads(key_all), preferred_element_type=SINGLE)
        * scale
    )
    key_grad = (
        jnp.einsum("hqk,qhd->khd", score_grad, query_heads, preferred_element_type=SINGLE) * scale
    ).reshape(key_all.shape)
    if own_probs is None:
        return (query_grad.reshape(queries.shape), key_grad, val_grad, score_grad, None, None, None)
    own_score_grad = (own_probs * (own_prob_grad - rowdot)).astype(BFLOAT)
    own_rows = jnp.transpose(own_score_grad).astype(SINGLE)[:, :, None]
    query_grad = query_grad + own_rows * split_heads(key_own).astype(SINGLE) * scale
    key_own_grad = (own_rows * query_heads.astype(SINGLE) * scale).reshape(queries.shape)
    val_own_grad = (jnp.transpose(own_probs)[:, :, None] * grad_heads.astype(SINGLE)).reshape(
        queries.shape
    )
    return (
        query_grad.reshape(queries.shape),
        key_grad,
        val_grad,
        score_grad,
        own_score_grad,
        key_own_grad,
        val_own_grad,
    )


def rel_lookup(rel_rows, onehot, own_hot):
    shaped = rel_rows.reshape(rel_rows.shape[0], H, NB)
    main_bias = jnp.einsum(
        "qkb,qhb->hqk",
        onehot.astype(SINGLE),
        shaped,
        precision=lax.Precision.HIGHEST,
        preferred_element_type=SINGLE,
    )
    own_bias = jnp.transpose(jnp.sum(shaped * own_hot[None, None, :], axis=2))
    return (main_bias, own_bias)


def rel_back(score_grad, own_cot, onehot, own_hot):
    main_grad = jnp.einsum("hqk,qkb->qhb", score_grad, onehot, preferred_element_type=SINGLE)
    own_grad = jnp.transpose(own_cot)[:, :, None] * own_hot[None, None, :]
    total = main_grad + own_grad
    return total.reshape(total.shape[0], H * NB)


def forward_tail(inputs, context, weights):
    gains = weights[6].astype(SINGLE)
    shifts = weights[7].astype(SINGLE)
    attended = project(context, weights[1], weights[5][2])
    hidden = normed(inputs + attended, gains[0], shifts[0])
    hidden_low = hidden.astype(BFLOAT)
    inner = project(hidden_low, weights[2], weights[4])
    active = jax.nn.gelu(inner, approximate=False).astype(BFLOAT)
    branch = project(active, weights[3], weights[5][3])
    output = normed(hidden + branch, gains[1], shifts[1])
    return (output, (attended, hidden, hidden_low, inner, active, branch))


def backward_tail(output_grad, inputs, context, kept, weights):
    attended, hidden, hidden_low, inner, active, branch = kept
    gains = weights[6].astype(SINGLE)
    shifts = weights[7].astype(SINGLE)
    _, pull_second = jax.vjp(normed, hidden + branch, gains[1], shifts[1])
    sum_grad, gain_two, shift_two = pull_second(output_grad)
    branch_grad = sum_grad.astype(BFLOAT)
    active_grad = back_rows(branch_grad, weights[3])
    _, pull_gelu = jax.vjp(partial(jax.nn.gelu, approximate=False), inner)
    inner_grad = pull_gelu(active_grad)[0].astype(BFLOAT)
    hidden_grad = sum_grad + back_rows(inner_grad, weights[2])
    _, pull_first = jax.vjp(normed, inputs + attended, gains[0], shifts[0])
    input_grad, gain_one, shift_one = pull_first(hidden_grad)
    attended_grad = input_grad.astype(BFLOAT)
    context_grad = back_rows(attended_grad, weights[1]).astype(BFLOAT)
    tail = (
        outer_sum(context, attended_grad),
        outer_sum(hidden_low, inner_grad),
        outer_sum(active, branch_grad),
        column_sum(inner_grad),
        column_sum(attended_grad),
        column_sum(branch_grad),
        gain_one,
        gain_two,
        shift_one,
        shift_two,
    )
    return (input_grad, context_grad, tail)


def per_device(
    enc_input,
    pred_input,
    cotangent,
    bucket_len,
    pad_len,
    rel_table,
    enc_qkv,
    enc_out,
    enc_ffn_in,
    enc_ffn_out,
    enc_ffn_bias,
    enc_bias,
    enc_gain,
    enc_shift,
    dec_qkv,
    dec_out,
    dec_rel,
    dec_rel_bias,
    dec_ffn_in,
    dec_ffn_out,
    dec_ffn_bias,
    dec_bias,
    dec_gain,
    dec_shift,
):
    stream_index = lax.axis_index("stream")
    holders = lax.axis_size("stream")
    rows = enc_input.shape[0]
    bucket = bucket_len[0]
    quarter = bucket // holders
    padding_rows = pad_len[0]
    slot_ids = jnp.arange(padding_rows.shape[0], dtype=jnp.int32)

    def place(holder, within):
        sequence = within // quarter
        position = holder * quarter + within % quarter
        padding = jnp.sum(
            jnp.where(sequence[:, None] == slot_ids[None, :], padding_rows[None, :], 0), axis=1
        )
        return (sequence, position, position < bucket - padding)

    within_rows = jnp.arange(rows, dtype=jnp.int32)
    query_seq, query_pos, _ = place(stream_index + 0 * within_rows, within_rows)
    everyone = jnp.arange(holders * rows, dtype=jnp.int32)
    key_seq, key_pos, key_valid = place(everyone // rows, everyone % rows)
    same = (query_seq[:, None] == key_seq[None, :]) & key_valid[None, :]
    earlier = key_pos[None, :] < query_pos[:, None]
    main_allowed = same & (earlier | (key_pos[None, :] == query_pos[:, None]))
    pred_allowed = same & earlier
    distance = jnp.clip(query_pos[:, None] - key_pos[None, :], 0, rel_table.shape[0] - 1)
    bucket_ids = jnp.arange(NB, dtype=jnp.int32)
    onehot = (rel_table[distance][:, :, None] == bucket_ids[None, None, :]).astype(BFLOAT)
    own_hot = (rel_table[0] == bucket_ids).astype(SINGLE)
    scale = HD ** (-0.5)
    enc_weights = (
        lax.all_gather(enc_qkv, "dp", axis=1, tiled=True),
        lax.all_gather(enc_out, "dp", axis=0, tiled=True),
        lax.all_gather(enc_ffn_in, "dp", axis=0, tiled=True),
        lax.all_gather(enc_ffn_out, "dp", axis=0, tiled=True),
        lax.all_gather(enc_ffn_bias, "dp", axis=0, tiled=True),
        lax.all_gather(enc_bias, "dp", axis=1, tiled=True),
        lax.all_gather(enc_gain, "dp", axis=1, tiled=True),
        lax.all_gather(enc_shift, "dp", axis=1, tiled=True),
    )
    enc_query, enc_key, enc_val = projections(enc_input, enc_weights)
    enc_key_all, enc_val_all = (
        lax.all_gather(enc_key, "stream", axis=0, tiled=True),
        lax.all_gather(enc_val, "stream", axis=0, tiled=True),
    )
    enc_probs, _ = soft_weights(enc_query, enc_key_all, same, None, None)
    enc_context = context_of(enc_probs, None, enc_val_all, None).astype(BFLOAT)
    enc_inputs = enc_input.astype(SINGLE)
    main_rows, enc_kept = forward_tail(enc_inputs, enc_context, enc_weights)
    dec_all = (
        lax.all_gather(dec_qkv, "dp", axis=1, tiled=True),
        lax.all_gather(dec_out, "dp", axis=0, tiled=True),
        lax.all_gather(dec_rel, "dp", axis=0, tiled=True),
        lax.all_gather(dec_rel_bias, "dp", axis=0, tiled=True),
        lax.all_gather(dec_ffn_in, "dp", axis=0, tiled=True),
        lax.all_gather(dec_ffn_out, "dp", axis=0, tiled=True),
        lax.all_gather(dec_ffn_bias, "dp", axis=0, tiled=True),
        lax.all_gather(dec_bias, "dp", axis=1, tiled=True),
        lax.all_gather(dec_gain, "dp", axis=1, tiled=True),
        lax.all_gather(dec_shift, "dp", axis=1, tiled=True),
    )
    dec_weights = (
        dec_all[0],
        dec_all[1],
        dec_all[4],
        dec_all[5],
        dec_all[6],
        dec_all[7],
        dec_all[8],
        dec_all[9],
    )
    stream_inputs = (main_rows, pred_input[0].astype(SINGLE), pred_input[1].astype(SINGLE))
    stream_low = (main_rows.astype(BFLOAT), pred_input[0], pred_input[1])
    projected = [projections(low_rows, dec_weights) for low_rows in stream_low]
    rel_rows = [project(low_rows, dec_all[2], dec_all[3]) for low_rows in stream_low]
    main_key_all, main_val_all = (
        lax.all_gather(projected[0][1], "stream", axis=0, tiled=True),
        lax.all_gather(projected[0][2], "stream", axis=0, tiled=True),
    )

    def dec_probs(number):
        queries, key_rows, val_rows = projected[number]
        main_bias, own_bias = rel_lookup(rel_rows[number], onehot, own_hot)
        if number == 0:
            return soft_weights(queries, main_key_all, main_allowed, main_bias, None)
        own_dot = jnp.sum(
            split_heads(queries).astype(SINGLE) * split_heads(key_rows).astype(SINGLE), axis=2
        )
        own_score = jnp.transpose(own_dot) * scale + own_bias
        return soft_weights(queries, main_key_all, pred_allowed, main_bias, own_score)

    dec_contexts = []
    dec_kept = []
    dec_outputs = []
    for number in range(3):
        probs, own_probs = dec_probs(number)
        context = context_of(probs, own_probs, main_val_all, projected[number][2]).astype(BFLOAT)
        output, kept = forward_tail(stream_inputs[number], context, dec_weights)
        dec_contexts.append(context)
        dec_kept.append(kept)
        dec_outputs.append(output)
    key_grad_all = jnp.zeros(main_key_all.shape, SINGLE)
    val_grad_all = jnp.zeros(main_val_all.shape, SINGLE)
    residuals = []
    query_grads = []
    rel_grads = []
    own_key_grads = []
    own_val_grads = []
    tails = []
    for number in range(3):
        residual, context_grad, tail = backward_tail(
            cotangent[number].astype(SINGLE),
            stream_inputs[number],
            dec_contexts[number],
            dec_kept[number],
            dec_weights,
        )
        probs, own_probs = dec_probs(number)
        queries, key_rows, val_rows = projected[number]
        query_grad, key_grad, val_grad, score_grad, own_score_grad, key_own_grad, val_own_grad = (
            attention_back(
                context_grad,
                queries,
                main_key_all,
                main_val_all,
                key_rows,
                val_rows,
                probs,
                own_probs,
            )
        )
        key_grad_all = key_grad_all + key_grad
        val_grad_all = val_grad_all + val_grad
        if own_probs is None:
            own_cot = jnp.zeros((H, rows), SINGLE)
        else:
            own_cot = own_score_grad.astype(SINGLE)
        rel_grads.append(rel_back(score_grad, own_cot, onehot, own_hot).astype(BFLOAT))
        residuals.append(residual)
        query_grads.append(query_grad.astype(BFLOAT))
        own_key_grads.append(key_own_grad)
        own_val_grads.append(val_own_grad)
        tails.append(tail)
    main_key_grad, main_val_grad = (
        lax.psum_scatter(
            key_grad_all.astype(jnp.bfloat16), "stream", scatter_dimension=0, tiled=True
        ).astype(jnp.float32),
        lax.psum_scatter(
            val_grad_all.astype(jnp.bfloat16), "stream", scatter_dimension=0, tiled=True
        ).astype(jnp.float32),
    )
    key_grads = [
        main_key_grad.astype(BFLOAT),
        own_key_grads[1].astype(BFLOAT),
        own_key_grads[2].astype(BFLOAT),
    ]
    val_grads = [
        main_val_grad.astype(BFLOAT),
        own_val_grads[1].astype(BFLOAT),
        own_val_grads[2].astype(BFLOAT),
    ]
    input_grads = []
    for number in range(3):
        total = (
            residuals[number]
            + back_rows(query_grads[number], dec_all[0][0])
            + back_rows(key_grads[number], dec_all[0][1])
        )
        total = (
            total
            + back_rows(val_grads[number], dec_all[0][2])
            + back_rows(rel_grads[number], dec_all[2])
        )
        input_grads.append(total)
    low_all = jnp.concatenate(stream_low, axis=0)
    query_all = jnp.concatenate(query_grads, axis=0)
    key_all_rows = jnp.concatenate(key_grads, axis=0)
    val_all_rows = jnp.concatenate(val_grads, axis=0)
    rel_all = jnp.concatenate(rel_grads, axis=0)
    dec_tail = jax.tree.map(
        lambda first, second, third: first + second + third, tails[0], tails[1], tails[2]
    )
    dec_qkv_part = jnp.stack(
        [
            outer_sum(low_all, query_all),
            outer_sum(low_all, key_all_rows),
            outer_sum(low_all, val_all_rows),
        ]
    )
    dec_out_part = dec_tail[0]
    dec_rel_part = outer_sum(low_all, rel_all)
    dec_rel_bias_part = column_sum(rel_all)
    dec_in_part = dec_tail[1]
    dec_back_part = dec_tail[2]
    dec_inner_part = dec_tail[3]
    dec_bias_part = jnp.stack(
        [column_sum(query_all), column_sum(val_all_rows), dec_tail[4], dec_tail[5]]
    )
    dec_gain_part = jnp.stack([dec_tail[6], dec_tail[7]])
    dec_shift_part = jnp.stack([dec_tail[8], dec_tail[9]])
    residual, context_grad, enc_tail = backward_tail(
        input_grads[0], enc_inputs, enc_context, enc_kept, enc_weights
    )
    enc_probs, _ = soft_weights(enc_query, enc_key_all, same, None, None)
    query_grad, key_grad, val_grad, _, _, _, _ = attention_back(
        context_grad, enc_query, enc_key_all, enc_val_all, None, None, enc_probs, None
    )
    enc_key_grad, enc_val_grad = (
        lax.psum_scatter(
            key_grad.astype(jnp.bfloat16), "stream", scatter_dimension=0, tiled=True
        ).astype(jnp.float32),
        lax.psum_scatter(
            val_grad.astype(jnp.bfloat16), "stream", scatter_dimension=0, tiled=True
        ).astype(jnp.float32),
    )
    enc_query_low = query_grad.astype(BFLOAT)
    enc_key_low = enc_key_grad.astype(BFLOAT)
    enc_val_low = enc_val_grad.astype(BFLOAT)
    enc_input_grad = (
        residual
        + back_rows(enc_query_low, enc_weights[0][0])
        + back_rows(enc_key_low, enc_weights[0][1])
        + back_rows(enc_val_low, enc_weights[0][2])
    )
    enc_qkv_part = jnp.stack(
        [
            outer_sum(enc_input, enc_query_low),
            outer_sum(enc_input, enc_key_low),
            outer_sum(enc_input, enc_val_low),
        ]
    )
    enc_bias_part = jnp.stack(
        [column_sum(enc_query_low), column_sum(enc_val_low), enc_tail[4], enc_tail[5]]
    )
    enc_gain_part = jnp.stack([enc_tail[6], enc_tail[7]])
    enc_shift_part = jnp.stack([enc_tail[8], enc_tail[9]])
    all_sums = (
        lax.psum_scatter(
            enc_qkv_part.astype(jnp.bfloat16), "dp", scatter_dimension=1, tiled=True
        ).astype(jnp.float32),
        lax.psum_scatter(
            enc_tail[0].astype(jnp.bfloat16), "dp", scatter_dimension=0, tiled=True
        ).astype(jnp.float32),
        lax.psum_scatter(
            enc_tail[1].astype(jnp.bfloat16), "dp", scatter_dimension=0, tiled=True
        ).astype(jnp.float32),
        lax.psum_scatter(
            enc_tail[2].astype(jnp.bfloat16), "dp", scatter_dimension=0, tiled=True
        ).astype(jnp.float32),
        lax.psum_scatter(
            enc_tail[3].astype(jnp.bfloat16), "dp", scatter_dimension=0, tiled=True
        ).astype(jnp.float32),
        lax.psum_scatter(
            enc_bias_part.astype(jnp.bfloat16), "dp", scatter_dimension=1, tiled=True
        ).astype(jnp.float32),
        lax.psum_scatter(
            enc_gain_part.astype(jnp.bfloat16), "dp", scatter_dimension=1, tiled=True
        ).astype(jnp.float32),
        lax.psum_scatter(
            enc_shift_part.astype(jnp.bfloat16), "dp", scatter_dimension=1, tiled=True
        ).astype(jnp.float32),
        lax.psum_scatter(
            dec_qkv_part.astype(jnp.bfloat16), "dp", scatter_dimension=1, tiled=True
        ).astype(jnp.float32),
        lax.psum_scatter(
            dec_out_part.astype(jnp.bfloat16), "dp", scatter_dimension=0, tiled=True
        ).astype(jnp.float32),
        lax.psum_scatter(
            dec_rel_part.astype(jnp.bfloat16), "dp", scatter_dimension=0, tiled=True
        ).astype(jnp.float32),
        lax.psum_scatter(
            dec_rel_bias_part.astype(jnp.bfloat16), "dp", scatter_dimension=0, tiled=True
        ).astype(jnp.float32),
        lax.psum_scatter(
            dec_in_part.astype(jnp.bfloat16), "dp", scatter_dimension=0, tiled=True
        ).astype(jnp.float32),
        lax.psum_scatter(
            dec_back_part.astype(jnp.bfloat16), "dp", scatter_dimension=0, tiled=True
        ).astype(jnp.float32),
        lax.psum_scatter(
            dec_inner_part.astype(jnp.bfloat16), "dp", scatter_dimension=0, tiled=True
        ).astype(jnp.float32),
        lax.psum_scatter(
            dec_bias_part.astype(jnp.bfloat16), "dp", scatter_dimension=1, tiled=True
        ).astype(jnp.float32),
        lax.psum_scatter(
            dec_gain_part.astype(jnp.bfloat16), "dp", scatter_dimension=1, tiled=True
        ).astype(jnp.float32),
        lax.psum_scatter(
            dec_shift_part.astype(jnp.bfloat16), "dp", scatter_dimension=1, tiled=True
        ).astype(jnp.float32),
    )
    all_final = (
        lax.psum(all_sums[0].astype(jnp.bfloat16), "stream").astype(jnp.float32),
        lax.psum(all_sums[1].astype(jnp.bfloat16), "stream").astype(jnp.float32),
        lax.psum(all_sums[2].astype(jnp.bfloat16), "stream").astype(jnp.float32),
        lax.psum(all_sums[3].astype(jnp.bfloat16), "stream").astype(jnp.float32),
        lax.psum(all_sums[4].astype(jnp.bfloat16), "stream").astype(jnp.float32),
        lax.psum(all_sums[5].astype(jnp.bfloat16), "stream").astype(jnp.float32),
        lax.psum(all_sums[6].astype(jnp.bfloat16), "stream").astype(jnp.float32),
        lax.psum(all_sums[7].astype(jnp.bfloat16), "stream").astype(jnp.float32),
        lax.psum(all_sums[8].astype(jnp.bfloat16), "stream").astype(jnp.float32),
        lax.psum(all_sums[9].astype(jnp.bfloat16), "stream").astype(jnp.float32),
        lax.psum(all_sums[10].astype(jnp.bfloat16), "stream").astype(jnp.float32),
        lax.psum(all_sums[11].astype(jnp.bfloat16), "stream").astype(jnp.float32),
        lax.psum(all_sums[12].astype(jnp.bfloat16), "stream").astype(jnp.float32),
        lax.psum(all_sums[13].astype(jnp.bfloat16), "stream").astype(jnp.float32),
        lax.psum(all_sums[14].astype(jnp.bfloat16), "stream").astype(jnp.float32),
        lax.psum(all_sums[15].astype(jnp.bfloat16), "stream").astype(jnp.float32),
        lax.psum(all_sums[16].astype(jnp.bfloat16), "stream").astype(jnp.float32),
        lax.psum(all_sums[17].astype(jnp.bfloat16), "stream").astype(jnp.float32),
    )
    enc_final = all_final[:8]
    dec_final = all_final[8:]
    dec_output = jnp.stack(dec_outputs)
    pred_input_grad = jnp.stack([input_grads[1], input_grads[2]])
    return (
        dec_output,
        enc_input_grad,
        pred_input_grad,
        enc_final[0],
        enc_final[1],
        enc_final[2],
        enc_final[3],
        enc_final[4],
        enc_final[5],
        enc_final[6],
        enc_final[7],
        dec_final[0],
        dec_final[1],
        dec_final[2],
        dec_final[3],
        dec_final[4],
        dec_final[5],
        dec_final[6],
        dec_final[7],
        dec_final[8],
        dec_final[9],
    )


def solution(mesh):
    placed = (
        P(("stream", "dp"), None),
        P(None, ("stream", "dp"), None),
        P(None, ("stream", "dp"), None),
        P("dp"),
        P("dp", None),
        P(),
        P(None, "dp", None),
        P("dp", None),
        P("dp", None),
        P("dp", None),
        P("dp"),
        P(None, "dp"),
        P(None, "dp"),
        P(None, "dp"),
        P(None, "dp", None),
        P("dp", None),
        P("dp", None),
        P("dp"),
        P("dp", None),
        P("dp", None),
        P("dp"),
        P(None, "dp"),
        P(None, "dp"),
        P(None, "dp"),
    )
    return jax.shard_map(
        per_device,
        mesh=mesh,
        in_specs=placed,
        out_specs=(
            P(None, ("stream", "dp"), None),
            P(("stream", "dp"), None),
            P(None, ("stream", "dp"), None),
            P(None, "dp", None),
            P("dp", None),
            P("dp", None),
            P("dp", None),
            P("dp"),
            P(None, "dp"),
            P(None, "dp"),
            P(None, "dp"),
            P(None, "dp", None),
            P("dp", None),
            P("dp", None),
            P("dp"),
            P("dp", None),
            P("dp", None),
            P("dp"),
            P(None, "dp"),
            P(None, "dp"),
            P(None, "dp"),
        ),
        check_vma=False,
    )
```

profile of v0, /device:TPU:1, one launch (start us, length us, event | category | flops | bytes accessed | tf_op | source)
XLA Modules:
  0.0 3053.1 jit_solution(11035386252438517870)
XLA Ops:
  8.0 102.9 %all-gather.16.cloned.1.call-done = bf16[3,1024,1024]{2,1,0:T(8,128)(2,1)} async-done(((bf16[3,128,1024]{2,1,0:T(8,128)(2,1)}), bf16[3,1024,1024]{2,1,0:T(8,128)(2,1)}) %all-gather.16.cloned.1.call-update) | async-done | bytes 6291472 | tf_op jit(solution)/shard_map/all_gather | solution.py:256
  113.8 14.7 all_gather.67
  135.5 13.1 all_gather.71
  148.6 14.5 all_gather.72
  163.2 22.0 all-gather
  201.7 123.7 %all-gather.24.cloned.1.call-done = bf16[1024,4096]{1,0:T(8,128)(2,1)} async-done(((bf16[128,4096]{1,0:T(8,128)(2,1)}), bf16[1024,4096]{1,0:T(8,128)(2,1)}) %all-gather.24.cloned.1.call-update) | async-done | bytes 8388624 | tf_op jit(solution)/shard_map/all_gather | solution.py:258
  325.5 9.4 multiply_convert_fusion.9
  334.9 115.7 %all-gather.26.cloned.1.call-done = bf16[4096,1024]{1,0:T(8,128)(2,1)} async-done(((bf16[512,1024]{1,0:T(8,128)(2,1)}), bf16[4096,1024]{1,0:T(8,128)(2,1)}) %all-gather.26.cloned.1.call-update) | async-done | bytes 8388624 | tf_op jit(solution)/shard_map/all_gather | solution.py:259
  455.9 94.0 %all-gather.28.cloned.1.call-done = bf16[3,1024,1024]{2,1,0:T(8,128)(2,1)} async-done(((bf16[3,128,1024]{2,1,0:T(8,128)(2,1)}), bf16[3,1024,1024]{2,1,0:T(8,128)(2,1)}) %all-gather.28.cloned.1.call-update) | async-done | bytes 6291472 | tf_op jit(solution)/shard_map/all_gather | solution.py:275
  552.7 14.7 all_gather.77
  574.7 14.0 all-reduce
  589.5 408.2 %gather_fusion = s32[65536]{0:T(1024)S(1)} fusion(s32[512]{0:T(512)S(1)} %copy-done, s32[65536]{0:T(1024)S(1)} %broadcast_clamp_fusion), kind=kCustom, calls=%fused_computation | custom fusion | bytes 786432 | tf_op jit(solution)/shard_map/gather | solution.py:252
  997.9 21.4 all-gather.1
  1019.9 13.9 all_gather.83
  1033.8 12.9 all_gather.84
  1105.6 11.1 copy.235
  1151.0 9.4 multiply_convert_fusion.8
  1169.4 9.2 multiply_convert_fusion.7
  1183.4 8.9 multiply_convert_fusion.6
  1280.6 8.6 fusion.118
  1308.0 14.3 reduce-scatter.38.cloned.1.call-done
  1324.8 24.9 reduce-scatter.40.cloned.1.call-done
  1355.4 8.2 fusion.229
  1394.0 13.4 reduce-scatter.58.cloned.1.call-done
  1410.4 25.1 reduce-scatter.60.cloned.1.call-done
  1441.9 14.4 copy.280
  1456.3 10.1 copy.296
  1520.1 8.2 fusion.269
  1528.3 15.6 add_convert_fusion
  1545.0 9.6 fusion.213
  1554.7 8.2 fusion.216
  1562.9 15.9 add_convert_fusion.1
  1616.2 33.2 %reduce-scatter.52.cloned.1.call-done = bf16[128,512]{1,0:T(8,128)(2,1)} async-done(((bf16[1024,512]{1,0:T(8,128)(2,1)}), bf16[128,512]{1,0:T(8,128)(2,1)}) %reduce-scatter.52.cloned.1.call-update) | async-done | bytes 131088 | tf_op jit(solution)/shard_map/reduce_scatter | solution.py:492
  1649.4 71.0 %reduce-scatter.50.cloned.1.call-done = bf16[128,1024]{1,0:T(8,128)(2,1)} async-done(((bf16[1024,1024]{1,0:T(8,128)(2,1)}), bf16[128,1024]{1,0:T(8,128)(2,1)}) %reduce-scatter.50.cloned.1.call-update) | async-done | bytes 262160 | tf_op jit(solution)/shard_map/reduce_scatter | solution.py:489
  1720.4 71.6 %reduce-scatter.42.cloned.1.call-done = bf16[128,1024]{1,0:T(8,128)(2,1)} async-done(((bf16[1024,1024]{1,0:T(8,128)(2,1)}), bf16[128,1024]{1,0:T(8,128)(2,1)}) %reduce-scatter.42.cloned.1.call-update) | async-done | bytes 262160 | tf_op jit(solution)/shard_map/reduce_scatter | solution.py:465
  1792.1 121.8 %reduce-scatter.48.cloned.1.call-done = bf16[3,128,1024]{2,1,0:T(8,128)(2,1)} async-done(((bf16[3,1024,1024]{2,1,0:T(8,128)(2,1)}), bf16[3,128,1024]{2,1,0:T(8,128)(2,1)}) %reduce-scatter.48.cloned.1.call-update) | async-done | bytes 786448 | tf_op jit(solution)/shard_map/reduce_scatter | solution.py:486
  1913.9 153.1 %reduce-scatter.56.cloned.1.call-done = bf16[512,1024]{1,0:T(8,128)(2,1)} async-done(((bf16[4096,1024]{1,0:T(8,128)(2,1)}), bf16[512,1024]{1,0:T(8,128)(2,1)}) %reduce-scatter.56.cloned.1.call-update) | async-done | bytes 1048592 | tf_op jit(solution)/shard_map/reduce_scatter | solution.py:501
  2067.0 151.5 %reduce-scatter.54.cloned.1.call-done = bf16[128,4096]{1,0:T(8,128)(2,1)} async-done(((bf16[1024,4096]{1,0:T(8,128)(2,1)}), bf16[128,4096]{1,0:T(8,128)(2,1)}) %reduce-scatter.54.cloned.1.call-update) | async-done | bytes 1048592 | tf_op jit(solution)/shard_map/reduce_scatter | solution.py:498
  2218.5 152.1 %reduce-scatter.44.cloned.1.call-done = bf16[128,4096]{1,0:T(8,128)(2,1)} async-done(((bf16[1024,4096]{1,0:T(8,128)(2,1)}), bf16[128,4096]{1,0:T(8,128)(2,1)}) %reduce-scatter.44.cloned.1.call-update) | async-done | bytes 1048592 | tf_op jit(solution)/shard_map/reduce_scatter | solution.py:468
  2370.7 151.5 %reduce-scatter.46.cloned.1.call-done = bf16[512,1024]{1,0:T(8,128)(2,1)} async-done(((bf16[4096,1024]{1,0:T(8,128)(2,1)}), bf16[512,1024]{1,0:T(8,128)(2,1)}) %reduce-scatter.46.cloned.1.call-update) | async-done | bytes 1048592 | tf_op jit(solution)/shard_map/reduce_scatter | solution.py:471
  2534.4 49.7 %reduce-scatter.72.cloned.1.call-done = bf16[128,2]{1,0:T(8,128)(2,1)} async-done(((bf16[1024,2]{1,0:T(8,128)(2,1)}), bf16[128,2]{1,0:T(8,128)(2,1)}) %reduce-scatter.72.cloned.1.call-update) | async-done | bytes 528
  2584.8 63.1 %reduce-scatter.74.cloned.1.call-done = bf16[128,2]{1,0:T(8,128)(2,1)} async-done(((bf16[1024,2]{1,0:T(8,128)(2,1)}), bf16[128,2]{1,0:T(8,128)(2,1)}) %reduce-scatter.74.cloned.1.call-update) | async-done | bytes 528
  2648.8 28.2 all-reduce.4
  2679.7 32.8 %reduce-scatter.66.cloned.1.call-done = bf16[128,2]{1,0:T(8,128)(2,1)} async-done(((bf16[1024,2]{1,0:T(8,128)(2,1)}), bf16[128,2]{1,0:T(8,128)(2,1)}) %reduce-scatter.66.cloned.1.call-update) | async-done | bytes 528
  2713.4 63.5 %reduce-scatter.68.cloned.1.call-done = bf16[128,2]{1,0:T(8,128)(2,1)} async-done(((bf16[1024,2]{1,0:T(8,128)(2,1)}), bf16[128,2]{1,0:T(8,128)(2,1)}) %reduce-scatter.68.cloned.1.call-update) | async-done | bytes 528
  2777.7 63.2 %reduce-scatter.70.cloned.1.call-done = bf16[128,4]{1,0:T(8,128)(2,1)} async-done(((bf16[1024,4]{1,0:T(8,128)(2,1)}), bf16[128,4]{1,0:T(8,128)(2,1)}) %reduce-scatter.70.cloned.1.call-update) | async-done | bytes 1040
  2847.4 58.1 %reduce-scatter.64.cloned.1.call-done = bf16[128,4]{1,0:T(8,128)(2,1)} async-done(((bf16[1024,4]{1,0:T(8,128)(2,1)}), bf16[128,4]{1,0:T(8,128)(2,1)}) %reduce-scatter.64.cloned.1.call-update) | async-done | bytes 1040
  2919.1 114.0 %all-reduce.9.cloned.1.call-done = (bf16[3,128,1024]{1,2,0:T(8,128)(2,1)}, bf16[128,1024]{1,0:T(8,128)(2,1)}, bf16[128,4096]{1,0:T(8,128)(2,1)}, bf16[512,1024]{...) async-done(((bf16[3,128,1024]{1,2,0:T(8,128)(2,1)}, ...) | async-done | bytes 6422544 | tf_op jit(solution)/shard_map/psum | solution.py:518
  (948 shorter events, 442.8 us)
Async XLA Ops:
  7.2 103.6 %all-gather.16.cloned.1.call-start = ((), (), s32[]{:S(2)}) async-start(), calls=%async_computation.19 | async-start | bytes 7077888 | tf_op jit(solution)/shard_map/all_gather | solution.py:256
  7.9 180.1 %all-gather.20.cloned.1.call-start = ((), (), s32[]{:S(2)}) async-start(), calls=%async_computation.21 | async-start | bytes 1310720 | tf_op jit(solution)/shard_map/all_gather | solution.py:267
  113.7 79.4 %all-gather.18.cloned.1.call-start = ((), (), s32[]{:S(2)}) async-start(), calls=%async_computation.20 | async-start | bytes 1310720 | tf_op jit(solution)/shard_map/all_gather | solution.py:268
  131.3 68.1 %all-gather.22.cloned.1.call-start = ((), (), s32[]{:S(2)}) async-start(), calls=%async_computation.22 | async-start | bytes 2359296 | tf_op jit(solution)/shard_map/all_gather | solution.py:257
  131.9 193.6 %all-gather.24.cloned.1.call-start = ((), (), s32[]{:S(2)}) async-start(), calls=%async_computation.23 | async-start | bytes 9437184 | tf_op jit(solution)/shard_map/all_gather | solution.py:258
  132.4 318.1 %all-gather.26.cloned.1.call-start = ((), (), s32[]{:S(2)}) async-start(), calls=%async_computation.24 | async-start | bytes 9437184 | tf_op jit(solution)/shard_map/all_gather | solution.py:259
  133.0 416.9 %all-gather.28.cloned.1.call-start = ((), (), s32[]{:S(2)}) async-start(), calls=%async_computation.25 | async-start | bytes 7077888 | tf_op jit(solution)/shard_map/all_gather | solution.py:275
  133.8 915.3 %all-gather.34.cloned.1.call-start = ((), (), s32[]{:S(2)}) async-start(), calls=%async_computation.28 | async-start | bytes 1179648 | tf_op jit(solution)/shard_map/all_gather | solution.py:277
  134.5 969.6 %all-gather.32.cloned.1.call-start = ((), (), s32[]{:S(2)}) async-start(), calls=%async_computation.27 | async-start | bytes 1310720 | tf_op jit(solution)/shard_map/all_gather | solution.py:301
  148.6 302.0 %copy-start.155 = (f32[1,1024]{1,0:T(1,128)}, f32[1,1024]{1,0:T(1,128)S(1)}, u32[]{:S(2)}) copy-start(f32[1,1024]{1,0:T(1,128)S(1)} %get-tuple-element.267) | copy-start | bytes 12292
  148.6 984.6 %copy-start.162 = (f32[1,1024]{1,0:T(1,128)}, f32[1,1024]{1,0:T(1,128)S(1)}, u32[]{:S(2)}) copy-start(f32[1,1024]{1,0:T(1,128)S(1)} %get-tuple-element.266) | copy-start | bytes 12292
  163.2 287.4 %copy-start.157 = (f32[1,1024]{1,0:T(1,128)}, f32[1,1024]{1,0:T(1,128)S(1)}, u32[]{:S(2)}) copy-start(f32[1,1024]{1,0:T(1,128)S(1)} %get-tuple-element.269) | copy-start | bytes 12292
  163.2 292.5 %copy-start.171 = (f32[1,1024]{1,0:T(1,128)}, f32[1,1024]{1,0:T(1,128)S(1)}, u32[]{:S(2)}) copy-start(f32[1,1024]{1,0:T(1,128)S(1)} %get-tuple-element.268) | copy-start | bytes 12292
  201.5 249.1 %copy-start.12 = (f32[128,1024]{1,0:T(8,128)}, f32[128,1024]{1,0:T(8,128)S(1)}, u32[]{:S(2)}) copy-start(f32[128,1024]{1,0:T(8,128)S(1)} %get-tuple-element.276) | copy-start | bytes 1572868
  201.5 249.1 %copy-start.186 = (f32[128]{0:T(128)}, f32[128]{0:T(128)S(1)}, u32[]{:S(2)}) copy-start(f32[128]{0:T(128)S(1)} %broadcast_multiply_fusion.7) | copy-start | bytes 1540
  201.7 248.9 %copy-start.220 = (f32[128]{0:T(128)}, f32[128]{0:T(128)S(1)}, u32[]{:S(2)}) copy-start(f32[128]{0:T(128)S(1)} %fusion.197) | copy-start | bytes 1540
  455.4 677.8 %copy-start.16 = (f32[128,1024]{1,0:T(8,128)}, f32[128,1024]{1,0:T(8,128)S(1)}, u32[]{:S(2)}) copy-start(f32[128,1024]{1,0:T(8,128)S(1)} %get-tuple-element.279) | copy-start | bytes 1572868
  552.7 552.9 %all-gather.30.cloned.1.call-start = ((), (), s32[]{:S(2)}) async-start(), calls=%async_computation.26 | async-start | bytes 1310720 | tf_op jit(solution)/shard_map/all_gather | solution.py:302
  570.8 562.4 %all-gather.36.cloned.1.call-start = ((), (), s32[]{:S(2)}) async-start(), calls=%async_computation.29 | async-start | bytes 2359296 | tf_op jit(solution)/shard_map/all_gather | solution.py:276
  571.6 579.4 %all-gather.38.cloned.1.call-start = ((), (), s32[]{:S(2)}) async-start(), calls=%async_computation.30 | async-start | bytes 9437184 | tf_op jit(solution)/shard_map/all_gather | solution.py:279
  572.1 588.3 %all-gather.40.cloned.1.call-start = ((), (), s32[]{:S(2)}) async-start(), calls=%async_computation.31 | async-start | bytes 9437184 | tf_op jit(solution)/shard_map/all_gather | solution.py:280
  572.9 749.4 %reduce-scatter.38.cloned.1.call-start = ((), (), s32[]{:S(2)}) async-start(), calls=%async_computation.32 | async-start | bytes 1310720 | tf_op jit(solution)/shard_map/reduce_scatter | solution.py:369
  588.7 460.3 %copy-start.176 = (f32[512]{0:T(512)}, f32[512]{0:T(512)S(1)}, u32[]{:S(2)}) copy-start(f32[512]{0:T(512)S(1)} %convert_element_type.650) | copy-start | bytes 6148
  589.5 408.4 %copy-start.254 = (bf16[512]{0:T(512)(128)(2,1)S(1)}, bf16[512]{0:T(512)(128)(2,1)}, u32[]{:S(2)}) copy-start(bf16[512]{0:T(512)(128)(2,1)} %param.44) | copy-start | bytes 3076
  589.5 430.4 %copy-start.259 = (bf16[2,128]{1,0:T(2,128)(2,1)S(1)}, bf16[2,128]{1,0:T(2,128)(2,1)}, u32[]{:S(2)}) copy-start(bf16[2,128]{1,0:T(2,128)(2,1)} %param.46) | copy-start | bytes 1540
  589.5 444.3 %copy-start.260 = (bf16[2,128]{1,0:T(2,128)(2,1)S(1)}, bf16[2,128]{1,0:T(2,128)(2,1)}, u32[]{:S(2)}) copy-start(bf16[2,128]{1,0:T(2,128)(2,1)} %param.47) | copy-start | bytes 1540
  589.5 459.5 %copy-start.53 = (bf16[2,128,1024]{2,1,0:T(8,128)(2,1)S(1)}, bf16[2,128,1024]{2,1,0:T(8,128)(2,1)}, u32[]{:S(2)}) copy-start(bf16[2,128,1024]{2,1,0:T(8,128)(2,1)} %param.25) | copy-start | bytes 1572868
  1048.4 185.7 %copy-start.140 = (f32[1,1024]{1,0:T(1,128)}, f32[1,1024]{1,0:T(1,128)S(1)}, u32[]{:S(2)}) copy-start(f32[1,1024]{1,0:T(1,128)S(1)} %get-tuple-element.263) | copy-start | bytes 12292
  1280.5 69.2 %reduce-scatter.40.cloned.1.call-start = ((), (), s32[]{:S(2)}) async-start(), calls=%async_computation.33 | async-start | bytes 1310720 | tf_op jit(solution)/shard_map/reduce_scatter | solution.py:372
  1297.9 109.5 %reduce-scatter.58.cloned.1.call-start = ((), (), s32[]{:S(2)}) async-start(), calls=%async_computation.42 | async-start | bytes 1310720
  1382.3 53.2 %reduce-scatter.60.cloned.1.call-start = ((), (), s32[]{:S(2)}) async-start(), calls=%async_computation.43 | async-start | bytes 1310720
  1388.4 223.6 %reduce-scatter.62.cloned.1.call-start = ((), (), s32[]{:S(2)}) async-start(), calls=%async_computation.44 | async-start | bytes 7077888
  1466.4 183.0 %reduce-scatter.52.cloned.1.call-start = ((), (), s32[]{:S(2)}) async-start(), calls=%async_computation.39 | async-start | bytes 1179648 | tf_op jit(solution)/shard_map/reduce_scatter | solution.py:492
  1485.1 235.3 %reduce-scatter.50.cloned.1.call-start = ((), (), s32[]{:S(2)}) async-start(), calls=%async_computation.38 | async-start | bytes 2359296 | tf_op jit(solution)/shard_map/reduce_scatter | solution.py:489
  1489.2 302.8 %reduce-scatter.42.cloned.1.call-start = ((), (), s32[]{:S(2)}) async-start(), calls=%async_computation.34 | async-start | bytes 2359296 | tf_op jit(solution)/shard_map/reduce_scatter | solution.py:465
  1492.3 421.6 %reduce-scatter.48.cloned.1.call-start = ((), (), s32[]{:S(2)}) async-start(), calls=%async_computation.37 | async-start | bytes 7077888 | tf_op jit(solution)/shard_map/reduce_scatter | solution.py:486
  1510.7 556.3 %reduce-scatter.56.cloned.1.call-start = ((), (), s32[]{:S(2)}) async-start(), calls=%async_computation.41 | async-start | bytes 9437184 | tf_op jit(solution)/shard_map/reduce_scatter | solution.py:501
  1544.0 674.5 %reduce-scatter.54.cloned.1.call-start = ((), (), s32[]{:S(2)}) async-start(), calls=%async_computation.40 | async-start | bytes 9437184 | tf_op jit(solution)/shard_map/reduce_scatter | solution.py:498
  1578.9 791.8 %reduce-scatter.44.cloned.1.call-start = ((), (), s32[]{:S(2)}) async-start(), calls=%async_computation.35 | async-start | bytes 9437184 | tf_op jit(solution)/shard_map/reduce_scatter | solution.py:468
  1585.9 936.2 %reduce-scatter.46.cloned.1.call-start = ((), (), s32[]{:S(2)}) async-start(), calls=%async_computation.36 | async-start | bytes 9437184 | tf_op jit(solution)/shard_map/reduce_scatter | solution.py:471
  1593.1 991.0 %reduce-scatter.72.cloned.1.call-start = ((), (), s32[]{:S(2)}) async-start(), calls=%async_computation.49 | async-start | bytes 294912
  1595.8 1052.2 %reduce-scatter.74.cloned.1.call-start = ((), (), s32[]{:S(2)}) async-start(), calls=%async_computation.50 | async-start | bytes 294912
  1597.0 1115.5 %reduce-scatter.66.cloned.1.call-start = ((), (), s32[]{:S(2)}) async-start(), calls=%async_computation.46 | async-start | bytes 294912
  1603.5 1173.4 %reduce-scatter.68.cloned.1.call-start = ((), (), s32[]{:S(2)}) async-start(), calls=%async_computation.47 | async-start | bytes 294912
  1605.3 1235.6 %reduce-scatter.70.cloned.1.call-start = ((), (), s32[]{:S(2)}) async-start(), calls=%async_computation.48 | async-start | bytes 294912
  1607.6 1297.9 %reduce-scatter.64.cloned.1.call-start = ((), (), s32[]{:S(2)}) async-start(), calls=%async_computation.45 | async-start | bytes 294912
  1608.7 1424.4 %all-reduce.9.cloned.1.call-start = ((), (), s32[]{:S(2)}) async-start(), calls=%async_computation.51 | async-start | bytes 12845056 | tf_op jit(solution)/shard_map/psum | solution.py:518
  2534.3 307.4 %copy-start.100 = (bf16[128,1024]{1,0:T(8,128)(2,1)S(1)}, bf16[128,1024]{1,0:T(8,128)(2,1)}, u32[]{:S(2)}) copy-start(bf16[128,1024]{1,0:T(8,128)(2,1)} %reduce-scatter.60.cloned.1.call-done) | copy-start | bytes 786436
  (263 other events, 3947.7 us)
Sparse Core Ops, SparseCore 0:
  10.2 100.5 all-gather.15
  113.8 15.8 all-gather.19
  131.8 17.4 all-gather.17
  151.3 47.9 all-gather.21
  201.3 124.1 all-gather.23
  327.4 123.1 all-gather.25
  452.8 97.0 all-gather.27
  552.0 38.0 all-gather.33
  592.3 16.9 all-gather.31
  611.3 16.7 all-gather.29
  630.1 47.7 all-gather.35
  680.0 124.2 all-gather.37
  806.4 123.0 all-gather.39
  1280.6 41.5 reduce-scatter.37
  1324.8 24.8 reduce-scatter.39
  1382.5 24.9 reduce-scatter.57
  1410.5 24.9 reduce-scatter.59
  1466.5 117.1 reduce-scatter.61
  1587.7 61.6 reduce-scatter.51
  1653.8 66.5 reduce-scatter.49
  1724.9 67.0 reduce-scatter.41
  1796.1 117.7 reduce-scatter.47
  1918.0 148.9 reduce-scatter.55
  2070.5 148.0 reduce-scatter.53
  2222.6 148.0 reduce-scatter.43
  2374.1 147.9 reduce-scatter.45
  2525.7 58.2 reduce-scatter.71
  2587.7 60.2 reduce-scatter.73
  2652.2 60.2 reduce-scatter.65
  2716.6 60.2 reduce-scatter.67
  2780.6 60.2 reduce-scatter.69
  2845.2 60.2 reduce-scatter.63
  2909.2 123.8 all-reduce.8
where the time goes:
time: 3070 us; the launch traced here: 3050 us
  waiting for transfers between devices  1870 us (61%)
  local copies, waits for them, and re-layouts  537 us (17%)
  matrix products  378 us (12%)
  blocking collectives  177 us (6%)
  other arithmetic  65.1 us (2%)
    gather x2, local copies, waits for them, and re-layouts, per_device(): rel_table[distance][:, :, None] == bucket_ids[None, None, :]  408 us
    unnamed x42, waiting for transfers between devices  375 us
    reduce_scatter x1, waiting for transfers between devices, per_device(): lax.psum_scatter(dec_back_part.astype(jnp.bfloat16), 'dp', scatter_dimens...  153 us
    reduce_scatter x1, waiting for transfers between devices, per_device(): lax.psum_scatter(enc_tail[1].astype(jnp.bfloat16), 'dp', scatter_dimensio...  152 us
    reduce_scatter x1, waiting for transfers between devices, per_device(): lax.psum_scatter(dec_in_part.astype(jnp.bfloat16), 'dp', scatter_dimensio...  152 us
    reduce_scatter x1, waiting for transfers between devices, per_device(): lax.psum_scatter(enc_tail[2].astype(jnp.bfloat16), 'dp', scatter_dimensio...  152 us
    all_gather x1, waiting for transfers between devices, per_device(): lax.all_gather(enc_ffn_in, 'dp', axis=0, tiled=True)  124 us
    reduce_scatter x1, waiting for transfers between devices, per_device(): lax.psum_scatter(dec_qkv_part.astype(jnp.bfloat16), 'dp', scatter_dimensi...  122 us
  transfers between devices with their start and end apart: 33, of which 24 were waited for; matrix products, arithmetic and copies ran while one was open for 25% of the time, Pallas kernels for 0%

commit v1 on v0

v1 whole, which is shorter than its diff:
```python
from functools import partial

import jax
import jax.numpy as jnp
from jax import lax
from jax.experimental import pallas as pl
from jax.experimental.pallas import tpu as pltpu
from jax.sharding import PartitionSpec as P

H = 16
NB = 32
HD = 64
EPSILON = 1e-05
MASKED = -1000000000.0
BF = jnp.bfloat16
F32 = jnp.float32
TILE = 128
STREAMS = 4
XOR = (0, 2, 1, 3)
VMEM_LIMIT = 60 * 1024 * 1024


def dot(a, b):
    return jnp.dot(a, b, preferred_element_type=F32)


def dot_nt(a, b):
    return lax.dot_general(a, b, (((1,), (1,)), ((), ())), preferred_element_type=F32)


def dot_tn(a, b):
    return lax.dot_general(a, b, (((0,), (0,)), ((), ())), preferred_element_type=F32)


def swap(values, bit):
    return lax.ppermute(values, "stream", [(i, i ^ bit) for i in range(STREAMS)])


def gather_rows(rows):
    far = swap(rows, 2)
    half = jnp.concatenate([rows, far], axis=0)
    return jnp.concatenate([half, swap(half, 1)], axis=0)


def scatter_rows(partials):
    n = partials.shape[0] // 4
    near = swap(partials[2 * n :].astype(BF), 1)
    keep = partials[: 2 * n].astype(F32) + near.astype(F32)
    far = swap(keep[n:].astype(BF), 2)
    return keep[:n] + far.astype(F32)


def turn_blocks(blocks):
    far = swap(jnp.stack([blocks[1], blocks[3]]), 2)
    near = swap(jnp.stack([blocks[2], far[1]]), 1)
    return [blocks[0], far[0], near[0], near[1]]


def by_absolute(blocks, here):
    stacked = jnp.stack([blocks[XOR.index(j)] for j in range(4)])
    return [lax.dynamic_index_in_dim(stacked, here ^ a, 0, keepdims=False) for a in range(4)]


def ring_order(n):
    return list(range(0, n, 2)) + list(range(n - 1, 0, -2))


def ring_member(place, n):
    place = lax.rem(place + 2 * n, n)
    return jnp.where(place < n // 2, 2 * place, 2 * (n - place) - 1)


def ring_place(g, n):
    return jnp.where(g % 2 == 0, g // 2, n - (g + 1) // 2)


def ring_step(values, n, step):
    order = ring_order(n)
    pairs = [(order[i], order[(i + step) % n]) for i in range(n)]
    return lax.ppermute(values, "dp", pairs)


def ring_pieces(own, n):
    rows = own.shape[0]
    pieces = [(0, 0, own)]
    ahead = back = own
    for k in range(1, n // 2):
        ahead = ring_step(ahead, n, 1)
        back = ring_step(back, n, -1)
        pieces += [(k, 0, ahead), (n - k, 0, back)]
    half = halved(rows)
    top = ring_step(ahead[:half], n, 1)
    bottom = ring_step(back[half:], n, -1)
    pieces += [(n // 2, 0, top), (n // 2, half, bottom)]
    return pieces


def assemble(pieces, index, regions, shapes, n):
    moves = []
    for number, (behind, first, piece) in enumerate(pieces):
        last = first + piece.shape[0]
        for r0, r1, c0, c1, which, to_row, to_col in regions:
            lo, hi = max(r0, first), min(r1, last)
            if lo < hi:
                moves.append((number, behind, lo - first, hi - first, c0, c1, which, to_row + lo - r0, to_col))

    def kernel(index_ref, *refs):
        sources = refs[: len(pieces)]
        outs = refs[len(pieces) :]
        for number, behind, lo, hi, c0, c1, which, row, col in moves:
            g = index_ref[behind]
            outs[which][g, row : row + hi - lo, col : col + c1 - c0] = sources[number][lo:hi, c0:c1]

    vmem = pl.BlockSpec(memory_space=pltpu.VMEM)
    return pl.pallas_call(
        kernel,
        out_shape=[jax.ShapeDtypeStruct((n,) + shape, BF) for shape in shapes],
        in_specs=[pl.BlockSpec(memory_space=pltpu.SMEM)] + [vmem] * len(pieces),
        out_specs=[vmem] * len(shapes),
        compiler_params=pltpu.CompilerParams(vmem_limit_bytes=VMEM_LIMIT),
    )(index, *[piece for _, _, piece in pieces])


def halved(rows):
    return rows // 32 * 16


def ring_sum(arrays, n, place):
    def part(ahead):
        g = ring_member(place + ahead, n)
        return jnp.concatenate(
            [lax.dynamic_index_in_dim(a, g, 0, keepdims=False) for a in arrays], axis=0
        ).astype(F32)

    middle = part(n // 2)
    half = halved(middle.shape[0])
    up = ring_step(middle[:half].astype(BF), n, 1).astype(F32)
    down = ring_step(middle[half:].astype(BF), n, -1).astype(F32)
    for k in range(n // 2 - 1, 0, -1):
        ahead, back = part(k), part(-k)
        if k == n // 2 - 1:
            ahead = jnp.concatenate([ahead[:half] + up, ahead[half:]], axis=0)
            back = jnp.concatenate([back[:half], back[half:] + down], axis=0)
        else:
            ahead, back = ahead + up, back + down
        up = ring_step(ahead.astype(BF), n, 1).astype(F32)
        down = ring_step(back.astype(BF), n, -1).astype(F32)
    return part(0) + up + down


def tile_width(t, causal, total):
    return TILE * (t + 1) if causal else total


def head_mask(e):
    lane = lax.broadcasted_iota(jnp.int32, (1, TILE), 1)
    return ((lane // HD) == e).astype(F32)


def rel_mask(h):
    lane = lax.broadcasted_iota(jnp.int32, (1, TILE), 1)
    return ((lane // NB) == h).astype(F32)


def allowed_keys(t, width, meta, causal, strict):
    bucket = meta[8]
    shape = (TILE, width)
    row = lax.broadcasted_iota(jnp.int32, shape, 0) + t * TILE
    col = lax.broadcasted_iota(jnp.int32, shape, 1)
    pos = col & (bucket - 1)
    first = col < bucket
    limit = bucket - jnp.where(first, meta[9], meta[10])
    allowed = (pos < limit) & ((row < bucket) == first)
    if causal:
        allowed = allowed & ((col < row) if strict else (col <= row))
    return allowed


def load_rows(meta, target, source, c0, c1):
    for chunk in range(8):
        start = pl.multiple_of(meta[chunk], 64)
        target[pl.ds(start, 64), :] = source[chunk * 64 : chunk * 64 + 64, c0:c1]


def store_rows(meta, target, source, c0, c1):
    for chunk in range(8):
        start = pl.multiple_of(meta[chunk], 64)
        target[chunk * 64 : chunk * 64 + 64, c0:c1] = source[pl.ds(start, 64), :].astype(target.dtype)


def rel_bias(rel_rows, h, table):
    high = rel_rows.astype(BF)
    rest = (rel_rows - high.astype(F32)).astype(BF)
    mask = rel_mask(h)
    both = jnp.concatenate(
        [(high.astype(F32) * mask).astype(BF), (rest.astype(F32) * mask).astype(BF)], axis=1
    )
    spread = dot(both, table)
    return pltpu.roll(spread, 0, 1, stride=1, stride_axis=0)


def scores_of(t, h, width, meta, qs, ks, rs, table_ref, causal, strict):
    pair, e = h // 2, h % 2
    lanes = slice(TILE * pair, TILE * (pair + 1))
    rows = slice(TILE * t, TILE * (t + 1))
    query = (qs[rows, lanes].astype(F32) * (head_mask(e) * HD**-0.5)).astype(BF)
    scores = dot_nt(query, ks[0:width, lanes])
    if rs is not None:
        first = sum(TILE * (u + 1) for u in range(t))
        scores = scores + rel_bias(rs[rows, :], h, table_ref[:, first : first + width])
    return query, jnp.where(allowed_keys(t, width, meta, causal, strict), scores, MASKED)


def attention_forward(meta, qkv, main=None, rel=None, tables=None):
    total = qkv.shape[0]
    width_all = qkv.shape[1] // 3
    heads = width_all // HD
    causal = rel is not None
    own = main is not None

    def kernel(meta_ref, *refs):
        refs = list(refs)
        qkv_ref = refs.pop(0)
        main_ref = refs.pop(0) if own else qkv_ref
        rel_ref, table_ref, hot_ref = (refs.pop(0), refs.pop(0), refs.pop(0)) if causal else (None,) * 3
        ctx_ref, lse_ref, qs, ks, vs, cs = refs[:6]
        refs = refs[6:]
        rs = refs.pop(0) if causal else None
        load_rows(meta_ref, qs, qkv_ref, 0, width_all)
        load_rows(meta_ref, ks, main_ref, width_all, 2 * width_all)
        load_rows(meta_ref, vs, main_ref, 2 * width_all, 3 * width_all)
        if causal:
            load_rows(meta_ref, rs, rel_ref, 0, rel.shape[1])
        if own:
            kn, vn = refs
            load_rows(meta_ref, kn, qkv_ref, width_all, 2 * width_all)
            load_rows(meta_ref, vn, qkv_ref, 2 * width_all, 3 * width_all)
        for t in range(total // TILE):
            rows = slice(TILE * t, TILE * (t + 1))
            width = tile_width(t, causal, total)
            lse_lane = lax.broadcasted_iota(jnp.int32, (TILE, TILE), 1)
            lse = jnp.zeros((TILE, TILE), F32)
            for pair in range(heads // 2):
                lanes = slice(TILE * pair, TILE * (pair + 1))
                context = jnp.zeros((TILE, TILE), F32)
                for e in range(2):
                    h = 2 * pair + e
                    query, scores = scores_of(t, h, width, meta_ref, qs, ks, rs, table_ref, causal, own)
                    top = jnp.max(scores, axis=1, keepdims=True)
                    if own:
                        own_score = jnp.sum(
                            query.astype(F32) * kn[rows, lanes].astype(F32), axis=1, keepdims=True
                        ) + jnp.sum(rs[rows, :] * (hot_ref[...] * rel_mask(h)), axis=1, keepdims=True)
                        top = jnp.maximum(top, own_score)
                    expos = jnp.exp(scores - top)
                    sums = jnp.sum(expos, axis=1, keepdims=True)
                    if own:
                        own_expo = jnp.exp(own_score - top)
                        sums = sums + own_expo
                    inverse = 1.0 / sums
                    probs = (expos * inverse).astype(BF)
                    part = dot(probs, vs[0:width, lanes])
                    if own:
                        part = part + (own_expo * inverse) * vn[rows, lanes].astype(F32)
                    context = context + part * head_mask(e)
                    lse = jnp.where(lse_lane == h, top + jnp.log(sums), lse)
                cs[rows, lanes] = context.astype(BF)
            lse_ref[rows, :] = lse
        store_rows(meta_ref, ctx_ref, cs, 0, width_all)

    vmem = pl.BlockSpec(memory_space=pltpu.VMEM)
    args = [qkv]
    scratch = [pltpu.VMEM((total, width_all), BF) for _ in range(4)]
    if own:
        args.append(main)
    if causal:
        args += [rel, tables[0], tables[2]]
        scratch.append(pltpu.VMEM((total, rel.shape[1]), F32))
    if own:
        scratch += [pltpu.VMEM((total, width_all), BF) for _ in range(2)]
    return pl.pallas_call(
        kernel,
        out_shape=(
            jax.ShapeDtypeStruct((total, width_all), BF),
            jax.ShapeDtypeStruct((total, TILE), F32),
        ),
        in_specs=[pl.BlockSpec(memory_space=pltpu.SMEM)] + [vmem] * len(args),
        out_specs=(vmem, vmem),
        scratch_shapes=scratch,
        compiler_params=pltpu.CompilerParams(vmem_limit_bytes=VMEM_LIMIT),
    )(meta, *args)


def attention_backward(meta, qkv, dctx, lse, main=None, rel=None, tables=None):
    total = qkv.shape[0]
    width_all = qkv.shape[1] // 3
    heads = width_all // HD
    causal = rel is not None
    own = main is not None

    def kernel(meta_ref, *refs):
        refs = list(refs)
        qkv_ref, dctx_ref, lse_ref = refs[:3]
        refs = refs[3:]
        main_ref = refs.pop(0) if own else qkv_ref
        rel_ref, table_ref, back_ref, hot_ref, flip_ref = (
            [refs.pop(0) for _ in range(5)] if causal else (None,) * 5
        )
        dq_ref, dk_ref, dv_ref = refs[:3]
        refs = refs[3:]
        drel_ref = refs.pop(0) if causal else None
        dkn_ref, dvn_ref = (refs.pop(0), refs.pop(0)) if own else (None, None)
        qs, ks, vs, gs, dqs, dks, dvs = refs[:7]
        refs = refs[7:]
        rs, drs = (refs.pop(0), refs.pop(0)) if causal else (None, None)
        load_rows(meta_ref, qs, qkv_ref, 0, width_all)
        load_rows(meta_ref, ks, main_ref, width_all, 2 * width_all)
        load_rows(meta_ref, vs, main_ref, 2 * width_all, 3 * width_all)
        load_rows(meta_ref, gs, dctx_ref, 0, width_all)
        if causal:
            load_rows(meta_ref, rs, rel_ref, 0, rel.shape[1])
        if own:
            kn, vn, dkn, dvn = refs
            load_rows(meta_ref, kn, qkv_ref, width_all, 2 * width_all)
            load_rows(meta_ref, vn, qkv_ref, 2 * width_all, 3 * width_all)
        dks[...] = jnp.zeros_like(dks)
        dvs[...] = jnp.zeros_like(dvs)
        for t in range(total // TILE):
            rows = slice(TILE * t, TILE * (t + 1))
            width = tile_width(t, causal, total)
            first = sum(TILE * (u + 1) for u in range(t))
            drel = jnp.zeros((TILE, TILE), F32)
            for pair in range(heads // 2):
                lanes = slice(TILE * pair, TILE * (pair + 1))
                dq = jnp.zeros((TILE, TILE), F32)
                dkey_own = jnp.zeros((TILE, TILE), F32)
                dval_own = jnp.zeros((TILE, TILE), F32)
                for e in range(2):
                    h = 2 * pair + e
                    mask = head_mask(e)
                    query, scores = scores_of(t, h, width, meta_ref, qs, ks, rs, table_ref, causal, own)
                    norm = lse_ref[rows, h : h + 1]
                    probs = jnp.exp(scores - norm)
                    grad = (gs[rows, lanes].astype(F32) * mask).astype(BF)
                    dprobs = dot_nt(grad, vs[0:width, lanes])
                    rowdot = jnp.sum(probs * dprobs, axis=1, keepdims=True)
                    if own:
                        own_score = jnp.sum(
                            query.astype(F32) * kn[rows, lanes].astype(F32), axis=1, keepdims=True
                        ) + jnp.sum(rs[rows, :] * (hot_ref[...] * rel_mask(h)), axis=1, keepdims=True)
                        own_prob = jnp.exp(own_score - norm)
                        own_dprob = jnp.sum(
                            grad.astype(F32) * vn[rows, lanes].astype(F32), axis=1, keepdims=True
                        )
                        rowdot = rowdot + own_prob * own_dprob
                        own_dscore = (own_prob * (own_dprob - rowdot)).astype(BF).astype(F32)
                        dq = dq + own_dscore * kn[rows, lanes].astype(F32) * (mask * HD**-0.5)
                        dkey_own = dkey_own + own_dscore * query.astype(F32)
                        dval_own = dval_own + own_prob * grad.astype(F32)
                        drel = drel + own_dscore * (hot_ref[...] * rel_mask(h))
                    dscores = (probs * (dprobs - rowdot)).astype(BF)
                    dq = dq + dot(dscores, ks[0:width, lanes]) * (mask * HD**-0.5)
                    dks[0:width, lanes] += dot_tn(dscores, query)
                    dvs[0:width, lanes] += dot_tn(probs.astype(BF), grad)
                    if causal:
                        blocks = [
                            dot(dscores[:, TILE * b : TILE * (b + 1)], flip_ref[...])
                            for b in reversed(range(width // TILE))
                        ]
                        mirrored = jnp.concatenate(blocks, axis=1) if len(blocks) > 1 else blocks[0]
                        turned = pltpu.roll(mirrored, 0, 1, stride=1, stride_axis=0).astype(BF)
                        drel = drel + dot(turned, back_ref[first : first + width, :]) * rel_mask(h)
                dqs[rows, lanes] = dq
                if own:
                    dkn[rows, lanes] = dkey_own
                    dvn[rows, lanes] = dval_own
            if causal:
                drs[rows, :] = drel
        store_rows(meta_ref, dq_ref, dqs, 0, width_all)
        store_rows(meta_ref, dk_ref, dks, 0, width_all)
        store_rows(meta_ref, dv_ref, dvs, 0, width_all)
        if causal:
            store_rows(meta_ref, drel_ref, drs, 0, rel.shape[1])
        if own:
            store_rows(meta_ref, dkn_ref, dkn, 0, width_all)
            store_rows(meta_ref, dvn_ref, dvn, 0, width_all)

    vmem = pl.BlockSpec(memory_space=pltpu.VMEM)
    args = [qkv, dctx, lse]
    shape = (total, width_all)
    outs = [jax.ShapeDtypeStruct(shape, BF), jax.ShapeDtypeStruct(shape, F32), jax.ShapeDtypeStruct(shape, F32)]
    scratch = [pltpu.VMEM(shape, BF) for _ in range(4)] + [pltpu.VMEM(shape, F32) for _ in range(3)]
    if own:
        args.append(main)
    if causal:
        args += [rel, tables[0], tables[1], tables[2], tables[3]]
        outs.append(jax.ShapeDtypeStruct((total, rel.shape[1]), BF))
        scratch += [pltpu.VMEM((total, rel.shape[1]), F32) for _ in range(2)]
    if own:
        outs += [jax.ShapeDtypeStruct(shape, BF) for _ in range(2)]
        scratch += [pltpu.VMEM(shape, BF) for _ in range(2)] + [pltpu.VMEM(shape, F32) for _ in range(2)]
    return pl.pallas_call(
        kernel,
        out_shape=outs,
        in_specs=[pl.BlockSpec(memory_space=pltpu.SMEM)] + [vmem] * len(args),
        out_specs=[vmem] * len(outs),
        scratch_shapes=scratch,
        compiler_params=pltpu.CompilerParams(vmem_limit_bytes=VMEM_LIMIT),
    )(meta, *args)


def rel_tables(rel_table, total):
    ahead, back = [], []
    for t in range(total // TILE):
        width = TILE * (t + 1)
        here = rel_table[:width]
        ahead += [jnp.flip(here[: TILE * t + 1]), jnp.flip(here[TILE * t + 1 :])]
        back += [here[width - TILE + 1 :], here[: width - TILE + 1]]
    ahead, back = jnp.concatenate(ahead), jnp.concatenate(back)
    rows = jnp.arange(2 * TILE, dtype=jnp.int32) % NB
    forward = (rows[:, None] == ahead[None, :]).astype(BF)
    backward = (back[:, None] == rows[None, :TILE]).astype(BF)
    hot = (rows[None, :TILE] == rel_table[0]).astype(F32)
    ids = jnp.arange(TILE, dtype=jnp.int32)
    flip = (ids[:, None] + ids[None, :] == TILE - 1).astype(BF)
    return forward, backward, hot, flip


def norm_parts(values):
    center = values - jnp.mean(values, axis=-1, keepdims=True)
    spread = jnp.mean(center * center, axis=-1, keepdims=True)
    inverse = lax.rsqrt(spread + EPSILON)
    return center * inverse, inverse


def norm_back(grad, unit, inverse, gain):
    inner = grad * gain
    mean = jnp.mean(inner, axis=-1, keepdims=True)
    along = jnp.mean(inner * unit, axis=-1, keepdims=True)
    return inverse * (inner - mean - unit * along), jnp.sum(grad * unit, axis=0), jnp.sum(grad, axis=0)


def gelu(inner):
    return jax.nn.gelu(inner, approximate=False)


class Layer:
    pass


def own_columns(matrix, here):
    width = matrix.shape[-1] // STREAMS
    return lax.dynamic_slice_in_dim(matrix, here * width, width, axis=matrix.ndim - 1)


def forward_tail(inputs, context, w):
    attended = scatter_rows(dot(context, w.out)) + w.bias[2]
    unit0, inverse0 = norm_parts(inputs + attended)
    hidden = unit0 * w.gain[0] + w.shift[0]
    hidden_all = gather_rows(hidden.astype(BF))
    inner = dot(hidden_all, w.ffn_in) + w.ffn_bias
    active = gelu(inner).astype(BF)
    branch = scatter_rows(dot(active, w.ffn_out)) + w.bias[3]
    unit1, inverse1 = norm_parts(hidden + branch)
    output = unit1 * w.gain[1] + w.shift[1]
    return output, (unit0, inverse0, hidden_all, inner, active, unit1, inverse1)


def backward_tail(grad, context, kept, w):
    unit0, inverse0, hidden_all, inner, active, unit1, inverse1 = kept
    sum_grad, gain1, shift1 = norm_back(grad, unit1, inverse1, w.gain[1])
    branch_low = sum_grad.astype(BF)
    branch_all = gather_rows(branch_low)
    active_grad = dot_nt(branch_all, w.ffn_out)
    _, pull = jax.vjp(gelu, inner)
    inner_grad = pull(active_grad)[0].astype(BF)
    hidden_grad = sum_grad + scatter_rows(dot_nt(inner_grad, w.ffn_in))
    input_grad, gain0, shift0 = norm_back(hidden_grad, unit0, inverse0, w.gain[0])
    attended_low = input_grad.astype(BF)
    attended_all = gather_rows(attended_low)
    context_grad = dot_nt(attended_all, w.out).astype(BF)
    weight_grads = (
        dot_tn(context, attended_all),
        dot_tn(hidden_all, inner_grad),
        dot_tn(active, branch_all),
    )
    small = (
        jnp.sum(inner_grad.astype(F32), axis=0),
        jnp.sum(attended_low.astype(F32), axis=0),
        jnp.sum(branch_low.astype(F32), axis=0),
        gain0,
        gain1,
        shift0,
        shift1,
    )
    return input_grad, context_grad, weight_grads, small


def per_device(
    enc_input, pred_input, cotangent, bucket_len, pad_len, rel_table,
    enc_qkv, enc_out, enc_ffn_in, enc_ffn_out, enc_ffn_bias, enc_bias, enc_gain, enc_shift,
    dec_qkv, dec_out, dec_rel, dec_rel_bias, dec_ffn_in, dec_ffn_out, dec_ffn_bias, dec_bias, dec_gain, dec_shift,
):
    here = lax.axis_index("stream")
    n = lax.axis_size("dp")
    group = lax.axis_index("dp")
    place = ring_place(group, n)
    rows = enc_input.shape[0]
    total = STREAMS * rows
    dim = enc_input.shape[1]
    share = enc_out.shape[0]
    quarter = dim // STREAMS
    ffn = enc_ffn_in.shape[1]
    ffn_share = enc_ffn_out.shape[0]
    ffn_part = ffn_share // STREAMS
    rel_all = dec_rel.shape[1]
    rel_part = rel_all // STREAMS

    bucket = bucket_len[0]
    starts = []
    for j in XOR:
        holder = here ^ j
        for chunk in range(2):
            starts.append(jnp.where(bucket == total, holder * rows + chunk * 64, chunk * bucket + holder * 64))
    meta = jnp.stack([v.astype(jnp.int32) for v in starts + [bucket, pad_len[0, 0], pad_len[0, 1]]])
    tables = rel_tables(rel_table, total)
    ring_index = jnp.stack([ring_member(place - o, n) for o in range(n)]).astype(jnp.int32)

    def ffn_columns(matrix):
        blocks = matrix.reshape(matrix.shape[0], n, ffn_share)
        part = lax.dynamic_slice_in_dim(blocks, here * ffn_part, ffn_part, axis=2)
        return part.reshape(matrix.shape[0], n * ffn_part)

    def ffn_rows(matrix):
        return lax.dynamic_slice_in_dim(matrix, here * ffn_part, ffn_part, axis=0)

    smalls = [
        a.reshape(-1)
        for a in (
            enc_ffn_bias, enc_bias, enc_gain, enc_shift, dec_ffn_bias, dec_bias, dec_gain, dec_shift, dec_rel_bias
        )
    ]
    small_own = jnp.concatenate(smalls)
    fixed = 4 * share
    small_rows = -(-small_own.shape[0] // quarter)
    small_rows += -small_rows % 16
    small_own = jnp.pad(small_own, (0, small_rows * quarter - small_own.shape[0])).reshape(small_rows, quarter)

    def attention_pack(qkv, out, more):
        return jnp.concatenate(
            [own_columns(qkv, here).reshape(3 * share, quarter), own_columns(out, here)] + more, axis=0
        )

    def ffn_pack(matrix_in, matrix_out):
        return jnp.concatenate([ffn_columns(matrix_in), ffn_rows(matrix_out)], axis=0)

    def attention_regions(extra):
        regions = [(i * share, (i + 1) * share, 0, quarter, 0, 0, i * quarter) for i in range(3)]
        regions.append((fixed - share, fixed, 0, quarter, 1, 0, 0))
        return regions + extra

    shapes = [(share, 3 * quarter), (share, quarter)]
    ffn_shapes = [(share, n * ffn_part), (ffn_part, dim)]
    ffn_regions = [
        (0, share, 0, dim, 0, 0, 0),
        (share, share + ffn_part, 0, dim, 1, 0, 0),
    ]
    pieces = ring_pieces(attention_pack(enc_qkv, enc_out, [small_own]), n)
    enc_wqkv, enc_wout, small_all = assemble(
        pieces,
        ring_index,
        attention_regions([(fixed, fixed + small_rows, 0, quarter, 2, 0, 0)]),
        shapes + [(small_rows, quarter)],
        n,
    )
    pieces = ring_pieces(ffn_pack(enc_ffn_in, enc_ffn_out), n)
    enc_win, enc_wback = assemble(pieces, ring_index, ffn_regions, ffn_shapes, n)
    half = share // 2
    rel_own = own_columns(dec_rel, here)
    rel_pack = jnp.concatenate([rel_own[:half], rel_own[half:]], axis=1)
    pieces = ring_pieces(attention_pack(dec_qkv, dec_out, [rel_pack]), n)
    dec_wqkv, dec_wout, dec_wrel = assemble(
        pieces,
        ring_index,
        attention_regions(
            [
                (fixed, fixed + half, 0, rel_part, 2, 0, 0),
                (fixed, fixed + half, rel_part, 2 * rel_part, 2, half, 0),
            ]
        ),
        shapes + [(share, rel_part)],
        n,
    )
    pieces = ring_pieces(ffn_pack(dec_ffn_in, dec_ffn_out), n)
    dec_win, dec_wback = assemble(pieces, ring_index, ffn_regions, ffn_shapes, n)

    small_all = small_all.reshape(n, -1).astype(F32)
    small_full = []
    offset = 0
    for arr in (enc_ffn_bias, enc_bias, enc_gain, enc_shift, dec_ffn_bias, dec_bias, dec_gain, dec_shift, dec_rel_bias):
        part = small_all[:, offset : offset + arr.size]
        offset += arr.size
        if arr.ndim == 1:
            small_full.append(part.reshape(-1))
        else:
            small_full.append(jnp.transpose(part.reshape((n,) + arr.shape), (1, 0, 2)).reshape(arr.shape[0], -1))

    def turn_out(columns):
        blocks = columns.reshape(dim, quarter)
        sent = [lax.dynamic_slice_in_dim(blocks, (here ^ j) * quarter, quarter, axis=0) for j in XOR]
        return jnp.concatenate(by_absolute(turn_blocks(sent), here), axis=1)

    def turn_out_back(grad):
        sent = [lax.dynamic_slice_in_dim(grad, (here ^ j) * quarter, quarter, axis=1) for j in XOR]
        return jnp.concatenate(by_absolute(turn_blocks(sent), here), axis=0).reshape(n, share, quarter)

    def layer(wqkv, wout, win, wback, bias_in, bias, gain, shift):
        w = Layer()
        w.qkv = wqkv.reshape(dim, 3 * quarter)
        w.out = turn_out(wout)
        w.ffn_in = win.reshape(dim, n * ffn_part)
        w.ffn_out = wback.reshape(n * ffn_part, dim)
        w.ffn_bias = lax.dynamic_slice_in_dim(
            bias_in.reshape(n, STREAMS, ffn_part), here, 1, axis=1
        ).reshape(-1)
        w.bias, w.gain, w.shift = bias, gain, shift
        mine = own_columns(bias, here)
        w.qkv_bias = jnp.concatenate([mine[0], jnp.zeros_like(mine[0]), mine[1]])
        return w

    enc = layer(enc_wqkv, enc_wout, enc_win, enc_wback, *small_full[:4])
    dec = layer(dec_wqkv, dec_wout, dec_win, dec_wback, *small_full[4:8])
    dec.rel = dec_wrel.reshape(dim, rel_part)
    dec.rel_bias = own_columns(small_full[8], here)

    enc_all = gather_rows(enc_input)
    enc_heads = (dot(enc_all, enc.qkv) + enc.qkv_bias).astype(BF)
    enc_context, enc_lse = attention_forward(meta, enc_heads)
    main_rows, enc_kept = forward_tail(enc_input.astype(F32), enc_context, enc)
    stream_inputs = (main_rows, pred_input[0].astype(F32), pred_input[1].astype(F32))
    stream_all = [gather_rows(low) for low in (main_rows.astype(BF), pred_input[0], pred_input[1])]
    heads = [(dot(low, dec.qkv) + dec.qkv_bias).astype(BF) for low in stream_all]
    rels = [dot(low, dec.rel) + dec.rel_bias for low in stream_all]
    contexts, lses, kept, outputs = [], [], [], []
    for i in range(3):
        context, lse = attention_forward(meta, heads[i], None if i == 0 else heads[0], rels[i], tables)
        output, keep = forward_tail(stream_inputs[i], context, dec)
        contexts.append(context)
        lses.append(lse)
        kept.append(keep)
        outputs.append(output)

    residuals, weight_grads, smalls, dheads, drels = [], [], [], [], []
    key_grad = val_grad = 0.0
    query_main = None
    for i in range(3):
        residual, dctx, weights, small = backward_tail(
            cotangent[i].astype(F32), contexts[i], kept[i], dec
        )
        result = attention_backward(
            meta, heads[i], dctx, lses[i], None if i == 0 else heads[0], rels[i], tables
        )
        key_grad = key_grad + result[1]
        val_grad = val_grad + result[2]
        drels.append(result[3])
        if i == 0:
            query_main = result[0]
            dheads.append(None)
        else:
            dheads.append(jnp.concatenate([result[0], result[4], result[5]], axis=1))
        residuals.append(residual)
        weight_grads.append(weights)
        smalls.append(small)
    dheads[0] = jnp.concatenate([query_main, key_grad.astype(BF), val_grad.astype(BF)], axis=1)
    input_grads = [
        residuals[i] + scatter_rows(dot_nt(dheads[i], dec.qkv) + dot_nt(drels[i], dec.rel)) for i in range(3)
    ]
    dec_qkv_part = sum(dot_tn(stream_all[i], dheads[i]) for i in range(3)).astype(BF)
    dec_rel_part = sum(dot_tn(stream_all[i], drels[i]) for i in range(3)).astype(BF)
    dec_out_part, dec_in_part, dec_back_part = [
        sum(weight_grads[i][k] for i in range(3)).astype(BF) for k in range(3)
    ]
    dec_small = [sum(smalls[i][k] for i in range(3)) for k in range(7)]
    head_sum = sum(jnp.sum(dheads[i].astype(F32), axis=0) for i in range(3))
    rel_sum = sum(jnp.sum(drels[i].astype(F32), axis=0) for i in range(3))

    def widen(part, size):
        return lax.dynamic_update_slice(jnp.zeros((size,), F32), part, (here * part.shape[0],))

    def small_pack(small, heads_grad, rel_grad=None):
        wide = jnp.stack([widen(heads_grad[:quarter], dim), widen(heads_grad[2 * quarter :], dim)] + list(small[1:]))
        parts = [
            jnp.transpose(wide.reshape(8, n, share), (1, 0, 2)).reshape(n, 8 * share),
            small[0].reshape(n, ffn_part),
        ]
        if rel_grad is not None:
            parts.append(widen(rel_grad, rel_all).reshape(n, rel_all // n))
        used = sum(p.shape[1] for p in parts)
        rows_used = -(-used // quarter)
        rows_used += -rows_used % 16
        parts.append(jnp.zeros((n, rows_used * quarter - used), F32))
        return jnp.concatenate(parts, axis=1).reshape(n, rows_used, quarter).astype(BF)

    def attention_sum(qkv_grad, out_grad, more):
        arrays = [qkv_grad.reshape(n, share, 3 * quarter)[:, :, i * quarter : (i + 1) * quarter] for i in range(3)]
        return ring_sum(arrays + [turn_out_back(out_grad)] + more, n, place)

    def ffn_sum(in_grad, back_grad):
        return ring_sum([in_grad.reshape(n, share, dim), back_grad.reshape(n, ffn_part, dim)], n, place)

    dec_ffn_sum = ffn_sum(dec_in_part, dec_back_part)
    rel_blocks = dec_rel_part.reshape(n, share, rel_part)
    dec_attention_sum = attention_sum(
        dec_qkv_part,
        dec_out_part,
        [
            jnp.concatenate([rel_blocks[:, :half], rel_blocks[:, half:]], axis=2),
            small_pack(dec_small, head_sum, rel_sum),
        ],
    )

    residual, dctx, enc_weights, enc_small = backward_tail(input_grads[0], enc_context, enc_kept, enc)
    dq, dk, dv = attention_backward(meta, enc_heads, dctx, enc_lse)
    enc_dheads = jnp.concatenate([dq, dk.astype(BF), dv.astype(BF)], axis=1)
    enc_input_grad = residual + scatter_rows(dot_nt(enc_dheads, enc.qkv))
    enc_ffn_sum = ffn_sum(enc_weights[1].astype(BF), enc_weights[2].astype(BF))
    enc_head_sum = jnp.sum(enc_dheads.astype(F32), axis=0)
    enc_attention_sum = attention_sum(
        dot_tn(enc_all, enc_dheads).astype(BF), enc_weights[0].astype(BF), [small_pack(enc_small, enc_head_sum)]
    )

    def spread(total_rows):
        low = total_rows.astype(BF)
        far = swap(low, 2)
        near = swap(jnp.stack([low, far]), 1)
        return by_absolute([low, far, near[0], near[1]], here)

    def attention_out(total_rows, with_rel):
        blocks = spread(total_rows)
        wide = jnp.concatenate([b[:fixed] for b in blocks], axis=1).astype(F32)
        qkv = wide[: 3 * share].reshape(3, share, dim)
        out = wide[3 * share :]
        at = fixed
        results = [qkv, out]
        if with_rel:
            parts = [
                jnp.concatenate([b[at : at + half, :rel_part], b[at : at + half, rel_part:]], axis=0) for b in blocks
            ]
            results.append(jnp.concatenate(parts, axis=1).astype(F32))
            at += half
        tiny = jnp.stack([b[at:] for b in blocks]).astype(F32).reshape(STREAMS, -1)
        inner = tiny[:, 8 * share : 8 * share + ffn_part].reshape(-1)
        summed = jnp.sum(tiny, axis=0)
        wide_sum = summed[: 8 * share].reshape(8, share)
        results += [inner, wide_sum[:4], wide_sum[4:6], wide_sum[6:8]]
        if with_rel:
            first = 8 * share + ffn_part
            results.append(summed[first : first + rel_all // n])
        return results

    def ffn_out(total_rows):
        blocks = spread(total_rows)
        grad_in = jnp.stack([b[:share].reshape(share, n, ffn_part) for b in blocks], axis=2)
        grad_out = jnp.concatenate([b[share:] for b in blocks], axis=0)
        return grad_in.reshape(share, ffn).astype(F32), grad_out.astype(F32)

    dec_in_grad, dec_back_grad = ffn_out(dec_ffn_sum)
    dec_qkv_grad, dec_out_grad, dec_rel_grad, *dec_tiny, dec_rel_bias_grad = attention_out(dec_attention_sum, True)
    enc_in_grad, enc_back_grad = ffn_out(enc_ffn_sum)
    enc_qkv_grad, enc_out_grad, *enc_tiny = attention_out(enc_attention_sum, False)

    return (
        jnp.stack(outputs),
        enc_input_grad,
        jnp.stack([input_grads[1], input_grads[2]]),
        enc_qkv_grad,
        enc_out_grad,
        enc_in_grad,
        enc_back_grad,
        *enc_tiny,
        dec_qkv_grad,
        dec_out_grad,
        dec_rel_grad,
        dec_rel_bias_grad,
        dec_in_grad,
        dec_back_grad,
        *dec_tiny,
    )


def solution(mesh):
    tokens = P(("stream", "dp"), None)
    streams = P(None, ("stream", "dp"), None)
    first, second, cube = P("dp", None), P(None, "dp"), P(None, "dp", None)
    flat = P("dp")
    return jax.shard_map(
        per_device,
        mesh=mesh,
        in_specs=(
            tokens, streams, streams, flat, first, P(),
            cube, first, first, first, flat, second, second, second,
            cube, first, first, flat, first, first, flat, second, second, second,
        ),
        out_specs=(
            streams, tokens, streams,
            cube, first, first, first, flat, second, second, second,
            cube, first, first, flat, first, first, flat, second, second, second,
        ),
        check_vma=False,
    )
```

time: 3070 us -> 728 us (0.24)
  waiting for transfers between devices: 1870 us -> 162 us
  local copies, waits for them, and re-layouts: 537 us -> 97.5 us
  matrix products: 378 us -> 123 us
  blocking collectives: 177 us -> 0 us
  starting transfers between devices: 2.81 us -> 152 us
  Pallas kernels: 0 us -> 101 us
    reduce_scatter x10 -> x0, waiting for transfers between devices: 945 us -> none  [the longest x1 153 us: per_device(): lax.psum_scatter(dec_back_part.astype(jnp.bfloat16), 'dp', scatter_dimens...]
    all_gather x13 -> x0, waiting for transfers between devices: 438 us -> none  [the longest x1 124 us: per_device(): lax.all_gather(enc_ffn_in, 'dp', axis=0, tiled=True)]
    gather x2 -> x0, local copies, waits for them, and re-layouts: 408 us -> none  [per_device(): rel_table[distance][:, :, None] == bucket_ids[None, None, :]]
    unnamed x42 -> x0, waiting for transfers between devices: 375 us -> none
    dot_general x102 -> x57, matrix products: 375 us -> 123 us  [the longest x19 56.3 us: dot(): return jnp.dot(a, b, preferred_element_type=F32)]
    ppermute x0 -> x144, waiting for transfers between devices: none -> 162 us  [the longest x80 105 us: swap(): lax.ppermute(values, 'stream', [(i, i ^ bit) for i in range(STREAMS)])]
    ppermute x0 -> x144, starting transfers between devices: none -> 152 us  [the longest x80 100 us: swap(): lax.ppermute(values, 'stream', [(i, i ^ bit) for i in range(STREAMS)])]
    all_gather x8 -> x0, blocking collectives: 127 us -> none  [the longest x1 22 us: per_device(): lax.all_gather(enc_ffn_bias, 'dp', axis=0, tiled=True)]
  transfers between devices with their start and end apart: 33 -> 144, of which waited for: 24 -> 48; matrix products, arithmetic and copies ran while one was open for 25% -> 32% of each run, Pallas kernels for 0% -> 14%
where the time goes in v1:
time: 728 us; the launch traced here: 717 us
  waiting for transfers between devices  162 us (22%)
  starting transfers between devices  152 us (21%)
  matrix products  123 us (17%)
  Pallas kernels  101 us (14%)
  local copies, waits for them, and re-layouts  97.5 us (13%)
  other arithmetic  74.1 us (10%)
    ppermute x80, waiting for transfers between devices, swap(): lax.ppermute(values, 'stream', [(i, i ^ bit) for i in range(STREAMS)])  105 us
    ppermute x80, starting transfers between devices, swap(): lax.ppermute(values, 'stream', [(i, i ^ bit) for i in range(STREAMS)])  100 us
    ppermute x64, waiting for transfers between devices, ring_step(): return lax.ppermute(values, 'dp', pairs)  57.2 us
    dot_general x19, matrix products, dot(): return jnp.dot(a, b, preferred_element_type=F32)  56.3 us
    ppermute x64, starting transfers between devices, ring_step(): return lax.ppermute(values, 'dp', pairs)  51.8 us
    pallas_call x4, Pallas kernels, attention_backward(): pl.pallas_call(kernel, out_shape=outs, in_specs=[pl.BlockSpec(memory_spac...  51.5 us
    dot_general x19, matrix products, dot_nt(): lax.dot_general(a, b, (((1,), (1,)), ((), ())), preferred_element_type=F32)  37.9 us
    unnamed x626, local copies, waits for them, and re-layouts  34.9 us
  transfers between devices with their start and end apart: 144, of which 48 were waited for; matrix products, arithmetic and copies ran while one was open for 32% of the time, Pallas kernels for 14%

profile of v1, /device:TPU:1, one launch (start us, length us, event | category | flops | bytes accessed | tf_op | source)
XLA Modules:
  0.0 716.7 jit_solution(4542076049857119827)
XLA Ops:
  55.4 3.4 collective-permute-done.10
  58.9 4.7 collective-permute-start.11
  65.4 7.9 %shard_map.392 = (bf16[512,256]{1,0:T(8,128)(2,1)}, f32[512,128]{1,0:T(8,128)}) custom-call(s32[11]{0:T(128)} %stack.311.meta_ref, bf16[512,768]{1,0:T(8,128)(2,1)} %add_convert_fusion.10.refs_0_), custom_call_target="tpu_custom_call" | custom-call | tf_op jit(solution)/shard_map/pallas_call | solution.py:281
  82.0 7.1 collective-permute-done.18.refs_3_
  100.2 3.5 collective-permute-done.60
  104.7 4.7 collective-permute-done.52
  117.0 4.1 collective-permute-done.34.refs_7_
  126.5 3.1 shard_map.394
  133.4 4.4 shard_map.393
  137.8 9.1 %multiply_convert_fusion.3 = (bf16[512,1024]{1,0:T(8,128)(2,1)S(1)}, f32[512,1024]{1,0:T(8,128)}, f32[512,1024]{1,0:T(8,128)}) fusion(f32[1024]{0:T(1024)S(1)} %copy-done.225, bf16[1024,1024]{1,0:T(8,128)(2,1)} %bitcast.943, bf16[256,1024]{1,0:T(8,128)(2,1)} %collective-permute-done.15, bf16[128,1024]{1,0:T(8,128)(2,1)S(1)} %copy-done.128, ...), kind=kOutput, calls=%fused_computation.59 | convolution fusion | flops 1111490560 | bytes 8392704 | tf_op jit(solution)/shard_map/dot_general | solution.py:24
  158.8 5.0 collective-permute-done.25
  167.3 4.3 collective-permute-done.26
  178.9 8.6 %shard_map.395 = (bf16[512,256]{1,0:T(8,128)(2,1)}, f32[512,128]{1,0:T(8,128)}) custom-call(s32[11]{0:T(128)} %stack.311.meta_ref, bf16[512,768]{1,0:T(8,128)(2,1)} %add_convert_fusion.9.refs_0_.refs_1_.refs_3_, f32[512,128]{1,0:T(8,128)} %convolution_add_fusion.7.refs_1_.refs_3_, bf16[256,1280]{1,0:T(8,128)(2,1)} %compare_convert_fusion.refs_2_.refs_3_.refs_4_.refs_5_, ...), custom_call_target="tpu_custom_call" | custom-call | tf_op jit(solution)/shard_map/pallas_call | solution.py:281
  191.2 9.2 %shard_map.398 = (bf16[512,256]{1,0:T(8,128)(2,1)}, f32[512,128]{1,0:T(8,128)}) custom-call(s32[11]{0:T(128)} %stack.311.meta_ref, bf16[512,768]{1,0:T(8,128)(2,1)} %add_convert_fusion.7.refs_0_, bf16[512,768]{1,0:T(8,128)(2,1)} %add_convert_fusion.9.refs_0_.refs_1_.refs_3_, f32[512,128]{1,0:T(8,128)} %convolution_add_fusion.5.refs_2_.refs_4_, ...), custom_call_target="tpu_custom_call" | custom-call | tf_op jit(solution)/shard_map/pallas_call | solution.py:281
  204.5 8.8 %shard_map.397 = (bf16[512,256]{1,0:T(8,128)(2,1)}, f32[512,128]{1,0:T(8,128)}) custom-call(s32[11]{0:T(128)} %stack.311.meta_ref, bf16[512,768]{1,0:T(8,128)(2,1)} %add_convert_fusion.8.refs_0_, bf16[512,768]{1,0:T(8,128)(2,1)} %add_convert_fusion.9.refs_0_.refs_1_.refs_3_, f32[512,128]{1,0:T(8,128)} %convolution_add_fusion.6.refs_2_.refs_4_, ...), custom_call_target="tpu_custom_call" | custom-call | tf_op jit(solution)/shard_map/pallas_call | solution.py:281
  224.1 5.6 collective-permute-done.63
  229.7 5.6 collective-permute-done.55
  239.1 5.1 collective-permute-done.64
  245.0 3.8 collective-permute-start.65
  259.6 4.4 shard_map.396
  266.2 3.1 fusion.102
  272.2 18.3 %multiply_convert_fusion.2 = (bf16[512,1024]{1,0:T(8,128)(2,1)S(1)}, f32[512,1024]{1,0:T(8,128)}, bf16[512,1024]{1,0:T(8,128)(2,1)S(1)}, f32[512,1024]{1,0:T(8,1...) fusion(f32[1024]{0:T(1024)S(1)} %fusion.154, f32[512,1024]{1,0:T(8,128)S(1)} %fusion.102, ...), kind=kOutput, calls=%fused_computation.46 | convolution fusion | flops 1180696576 | bytes 18878464 | tf_op jit(solution)/shard_map/dot_general | solution.py:24
  299.1 4.0 collective-permute-done.51
  303.1 5.6 collective-permute-done.59
  308.7 5.6 collective-permute-done.67
  329.0 3.8 collective-permute-start.81
  340.7 3.6 collective-permute-done.68
  345.9 4.6 convert_reduce_fusion
  352.9 3.1 convert_reduce_fusion.1
  379.4 4.9 collective-permute-done.134
  389.6 7.9 %collective-permute-done.77 = bf16[128,1024]{1,0:T(8,128)(2,1)S(1)} collective-permute-done((bf16[128,1024]{1,0:T(8,128)(2,1)S(1)}, bf16[128,1024]{1,0:T(8,128)(2,1)S(1)}, u32[]{:S(2)}, u32[]{:S(2)}) %collective-permute-start.77) | collective-permute-done | bytes 262176 | tf_op jit(solution)/shard_map/ppermute | solution.py:36
  399.9 3.2 collective-permute-done.71
  413.6 5.9 collective-permute-start.73
  419.6 4.3 collective-permute-start.85
  432.5 14.7 %shard_map.401 = (bf16[512,256]{1,0:T(8,128)(2,1)}, f32[512,256]{1,0:T(8,128)}, f32[512,256]{1,0:T(8,128)}, bf16[512,128]{1,0:T(8,128)(2,1)}, bf16[512,256]{1,0:T(8,128)(2,1)}, /*index=5*/bf16[512,256]{1,0:T(8,128)(2,1)}) custom-call(s32[11]{0:T(128)} %stack.311.meta_ref, bf16[512,768]{1,0:T(8,128)(2,1)} %add_convert_fusion.7.refs_0_, ...), custom_call_target="tpu_custom_call" | custom-call | tf_op jit(solution)/shard_map/pallas_call | solution.py:402
  451.0 13.0 %shard_map.399 = (bf16[512,256]{1,0:T(8,128)(2,1)}, f32[512,256]{1,0:T(8,128)}, f32[512,256]{1,0:T(8,128)}, bf16[512,128]{1,0:T(8,128)(2,1)}) custom-call(s32[11]{0:T(128)} %stack.311.meta_ref, bf16[512,768]{1,0:T(8,128)(2,1)} %add_convert_fusion.9.refs_0_.refs_1_.refs_3_, bf16[512,256]{1,0:T(8,128)(2,1)} %convolution_convert_fusion.7.refs_1_, ...), custom_call_target="tpu_custom_call" | custom-call | tf_op jit(solution)/shard_map/pallas_call | solution.py:402
  472.2 14.9 %shard_map.400 = (bf16[512,256]{1,0:T(8,128)(2,1)}, f32[512,256]{1,0:T(8,128)}, f32[512,256]{1,0:T(8,128)}, bf16[512,128]{1,0:T(8,128)(2,1)}, bf16[512,256]{1,0:T(8,128)(2,1)}, /*index=5*/bf16[512,256]{1,0:T(8,128)(2,1)}) custom-call(s32[11]{0:T(128)} %stack.311.meta_ref, bf16[512,768]{1,0:T(8,128)(2,1)} %add_convert_fusion.8.refs_0_, ...), custom_call_target="tpu_custom_call" | custom-call | tf_op jit(solution)/shard_map/pallas_call | solution.py:402
  536.7 3.9 collective-permute-done.128
  541.8 8.0 %collective-permute-done.87 = bf16[128,1024]{1,0:T(8,128)(2,1)S(1)} collective-permute-done((bf16[128,1024]{1,0:T(8,128)(2,1)S(1)}, bf16[128,1024]{1,0:T(8,128)(2,1)S(1)}, u32[]{:S(2)}, u32[]{:S(2)}) %collective-permute-start.87) | collective-permute-done | bytes 262176 | tf_op jit(solution)/shard_map/ppermute | solution.py:36
  551.0 4.5 collective-permute-done.99
  557.1 4.0 collective-permute-done.97
  562.9 3.8 collective-permute-done.88
  593.4 3.6 collective-permute-done.91
  607.2 4.0 collective-permute-done.118
  617.7 8.9 %shard_map.402 = (bf16[512,256]{1,0:T(8,128)(2,1)}, f32[512,256]{1,0:T(8,128)}, f32[512,256]{1,0:T(8,128)}) custom-call(s32[11]{0:T(128)} %stack.311.meta_ref, bf16[512,768]{1,0:T(8,128)(2,1)} %add_convert_fusion.10.refs_0_, bf16[512,256]{1,0:T(8,128)(2,1)} %convolution_convert_fusion.4.refs_1_, f32[512,128]{1,0:T(8,128)} %get-tuple-element.83.refs_2_), custom_call_target="tpu_custom_call" | custom-call | tf_op jit(solution)/shard_map/pallas_call | solution.py:402
  648.9 3.4 collective-permute-done.106
  673.4 4.6 collective-permute-done.110
  678.8 3.6 collective-permute-start.111
  (1302 shorter events, 424.8 us)
Async XLA Ops:
  14.9 29.4 %collective-permute-start.28 = (bf16[576,256]{1,0:T(8,128)(2,1)S(1)}, bf16[576,256]{1,0:T(8,128)(2,1)}, u32[]{:S(2)}, u32[]{:S(2)}) collective-permute-start(bf16[576,256]{1,0:T(8,128)(2,1)S(1)} %maximum_maximum_fusion.refs_0_), channel_id=1, source_target_pairs={{0,2},{2,4},{4,6},{6,7},{7,5},{5,3},{3,1},{1,0},{8,10},{10,12},{12... | collective-permute-start | bytes 884744 | tf_op jit(solution)/shard_map/ppermute | solution.py:80
  16.4 27.9 %collective-permute-start.29 = (bf16[576,256]{1,0:T(8,128)(2,1)S(1)}, bf16[576,256]{1,0:T(8,128)(2,1)}, u32[]{:S(2)}, u32[]{:S(2)}) collective-permute-start(bf16[576,256]{1,0:T(8,128)(2,1)S(1)} %maximum_maximum_fusion.refs_0_), channel_id=1, source_target_pairs={{0,1},{2,0},{4,2},{6,4},{7,6},{5,7},{3,5},{1,3},{8,9},{10,8},{12,1... | collective-permute-start | bytes 884744 | tf_op jit(solution)/shard_map/ppermute | solution.py:80
  24.7 16.2 %collective-permute-start.1 = (bf16[256,1024]{1,0:T(8,128)(2,1)}, bf16[256,1024]{1,0:T(8,128)(2,1)}, u32[]{:S(2)}, u32[]{:S(2)}) collective-permute-start(bf16[256,1024]{1,0:T(8,128)(2,1)} %pad_maximum_fusion.27), channel_id=1, source_target_pairs={{0,8},{8,0},{16,24},{24,16},{1,9},{9,1},{17,25},{25,17},{2,10},{10... | collective-permute-start | bytes 1572872 | tf_op jit(solution)/shard_map/ppermute | solution.py:36
  40.9 35.1 %collective-permute-start.16 = (bf16[256,1024]{1,0:T(8,128)(2,1)S(1)}, bf16[256,1024]{1,0:T(8,128)(2,1)S(1)}, u32[]{:S(2)}, u32[]{:S(2)}) collective-permute-start(bf16[256,1024]{1,0:T(8,128)(2,1)S(1)} %pad_maximum_fusion.31.refs_0_), channel_id=1, source_target_pairs={{0,2},{2,4},{4,6},{6,7},{7,5},{5,3},{3,1},{1,0},{8,10},{10,12},{12... | collective-permute-start | bytes 1572872 | tf_op jit(solution)/shard_map/ppermute | solution.py:80
  44.3 33.1 %collective-permute-start.17 = (bf16[256,1024]{1,0:T(8,128)(2,1)S(1)}, bf16[256,1024]{1,0:T(8,128)(2,1)S(1)}, u32[]{:S(2)}, u32[]{:S(2)}) collective-permute-start(bf16[256,1024]{1,0:T(8,128)(2,1)S(1)} %pad_maximum_fusion.31.refs_0_), channel_id=1, source_target_pairs={{0,1},{2,0},{4,2},{6,4},{7,6},{5,7},{3,5},{1,3},{8,9},{10,8},{12,1... | collective-permute-start | bytes 1572872 | tf_op jit(solution)/shard_map/ppermute | solution.py:80
  44.3 33.3 %collective-permute-start.30 = (bf16[576,256]{1,0:T(8,128)(2,1)}, bf16[576,256]{1,0:T(8,128)(2,1)}, u32[]{:S(2)}, u32[]{:S(2)}) collective-permute-start(bf16[576,256]{1,0:T(8,128)(2,1)} %collective-permute-done.28.refs_1_), channel_id=1, source_target_pairs={{0,2},{2,4},{4,6},{6,7},{7,5},{5,3},{3,1},{1,0},{8,10},{10,12},{12... | collective-permute-start | bytes 884744 | tf_op jit(solution)/shard_map/ppermute | solution.py:80
  45.7 33.1 %collective-permute-start.31 = (bf16[576,256]{1,0:T(8,128)(2,1)}, bf16[576,256]{1,0:T(8,128)(2,1)}, u32[]{:S(2)}, u32[]{:S(2)}) collective-permute-start(bf16[576,256]{1,0:T(8,128)(2,1)} %collective-permute-done.29.refs_2_), channel_id=1, source_target_pairs={{0,1},{2,0},{4,2},{6,4},{7,6},{5,7},{3,5},{1,3},{8,9},{10,8},{12,1... | collective-permute-start | bytes 884744 | tf_op jit(solution)/shard_map/ppermute | solution.py:80
  77.5 17.9 %collective-permute-start.32 = (bf16[576,256]{1,0:T(8,128)(2,1)}, bf16[576,256]{1,0:T(8,128)(2,1)S(1)}, u32[]{:S(2)}, u32[]{:S(2)}) collective-permute-start(bf16[576,256]{1,0:T(8,128)(2,1)} %collective-permute-done.30.refs_3_), channel_id=1, source_target_pairs={{0,2},{2,4},{4,6},{6,7},{7,5},{5,3},{3,1},{1,0},{8,10},{10,12},{12... | collective-permute-start | bytes 884744 | tf_op jit(solution)/shard_map/ppermute | solution.py:80
  78.8 18.0 %collective-permute-start.33 = (bf16[576,256]{1,0:T(8,128)(2,1)}, bf16[576,256]{1,0:T(8,128)(2,1)S(1)}, u32[]{:S(2)}, u32[]{:S(2)}) collective-permute-start(bf16[576,256]{1,0:T(8,128)(2,1)} %collective-permute-done.31.refs_4_), channel_id=1, source_target_pairs={{0,1},{2,0},{4,2},{6,4},{7,6},{5,7},{3,5},{1,3},{8,9},{10,8},{12,1... | collective-permute-start | bytes 884744 | tf_op jit(solution)/shard_map/ppermute | solution.py:80
  89.1 21.6 %collective-permute-start.20 = (bf16[256,1024]{1,0:T(8,128)(2,1)S(1)}, bf16[256,1024]{1,0:T(8,128)(2,1)S(1)}, u32[]{:S(2)}, u32[]{:S(2)}) collective-permute-start(bf16[256,1024]{1,0:T(8,128)(2,1)S(1)} %collective-permute-done.18.refs_3_), channel_id=1, source_target_pairs={{0,2},{2,4},{4,6},{6,7},{7,5},{5,3},{3,1},{1,0},{8,10},{10,12},{12... | collective-permute-start | bytes 1572872 | tf_op jit(solution)/shard_map/ppermute | solution.py:80
  90.4 20.5 %collective-permute-start.21 = (bf16[256,1024]{1,0:T(8,128)(2,1)S(1)}, bf16[256,1024]{1,0:T(8,128)(2,1)S(1)}, u32[]{:S(2)}, u32[]{:S(2)}) collective-permute-start(bf16[256,1024]{1,0:T(8,128)(2,1)S(1)} %collective-permute-done.19.refs_4_), channel_id=1, source_target_pairs={{0,1},{2,0},{4,2},{6,4},{7,6},{5,7},{3,5},{1,3},{8,9},{10,8},{12,1... | collective-permute-start | bytes 1572872 | tf_op jit(solution)/shard_map/ppermute | solution.py:80
  98.0 31.6 %collective-permute-start.42 = (bf16[256,1024]{1,0:T(8,128)(2,1)S(1)}, bf16[256,1024]{1,0:T(8,128)(2,1)}, u32[]{:S(2)}, u32[]{:S(2)}) collective-permute-start(bf16[256,1024]{1,0:T(8,128)(2,1)S(1)} %pad_maximum_fusion.36.refs_0_), channel_id=1, source_target_pairs={{0,2},{2,4},{4,6},{6,7},{7,5},{5,3},{3,1},{1,0},{8,10},{10,12},{12... | collective-permute-start | bytes 1572872 | tf_op jit(solution)/shard_map/ppermute | solution.py:80
  103.7 27.6 %collective-permute-start.43 = (bf16[256,1024]{1,0:T(8,128)(2,1)S(1)}, bf16[256,1024]{1,0:T(8,128)(2,1)}, u32[]{:S(2)}, u32[]{:S(2)}) collective-permute-start(bf16[256,1024]{1,0:T(8,128)(2,1)S(1)} %pad_maximum_fusion.36.refs_0_), channel_id=1, source_target_pairs={{0,1},{2,0},{4,2},{6,4},{7,6},{5,7},{3,5},{1,3},{8,9},{10,8},{12,1... | collective-permute-start | bytes 1572872 | tf_op jit(solution)/shard_map/ppermute | solution.py:80
  110.9 26.9 %collective-permute-start.15 = (bf16[256,1024]{1,0:T(8,128)(2,1)}, bf16[256,1024]{1,0:T(8,128)(2,1)}, u32[]{:S(2)}, u32[]{:S(2)}) collective-permute-start(bf16[256,1024]{1,0:T(8,128)(2,1)} %pad_maximum_fusion.30), channel_id=1, source_target_pairs={{0,8},{8,0},{16,24},{24,16},{1,9},{9,1},{17,25},{25,17},{2,10},{10... | collective-permute-start | bytes 1572872 | tf_op jit(solution)/shard_map/ppermute | solution.py:36
  129.7 20.5 %collective-permute-start.61 = (bf16[256,1024]{1,0:T(8,128)(2,1)}, bf16[256,1024]{1,0:T(8,128)(2,1)S(1)}, u32[]{:S(2)}, u32[]{:S(2)}) collective-permute-start(bf16[256,1024]{1,0:T(8,128)(2,1)} %pad_maximum_fusion.39), channel_id=1, source_target_pairs={{0,8},{8,0},{16,24},{24,16},{1,9},{9,1},{17,25},{25,17},{2,10},{10... | collective-permute-start | bytes 1572872 | tf_op jit(solution)/shard_map/ppermute | solution.py:36
  131.3 23.0 %collective-permute-start.53 = (bf16[256,1024]{1,0:T(8,128)(2,1)}, bf16[256,1024]{1,0:T(8,128)(2,1)}, u32[]{:S(2)}, u32[]{:S(2)}) collective-permute-start(bf16[256,1024]{1,0:T(8,128)(2,1)} %pad_maximum_fusion.37), channel_id=1, source_target_pairs={{0,8},{8,0},{16,24},{24,16},{1,9},{9,1},{17,25},{25,17},{2,10},{10... | collective-permute-start | bytes 1572872 | tf_op jit(solution)/shard_map/ppermute | solution.py:36
  131.4 88.7 %collective-permute-start.44 = (bf16[256,1024]{1,0:T(8,128)(2,1)}, bf16[256,1024]{1,0:T(8,128)(2,1)}, u32[]{:S(2)}, u32[]{:S(2)}) collective-permute-start(bf16[256,1024]{1,0:T(8,128)(2,1)} %collective-permute-done.42.refs_1_), channel_id=1, source_target_pairs={{0,2},{2,4},{4,6},{6,7},{7,5},{5,3},{3,1},{1,0},{8,10},{10,12},{12... | collective-permute-start | bytes 1572872 | tf_op jit(solution)/shard_map/ppermute | solution.py:80
  132.7 88.7 %collective-permute-start.45 = (bf16[256,1024]{1,0:T(8,128)(2,1)}, bf16[256,1024]{1,0:T(8,128)(2,1)}, u32[]{:S(2)}, u32[]{:S(2)}) collective-permute-start(bf16[256,1024]{1,0:T(8,128)(2,1)} %collective-permute-done.43.refs_2_), channel_id=1, source_target_pairs={{0,1},{2,0},{4,2},{6,4},{7,6},{5,7},{3,5},{1,3},{8,9},{10,8},{12,1... | collective-permute-start | bytes 1572872 | tf_op jit(solution)/shard_map/ppermute | solution.py:80
  191.2 24.0 %collective-permute-start.38 = (bf16[256,1024]{1,0:T(8,128)(2,1)}, bf16[256,1024]{1,0:T(8,128)(2,1)}, u32[]{:S(2)}, u32[]{:S(2)}) collective-permute-start(bf16[256,1024]{1,0:T(8,128)(2,1)} %slice.1525), channel_id=1, source_target_pairs={{0,8},{8,0},{16,24},{24,16},{1,9},{9,1},{17,25},{25,17},{2,10},{10... | collective-permute-start | bytes 1572872 | tf_op jit(solution)/shard_map/ppermute | solution.py:36
  218.7 16.6 %collective-permute-start.55 = (bf16[128,1024]{1,0:T(8,128)(2,1)S(1)}, bf16[128,1024]{1,0:T(8,128)(2,1)S(1)}, u32[]{:S(2)}, u32[]{:S(2)}) collective-permute-start(bf16[128,1024]{1,0:T(8,128)(2,1)S(1)} %slice.1539), channel_id=1, source_target_pairs={{0,16},{8,24},{16,0},{24,8},{1,17},{9,25},{17,1},{25,9},{2,18},{10... | collective-permute-start | bytes 786440 | tf_op jit(solution)/shard_map/ppermute | solution.py:36
  220.1 28.8 %collective-permute-start.46 = (bf16[256,1024]{1,0:T(8,128)(2,1)}, bf16[256,1024]{1,0:T(8,128)(2,1)S(1)}, u32[]{:S(2)}, u32[]{:S(2)}) collective-permute-start(bf16[256,1024]{1,0:T(8,128)(2,1)} %collective-permute-done.44.refs_3_), channel_id=1, source_target_pairs={{0,2},{2,4},{4,6},{6,7},{7,5},{5,3},{3,1},{1,0},{8,10},{10,12},{12... | collective-permute-start | bytes 1572872 | tf_op jit(solution)/shard_map/ppermute | solution.py:80
  221.4 29.6 %collective-permute-start.47 = (bf16[256,1024]{1,0:T(8,128)(2,1)}, bf16[256,1024]{1,0:T(8,128)(2,1)S(1)}, u32[]{:S(2)}, u32[]{:S(2)}) collective-permute-start(bf16[256,1024]{1,0:T(8,128)(2,1)} %collective-permute-done.45.refs_4_), channel_id=1, source_target_pairs={{0,1},{2,0},{4,2},{6,4},{7,6},{5,7},{3,5},{1,3},{8,9},{10,8},{12,1... | collective-permute-start | bytes 1572872 | tf_op jit(solution)/shard_map/ppermute | solution.py:80
  245.0 21.1 %collective-permute-start.65 = (bf16[256,1024]{1,0:T(8,128)(2,1)}, bf16[256,1024]{1,0:T(8,128)(2,1)}, u32[]{:S(2)}, u32[]{:S(2)}) collective-permute-start(bf16[256,1024]{1,0:T(8,128)(2,1)} %pad_maximum_fusion.40), channel_id=1, source_target_pairs={{0,8},{8,0},{16,24},{24,16},{1,9},{9,1},{17,25},{25,17},{2,10},{10... | collective-permute-start | bytes 1572872 | tf_op jit(solution)/shard_map/ppermute | solution.py:36
  297.6 16.7 %collective-permute-start.67 = (bf16[128,1024]{1,0:T(8,128)(2,1)S(1)}, bf16[128,1024]{1,0:T(8,128)(2,1)S(1)}, u32[]{:S(2)}, u32[]{:S(2)}) collective-permute-start(bf16[128,1024]{1,0:T(8,128)(2,1)S(1)} %slice.1536), channel_id=1, source_target_pairs={{0,16},{8,24},{16,0},{24,8},{1,17},{9,25},{17,1},{25,9},{2,18},{10... | collective-permute-start | bytes 786440 | tf_op jit(solution)/shard_map/ppermute | solution.py:36
  329.0 17.0 %collective-permute-start.81 = (bf16[256,1024]{1,0:T(8,128)(2,1)}, bf16[256,1024]{1,0:T(8,128)(2,1)}, u32[]{:S(2)}, u32[]{:S(2)}) collective-permute-start(bf16[256,1024]{1,0:T(8,128)(2,1)} %pad_maximum_fusion.45), channel_id=1, source_target_pairs={{0,8},{8,0},{16,24},{24,16},{1,9},{9,1},{17,25},{25,17},{2,10},{10... | collective-permute-start | bytes 1572872 | tf_op jit(solution)/shard_map/ppermute | solution.py:36
  352.0 33.7 %collective-permute-start.82 = (bf16[256,1024]{1,0:T(8,128)(2,1)S(1)}, bf16[256,1024]{1,0:T(8,128)(2,1)S(1)}, u32[]{:S(2)}, u32[]{:S(2)}) collective-permute-start(bf16[256,1024]{1,0:T(8,128)(2,1)S(1)} %slice.1517), channel_id=1, source_target_pairs={{0,8},{8,0},{16,24},{24,16},{1,9},{9,1},{17,25},{25,17},{2,10},{10... | collective-permute-start | bytes 1572872 | tf_op jit(solution)/shard_map/ppermute | solution.py:36
  357.4 30.0 %collective-permute-start.76 = (bf16[256,1024]{1,0:T(8,128)(2,1)S(1)}, bf16[256,1024]{1,0:T(8,128)(2,1)S(1)}, u32[]{:S(2)}, u32[]{:S(2)}) collective-permute-start(bf16[256,1024]{1,0:T(8,128)(2,1)S(1)} %slice.1518), channel_id=1, source_target_pairs={{0,8},{8,0},{16,24},{24,16},{1,9},{9,1},{17,25},{25,17},{2,10},{10... | collective-permute-start | bytes 1572872 | tf_op jit(solution)/shard_map/ppermute | solution.py:36
  361.7 26.1 %collective-permute-start.70 = (bf16[256,1024]{1,0:T(8,128)(2,1)S(1)}, bf16[256,1024]{1,0:T(8,128)(2,1)S(1)}, u32[]{:S(2)}, u32[]{:S(2)}) collective-permute-start(bf16[256,1024]{1,0:T(8,128)(2,1)S(1)} %slice.1519), channel_id=1, source_target_pairs={{0,8},{8,0},{16,24},{24,16},{1,9},{9,1},{17,25},{25,17},{2,10},{10... | collective-permute-start | bytes 1572872 | tf_op jit(solution)/shard_map/ppermute | solution.py:36
  379.1 30.3 %collective-permute-start.139 = (bf16[256,1024]{1,0:T(8,128)(2,1)S(1)}, bf16[256,1024]{1,0:T(8,128)(2,1)S(1)}, u32[]{:S(2)}, u32[]{:S(2)}) collective-permute-start(bf16[256,1024]{1,0:T(8,128)(2,1)S(1)} %pad_maximum_fusion.56), channel_id=1, source_target_pairs={{0,1},{2,0},{4,2},{6,4},{7,6},{5,7},{3,5},{1,3},{8,9},{10,8},{12,1... | collective-permute-start | bytes 1572872 | tf_op jit(solution)/shard_map/ppermute | solution.py:80
  384.4 25.5 %collective-permute-start.135 = (bf16[256,1024]{1,0:T(8,128)(2,1)S(1)}, bf16[256,1024]{1,0:T(8,128)(2,1)S(1)}, u32[]{:S(2)}, u32[]{:S(2)}) collective-permute-start(bf16[256,1024]{1,0:T(8,128)(2,1)S(1)} %pad_maximum_fusion.55), channel_id=1, source_target_pairs={{0,2},{2,4},{4,6},{6,7},{7,5},{5,3},{3,1},{1,0},{8,10},{10,12},{12... | collective-permute-start | bytes 1572872 | tf_op jit(solution)/shard_map/ppermute | solution.py:80
  409.7 17.7 %collective-permute-start.140 = (bf16[256,1024]{1,0:T(8,128)(2,1)S(1)}, bf16[256,1024]{1,0:T(8,128)(2,1)S(1)}, u32[]{:S(2)}, u32[]{:S(2)}) collective-permute-start(bf16[256,1024]{1,0:T(8,128)(2,1)S(1)} %add_convert_fusion.13), channel_id=1, source_target_pairs={{0,1},{2,0},{4,2},{6,4},{7,6},{5,7},{3,5},{1,3},{8,9},{10,8},{12,1... | collective-permute-start | bytes 1572872 | tf_op jit(solution)/shard_map/ppermute | solution.py:80
  410.2 18.5 %collective-permute-start.136 = (bf16[256,1024]{1,0:T(8,128)(2,1)S(1)}, bf16[256,1024]{1,0:T(8,128)(2,1)S(1)}, u32[]{:S(2)}, u32[]{:S(2)}) collective-permute-start(bf16[256,1024]{1,0:T(8,128)(2,1)S(1)} %add_convert_fusion.15), channel_id=1, source_target_pairs={{0,2},{2,4},{4,6},{6,7},{7,5},{5,3},{3,1},{1,0},{8,10},{10,12},{12... | collective-permute-start | bytes 1572872 | tf_op jit(solution)/shard_map/ppermute | solution.py:80
  413.6 35.1 %collective-permute-start.73 = (bf16[256,1024]{1,0:T(8,128)(2,1)}, bf16[256,1024]{1,0:T(8,128)(2,1)}, u32[]{:S(2)}, u32[]{:S(2)}) collective-permute-start(bf16[256,1024]{1,0:T(8,128)(2,1)} %pad_maximum_fusion.42), channel_id=1, source_target_pairs={{0,8},{8,0},{16,24},{24,16},{1,9},{9,1},{17,25},{25,17},{2,10},{10... | collective-permute-start | bytes 1572872 | tf_op jit(solution)/shard_map/ppermute | solution.py:36
  424.7 45.3 %collective-permute-start.79 = (bf16[256,1024]{1,0:T(8,128)(2,1)}, bf16[256,1024]{1,0:T(8,128)(2,1)}, u32[]{:S(2)}, u32[]{:S(2)}) collective-permute-start(bf16[256,1024]{1,0:T(8,128)(2,1)} %pad_maximum_fusion.44), channel_id=1, source_target_pairs={{0,8},{8,0},{16,24},{24,16},{1,9},{9,1},{17,25},{25,17},{2,10},{10... | collective-permute-start | bytes 1572872 | tf_op jit(solution)/shard_map/ppermute | solution.py:36
  428.4 100.3 %collective-permute-start.141 = (bf16[256,1024]{1,0:T(8,128)(2,1)}, bf16[256,1024]{1,0:T(8,128)(2,1)}, u32[]{:S(2)}, u32[]{:S(2)}) collective-permute-start(bf16[256,1024]{1,0:T(8,128)(2,1)} %add_convert_fusion.12), channel_id=1, source_target_pairs={{0,1},{2,0},{4,2},{6,4},{7,6},{5,7},{3,5},{1,3},{8,9},{10,8},{12,1... | collective-permute-start | bytes 1572872 | tf_op jit(solution)/shard_map/ppermute | solution.py:80
  429.7 99.4 %collective-permute-start.137 = (bf16[256,1024]{1,0:T(8,128)(2,1)}, bf16[256,1024]{1,0:T(8,128)(2,1)}, u32[]{:S(2)}, u32[]{:S(2)}) collective-permute-start(bf16[256,1024]{1,0:T(8,128)(2,1)} %add_convert_fusion.14), channel_id=1, source_target_pairs={{0,2},{2,4},{4,6},{6,7},{7,5},{5,3},{3,1},{1,0},{8,10},{10,12},{12... | collective-permute-start | bytes 1572872 | tf_op jit(solution)/shard_map/ppermute | solution.py:80
  499.5 31.3 %collective-permute-start.86 = (bf16[256,1024]{1,0:T(8,128)(2,1)}, bf16[256,1024]{1,0:T(8,128)(2,1)}, u32[]{:S(2)}, u32[]{:S(2)}) collective-permute-start(bf16[256,1024]{1,0:T(8,128)(2,1)} %slice.1516), channel_id=1, source_target_pairs={{0,8},{8,0},{16,24},{24,16},{1,9},{9,1},{17,25},{25,17},{2,10},{10... | collective-permute-start | bytes 1572872 | tf_op jit(solution)/shard_map/ppermute | solution.py:36
  530.8 20.0 %collective-permute-start.142 = (bf16[256,1024]{1,0:T(8,128)(2,1)S(1)}, bf16[256,1024]{1,0:T(8,128)(2,1)S(1)}, u32[]{:S(2)}, u32[]{:S(2)}) collective-permute-start(bf16[256,1024]{1,0:T(8,128)(2,1)S(1)} %add_convert_fusion.11), channel_id=1, source_target_pairs={{0,16},{8,24},{16,0},{24,8},{1,17},{9,25},{17,1},{25,9},{2,18},{10... | collective-permute-start | bytes 1572872 | tf_op jit(solution)/shard_map/ppermute | solution.py:36
  532.1 17.7 %collective-permute-start.87 = (bf16[128,1024]{1,0:T(8,128)(2,1)S(1)}, bf16[128,1024]{1,0:T(8,128)(2,1)S(1)}, u32[]{:S(2)}, u32[]{:S(2)}) collective-permute-start(bf16[128,1024]{1,0:T(8,128)(2,1)S(1)} %slice.1532), channel_id=1, source_target_pairs={{0,16},{8,24},{16,0},{24,8},{1,17},{9,25},{17,1},{25,9},{2,18},{10... | collective-permute-start | bytes 786440 | tf_op jit(solution)/shard_map/ppermute | solution.py:36
  533.9 21.6 %collective-permute-start.99 = (bf16[128,1024]{1,0:T(8,128)(2,1)S(1)}, bf16[128,1024]{1,0:T(8,128)(2,1)S(1)}, u32[]{:S(2)}, u32[]{:S(2)}) collective-permute-start(bf16[128,1024]{1,0:T(8,128)(2,1)S(1)} %slice.1528), channel_id=1, source_target_pairs={{0,16},{8,24},{16,0},{24,8},{1,17},{9,25},{17,1},{25,9},{2,18},{10... | collective-permute-start | bytes 786440 | tf_op jit(solution)/shard_map/ppermute | solution.py:36
  534.3 26.8 %collective-permute-start.97 = (bf16[128,1024]{1,0:T(8,128)(2,1)S(1)}, bf16[128,1024]{1,0:T(8,128)(2,1)S(1)}, u32[]{:S(2)}, u32[]{:S(2)}) collective-permute-start(bf16[128,1024]{1,0:T(8,128)(2,1)S(1)} %slice.1529), channel_id=1, source_target_pairs={{0,16},{8,24},{16,0},{24,8},{1,17},{9,25},{17,1},{25,9},{2,18},{10... | collective-permute-start | bytes 786440 | tf_op jit(solution)/shard_map/ppermute | solution.py:36
  540.6 20.6 %collective-permute-start.125 = (bf16[592,256]{1,0:T(8,128)(2,1)S(1)}, bf16[592,256]{1,0:T(8,128)(2,1)S(1)}, u32[]{:S(2)}, u32[]{:S(2)}) collective-permute-start(bf16[592,256]{1,0:T(8,128)(2,1)S(1)} %fusion.113), channel_id=1, source_target_pairs={{0,2},{2,4},{4,6},{6,7},{7,5},{5,3},{3,1},{1,0},{8,10},{10,12},{12... | collective-permute-start | bytes 909320 | tf_op jit(solution)/shard_map/ppermute | solution.py:80
  555.5 27.5 %collective-permute-start.143 = (bf16[2,256,1024]{2,1,0:T(8,128)(2,1)S(1)}, bf16[2,256,1024]{2,1,0:T(8,128)(2,1)S(1)}, u32[]{:S(2)}, u32[]{:S(2)}) collective-permute-start(bf16[2,256,1024]{2,1,0:T(8,128)(2,1)S(1)} %pad_maximum_fusion.22), channel_id=1, source_target_pairs={{0,8},{8,0},{16,24},{24,16},{1,9},{9,1},{17,25},{25,17},{2,10},{10... | collective-permute-start | bytes 3145736 | tf_op jit(solution)/shard_map/ppermute | solution.py:36
  612.2 33.3 %collective-permute-start.119 = (bf16[256,1024]{1,0:T(8,128)(2,1)}, bf16[256,1024]{1,0:T(8,128)(2,1)}, u32[]{:S(2)}, u32[]{:S(2)}) collective-permute-start(bf16[256,1024]{1,0:T(8,128)(2,1)} %add_convert_fusion.17), channel_id=1, source_target_pairs={{0,1},{2,0},{4,2},{6,4},{7,6},{5,7},{3,5},{1,3},{8,9},{10,8},{12,1... | collective-permute-start | bytes 1572872 | tf_op jit(solution)/shard_map/ppermute | solution.py:80
  615.3 30.2 %collective-permute-start.115 = (bf16[256,1024]{1,0:T(8,128)(2,1)}, bf16[256,1024]{1,0:T(8,128)(2,1)}, u32[]{:S(2)}, u32[]{:S(2)}) collective-permute-start(bf16[256,1024]{1,0:T(8,128)(2,1)} %add_convert_fusion.19), channel_id=1, source_target_pairs={{0,2},{2,4},{4,6},{6,7},{7,5},{5,3},{3,1},{1,0},{8,10},{10,12},{12... | collective-permute-start | bytes 1572872 | tf_op jit(solution)/shard_map/ppermute | solution.py:80
  632.9 33.0 %collective-permute-start.94 = (bf16[256,1024]{1,0:T(8,128)(2,1)S(1)}, bf16[256,1024]{1,0:T(8,128)(2,1)S(1)}, u32[]{:S(2)}, u32[]{:S(2)}) collective-permute-start(bf16[256,1024]{1,0:T(8,128)(2,1)S(1)} %slice.1514), channel_id=1, source_target_pairs={{0,8},{8,0},{16,24},{24,16},{1,9},{9,1},{17,25},{25,17},{2,10},{10... | collective-permute-start | bytes 1572872 | tf_op jit(solution)/shard_map/ppermute | solution.py:36
  660.6 21.8 %collective-permute-start.121 = (bf16[2,256,1024]{2,1,0:T(8,128)(2,1)S(1)}, bf16[2,256,1024]{2,1,0:T(8,128)(2,1)S(1)}, u32[]{:S(2)}, u32[]{:S(2)}) collective-permute-start(bf16[2,256,1024]{2,1,0:T(8,128)(2,1)S(1)} %pad_maximum_fusion.21), channel_id=1, source_target_pairs={{0,8},{8,0},{16,24},{24,16},{1,9},{9,1},{17,25},{25,17},{2,10},{10... | collective-permute-start | bytes 3145736 | tf_op jit(solution)/shard_map/ppermute | solution.py:36
  678.8 27.3 %collective-permute-start.111 = (bf16[2,528,256]{2,1,0:T(8,128)(2,1)}, bf16[2,528,256]{2,1,0:T(8,128)(2,1)}, u32[]{:S(2)}, u32[]{:S(2)}) collective-permute-start(bf16[2,528,256]{2,1,0:T(8,128)(2,1)} %pad_maximum_fusion.26), channel_id=1, source_target_pairs={{0,8},{8,0},{16,24},{24,16},{1,9},{9,1},{17,25},{25,17},{2,10},{10... | collective-permute-start | bytes 1622024 | tf_op jit(solution)/shard_map/ppermute | solution.py:36
  (377 other events, 4067.7 us)

commit v2 on v1

--- a/solution.py
+++ b/solution.py
@@ -17,7 +17,7 @@
 TILE = 128
 STREAMS = 4
 XOR = (0, 2, 1, 3)
-VMEM_LIMIT = 60 * 1024 * 1024
+VMEM_LIMIT = 16 * 1024 * 1024
 
 
 def dot(a, b):
@@ -36,18 +36,21 @@
     return lax.ppermute(values, "stream", [(i, i ^ bit) for i in range(STREAMS)])
 
 
-def gather_rows(rows):
-    far = swap(rows, 2)
-    half = jnp.concatenate([rows, far], axis=0)
-    return jnp.concatenate([half, swap(half, 1)], axis=0)
-
-
-def scatter_rows(partials):
-    n = partials.shape[0] // 4
-    near = swap(partials[2 * n :].astype(BF), 1)
-    keep = partials[: 2 * n].astype(F32) + near.astype(F32)
-    far = swap(keep[n:].astype(BF), 2)
-    return keep[:n] + far.astype(F32)
+def gather_halves(rows):
+    half = jnp.concatenate([rows, swap(rows, 2)], axis=0)
+    return half, swap(half, 1)
+
+
+def scatter_rows(keep, near):
+    n = keep.shape[0] // 2
+    near = swap(near, 1)
+    far = swap((keep[n:] + near[n:].astype(F32)).astype(BF), 2)
+    return keep[:n] + near[:n].astype(F32), far
+
+
+def scatter_dots(partials):
+    n = partials.shape[0] // 2
+    return scatter_rows(partials[:n], partials[n:].astype(BF))
 
 
 def turn_blocks(blocks):
@@ -199,16 +202,9 @@
     return pltpu.roll(spread, 0, 1, stride=1, stride_axis=0)
 
 
-def scores_of(t, h, width, meta, qs, ks, rs, table_ref, causal, strict):
-    pair, e = h // 2, h % 2
-    lanes = slice(TILE * pair, TILE * (pair + 1))
-    rows = slice(TILE * t, TILE * (t + 1))
-    query = (qs[rows, lanes].astype(F32) * (head_mask(e) * HD**-0.5)).astype(BF)
-    scores = dot_nt(query, ks[0:width, lanes])
-    if rs is not None:
-        first = sum(TILE * (u + 1) for u in range(t))
-        scores = scores + rel_bias(rs[rows, :], h, table_ref[:, first : first + width])
-    return query, jnp.where(allowed_keys(t, width, meta, causal, strict), scores, MASKED)
+def table_slice(t, width):
+    first = sum(TILE * (u + 1) for u in range(t))
+    return slice(first, first + width)
 
 
 def attention_forward(meta, qkv, main=None, rel=None, tables=None):
@@ -223,8 +219,8 @@
         qkv_ref = refs.pop(0)
         main_ref = refs.pop(0) if own else qkv_ref
         rel_ref, table_ref, hot_ref = (refs.pop(0), refs.pop(0), refs.pop(0)) if causal else (None,) * 3
-        ctx_ref, lse_ref, qs, ks, vs, cs = refs[:6]
-        refs = refs[6:]
+        ctx_ref, lse_ref, qs, ks, vs, cs, kt = refs[:7]
+        refs = refs[7:]
         rs = refs.pop(0) if causal else None
         load_rows(meta_ref, qs, qkv_ref, 0, width_all)
         load_rows(meta_ref, ks, main_ref, width_all, 2 * width_all)
@@ -235,42 +231,52 @@
             kn, vn = refs
             load_rows(meta_ref, kn, qkv_ref, width_all, 2 * width_all)
             load_rows(meta_ref, vn, qkv_ref, 2 * width_all, 3 * width_all)
+        kt[...] = ks[...].T
         for t in range(total // TILE):
             rows = slice(TILE * t, TILE * (t + 1))
             width = tile_width(t, causal, total)
+            allowed = allowed_keys(t, width, meta_ref, causal, own)
             lse_lane = lax.broadcasted_iota(jnp.int32, (TILE, TILE), 1)
             lse = jnp.zeros((TILE, TILE), F32)
-            for pair in range(heads // 2):
-                lanes = slice(TILE * pair, TILE * (pair + 1))
-                context = jnp.zeros((TILE, TILE), F32)
-                for e in range(2):
-                    h = 2 * pair + e
-                    query, scores = scores_of(t, h, width, meta_ref, qs, ks, rs, table_ref, causal, own)
-                    top = jnp.max(scores, axis=1, keepdims=True)
-                    if own:
-                        own_score = jnp.sum(
-                            query.astype(F32) * kn[rows, lanes].astype(F32), axis=1, keepdims=True
-                        ) + jnp.sum(rs[rows, :] * (hot_ref[...] * rel_mask(h)), axis=1, keepdims=True)
-                        top = jnp.maximum(top, own_score)
-                    expos = jnp.exp(scores - top)
-                    sums = jnp.sum(expos, axis=1, keepdims=True)
-                    if own:
-                        own_expo = jnp.exp(own_score - top)
-                        sums = sums + own_expo
-                    inverse = 1.0 / sums
-                    probs = (expos * inverse).astype(BF)
-                    part = dot(probs, vs[0:width, lanes])
-                    if own:
-                        part = part + (own_expo * inverse) * vn[rows, lanes].astype(F32)
-                    context = context + part * head_mask(e)
-                    lse = jnp.where(lse_lane == h, top + jnp.log(sums), lse)
-                cs[rows, lanes] = context.astype(BF)
+            query = [(qs[rows, HD * h : HD * (h + 1)].astype(F32) * HD**-0.5).astype(BF) for h in range(heads)]
+            scores = [dot(query[h], kt[HD * h : HD * (h + 1), 0:width]) for h in range(heads)]
+            if causal:
+                biases = [rel_bias(rs[rows, :], h, table_ref[:, table_slice(t, width)]) for h in range(heads)]
+                scores = [a + b for a, b in zip(scores, biases)]
+            scores = [jnp.where(allowed, a, MASKED) for a in scores]
+            tops = [jnp.max(a, axis=1, keepdims=True) for a in scores]
+            if own:
+                own_scores = [
+                    jnp.sum(
+                        query[h].astype(F32) * kn[rows, HD * h : HD * (h + 1)].astype(F32), axis=1, keepdims=True
+                    )
+                    + jnp.sum(rs[rows, :] * (hot_ref[...] * rel_mask(h)), axis=1, keepdims=True)
+                    for h in range(heads)
+                ]
+                tops = [jnp.maximum(a, b) for a, b in zip(tops, own_scores)]
+            expos = [jnp.exp(a - b) for a, b in zip(scores, tops)]
+            sums = [jnp.sum(a, axis=1, keepdims=True) for a in expos]
+            if own:
+                own_expos = [jnp.exp(a - b) for a, b in zip(own_scores, tops)]
+                sums = [a + b for a, b in zip(sums, own_expos)]
+            inverses = [1.0 / a for a in sums]
+            parts = [
+                dot((expos[h] * inverses[h]).astype(BF), vs[0:width, HD * h : HD * (h + 1)]) for h in range(heads)
+            ]
+            if own:
+                parts = [
+                    parts[h] + (own_expos[h] * inverses[h]) * vn[rows, HD * h : HD * (h + 1)].astype(F32)
+                    for h in range(heads)
+                ]
+            cs[rows, :] = jnp.concatenate(parts, axis=1).astype(BF)
+            for h in range(heads):
+                lse = jnp.where(lse_lane == h, tops[h] + jnp.log(sums[h]), lse)
             lse_ref[rows, :] = lse
         store_rows(meta_ref, ctx_ref, cs, 0, width_all)
 
     vmem = pl.BlockSpec(memory_space=pltpu.VMEM)
     args = [qkv]
-    scratch = [pltpu.VMEM((total, width_all), BF) for _ in range(4)]
+    scratch = [pltpu.VMEM((total, width_all), BF) for _ in range(4)] + [pltpu.VMEM((width_all, total), BF)]
     if own:
         args.append(main)
     if causal:
@@ -310,8 +316,8 @@
         refs = refs[3:]
         drel_ref = refs.pop(0) if causal else None
         dkn_ref, dvn_ref = (refs.pop(0), refs.pop(0)) if own else (None, None)
-        qs, ks, vs, gs, dqs, dks, dvs = refs[:7]
-        refs = refs[7:]
+        qs, ks, vs, gs, dqs, dks, kt, vt, qt, gt, dkt, dvt = refs[:12]
+        refs = refs[12:]
         rs, drs = (refs.pop(0), refs.pop(0)) if causal else (None, None)
         load_rows(meta_ref, qs, qkv_ref, 0, width_all)
         load_rows(meta_ref, ks, main_ref, width_all, 2 * width_all)
@@ -323,62 +329,72 @@
             kn, vn, dkn, dvn = refs
             load_rows(meta_ref, kn, qkv_ref, width_all, 2 * width_all)
             load_rows(meta_ref, vn, qkv_ref, 2 * width_all, 3 * width_all)
-        dks[...] = jnp.zeros_like(dks)
-        dvs[...] = jnp.zeros_like(dvs)
+        qs[...] = (qs[...].astype(F32) * HD**-0.5).astype(BF)
+        kt[...] = ks[...].T
+        vt[...] = vs[...].T
+        qt[...] = qs[...].T
+        gt[...] = gs[...].T
+        dkt[...] = jnp.zeros_like(dkt)
+        dvt[...] = jnp.zeros_like(dvt)
+        each = range(heads)
+        feat = [slice(HD * h, HD * (h + 1)) for h in each]
         for t in range(total // TILE):
             rows = slice(TILE * t, TILE * (t + 1))
             width = tile_width(t, causal, total)
-            first = sum(TILE * (u + 1) for u in range(t))
-            drel = jnp.zeros((TILE, TILE), F32)
-            for pair in range(heads // 2):
-                lanes = slice(TILE * pair, TILE * (pair + 1))
-                dq = jnp.zeros((TILE, TILE), F32)
-                dkey_own = jnp.zeros((TILE, TILE), F32)
-                dval_own = jnp.zeros((TILE, TILE), F32)
-                for e in range(2):
-                    h = 2 * pair + e
-                    mask = head_mask(e)
-                    query, scores = scores_of(t, h, width, meta_ref, qs, ks, rs, table_ref, causal, own)
-                    norm = lse_ref[rows, h : h + 1]
-                    probs = jnp.exp(scores - norm)
-                    grad = (gs[rows, lanes].astype(F32) * mask).astype(BF)
-                    dprobs = dot_nt(grad, vs[0:width, lanes])
-                    rowdot = jnp.sum(probs * dprobs, axis=1, keepdims=True)
+            allowed = allowed_keys(t, width, meta_ref, causal, own)
+            norms = [lse_ref[rows, h : h + 1] for h in each]
+            query = [qs[rows, feat[h]] for h in each]
+            grad = [gs[rows, feat[h]] for h in each]
+            scores = [dot(query[h], kt[feat[h], 0:width]) for h in each]
+            dprobs = [dot(grad[h], vt[feat[h], 0:width]) for h in each]
+            if causal:
+                biases = [rel_bias(rs[rows, :], h, table_ref[:, table_slice(t, width)]) for h in each]
+                scores = [a + b for a, b in zip(scores, biases)]
+            probs = [jnp.exp(jnp.where(allowed, scores[h], MASKED) - norms[h]) for h in each]
+            rowdots = [jnp.sum(probs[h] * dprobs[h], axis=1, keepdims=True) for h in each]
+            if own:
+                own_keys = [kn[rows, feat[h]].astype(F32) for h in each]
+                own_scores = [
+                    jnp.sum(query[h].astype(F32) * own_keys[h], axis=1, keepdims=True)
+                    + jnp.sum(rs[rows, :] * (hot_ref[...] * rel_mask(h)), axis=1, keepdims=True)
+                    for h in each
+                ]
+                own_probs = [jnp.exp(own_scores[h] - norms[h]) for h in each]
+                own_dprobs = [
+                    jnp.sum(grad[h].astype(F32) * vn[rows, feat[h]].astype(F32), axis=1, keepdims=True) for h in each
+                ]
+                rowdots = [rowdots[h] + own_probs[h] * own_dprobs[h] for h in each]
+                own_dscores = [
+                    (own_probs[h] * (own_dprobs[h] - rowdots[h])).astype(BF).astype(F32) for h in each
+                ]
+            dscores = [(probs[h] * (dprobs[h] - rowdots[h])).astype(BF) for h in each]
+            dqs_parts = [dot(dscores[h], ks[0:width, feat[h]]) for h in each]
+            if own:
+                dqs_parts = [dqs_parts[h] + own_dscores[h] * own_keys[h] for h in each]
+                dkn[rows, :] = jnp.concatenate([own_dscores[h] * query[h].astype(F32) for h in each], axis=1)
+                dvn[rows, :] = jnp.concatenate([own_probs[h] * grad[h].astype(F32) for h in each], axis=1)
+            dqs[rows, :] = jnp.concatenate(dqs_parts, axis=1) * HD**-0.5
+            for h in each:
+                dkt[feat[h], 0:width] += dot(qt[feat[h], rows], dscores[h])
+                dvt[feat[h], 0:width] += dot(gt[feat[h], rows], probs[h].astype(BF))
+            if causal:
+                drel = jnp.zeros((TILE, TILE), F32)
+                for h in each:
+                    blocks = [
+                        dot(dscores[h][:, TILE * b : TILE * (b + 1)], flip_ref[...])
+                        for b in reversed(range(width // TILE))
+                    ]
+                    mirrored = jnp.concatenate(blocks, axis=1) if len(blocks) > 1 else blocks[0]
+                    turned = pltpu.roll(mirrored, 0, 1, stride=1, stride_axis=0).astype(BF)
+                    drel = drel + dot(turned, back_ref[table_slice(t, width), :]) * rel_mask(h)
                     if own:
-                        own_score = jnp.sum(
-                            query.astype(F32) * kn[rows, lanes].astype(F32), axis=1, keepdims=True
-                        ) + jnp.sum(rs[rows, :] * (hot_ref[...] * rel_mask(h)), axis=1, keepdims=True)
-                        own_prob = jnp.exp(own_score - norm)
-                        own_dprob = jnp.sum(
-                            grad.astype(F32) * vn[rows, lanes].astype(F32), axis=1, keepdims=True
-                        )
-                        rowdot = rowdot + own_prob * own_dprob
-                        own_dscore = (own_prob * (own_dprob - rowdot)).astype(BF).astype(F32)
-                        dq = dq + own_dscore * kn[rows, lanes].astype(F32) * (mask * HD**-0.5)
-                        dkey_own = dkey_own + own_dscore * query.astype(F32)
-                        dval_own = dval_own + own_prob * grad.astype(F32)
-                        drel = drel + own_dscore * (hot_ref[...] * rel_mask(h))
-                    dscores = (probs * (dprobs - rowdot)).astype(BF)
-                    dq = dq + dot(dscores, ks[0:width, lanes]) * (mask * HD**-0.5)
-                    dks[0:width, lanes] += dot_tn(dscores, query)
-                    dvs[0:width, lanes] += dot_tn(probs.astype(BF), grad)
-                    if causal:
-                        blocks = [
-                            dot(dscores[:, TILE * b : TILE * (b + 1)], flip_ref[...])
-                            for b in reversed(range(width // TILE))
-                        ]
-                        mirrored = jnp.concatenate(blocks, axis=1) if len(blocks) > 1 else blocks[0]
-                        turned = pltpu.roll(mirrored, 0, 1, stride=1, stride_axis=0).astype(BF)
-                        drel = drel + dot(turned, back_ref[first : first + width, :]) * rel_mask(h)
-                dqs[rows, lanes] = dq
-                if own:
-                    dkn[rows, lanes] = dkey_own
-                    dvn[rows, lanes] = dval_own
-            if causal:
+                        drel = drel + own_dscores[h] * (hot_ref[...] * rel_mask(h))
                 drs[rows, :] = drel
         store_rows(meta_ref, dq_ref, dqs, 0, width_all)
+        dks[...] = dkt[...].T
         store_rows(meta_ref, dk_ref, dks, 0, width_all)
-        store_rows(meta_ref, dv_ref, dvs, 0, width_all)
+        dks[...] = dvt[...].T
+        store_rows(meta_ref, dv_ref, dks, 0, width_all)
         if causal:
             store_rows(meta_ref, drel_ref, drs, 0, rel.shape[1])
         if own:
@@ -388,8 +404,10 @@
     vmem = pl.BlockSpec(memory_space=pltpu.VMEM)
     args = [qkv, dctx, lse]
     shape = (total, width_all)
+    turned = (width_all, total)
     outs = [jax.ShapeDtypeStruct(shape, BF), jax.ShapeDtypeStruct(shape, F32), jax.ShapeDtypeStruct(shape, F32)]
-    scratch = [pltpu.VMEM(shape, BF) for _ in range(4)] + [pltpu.VMEM(shape, F32) for _ in range(3)]
+    scratch = [pltpu.VMEM(shape, BF) for _ in range(4)] + [pltpu.VMEM(shape, F32) for _ in range(2)]
+    scratch += [pltpu.VMEM(turned, BF) for _ in range(4)] + [pltpu.VMEM(turned, F32) for _ in range(2)]
     if own:
         args.append(main)
     if causal:
@@ -426,22 +444,169 @@
     return forward, backward, hot, flip
 
 
-def norm_parts(values):
+def whole(kernel, outs, *args):
+    vmem = pl.BlockSpec(memory_space=pltpu.VMEM)
+    return pl.pallas_call(
+        kernel,
+        out_shape=[jax.ShapeDtypeStruct(shape, kind) for shape, kind in outs],
+        in_specs=[vmem] * len(args),
+        out_specs=[vmem] * len(outs),
+        compiler_params=pltpu.CompilerParams(vmem_limit_bytes=VMEM_LIMIT),
+    )(*args)
+
+
+def unit_of(values):
     center = values - jnp.mean(values, axis=-1, keepdims=True)
     spread = jnp.mean(center * center, axis=-1, keepdims=True)
     inverse = lax.rsqrt(spread + EPSILON)
     return center * inverse, inverse
 
 
-def norm_back(grad, unit, inverse, gain):
+def unit_back(grad, unit, inverse, gain):
     inner = grad * gain
     mean = jnp.mean(inner, axis=-1, keepdims=True)
     along = jnp.mean(inner * unit, axis=-1, keepdims=True)
-    return inverse * (inner - mean - unit * along), jnp.sum(grad * unit, axis=0), jnp.sum(grad, axis=0)
-
-
-def gelu(inner):
-    return jax.nn.gelu(inner, approximate=False)
+    return inverse * (inner - mean - unit * along)
+
+
+def column(values):
+    return jnp.sum(values, axis=0, keepdims=True)
+
+
+def norm_first(inputs, keep, far, w):
+    rows, dim = inputs.shape
+
+    def kernel(in_ref, keep_ref, far_ref, small_ref, unit_ref, inverse_ref, low_ref):
+        values = in_ref[...].astype(F32) + keep_ref[...] + far_ref[...].astype(F32) + small_ref[2:3, :]
+        unit, inverse = unit_of(values)
+        unit_ref[...] = unit
+        inverse_ref[...] = inverse
+        low_ref[...] = (unit * small_ref[4:5, :] + small_ref[6:7, :]).astype(BF)
+
+    return whole(kernel, [((rows, dim), F32), ((rows, 1), F32), ((rows, dim), BF)], inputs, keep, far, w.small)
+
+
+def norm_second(unit0, keep, far, w):
+    rows, dim = unit0.shape
+
+    def kernel(unit_ref, keep_ref, far_ref, small_ref, unit1_ref, inverse_ref, out_ref, low_ref):
+        hidden = unit_ref[...] * small_ref[4:5, :] + small_ref[6:7, :]
+        unit, inverse = unit_of(hidden + keep_ref[...] + far_ref[...].astype(F32) + small_ref[3:4, :])
+        out = unit * small_ref[5:6, :] + small_ref[7:8, :]
+        unit1_ref[...] = unit
+        inverse_ref[...] = inverse
+        out_ref[...] = out
+        low_ref[...] = out.astype(BF)
+
+    outs = [((rows, dim), F32), ((rows, 1), F32), ((rows, dim), F32), ((rows, dim), BF)]
+    return whole(kernel, outs, unit0, keep, far, w.small)
+
+
+def norm_second_back(residual, keep, far, unit1, inverse, w):
+    rows, dim = residual.shape
+
+    def kernel(res_ref, keep_ref, far_ref, unit_ref, inverse_ref, small_ref, sum_ref, low_ref, tiny_ref):
+        grad = res_ref[...] + keep_ref[...] + far_ref[...].astype(F32)
+        unit = unit_ref[...]
+        back = unit_back(grad, unit, inverse_ref[...], small_ref[5:6, :])
+        low = back.astype(BF)
+        sum_ref[...] = back
+        low_ref[...] = low
+        tiny_ref[...] = jnp.concatenate([column(low.astype(F32)), column(grad * unit), column(grad)], axis=0)
+
+    outs = [((rows, dim), F32), ((rows, dim), BF), ((3, dim), F32)]
+    return whole(kernel, outs, residual, keep, far, unit1, inverse, w.small)
+
+
+def norm_second_both(unit0, keep, far, cotangent, w):
+    rows, dim = unit0.shape
+
+    def kernel(unit_ref, keep_ref, far_ref, cot_ref, small_ref, out_ref, sum_ref, low_ref, tiny_ref):
+        hidden = unit_ref[...] * small_ref[4:5, :] + small_ref[6:7, :]
+        unit, inverse = unit_of(hidden + keep_ref[...] + far_ref[...].astype(F32) + small_ref[3:4, :])
+        out_ref[...] = unit * small_ref[5:6, :] + small_ref[7:8, :]
+        grad = cot_ref[...].astype(F32)
+        back = unit_back(grad, unit, inverse, small_ref[5:6, :])
+        low = back.astype(BF)
+        sum_ref[...] = back
+        low_ref[...] = low
+        tiny_ref[...] = jnp.concatenate([column(low.astype(F32)), column(grad * unit), column(grad)], axis=0)
+
+    outs = [((rows, dim), F32), ((rows, dim), F32), ((rows, dim), BF), ((3, dim), F32)]
+    return whole(kernel, outs, unit0, keep, far, cotangent, w.small)
+
+
+def norm_first_back(sum_grad, keep, far, unit0, inverse, w):
+    rows, dim = sum_grad.shape
+
+    def kernel(sum_ref, keep_ref, far_ref, unit_ref, inverse_ref, small_ref, out_ref, low_ref, tiny_ref):
+        grad = sum_ref[...] + keep_ref[...] + far_ref[...].astype(F32)
+        unit = unit_ref[...]
+        back = unit_back(grad, unit, inverse_ref[...], small_ref[4:5, :])
+        low = back.astype(BF)
+        out_ref[...] = back
+        low_ref[...] = low
+        tiny_ref[...] = jnp.concatenate([column(low.astype(F32)), column(grad * unit), column(grad)], axis=0)
+
+    outs = [((rows, dim), F32), ((rows, dim), BF), ((3, dim), F32)]
+    return whole(kernel, outs, sum_grad, keep, far, unit0, inverse, w.small)
+
+
+def gelu_and_slope(x):
+    bell = jnp.exp(-0.5 * x * x)
+    under = 1.0 + (0.3275911 * 0.5**0.5) * jnp.abs(x)
+    t = pl.reciprocal(under, approx=True)
+    t = t * (2.0 - under * t)
+    series = ((((1.061405429 * t - 1.453152027) * t + 1.421413741) * t - 0.284496736) * t + 0.254829592) * t
+    tail = (0.5 * series) * bell
+    below = jnp.where(x >= 0.0, 1.0 - tail, tail)
+    return x * below, below + x * bell * 0.3989422804014327
+
+
+FFN_TILE = 256
+
+
+def ffn_forward(near_half, far_half, w):
+    half, dim = near_half.shape
+    units = w.ffn_in.shape[1]
+
+    def kernel(a_ref, b_ref, in_ref, out_ref, bias_ref, keep_ref, near_ref, act_ref, slope_ref):
+        for part, rows_ref in enumerate((a_ref, b_ref)):
+            rows = slice(part * half, (part + 1) * half)
+            for u in range(0, units, FFN_TILE):
+                tile = slice(u, u + FFN_TILE)
+                active, slope = gelu_and_slope(dot(rows_ref[...], in_ref[:, tile]) + bias_ref[:, tile])
+                act_ref[rows, tile] = active.astype(BF)
+                slope_ref[rows, tile] = slope.astype(BF)
+            branch = dot(act_ref[rows, :], out_ref[...])
+            if part == 0:
+                keep_ref[...] = branch
+            else:
+                near_ref[...] = branch.astype(BF)
+
+    outs = [((half, dim), F32), ((half, dim), BF), ((2 * half, units), BF), ((2 * half, units), BF)]
+    return whole(kernel, outs, near_half, far_half, w.ffn_in, w.ffn_out, w.ffn_bias)
+
+
+def ffn_backward(near_half, far_half, slope, w):
+    half, dim = near_half.shape
+    units = w.ffn_in.shape[1]
+
+    def kernel(a_ref, b_ref, in_ref, out_ref, slope_ref, keep_ref, near_ref, inner_ref):
+        for part, rows_ref in enumerate((a_ref, b_ref)):
+            rows = slice(part * half, (part + 1) * half)
+            for u in range(0, units, FFN_TILE):
+                tile = slice(u, u + FFN_TILE)
+                back = dot_nt(rows_ref[...], out_ref[tile, :])
+                inner_ref[rows, tile] = (back * slope_ref[rows, tile].astype(F32)).astype(BF)
+            hidden = dot_nt(inner_ref[rows, :], in_ref[...])
+            if part == 0:
+                keep_ref[...] = hidden
+            else:
+                near_ref[...] = hidden.astype(BF)
+
+    outs = [((half, dim), F32), ((half, dim), BF), ((2 * half, units), BF)]
+    return whole(kernel, outs, near_half, far_half, w.ffn_in, w.ffn_out, slope)
 
 
 class Layer:
@@ -454,46 +619,28 @@
 
 
 def forward_tail(inputs, context, w):
-    attended = scatter_rows(dot(context, w.out)) + w.bias[2]
-    unit0, inverse0 = norm_parts(inputs + attended)
-    hidden = unit0 * w.gain[0] + w.shift[0]
-    hidden_all = gather_rows(hidden.astype(BF))
-    inner = dot(hidden_all, w.ffn_in) + w.ffn_bias
-    active = gelu(inner).astype(BF)
-    branch = scatter_rows(dot(active, w.ffn_out)) + w.bias[3]
-    unit1, inverse1 = norm_parts(hidden + branch)
-    output = unit1 * w.gain[1] + w.shift[1]
-    return output, (unit0, inverse0, hidden_all, inner, active, unit1, inverse1)
-
-
-def backward_tail(grad, context, kept, w):
-    unit0, inverse0, hidden_all, inner, active, unit1, inverse1 = kept
-    sum_grad, gain1, shift1 = norm_back(grad, unit1, inverse1, w.gain[1])
-    branch_low = sum_grad.astype(BF)
-    branch_all = gather_rows(branch_low)
-    active_grad = dot_nt(branch_all, w.ffn_out)
-    _, pull = jax.vjp(gelu, inner)
-    inner_grad = pull(active_grad)[0].astype(BF)
-    hidden_grad = sum_grad + scatter_rows(dot_nt(inner_grad, w.ffn_in))
-    input_grad, gain0, shift0 = norm_back(hidden_grad, unit0, inverse0, w.gain[0])
-    attended_low = input_grad.astype(BF)
-    attended_all = gather_rows(attended_low)
-    context_grad = dot_nt(attended_all, w.out).astype(BF)
+    keep, far = scatter_dots(dot(context, w.out))
+    unit0, inverse0, low = norm_first(inputs, keep, far, w)
+    halves = gather_halves(low)
+    keep, near, active, slope = ffn_forward(*halves, w)
+    return scatter_rows(keep, near), (unit0, inverse0, halves, active, slope)
+
+
+def backward_tail(sum_grad, low, kept, context, w):
+    unit0, inverse0, halves, active, slope = kept
+    branch = gather_halves(low)
+    keep, near, inner = ffn_backward(*branch, slope, w)
+    keep, far = scatter_rows(keep, near)
+    input_grad, attended_low, tiny = norm_first_back(sum_grad, keep, far, unit0, inverse0, w)
+    attended = jnp.concatenate(gather_halves(attended_low), axis=0)
+    context_grad = dot_nt(attended, w.out).astype(BF)
     weight_grads = (
-        dot_tn(context, attended_all),
-        dot_tn(hidden_all, inner_grad),
-        dot_tn(active, branch_all),
+        dot_tn(context, attended),
+        dot_tn(jnp.concatenate(halves, axis=0), inner),
+        dot_tn(active, jnp.concatenate(branch, axis=0)),
+        jnp.sum(inner.astype(F32), axis=0),
     )
-    small = (
-        jnp.sum(inner_grad.astype(F32), axis=0),
-        jnp.sum(attended_low.astype(F32), axis=0),
-        jnp.sum(branch_low.astype(F32), axis=0),
-        gain0,
-        gain1,
-        shift0,
-        shift1,
-    )
-    return input_grad, context_grad, weight_grads, small
+    return input_grad, context_grad, weight_grads, tiny
 
 
 def per_device(
@@ -622,8 +769,8 @@
         w.ffn_out = wback.reshape(n * ffn_part, dim)
         w.ffn_bias = lax.dynamic_slice_in_dim(
             bias_in.reshape(n, STREAMS, ffn_part), here, 1, axis=1
-        ).reshape(-1)
-        w.bias, w.gain, w.shift = bias, gain, shift
+        ).reshape(1, -1)
+        w.small = jnp.concatenate([bias, gain, shift], axis=0)
         mine = own_columns(bias, here)
         w.qkv_bias = jnp.concatenate([mine[0], jnp.zeros_like(mine[0]), mine[1]])
         return w
@@ -633,30 +780,34 @@
     dec.rel = dec_wrel.reshape(dim, rel_part)
     dec.rel_bias = own_columns(small_full[8], here)
 
-    enc_all = gather_rows(enc_input)
+    enc_all = jnp.concatenate(gather_halves(enc_input), axis=0)
     enc_heads = (dot(enc_all, enc.qkv) + enc.qkv_bias).astype(BF)
     enc_context, enc_lse = attention_forward(meta, enc_heads)
-    main_rows, enc_kept = forward_tail(enc_input.astype(F32), enc_context, enc)
-    stream_inputs = (main_rows, pred_input[0].astype(F32), pred_input[1].astype(F32))
-    stream_all = [gather_rows(low) for low in (main_rows.astype(BF), pred_input[0], pred_input[1])]
+    branch, enc_kept = forward_tail(enc_input, enc_context, enc)
+    enc_unit1, enc_inverse1, main_rows, main_low = norm_second(enc_kept[0], *branch, enc)
+    stream_inputs = (main_rows, pred_input[0], pred_input[1])
+    stream_all = [
+        jnp.concatenate(gather_halves(low), axis=0) for low in (main_low, pred_input[0], pred_input[1])
+    ]
     heads = [(dot(low, dec.qkv) + dec.qkv_bias).astype(BF) for low in stream_all]
     rels = [dot(low, dec.rel) + dec.rel_bias for low in stream_all]
-    contexts, lses, kept, outputs = [], [], [], []
+    contexts, lses, kept, outputs, firsts = [], [], [], [], []
     for i in range(3):
         context, lse = attention_forward(meta, heads[i], None if i == 0 else heads[0], rels[i], tables)
-        output, keep = forward_tail(stream_inputs[i], context, dec)
+        branch, keep = forward_tail(stream_inputs[i], context, dec)
+        output, *first = norm_second_both(keep[0], *branch, cotangent[i], dec)
         contexts.append(context)
         lses.append(lse)
         kept.append(keep)
         outputs.append(output)
-
-    residuals, weight_grads, smalls, dheads, drels = [], [], [], [], []
+        firsts.append(first)
+
+    residuals, weight_grads, tinies, dheads, drels = [], [], [], [], []
     key_grad = val_grad = 0.0
     query_main = None
     for i in range(3):
-        residual, dctx, weights, small = backward_tail(
-            cotangent[i].astype(F32), contexts[i], kept[i], dec
-        )
+        sum_grad, low, tiny1 = firsts[i]
+        residual, dctx, weights, tiny0 = backward_tail(sum_grad, low, kept[i], contexts[i], dec)
         result = attention_backward(
             meta, heads[i], dctx, lses[i], None if i == 0 else heads[0], rels[i], tables
         )
@@ -670,28 +821,42 @@
             dheads.append(jnp.concatenate([result[0], result[4], result[5]], axis=1))
         residuals.append(residual)
         weight_grads.append(weights)
-        smalls.append(small)
+        tinies.append((tiny0, tiny1))
     dheads[0] = jnp.concatenate([query_main, key_grad.astype(BF), val_grad.astype(BF)], axis=1)
-    input_grads = [
-        residuals[i] + scatter_rows(dot_nt(dheads[i], dec.qkv) + dot_nt(drels[i], dec.rel)) for i in range(3)
+    input_parts = [
+        scatter_dots(dot_nt(dheads[i], dec.qkv) + dot_nt(drels[i], dec.rel)) for i in range(3)
     ]
+    pred_grads = [residuals[i] + input_parts[i][0] + input_parts[i][1].astype(F32) for i in (1, 2)]
     dec_qkv_part = sum(dot_tn(stream_all[i], dheads[i]) for i in range(3)).astype(BF)
     dec_rel_part = sum(dot_tn(stream_all[i], drels[i]) for i in range(3)).astype(BF)
     dec_out_part, dec_in_part, dec_back_part = [
         sum(weight_grads[i][k] for i in range(3)).astype(BF) for k in range(3)
     ]
-    dec_small = [sum(smalls[i][k] for i in range(3)) for k in range(7)]
+    dec_inner = sum(weight_grads[i][3] for i in range(3))
+    dec_tiny0, dec_tiny1 = [sum(tinies[i][k] for i in range(3)) for k in range(2)]
     head_sum = sum(jnp.sum(dheads[i].astype(F32), axis=0) for i in range(3))
     rel_sum = sum(jnp.sum(drels[i].astype(F32), axis=0) for i in range(3))
 
     def widen(part, size):
         return lax.dynamic_update_slice(jnp.zeros((size,), F32), part, (here * part.shape[0],))
 
-    def small_pack(small, heads_grad, rel_grad=None):
-        wide = jnp.stack([widen(heads_grad[:quarter], dim), widen(heads_grad[2 * quarter :], dim)] + list(small[1:]))
+    def small_pack(inner_grad, tiny0, tiny1, heads_grad, rel_grad=None):
+        wide = jnp.concatenate(
+            [
+                widen(heads_grad[:quarter], dim)[None],
+                widen(heads_grad[2 * quarter :], dim)[None],
+                tiny0[0:1],
+                tiny1[0:1],
+                tiny0[1:2],
+                tiny1[1:2],
+                tiny0[2:3],
+                tiny1[2:3],
+            ],
+            axis=0,
+        )
         parts = [
             jnp.transpose(wide.reshape(8, n, share), (1, 0, 2)).reshape(n, 8 * share),
-            small[0].reshape(n, ffn_part),
+            inner_grad.reshape(n, ffn_part),
         ]
         if rel_grad is not None:
             parts.append(widen(rel_grad, rel_all).reshape(n, rel_all // n))
@@ -715,18 +880,22 @@
         dec_out_part,
         [
             jnp.concatenate([rel_blocks[:, :half], rel_blocks[:, half:]], axis=2),
-            small_pack(dec_small, head_sum, rel_sum),
+            small_pack(dec_inner, dec_tiny0, dec_tiny1, head_sum, rel_sum),
         ],
     )
 
-    residual, dctx, enc_weights, enc_small = backward_tail(input_grads[0], enc_context, enc_kept, enc)
+    sum_grad, low, enc_tiny1 = norm_second_back(residuals[0], *input_parts[0], enc_unit1, enc_inverse1, enc)
+    residual, dctx, enc_weights, enc_tiny0 = backward_tail(sum_grad, low, enc_kept, enc_context, enc)
     dq, dk, dv = attention_backward(meta, enc_heads, dctx, enc_lse)
     enc_dheads = jnp.concatenate([dq, dk.astype(BF), dv.astype(BF)], axis=1)
-    enc_input_grad = residual + scatter_rows(dot_nt(enc_dheads, enc.qkv))
+    keep, far = scatter_dots(dot_nt(enc_dheads, enc.qkv))
+    enc_input_grad = residual + keep + far.astype(F32)
     enc_ffn_sum = ffn_sum(enc_weights[1].astype(BF), enc_weights[2].astype(BF))
     enc_head_sum = jnp.sum(enc_dheads.astype(F32), axis=0)
     enc_attention_sum = attention_sum(
-        dot_tn(enc_all, enc_dheads).astype(BF), enc_weights[0].astype(BF), [small_pack(enc_small, enc_head_sum)]
+        dot_tn(enc_all, enc_dheads).astype(BF),
+        enc_weights[0].astype(BF),
+        [small_pack(enc_weights[3], enc_tiny0, enc_tiny1, enc_head_sum)],
     )
 
     def spread(total_rows):
@@ -772,7 +941,7 @@
     return (
         jnp.stack(outputs),
         enc_input_grad,
-        jnp.stack([input_grads[1], input_grads[2]]),
+        jnp.stack(pred_grads),
         enc_qkv_grad,
         enc_out_grad,
         enc_in_grad,

time: 728 us -> 648 us (0.89)
  matrix products: 123 us -> 49.8 us
  other arithmetic: 74.1 us -> 47.7 us
  waiting for transfers between devices: 162 us -> 177 us
    dot_general x19 -> x11, matrix products: 56.3 us -> 9.17 us  [dot(): return jnp.dot(a, b, preferred_element_type=F32)]
    pallas_call x0 -> x21, Pallas kernels: none -> 40.6 us  [whole(): pl.pallas_call(kernel, out_shape=[jax.ShapeDtypeStruct(shape, kind) for s...]
    dot_general x19 -> x11, matrix products: 37.9 us -> 13.3 us  [dot_nt(): lax.dot_general(a, b, (((1,), (1,)), ((), ())), preferred_element_type=F32)]
    ppermute x64, waiting for transfers between devices: 57.2 us -> 79.5 us  [ring_step(): return lax.ppermute(values, 'dp', pairs)]
    pallas_call x4, Pallas kernels: 51.5 us -> 37.6 us  [attention_backward(): pl.pallas_call(kernel, out_shape=outs, in_specs=[pl.BlockSpec(memory_spac...]
    reduce_sum x23 -> x4, other arithmetic: 15.1 us -> 1.31 us  [backward_tail(): jnp.sum(inner.astype(F32), axis=0)]
    pallas_call x4, Pallas kernels: 34.6 us -> 22.2 us  [attention_forward(): pl.pallas_call(kernel, out_shape=(jax.ShapeDtypeStruct((total, width_all)...]
    pallas_call x4, Pallas kernels: 14.9 us -> 4.36 us  [assemble(): pl.pallas_call(kernel, out_shape=[jax.ShapeDtypeStruct((n,) + shape, BF)...]
  transfers between devices with their start and end apart: 144 -> 144, of which waited for: 48 -> 47; matrix products, arithmetic and copies ran while one was open for 32% -> 25% of each run, Pallas kernels for 14% -> 16%
where the time goes in v2:
time: 648 us; the launch traced here: 637 us
  waiting for transfers between devices  177 us (27%)
  starting transfers between devices  152 us (23%)
  Pallas kernels  105 us (16%)
  local copies, waits for them, and re-layouts  99.4 us (15%)
  matrix products  49.8 us (8%)
  other arithmetic  47.7 us (7%)
  between operations  6.75 us (1%)
    ppermute x80, waiting for transfers between devices, swap(): lax.ppermute(values, 'stream', [(i, i ^ bit) for i in range(STREAMS)])  97.4 us
    ppermute x80, starting transfers between devices, swap(): lax.ppermute(values, 'stream', [(i, i ^ bit) for i in range(STREAMS)])  96.6 us
    ppermute x64, waiting for transfers between devices, ring_step(): return lax.ppermute(values, 'dp', pairs)  79.5 us
    ppermute x64, starting transfers between devices, ring_step(): return lax.ppermute(values, 'dp', pairs)  55.5 us
    pallas_call x21, Pallas kernels, whole(): pl.pallas_call(kernel, out_shape=[jax.ShapeDtypeStruct(shape, kind) for s...  40.6 us
    unnamed x701, local copies, waits for them, and re-layouts  40.2 us
    pallas_call x4, Pallas kernels, attention_backward(): pl.pallas_call(kernel, out_shape=outs, in_specs=[pl.BlockSpec(memory_spac...  37.6 us
    dot_general x19, matrix products, dot_tn(): lax.dot_general(a, b, (((0,), (0,)), ((), ())), preferred_element_type=F32)  27.3 us
  transfers between devices with their start and end apart: 144, of which 47 were waited for; matrix products, arithmetic and copies ran while one was open for 25% of the time, Pallas kernels for 16%

profile of v2, /device:TPU:1, one launch (start us, length us, event | category | flops | bytes accessed | tf_op | source)
XLA Modules:
  0.0 637.3 jit_solution(16220605378661184276)
XLA Ops:
  14.0 9.2 %collective-permute-done.3.refs_2_ = bf16[528,256]{1,0:T(8,128)(2,1)S(1)} collective-permute-done((bf16[528,256]{1,0:T(8,128)(2,1)S(1)}, bf16[528,256]{1,0:T(8,128)(2,1)S(1)}, u32[]{:S(2)}, u32[]{:S(2)}) %collective-permute-start.3) | collective-permute-done | bytes 270368 | tf_op jit(solution)/shard_map/ppermute | solution.py:83
  45.6 3.5 collective-permute-done.10
  49.2 6.5 %collective-permute-start.11 = (bf16[2,256,256]{2,1,0:T(8,128)(2,1)S(1)}, bf16[2,256,256]{2,1,0:T(8,128)(2,1)S(1)}, u32[]{:S(2)}, u32[]{:S(2)}) collective-permute-start(bf16[2,256,256]{2,1,0:T(8,128)(2,1)S(1)} %pad_maximum_fusion.41), channel_id=1, source_target_pairs={{0,8},{8,0},{16,24},{24,16},{1,9},{9,1},{17,25},{25,17},{2,10},{10... | collective-permute-start | bytes 786440 | tf_op jit(solution)/shard_map/ppermute | solution.py:36
  56.7 4.7 shard_map.392
  69.2 3.9 collective-permute-done.30.refs_3_
  76.4 4.1 collective-permute-done.52
  85.9 4.8 collective-permute-done.32.refs_5_
  93.8 3.4 collective-permute-done.14
  105.8 7.5 %collective-permute-done.20.refs_5_ = bf16[256,1024]{1,0:T(8,128)(2,1)S(1)} collective-permute-done((bf16[256,1024]{1,0:T(8,128)(2,1)S(1)}, bf16[256,1024]{1,0:T(8,128)(2,1)S(1)}, u32[]{:S(2)}, u32[]{:S(2)}) %collective-permute-start.20) | collective-permute-done | bytes 524320 | tf_op jit(solution)/shard_map/ppermute | solution.py:83
  132.7 5.6 shard_map.395
  145.2 4.9 collective-permute-done.25.far_ref
  159.5 7.7 %collective-permute-done.46.refs_5_ = bf16[256,1024]{1,0:T(8,128)(2,1)S(1)} collective-permute-done((bf16[256,1024]{1,0:T(8,128)(2,1)S(1)}, bf16[256,1024]{1,0:T(8,128)(2,1)S(1)}, u32[]{:S(2)}, u32[]{:S(2)}) %collective-permute-start.46) | collective-permute-done | bytes 524320 | tf_op jit(solution)/shard_map/ppermute | solution.py:83
  170.4 5.9 shard_map.403
  178.2 5.9 shard_map.407
  185.3 5.8 shard_map.398
  194.1 6.2 collective-permute-done.55.far_ref
  202.4 3.5 collective-permute-done.63.far_ref
  207.5 4.0 collective-permute-done.56
  213.5 3.7 collective-permute-done.39.far_ref
  218.6 4.2 collective-permute-done.64
  229.3 4.3 shard_map.405
  235.3 4.7 shard_map.409
  242.0 4.3 shard_map.401
  290.6 3.8 shard_map.414
  294.5 3.7 shard_map.417
  298.7 3.7 shard_map.411
  318.6 5.4 collective-permute-done.138
  332.4 3.9 collective-permute-done.83.far_ref
  337.3 4.7 collective-permute-done.71.far_ref
  347.6 4.1 collective-permute-start.79
  353.2 4.1 collective-permute-start.85
  371.1 7.9 %shard_map.413 = (bf16[512,256]{1,0:T(8,128)(2,1)S(1)}, f32[512,256]{1,0:T(8,128)S(1)}, f32[512,256]{1,0:T(8,128)S(1)}, bf16[512,128]{1,0:T(8,128)(2,1)S(1)}) custom-call(s32[11]{0:T(128)S(1)} %stack.259.meta_ref, bf16[512,768]{1,0:T(8,128)(2,1)S(1)} %add_convert_fusion.5.refs_0_.refs_1_.refs_3_, bf16[512,256]{1,0:T(8,128)(2,1)S(1)} %convolution_convert_fusion.7.refs_1_, ...), custom_call_target="tpu_custom_call" | custom-call | tf_op jit(solution)/shard_map/pallas_call | solution.py:420
  379.6 11.6 %shard_map.416 = (bf16[512,256]{1,0:T(8,128)(2,1)S(1)}, f32[512,256]{1,0:T(8,128)S(1)}, f32[512,256]{1,0:T(8,128)S(1)}, bf16[512,128]{1,0:T(8,128)(2,1)S(1)}, bf...) custom-call(s32[11]{0:T(128)S(1)} %stack.259.meta_ref, bf16[512,768]{1,0:T(8,128)(2,1)S(1)} %copy-done.23, ...), custom_call_target="tpu_custom_call" | custom-call | tf_op jit(solution)/shard_map/pallas_call | solution.py:420
  391.3 11.7 %shard_map.419 = (bf16[512,256]{1,0:T(8,128)(2,1)S(1)}, f32[512,256]{1,0:T(8,128)S(1)}, f32[512,256]{1,0:T(8,128)S(1)}, bf16[512,128]{1,0:T(8,128)(2,1)S(1)}, bf...) custom-call(s32[11]{0:T(128)S(1)} %stack.259.meta_ref, bf16[512,768]{1,0:T(8,128)(2,1)S(1)} %copy-done.21, ...), custom_call_target="tpu_custom_call" | custom-call | tf_op jit(solution)/shard_map/pallas_call | solution.py:420
  437.5 14.0 %collective-permute-done.87.far_ref = bf16[128,1024]{1,0:T(8,128)(2,1)S(1)} collective-permute-done((bf16[128,1024]{1,0:T(8,128)(2,1)S(1)}, bf16[128,1024]{1,0:T(8,128)(2,1)S(1)}, u32[]{:S(2)}, u32[]{:S(2)}) %collective-permute-start.87) | collective-permute-done | bytes 262176 | tf_op jit(solution)/shard_map/ppermute | solution.py:36
  457.1 5.6 collective-permute-done.88
  464.7 3.6 collective-permute-done.99
  491.5 5.2 collective-permute-done.113
  502.6 4.4 collective-permute-done.92
  507.0 4.2 collective-permute-start.93
  515.7 6.3 shard_map.423
  538.4 3.2 collective-permute-start.94
  553.5 4.2 collective-permute-done.106
  566.7 5.2 collective-permute-done.129
  573.4 4.1 collective-permute-done.108
  579.9 4.1 collective-permute-done.130
  585.6 4.2 collective-permute-done.109
  597.4 8.8 %collective-permute-start.111 = (bf16[2,528,256]{2,1,0:T(8,128)(2,1)}, bf16[2,528,256]{2,1,0:T(8,128)(2,1)}, u32[]{:S(2)}, u32[]{:S(2)}) collective-permute-start(bf16[2,528,256]{2,1,0:T(8,128)(2,1)} %pad_maximum_fusion.13), channel_id=1, source_target_pairs={{0,8},{8,0},{16,24},{24,16},{1,9},{9,1},{17,25},{25,17},{2,10},{10... | collective-permute-start | bytes 1622024 | tf_op jit(solution)/shard_map/ppermute | solution.py:36
  (1303 shorter events, 370.5 us)
Async XLA Ops:
  2.7 63.4 %collective-permute-start.16 = (bf16[256,1024]{1,0:T(8,128)(2,1)S(1)}, bf16[256,1024]{1,0:T(8,128)(2,1)}, u32[]{:S(2)}, u32[]{:S(2)}) collective-permute-start(bf16[256,1024]{1,0:T(8,128)(2,1)S(1)} %pad_maximum_fusion.17.refs_0_), channel_id=1, source_target_pairs={{0,2},{2,4},{4,6},{6,7},{7,5},{5,3},{3,1},{1,0},{8,10},{10,12},{12... | collective-permute-start | bytes 1572872 | tf_op jit(solution)/shard_map/ppermute | solution.py:83
  4.9 61.9 %collective-permute-start.17 = (bf16[256,1024]{1,0:T(8,128)(2,1)S(1)}, bf16[256,1024]{1,0:T(8,128)(2,1)}, u32[]{:S(2)}, u32[]{:S(2)}) collective-permute-start(bf16[256,1024]{1,0:T(8,128)(2,1)S(1)} %pad_maximum_fusion.17.refs_0_), channel_id=1, source_target_pairs={{0,1},{2,0},{4,2},{6,4},{7,6},{5,7},{3,5},{1,3},{8,9},{10,8},{12,1... | collective-permute-start | bytes 1572872 | tf_op jit(solution)/shard_map/ppermute | solution.py:83
  38.2 26.3 %collective-permute-start.28 = (bf16[576,256]{1,0:T(8,128)(2,1)S(1)}, bf16[576,256]{1,0:T(8,128)(2,1)S(1)}, u32[]{:S(2)}, u32[]{:S(2)}) collective-permute-start(bf16[576,256]{1,0:T(8,128)(2,1)S(1)} %maximum_maximum_fusion.refs_0_), channel_id=1, source_target_pairs={{0,2},{2,4},{4,6},{6,7},{7,5},{5,3},{3,1},{1,0},{8,10},{10,12},{12... | collective-permute-start | bytes 884744 | tf_op jit(solution)/shard_map/ppermute | solution.py:83
  41.1 24.2 %collective-permute-start.29 = (bf16[576,256]{1,0:T(8,128)(2,1)S(1)}, bf16[576,256]{1,0:T(8,128)(2,1)S(1)}, u32[]{:S(2)}, u32[]{:S(2)}) collective-permute-start(bf16[576,256]{1,0:T(8,128)(2,1)S(1)} %maximum_maximum_fusion.refs_0_), channel_id=1, source_target_pairs={{0,1},{2,0},{4,2},{6,4},{7,6},{5,7},{3,5},{1,3},{8,9},{10,8},{12,1... | collective-permute-start | bytes 884744 | tf_op jit(solution)/shard_map/ppermute | solution.py:83
  66.1 18.3 %collective-permute-start.18 = (bf16[256,1024]{1,0:T(8,128)(2,1)}, bf16[256,1024]{1,0:T(8,128)(2,1)S(1)}, u32[]{:S(2)}, u32[]{:S(2)}) collective-permute-start(bf16[256,1024]{1,0:T(8,128)(2,1)} %collective-permute-done.16.refs_1_), channel_id=1, source_target_pairs={{0,2},{2,4},{4,6},{6,7},{7,5},{5,3},{3,1},{1,0},{8,10},{10,12},{12... | collective-permute-start | bytes 1572872 | tf_op jit(solution)/shard_map/ppermute | solution.py:83
  66.8 18.3 %collective-permute-start.19 = (bf16[256,1024]{1,0:T(8,128)(2,1)}, bf16[256,1024]{1,0:T(8,128)(2,1)S(1)}, u32[]{:S(2)}, u32[]{:S(2)}) collective-permute-start(bf16[256,1024]{1,0:T(8,128)(2,1)} %collective-permute-done.17.refs_2_), channel_id=1, source_target_pairs={{0,1},{2,0},{4,2},{6,4},{7,6},{5,7},{3,5},{1,3},{8,9},{10,8},{12,1... | collective-permute-start | bytes 1572872 | tf_op jit(solution)/shard_map/ppermute | solution.py:83
  74.4 16.3 %collective-permute-start.32 = (bf16[576,256]{1,0:T(8,128)(2,1)S(1)}, bf16[576,256]{1,0:T(8,128)(2,1)S(1)}, u32[]{:S(2)}, u32[]{:S(2)}) collective-permute-start(bf16[576,256]{1,0:T(8,128)(2,1)S(1)} %collective-permute-done.30.refs_3_), channel_id=1, source_target_pairs={{0,2},{2,4},{4,6},{6,7},{7,5},{5,3},{3,1},{1,0},{8,10},{10,12},{12... | collective-permute-start | bytes 884744 | tf_op jit(solution)/shard_map/ppermute | solution.py:83
  74.7 17.9 %collective-permute-start.33 = (bf16[576,256]{1,0:T(8,128)(2,1)S(1)}, bf16[576,256]{1,0:T(8,128)(2,1)S(1)}, u32[]{:S(2)}, u32[]{:S(2)}) collective-permute-start(bf16[576,256]{1,0:T(8,128)(2,1)S(1)} %collective-permute-done.31.refs_4_), channel_id=1, source_target_pairs={{0,1},{2,0},{4,2},{6,4},{7,6},{5,7},{3,5},{1,3},{8,9},{10,8},{12,1... | collective-permute-start | bytes 884744 | tf_op jit(solution)/shard_map/ppermute | solution.py:83
  80.5 24.6 %collective-permute-start.42 = (bf16[256,1024]{1,0:T(8,128)(2,1)S(1)}, bf16[256,1024]{1,0:T(8,128)(2,1)S(1)}, u32[]{:S(2)}, u32[]{:S(2)}) collective-permute-start(bf16[256,1024]{1,0:T(8,128)(2,1)S(1)} %pad_maximum_fusion.21.refs_0_), channel_id=1, source_target_pairs={{0,2},{2,4},{4,6},{6,7},{7,5},{5,3},{3,1},{1,0},{8,10},{10,12},{12... | collective-permute-start | bytes 1572872 | tf_op jit(solution)/shard_map/ppermute | solution.py:83
  84.4 28.9 %collective-permute-start.20 = (bf16[256,1024]{1,0:T(8,128)(2,1)S(1)}, bf16[256,1024]{1,0:T(8,128)(2,1)S(1)}, u32[]{:S(2)}, u32[]{:S(2)}) collective-permute-start(bf16[256,1024]{1,0:T(8,128)(2,1)S(1)} %collective-permute-done.18.refs_3_), channel_id=1, source_target_pairs={{0,2},{2,4},{4,6},{6,7},{7,5},{5,3},{3,1},{1,0},{8,10},{10,12},{12... | collective-permute-start | bytes 1572872 | tf_op jit(solution)/shard_map/ppermute | solution.py:83
  85.1 29.5 %collective-permute-start.21 = (bf16[256,1024]{1,0:T(8,128)(2,1)S(1)}, bf16[256,1024]{1,0:T(8,128)(2,1)S(1)}, u32[]{:S(2)}, u32[]{:S(2)}) collective-permute-start(bf16[256,1024]{1,0:T(8,128)(2,1)S(1)} %collective-permute-done.19.refs_4_), channel_id=1, source_target_pairs={{0,1},{2,0},{4,2},{6,4},{7,6},{5,7},{3,5},{1,3},{8,9},{10,8},{12,1... | collective-permute-start | bytes 1572872 | tf_op jit(solution)/shard_map/ppermute | solution.py:83
  97.2 29.5 %collective-permute-start.43 = (bf16[256,1024]{1,0:T(8,128)(2,1)S(1)}, bf16[256,1024]{1,0:T(8,128)(2,1)}, u32[]{:S(2)}, u32[]{:S(2)}) collective-permute-start(bf16[256,1024]{1,0:T(8,128)(2,1)S(1)} %pad_maximum_fusion.21.refs_0_), channel_id=1, source_target_pairs={{0,1},{2,0},{4,2},{6,4},{7,6},{5,7},{3,5},{1,3},{8,9},{10,8},{12,1... | collective-permute-start | bytes 1572872 | tf_op jit(solution)/shard_map/ppermute | solution.py:83
  102.9 35.5 %collective-permute-start.53 = (bf16[256,1024]{1,0:T(8,128)(2,1)}, bf16[256,1024]{1,0:T(8,128)(2,1)}, u32[]{:S(2)}, u32[]{:S(2)}) collective-permute-start(bf16[256,1024]{1,0:T(8,128)(2,1)} %pad_maximum_fusion.22), channel_id=1, source_target_pairs={{0,8},{8,0},{16,24},{24,16},{1,9},{9,1},{17,25},{25,17},{2,10},{10... | collective-permute-start | bytes 1572872 | tf_op jit(solution)/shard_map/ppermute | solution.py:36
  114.6 16.8 %collective-permute-start.15 = (bf16[256,1024]{1,0:T(8,128)(2,1)}, bf16[256,1024]{1,0:T(8,128)(2,1)}, u32[]{:S(2)}, u32[]{:S(2)}) collective-permute-start(bf16[256,1024]{1,0:T(8,128)(2,1)} %constant_dynamic-update-slice_fusion.3.a_ref), channel_id=1, source_target_pairs={{0,8},{8,0},{16,24},{24,16},{1,9},{9,1},{17,25},{25,17},{2,10},{10... | collective-permute-start | bytes 1572872 | tf_op jit(solution)/shard_map/ppermute | solution.py:36
  128.2 25.5 %collective-permute-start.44 = (bf16[256,1024]{1,0:T(8,128)(2,1)S(1)}, bf16[256,1024]{1,0:T(8,128)(2,1)S(1)}, u32[]{:S(2)}, u32[]{:S(2)}) collective-permute-start(bf16[256,1024]{1,0:T(8,128)(2,1)S(1)} %copy-done.90), channel_id=1, source_target_pairs={{0,2},{2,4},{4,6},{6,7},{7,5},{5,3},{3,1},{1,0},{8,10},{10,12},{12... | collective-permute-start | bytes 1572872 | tf_op jit(solution)/shard_map/ppermute | solution.py:83
  128.4 25.5 %collective-permute-start.45 = (bf16[256,1024]{1,0:T(8,128)(2,1)}, bf16[256,1024]{1,0:T(8,128)(2,1)S(1)}, u32[]{:S(2)}, u32[]{:S(2)}) collective-permute-start(bf16[256,1024]{1,0:T(8,128)(2,1)} %collective-permute-done.43.refs_2_), channel_id=1, source_target_pairs={{0,1},{2,0},{4,2},{6,4},{7,6},{5,7},{3,5},{1,3},{8,9},{10,8},{12,1... | collective-permute-start | bytes 1572872 | tf_op jit(solution)/shard_map/ppermute | solution.py:83
  167.3 57.5 %collective-permute-start.48 = (bf16[128,1024]{1,0:T(8,128)(2,1)S(1)}, bf16[128,1024]{1,0:T(8,128)(2,1)S(1)}, u32[]{:S(2)}, u32[]{:S(2)}) collective-permute-start(bf16[128,1024]{1,0:T(8,128)(2,1)S(1)} %slice.1227), channel_id=1, source_target_pairs={{0,2},{2,4},{4,6},{6,7},{7,5},{5,3},{3,1},{1,0},{8,10},{10,12},{12... | collective-permute-start | bytes 786440 | tf_op jit(solution)/shard_map/ppermute | solution.py:83
  167.5 57.3 %collective-permute-start.49 = (bf16[128,1024]{1,0:T(8,128)(2,1)S(1)}, bf16[128,1024]{1,0:T(8,128)(2,1)S(1)}, u32[]{:S(2)}, u32[]{:S(2)}) collective-permute-start(bf16[128,1024]{1,0:T(8,128)(2,1)S(1)} %slice.1228), channel_id=1, source_target_pairs={{0,1},{2,0},{4,2},{6,4},{7,6},{5,7},{3,5},{1,3},{8,9},{10,8},{12,1... | collective-permute-start | bytes 786440 | tf_op jit(solution)/shard_map/ppermute | solution.py:83
  212.2 17.1 %collective-permute-start.57 = (bf16[256,1024]{1,0:T(8,128)(2,1)S(1)}, bf16[256,1024]{1,0:T(8,128)(2,1)S(1)}, u32[]{:S(2)}, u32[]{:S(2)}) collective-permute-start(bf16[256,1024]{1,0:T(8,128)(2,1)S(1)} %constant_dynamic-update-slice_fusion.10.a_ref), channel_id=1, source_target_pairs={{0,8},{8,0},{16,24},{24,16},{1,9},{9,1},{17,25},{25,17},{2,10},{10... | collective-permute-start | bytes 1572872 | tf_op jit(solution)/shard_map/ppermute | solution.py:36
  251.6 16.0 %collective-permute-start.51 = (bf16[128,1024]{1,0:T(8,128)(2,1)}, bf16[128,1024]{1,0:T(8,128)(2,1)}, u32[]{:S(2)}, u32[]{:S(2)}) collective-permute-start(bf16[128,1024]{1,0:T(8,128)(2,1)} %get-tuple-element.309), channel_id=1, source_target_pairs={{0,16},{8,24},{16,0},{24,8},{1,17},{9,25},{17,1},{25,9},{2,18},{10... | collective-permute-start | bytes 786440 | tf_op jit(solution)/shard_map/ppermute | solution.py:36
  273.5 17.0 %collective-permute-start.75 = (bf16[256,1024]{1,0:T(8,128)(2,1)}, bf16[256,1024]{1,0:T(8,128)(2,1)}, u32[]{:S(2)}, u32[]{:S(2)}) collective-permute-start(bf16[256,1024]{1,0:T(8,128)(2,1)} %constant_dynamic-update-slice_fusion.19.a_ref), channel_id=1, source_target_pairs={{0,8},{8,0},{16,24},{24,16},{1,9},{9,1},{17,25},{25,17},{2,10},{10... | collective-permute-start | bytes 1572872 | tf_op jit(solution)/shard_map/ppermute | solution.py:36
  294.4 29.6 %collective-permute-start.76 = (bf16[256,1024]{1,0:T(8,128)(2,1)S(1)}, bf16[256,1024]{1,0:T(8,128)(2,1)S(1)}, u32[]{:S(2)}, u32[]{:S(2)}) collective-permute-start(bf16[256,1024]{1,0:T(8,128)(2,1)S(1)} %get-tuple-element.179), channel_id=1, source_target_pairs={{0,8},{8,0},{16,24},{24,16},{1,9},{9,1},{17,25},{25,17},{2,10},{10... | collective-permute-start | bytes 1572872 | tf_op jit(solution)/shard_map/ppermute | solution.py:36
  298.2 26.5 %collective-permute-start.82 = (bf16[256,1024]{1,0:T(8,128)(2,1)S(1)}, bf16[256,1024]{1,0:T(8,128)(2,1)S(1)}, u32[]{:S(2)}, u32[]{:S(2)}) collective-permute-start(bf16[256,1024]{1,0:T(8,128)(2,1)S(1)} %get-tuple-element.188), channel_id=1, source_target_pairs={{0,8},{8,0},{16,24},{24,16},{1,9},{9,1},{17,25},{25,17},{2,10},{10... | collective-permute-start | bytes 1572872 | tf_op jit(solution)/shard_map/ppermute | solution.py:36
  302.4 23.5 %collective-permute-start.70 = (bf16[256,1024]{1,0:T(8,128)(2,1)S(1)}, bf16[256,1024]{1,0:T(8,128)(2,1)S(1)}, u32[]{:S(2)}, u32[]{:S(2)}) collective-permute-start(bf16[256,1024]{1,0:T(8,128)(2,1)S(1)} %get-tuple-element.168), channel_id=1, source_target_pairs={{0,8},{8,0},{16,24},{24,16},{1,9},{9,1},{17,25},{25,17},{2,10},{10... | collective-permute-start | bytes 1572872 | tf_op jit(solution)/shard_map/ppermute | solution.py:36
  318.3 24.6 %collective-permute-start.135 = (bf16[256,1024]{1,0:T(8,128)(2,1)S(1)}, bf16[256,1024]{1,0:T(8,128)(2,1)S(1)}, u32[]{:S(2)}, u32[]{:S(2)}) collective-permute-start(bf16[256,1024]{1,0:T(8,128)(2,1)S(1)} %pad_maximum_fusion.34), channel_id=1, source_target_pairs={{0,2},{2,4},{4,6},{6,7},{7,5},{5,3},{3,1},{1,0},{8,10},{10,12},{12... | collective-permute-start | bytes 1572872 | tf_op jit(solution)/shard_map/ppermute | solution.py:83
  326.1 15.9 %collective-permute-start.71 = (bf16[128,1024]{1,0:T(8,128)(2,1)S(1)}, bf16[128,1024]{1,0:T(8,128)(2,1)S(1)}, u32[]{:S(2)}, u32[]{:S(2)}) collective-permute-start(bf16[128,1024]{1,0:T(8,128)(2,1)S(1)} %get-tuple-element.307), channel_id=1, source_target_pairs={{0,16},{8,24},{16,0},{24,8},{1,17},{9,25},{17,1},{25,9},{2,18},{10... | collective-permute-start | bytes 786440 | tf_op jit(solution)/shard_map/ppermute | solution.py:36
  326.7 16.6 %collective-permute-start.139 = (bf16[256,1024]{1,0:T(8,128)(2,1)S(1)}, bf16[256,1024]{1,0:T(8,128)(2,1)S(1)}, u32[]{:S(2)}, u32[]{:S(2)}) collective-permute-start(bf16[256,1024]{1,0:T(8,128)(2,1)S(1)} %pad_maximum_fusion.35), channel_id=1, source_target_pairs={{0,1},{2,0},{4,2},{6,4},{7,6},{5,7},{3,5},{1,3},{8,9},{10,8},{12,1... | collective-permute-start | bytes 1572872 | tf_op jit(solution)/shard_map/ppermute | solution.py:83
  336.8 16.4 %collective-permute-start.84 = (bf16[128,1024]{1,0:T(8,128)(2,1)S(1)}, bf16[128,1024]{1,0:T(8,128)(2,1)S(1)}, u32[]{:S(2)}, u32[]{:S(2)}) collective-permute-start(bf16[128,1024]{1,0:T(8,128)(2,1)S(1)} %get-tuple-element.190), channel_id=1, source_target_pairs={{0,16},{8,24},{16,0},{24,8},{1,17},{9,25},{17,1},{25,9},{2,18},{10... | collective-permute-start | bytes 786440 | tf_op jit(solution)/shard_map/ppermute | solution.py:36
  342.4 16.4 %collective-permute-start.72 = (bf16[128,1024]{1,0:T(8,128)(2,1)S(1)}, bf16[128,1024]{1,0:T(8,128)(2,1)S(1)}, u32[]{:S(2)}, u32[]{:S(2)}) collective-permute-start(bf16[128,1024]{1,0:T(8,128)(2,1)S(1)} %get-tuple-element.171), channel_id=1, source_target_pairs={{0,16},{8,24},{16,0},{24,8},{1,17},{9,25},{17,1},{25,9},{2,18},{10... | collective-permute-start | bytes 786440 | tf_op jit(solution)/shard_map/ppermute | solution.py:36
  343.1 18.1 %collective-permute-start.136 = (bf16[256,1024]{1,0:T(8,128)(2,1)S(1)}, bf16[256,1024]{1,0:T(8,128)(2,1)S(1)}, u32[]{:S(2)}, u32[]{:S(2)}) collective-permute-start(bf16[256,1024]{1,0:T(8,128)(2,1)S(1)} %add_convert_fusion.11), channel_id=1, source_target_pairs={{0,2},{2,4},{4,6},{6,7},{7,5},{5,3},{3,1},{1,0},{8,10},{10,12},{12... | collective-permute-start | bytes 1572872 | tf_op jit(solution)/shard_map/ppermute | solution.py:83
  343.5 18.9 %collective-permute-start.140 = (bf16[256,1024]{1,0:T(8,128)(2,1)S(1)}, bf16[256,1024]{1,0:T(8,128)(2,1)S(1)}, u32[]{:S(2)}, u32[]{:S(2)}) collective-permute-start(bf16[256,1024]{1,0:T(8,128)(2,1)S(1)} %add_convert_fusion.9), channel_id=1, source_target_pairs={{0,1},{2,0},{4,2},{6,4},{7,6},{5,7},{3,5},{1,3},{8,9},{10,8},{12,1... | collective-permute-start | bytes 1572872 | tf_op jit(solution)/shard_map/ppermute | solution.py:83
  347.6 17.5 %collective-permute-start.79 = (bf16[256,1024]{1,0:T(8,128)(2,1)S(1)}, bf16[256,1024]{1,0:T(8,128)(2,1)S(1)}, u32[]{:S(2)}, u32[]{:S(2)}) collective-permute-start(bf16[256,1024]{1,0:T(8,128)(2,1)S(1)} %pad_maximum_fusion.25), channel_id=1, source_target_pairs={{0,8},{8,0},{16,24},{24,16},{1,9},{9,1},{17,25},{25,17},{2,10},{10... | collective-permute-start | bytes 1572872 | tf_op jit(solution)/shard_map/ppermute | solution.py:36
  362.3 68.4 %collective-permute-start.137 = (bf16[256,1024]{1,0:T(8,128)(2,1)}, bf16[256,1024]{1,0:T(8,128)(2,1)}, u32[]{:S(2)}, u32[]{:S(2)}) collective-permute-start(bf16[256,1024]{1,0:T(8,128)(2,1)} %add_convert_fusion.10), channel_id=1, source_target_pairs={{0,2},{2,4},{4,6},{6,7},{7,5},{5,3},{3,1},{1,0},{8,10},{10,12},{12... | collective-permute-start | bytes 1572872 | tf_op jit(solution)/shard_map/ppermute | solution.py:83
  363.4 67.6 %collective-permute-start.141 = (bf16[256,1024]{1,0:T(8,128)(2,1)}, bf16[256,1024]{1,0:T(8,128)(2,1)}, u32[]{:S(2)}, u32[]{:S(2)}) collective-permute-start(bf16[256,1024]{1,0:T(8,128)(2,1)} %add_convert_fusion.8), channel_id=1, source_target_pairs={{0,1},{2,0},{4,2},{6,4},{7,6},{5,7},{3,5},{1,3},{8,9},{10,8},{12,1... | collective-permute-start | bytes 1572872 | tf_op jit(solution)/shard_map/ppermute | solution.py:83
  411.1 21.9 %collective-permute-start.86 = (bf16[256,1024]{1,0:T(8,128)(2,1)}, bf16[256,1024]{1,0:T(8,128)(2,1)}, u32[]{:S(2)}, u32[]{:S(2)}) collective-permute-start(bf16[256,1024]{1,0:T(8,128)(2,1)} %slice.1465), channel_id=1, source_target_pairs={{0,8},{8,0},{16,24},{24,16},{1,9},{9,1},{17,25},{25,17},{2,10},{10... | collective-permute-start | bytes 1572872 | tf_op jit(solution)/shard_map/ppermute | solution.py:36
  419.2 16.1 %collective-permute-start.124 = (bf16[288,256]{1,0:T(8,128)(2,1)}, bf16[288,256]{1,0:T(8,128)(2,1)}, u32[]{:S(2)}, u32[]{:S(2)}) collective-permute-start(bf16[288,256]{1,0:T(8,128)(2,1)} %pad_maximum_fusion.54), channel_id=1, source_target_pairs={{0,2},{2,4},{4,6},{6,7},{7,5},{5,3},{3,1},{1,0},{8,10},{10,12},{12... | collective-permute-start | bytes 442376 | tf_op jit(solution)/shard_map/ppermute | solution.py:83
  430.7 21.7 %collective-permute-start.98 = (bf16[256,1024]{1,0:T(8,128)(2,1)S(1)}, bf16[256,1024]{1,0:T(8,128)(2,1)S(1)}, u32[]{:S(2)}, u32[]{:S(2)}) collective-permute-start(bf16[256,1024]{1,0:T(8,128)(2,1)S(1)} %slice.1462), channel_id=1, source_target_pairs={{0,8},{8,0},{16,24},{24,16},{1,9},{9,1},{17,25},{25,17},{2,10},{10... | collective-permute-start | bytes 1572872 | tf_op jit(solution)/shard_map/ppermute | solution.py:36
  432.5 21.0 %collective-permute-start.142 = (bf16[256,1024]{1,0:T(8,128)(2,1)S(1)}, bf16[256,1024]{1,0:T(8,128)(2,1)S(1)}, u32[]{:S(2)}, u32[]{:S(2)}) collective-permute-start(bf16[256,1024]{1,0:T(8,128)(2,1)S(1)} %add_convert_fusion.7), channel_id=1, source_target_pairs={{0,16},{8,24},{16,0},{24,8},{1,17},{9,25},{17,1},{25,9},{2,18},{10... | collective-permute-start | bytes 1572872 | tf_op jit(solution)/shard_map/ppermute | solution.py:36
  434.2 17.2 %collective-permute-start.87 = (bf16[128,1024]{1,0:T(8,128)(2,1)S(1)}, bf16[128,1024]{1,0:T(8,128)(2,1)S(1)}, u32[]{:S(2)}, u32[]{:S(2)}) collective-permute-start(bf16[128,1024]{1,0:T(8,128)(2,1)S(1)} %get-tuple-element.241), channel_id=1, source_target_pairs={{0,16},{8,24},{16,0},{24,8},{1,17},{9,25},{17,1},{25,9},{2,18},{10... | collective-permute-start | bytes 786440 | tf_op jit(solution)/shard_map/ppermute | solution.py:36
  437.0 27.6 %collective-permute-start.97 = (bf16[128,1024]{1,0:T(8,128)(2,1)S(1)}, bf16[128,1024]{1,0:T(8,128)(2,1)S(1)}, u32[]{:S(2)}, u32[]{:S(2)}) collective-permute-start(bf16[128,1024]{1,0:T(8,128)(2,1)S(1)} %fusion.60), channel_id=1, source_target_pairs={{0,16},{8,24},{16,0},{24,8},{1,17},{9,25},{17,1},{25,9},{2,18},{10... | collective-permute-start | bytes 786440 | tf_op jit(solution)/shard_map/ppermute | solution.py:36
  454.7 29.0 %collective-permute-start.143 = (bf16[2,256,1024]{2,1,0:T(8,128)(2,1)}, bf16[2,256,1024]{2,1,0:T(8,128)(2,1)}, u32[]{:S(2)}, u32[]{:S(2)}) collective-permute-start(bf16[2,256,1024]{2,1,0:T(8,128)(2,1)} %pad_maximum_fusion.9), channel_id=1, source_target_pairs={{0,8},{8,0},{16,24},{24,16},{1,9},{9,1},{17,25},{25,17},{2,10},{10... | collective-permute-start | bytes 3145736 | tf_op jit(solution)/shard_map/ppermute | solution.py:36
  511.4 31.2 %collective-permute-start.115 = (bf16[256,1024]{1,0:T(8,128)(2,1)S(1)}, bf16[256,1024]{1,0:T(8,128)(2,1)}, u32[]{:S(2)}, u32[]{:S(2)}) collective-permute-start(bf16[256,1024]{1,0:T(8,128)(2,1)S(1)} %add_convert_fusion.15), channel_id=1, source_target_pairs={{0,2},{2,4},{4,6},{6,7},{7,5},{5,3},{3,1},{1,0},{8,10},{10,12},{12... | collective-permute-start | bytes 1572872 | tf_op jit(solution)/shard_map/ppermute | solution.py:83
  512.7 30.0 %collective-permute-start.119 = (bf16[256,1024]{1,0:T(8,128)(2,1)}, bf16[256,1024]{1,0:T(8,128)(2,1)}, u32[]{:S(2)}, u32[]{:S(2)}) collective-permute-start(bf16[256,1024]{1,0:T(8,128)(2,1)} %add_convert_fusion.13), channel_id=1, source_target_pairs={{0,1},{2,0},{4,2},{6,4},{7,6},{5,7},{3,5},{1,3},{8,9},{10,8},{12,1... | collective-permute-start | bytes 1572872 | tf_op jit(solution)/shard_map/ppermute | solution.py:83
  527.5 17.3 %collective-permute-start.122 = (bf16[2,256,256]{2,1,0:T(8,128)(2,1)}, bf16[2,256,256]{2,1,0:T(8,128)(2,1)}, u32[]{:S(2)}, u32[]{:S(2)}) collective-permute-start(bf16[2,256,256]{2,1,0:T(8,128)(2,1)} %pad_maximum_fusion.46), channel_id=1, source_target_pairs={{0,16},{8,24},{16,0},{24,8},{1,17},{9,25},{17,1},{25,9},{2,18},{10... | collective-permute-start | bytes 786440 | tf_op jit(solution)/shard_map/ppermute | solution.py:36
  557.8 32.6 %collective-permute-start.95 = (bf16[128,1024]{1,0:T(8,128)(2,1)S(1)}, bf16[128,1024]{1,0:T(8,128)(2,1)S(1)}, u32[]{:S(2)}, u32[]{:S(2)}) collective-permute-start(bf16[128,1024]{1,0:T(8,128)(2,1)S(1)} %fusion.64), channel_id=1, source_target_pairs={{0,16},{8,24},{16,0},{24,8},{1,17},{9,25},{17,1},{25,9},{2,18},{10... | collective-permute-start | bytes 786440 | tf_op jit(solution)/shard_map/ppermute | solution.py:36
  562.6 43.6 %collective-permute-start.121 = (bf16[2,256,1024]{2,1,0:T(8,128)(2,1)S(1)}, bf16[2,256,1024]{2,1,0:T(8,128)(2,1)S(1)}, u32[]{:S(2)}, u32[]{:S(2)}) collective-permute-start(bf16[2,256,1024]{2,1,0:T(8,128)(2,1)S(1)} %pad_maximum_fusion.8), channel_id=1, source_target_pairs={{0,8},{8,0},{16,24},{24,16},{1,9},{9,1},{17,25},{25,17},{2,10},{10... | collective-permute-start | bytes 3145736 | tf_op jit(solution)/shard_map/ppermute | solution.py:36
  596.1 29.2 %collective-permute-start.132 = (bf16[592,256]{1,0:T(8,128)(2,1)S(1)}, bf16[592,256]{1,0:T(8,128)(2,1)S(1)}, u32[]{:S(2)}, u32[]{:S(2)}) collective-permute-start(bf16[592,256]{1,0:T(8,128)(2,1)S(1)} %add_convert_fusion.17), channel_id=1, source_target_pairs={{0,16},{8,24},{16,0},{24,8},{1,17},{9,25},{17,1},{25,9},{2,18},{10... | collective-permute-start | bytes 909320 | tf_op jit(solution)/shard_map/ppermute | solution.py:36
  597.4 28.0 %collective-permute-start.111 = (bf16[2,528,256]{2,1,0:T(8,128)(2,1)}, bf16[2,528,256]{2,1,0:T(8,128)(2,1)}, u32[]{:S(2)}, u32[]{:S(2)}) collective-permute-start(bf16[2,528,256]{2,1,0:T(8,128)(2,1)} %pad_maximum_fusion.13), channel_id=1, source_target_pairs={{0,8},{8,0},{16,24},{24,16},{1,9},{9,1},{17,25},{25,17},{2,10},{10... | collective-permute-start | bytes 1622024 | tf_op jit(solution)/shard_map/ppermute | solution.py:36
  (408 other events, 3749.9 us)

commit v3 on v2

v3 whole, which is shorter than its diff:
```python
from functools import partial

import jax
import jax.numpy as jnp
from jax import lax
from jax.experimental import pallas as pl
from jax.experimental.pallas import tpu as pltpu
from jax.sharding import PartitionSpec as P

H = 16
NB = 32
HD = 64
EPSILON = 1e-05
MASKED = -1000000000.0
BF = jnp.bfloat16
F32 = jnp.float32
TILE = 128
STREAMS = 4
XOR = (0, 2, 1, 3)
MIB = 1024 * 1024


def dot(a, b):
    return jnp.dot(a, b, preferred_element_type=F32)


def dot_nt(a, b):
    return lax.dot_general(a, b, (((1,), (1,)), ((), ())), preferred_element_type=F32)


def dot_tn(a, b):
    return lax.dot_general(a, b, (((0,), (0,)), ((), ())), preferred_element_type=F32)


def swap(values, bit):
    return lax.ppermute(values, "stream", [(i, i ^ bit) for i in range(STREAMS)])


class Chain:
    def __init__(self):
        self.last = None

    def __call__(self, kernel, outs, args, scalars=(), away=(), stored=(), scratch=(), after=(), room=3, cost=1):
        ties = list(after)
        if self.last is not None:
            ties.append(self.last)
        reads = len(scalars) + len(args) + len(away) + len(stored)

        def body(*refs):
            kernel(*refs[:reads], *refs[reads + len(ties) :])

        vmem = pl.BlockSpec(memory_space=pltpu.VMEM)
        anywhere = pl.BlockSpec(memory_space=pl.ANY)
        results = pl.pallas_call(
            body,
            out_shape=[jax.ShapeDtypeStruct(shape, kind) for shape, kind in outs],
            in_specs=[pl.BlockSpec(memory_space=pltpu.SMEM)] * len(scalars)
            + [vmem] * len(args)
            + [anywhere] * len(away)
            + [pl.BlockSpec(memory_space=pltpu.HBM)] * len(stored)
            + [anywhere] * len(ties),
            out_specs=[vmem] * len(outs),
            scratch_shapes=list(scratch),
            compiler_params=pltpu.CompilerParams(vmem_limit_bytes=room * MIB),
            cost_estimate=pl.CostEstimate(flops=10**10, bytes_accessed=10**7, transcendentals=0),
        )(*scalars, *args, *away, *[pltpu.with_memory_space_constraint(a, pltpu.HBM) for a in stored], *ties)
        self.last = results[0]
        return results


def gather_rows(rows):
    far = swap(rows, 2)
    return rows, far, swap(rows, 1), swap(far, 1)


class Scatter:
    def __init__(self, parts):
        self.own, self.across, near = parts
        self.near = swap(near, 1)

    def middle(self, chain, after=()):
        rows, dim = self.own.shape

        def kernel(across_ref, near_ref, out_ref):
            out_ref[...] = (across_ref[...] + near_ref[rows:, :].astype(F32)).astype(BF)

        (low,) = chain(kernel, [((rows, dim), BF)], [self.across, self.near], after=after, cost=0.1)
        self.far = swap(low, 2)

    def parts(self):
        return [self.own, self.near, self.far]


def scattered(own_ref, near_ref, far_ref):
    rows = own_ref.shape[0]
    return own_ref[...] + near_ref[:rows, :].astype(F32) + far_ref[...].astype(F32)


def scatter_outs(rows, dim):
    return [((rows, dim), F32), ((rows, dim), F32), ((2 * rows, dim), BF)]


def store_partials(part, value, own_ref, across_ref, near_ref):
    rows = own_ref.shape[0]
    if part == 0:
        own_ref[...] = value[:rows, :]
        across_ref[...] = value[rows:, :]
    else:
        near_ref[...] = value.astype(BF)


def join(target, refs):
    rows = refs[0].shape[0]
    for i, ref in enumerate(refs):
        target[i * rows : (i + 1) * rows, :] = ref[...]


def turn_blocks(blocks):
    far = swap(jnp.stack([blocks[1], blocks[3]]), 2)
    near = swap(jnp.stack([blocks[2], far[1]]), 1)
    return [blocks[0], far[0], near[0], near[1]]


def by_absolute(blocks, here):
    stacked = jnp.stack([blocks[XOR.index(j)] for j in range(4)])
    return [lax.dynamic_index_in_dim(stacked, here ^ a, 0, keepdims=False) for a in range(4)]


def ring_order(n):
    return list(range(0, n, 2)) + list(range(n - 1, 0, -2))


def ring_member(place, n):
    place = lax.rem(place + 2 * n, n)
    return jnp.where(place < n // 2, 2 * place, 2 * (n - place) - 1)


def ring_place(g, n):
    return jnp.where(g % 2 == 0, g // 2, n - (g + 1) // 2)


def ring_step(values, n, step):
    order = ring_order(n)
    pairs = [(order[i], order[(i + step) % n]) for i in range(n)]
    return lax.ppermute(values, "dp", pairs)


def ring_pieces(own, n):
    rows = own.shape[0]
    pieces = [(0, 0, own)]
    ahead = back = own
    for k in range(1, n // 2):
        ahead = ring_step(ahead, n, 1)
        back = ring_step(back, n, -1)
        pieces += [(k, 0, ahead), (n - k, 0, back)]
    half = halved(rows)
    top = ring_step(ahead[:half], n, 1)
    bottom = ring_step(back[half:], n, -1)
    pieces += [(n // 2, 0, top), (n // 2, half, bottom)]
    return pieces


def halved(rows):
    return rows // 32 * 16


def assemble(chain, pieces, index, regions, shapes, n, after=()):
    moves = []
    for number, (behind, first, piece) in enumerate(pieces):
        last = first + piece.shape[0]
        for r0, r1, c0, c1, which, to_row, to_col in regions:
            lo, hi = max(r0, first), min(r1, last)
            if lo < hi:
                moves.append((number, behind, lo - first, hi - first, c0, c1, which, to_row + lo - r0, to_col))

    def kernel(index_ref, *refs):
        sources = refs[: len(pieces)]
        outs = refs[len(pieces) : -1]
        copy_all(
            [
                (
                    sources[number].at[lo:hi, c0:c1],
                    outs[which].at[index_ref[behind], row : row + hi - lo, col : col + c1 - c0],
                )
                for number, behind, lo, hi, c0, c1, which, row, col in moves
            ],
            refs[-1],
        )

    return chain(
        kernel,
        [((n,) + shape, BF) for shape in shapes],
        [],
        scalars=[index],
        away=[piece for _, _, piece in pieces],
        scratch=[pltpu.SemaphoreType.DMA((len(moves),))],
        after=after,
    )


class RingSum:
    def __init__(self, chain, arrays, regions, columns, n, index):
        self.chain, self.arrays, self.regions, self.n, self.index = chain, arrays, regions, n, index
        self.columns = columns
        self.rows = sum(r[3] for r in regions)
        self.half = halved(self.rows)
        self.up = self.down = None
        self.done = 0
        self.left = n // 2

    def fetch(self, index_ref, offsets, refs, buffers, sems):
        copies = []
        for slot, offset in enumerate(offsets):
            g = index_ref[offset]
            for i, (which, column, row, rows) in enumerate(self.regions):
                copies.append(
                    pltpu.make_async_copy(
                        refs[which].at[g, :, column : column + self.columns],
                        buffers.at[slot, row : row + rows, :],
                        sems.at[slot * len(self.regions) + i],
                    )
                )
                copies[-1].start()
        for copy in copies:
            copy.wait()

    def step(self, after=()):
        rows, half, columns, count = self.rows, self.half, self.columns, len(self.arrays)
        first = self.left == self.n // 2
        last = self.left == 0
        joined = self.left == self.n // 2 - 1
        offsets = [(self.n - self.left) % self.n] + ([] if first or last else [self.left])
        received = [] if first else [self.up, self.down]

        def kernel(index_ref, *refs):
            ups = refs[: len(received)]
            arrays = refs[len(received) : len(received) + count]
            outs = refs[len(received) + count : -2]
            buffers, sems = refs[-2:]
            self.fetch(index_ref, offsets, arrays, buffers, sems)
            if first:
                outs[0][...] = buffers[0, :half, :]
                outs[1][...] = buffers[0, half:, :]
            elif last:
                outs[0][...] = (
                    buffers[0].astype(F32) + ups[0][...].astype(F32) + ups[1][...].astype(F32)
                ).astype(BF)
            elif joined:
                outs[0][:half, :] = (buffers[0, :half, :].astype(F32) + ups[0][...].astype(F32)).astype(BF)
                outs[0][half:, :] = buffers[0, half:, :]
                outs[1][:half, :] = buffers[1, :half, :]
                outs[1][half:, :] = (buffers[1, half:, :].astype(F32) + ups[1][...].astype(F32)).astype(BF)
            else:
                outs[0][...] = (buffers[0].astype(F32) + ups[0][...].astype(F32)).astype(BF)
                outs[1][...] = (buffers[1].astype(F32) + ups[1][...].astype(F32)).astype(BF)

        if first:
            outs = [((half, columns), BF), ((rows - half, columns), BF)]
        else:
            outs = [((rows, columns), BF)] * (1 if last else 2)
        results = self.chain(
            kernel,
            outs,
            received,
            scalars=[self.index],
            away=self.arrays,
            scratch=[
                pltpu.VMEM((len(offsets), rows, columns), BF),
                pltpu.SemaphoreType.DMA((len(offsets) * len(self.regions),)),
            ],
            after=after,
        )
        self.left -= 1
        if last:
            return results[0]
        self.up = ring_step(results[0], self.n, 1)
        self.down = ring_step(results[1], self.n, -1)
        return None


def tile_width(t, causal, total):
    return TILE * (t + 1) if causal else total


def head_mask(e):
    lane = lax.broadcasted_iota(jnp.int32, (1, TILE), 1)
    return ((lane // HD) == e).astype(F32)


def rel_mask(h):
    lane = lax.broadcasted_iota(jnp.int32, (1, TILE), 1)
    return ((lane // NB) == h).astype(F32)


def allowed_keys(t, width, meta, causal, strict):
    bucket = meta[8]
    shape = (TILE, width)
    row = lax.broadcasted_iota(jnp.int32, shape, 0) + t * TILE
    col = lax.broadcasted_iota(jnp.int32, shape, 1)
    pos = col & (bucket - 1)
    first = col < bucket
    limit = bucket - jnp.where(first, meta[9], meta[10])
    allowed = (pos < limit) & ((row < bucket) == first)
    if causal:
        allowed = allowed & ((col < row) if strict else (col <= row))
    return allowed


def load_rows(meta, target, source, c0, c1):
    for chunk in range(8):
        start = pl.multiple_of(meta[chunk], 64)
        target[pl.ds(start, 64), :] = source[chunk * 64 : chunk * 64 + 64, c0:c1].astype(target.dtype)


def store_rows(meta, target, source, c0, c1):
    for chunk in range(8):
        start = pl.multiple_of(meta[chunk], 64)
        target[chunk * 64 : chunk * 64 + 64, c0:c1] = source[pl.ds(start, 64), :].astype(target.dtype)


def rel_bias(rel_rows, h, table):
    high = rel_rows.astype(BF)
    rest = (rel_rows - high.astype(F32)).astype(BF)
    mask = rel_mask(h)
    both = jnp.concatenate(
        [(high.astype(F32) * mask).astype(BF), (rest.astype(F32) * mask).astype(BF)], axis=1
    )
    spread = dot(both, table)
    return pltpu.roll(spread, 0, 1, stride=1, stride_axis=0)


def table_slice(t, width):
    first = sum(TILE * (u + 1) for u in range(t))
    return slice(first, first + width)


def attention_forward(chain, meta, qkv, main=None, rel=None, tables=None, w_out=None, after=()):
    total = qkv.shape[0]
    width_all = qkv.shape[1] // 3
    heads = width_all // HD
    causal = rel is not None
    own = main is not None
    project = w_out is not None
    block = total // STREAMS

    def kernel(meta_ref, *refs):
        refs = list(refs)
        qkv_ref = refs.pop(0)
        main_ref = refs.pop(0) if own else qkv_ref
        rel_ref, table_ref, hot_ref = (refs.pop(0), refs.pop(0), refs.pop(0)) if causal else (None,) * 3
        out_ref = refs.pop(0) if project else None
        ctx_ref, lse_ref = refs.pop(0), refs.pop(0)
        parts_refs = [refs.pop(0) for _ in range(3)] if project else None
        qs, ks, vs, cs, kt = refs[:5]
        refs = refs[5:]
        rs = refs.pop(0) if causal else None
        load_rows(meta_ref, qs, qkv_ref, 0, width_all)
        load_rows(meta_ref, ks, main_ref, width_all, 2 * width_all)
        load_rows(meta_ref, vs, main_ref, 2 * width_all, 3 * width_all)
        if causal:
            load_rows(meta_ref, rs, rel_ref, 0, rel.shape[1])
        if own:
            kn, vn = refs
            load_rows(meta_ref, kn, qkv_ref, width_all, 2 * width_all)
            load_rows(meta_ref, vn, qkv_ref, 2 * width_all, 3 * width_all)
        kt[...] = ks[...].T
        for t in range(total // TILE):
            rows = slice(TILE * t, TILE * (t + 1))
            width = tile_width(t, causal, total)
            allowed = allowed_keys(t, width, meta_ref, causal, own)
            lse_lane = lax.broadcasted_iota(jnp.int32, (TILE, TILE), 1)
            lse = jnp.zeros((TILE, TILE), F32)
            query = [(qs[rows, HD * h : HD * (h + 1)].astype(F32) * HD**-0.5).astype(BF) for h in range(heads)]
            scores = [dot(query[h], kt[HD * h : HD * (h + 1), 0:width]) for h in range(heads)]
            if causal:
                biases = [rel_bias(rs[rows, :], h, table_ref[:, table_slice(t, width)]) for h in range(heads)]
                scores = [a + b for a, b in zip(scores, biases)]
            scores = [jnp.where(allowed, a, MASKED) for a in scores]
            tops = [jnp.max(a, axis=1, keepdims=True) for a in scores]
            if own:
                own_scores = [
                    jnp.sum(
                        query[h].astype(F32) * kn[rows, HD * h : HD * (h + 1)].astype(F32), axis=1, keepdims=True
                    )
                    + jnp.sum(rs[rows, :] * (hot_ref[...] * rel_mask(h)), axis=1, keepdims=True)
                    for h in range(heads)
                ]
                tops = [jnp.maximum(a, b) for a, b in zip(tops, own_scores)]
            expos = [jnp.exp(a - b) for a, b in zip(scores, tops)]
            sums = [jnp.sum(a, axis=1, keepdims=True) for a in expos]
            if own:
                own_expos = [jnp.exp(a - b) for a, b in zip(own_scores, tops)]
                sums = [a + b for a, b in zip(sums, own_expos)]
            inverses = [1.0 / a for a in sums]
            parts = [
                dot((expos[h] * inverses[h]).astype(BF), vs[0:width, HD * h : HD * (h + 1)]) for h in range(heads)
            ]
            if own:
                own_probs = [own_expos[h] * inverses[h] for h in range(heads)]
                parts = [
                    parts[h] + own_probs[h] * vn[rows, HD * h : HD * (h + 1)].astype(F32) for h in range(heads)
                ]
            cs[rows, :] = jnp.concatenate(parts, axis=1).astype(BF)
            for h in range(heads):
                lse = jnp.where(lse_lane == h, tops[h] + jnp.log(sums[h]), lse)
                if own:
                    lse = jnp.where(lse_lane == heads + h, own_probs[h], lse)
            lse_ref[rows, :] = lse
        store_rows(meta_ref, ctx_ref, cs, 0, width_all)
        if project:
            for part in range(2):
                value = dot(ctx_ref[part * 2 * block : (part + 1) * 2 * block, :], out_ref[...])
                store_partials(part, value, *parts_refs)

    args = [qkv]
    scratch = [pltpu.VMEM((total, width_all), BF) for _ in range(4)] + [pltpu.VMEM((width_all, total), BF)]
    outs = [((total, width_all), BF), ((total, TILE), F32)]
    if own:
        args.append(main)
    if causal:
        args += [rel, tables[0], tables[2]]
        scratch.append(pltpu.VMEM((total, rel.shape[1]), F32))
    if own:
        scratch += [pltpu.VMEM((total, width_all), BF) for _ in range(2)]
    if project:
        args.append(w_out)
        outs += scatter_outs(block, w_out.shape[1])
    context, lse, *parts = chain(kernel, outs, args, scalars=[meta], scratch=scratch, after=after, room=8, cost=6)
    return context, lse, parts


def attention_backward(chain, meta, qkv, attended, w_out, lse, main=None, rel=None, tables=None, after=()):
    total = qkv.shape[0]
    width_all = qkv.shape[1] // 3
    heads = width_all // HD
    causal = rel is not None
    own = main is not None

    def kernel(meta_ref, *refs):
        refs = list(refs)
        qkv_ref = refs.pop(0)
        attended_refs = [refs.pop(0) for _ in range(STREAMS)]
        out_ref, lse_ref = refs.pop(0), refs.pop(0)
        main_ref = refs.pop(0) if own else qkv_ref
        rel_ref, table_ref, back_ref, hot_ref, flip_ref = (
            [refs.pop(0) for _ in range(5)] if causal else (None,) * 5
        )
        dq_ref, dk_ref, dv_ref, joined_ref = refs[:4]
        refs = refs[4:]
        drel_ref = refs.pop(0) if causal else None
        dkn_ref, dvn_ref = (refs.pop(0), refs.pop(0)) if own else (None, None)
        qs, ks, vs, gs, dqs, dks, kt, vt, qt, gt, dkt, dvt = refs[:12]
        refs = refs[12:]
        rs, drs = (refs.pop(0), refs.pop(0)) if causal else (None, None)
        join(joined_ref, attended_refs)
        dqs[...] = dot_nt(joined_ref[...], out_ref[...])
        load_rows(meta_ref, qs, qkv_ref, 0, width_all)
        load_rows(meta_ref, ks, main_ref, width_all, 2 * width_all)
        load_rows(meta_ref, vs, main_ref, 2 * width_all, 3 * width_all)
        load_rows(meta_ref, gs, dqs, 0, width_all)
        if causal:
            load_rows(meta_ref, rs, rel_ref, 0, rel.shape[1])
        if own:
            kn, vn, dkn, dvn = refs
            load_rows(meta_ref, kn, qkv_ref, width_all, 2 * width_all)
            load_rows(meta_ref, vn, qkv_ref, 2 * width_all, 3 * width_all)
        qs[...] = (qs[...].astype(F32) * HD**-0.5).astype(BF)
        kt[...] = ks[...].T
        vt[...] = vs[...].T
        qt[...] = qs[...].T
        gt[...] = gs[...].T
        dkt[...] = jnp.zeros_like(dkt)
        dvt[...] = jnp.zeros_like(dvt)
        each = range(heads)
        feat = [slice(HD * h, HD * (h + 1)) for h in each]
        for t in range(total // TILE):
            rows = slice(TILE * t, TILE * (t + 1))
            width = tile_width(t, causal, total)
            allowed = allowed_keys(t, width, meta_ref, causal, own)
            norms = [lse_ref[rows, h : h + 1] for h in each]
            query = [qs[rows, feat[h]] for h in each]
            grad = [gs[rows, feat[h]] for h in each]
            scores = [dot(query[h], kt[feat[h], 0:width]) for h in each]
            dprobs = [dot(grad[h], vt[feat[h], 0:width]) for h in each]
            if causal:
                biases = [rel_bias(rs[rows, :], h, table_ref[:, table_slice(t, width)]) for h in each]
                scores = [a + b for a, b in zip(scores, biases)]
            probs = [jnp.exp(jnp.where(allowed, scores[h], MASKED) - norms[h]) for h in each]
            rowdots = [jnp.sum(probs[h] * dprobs[h], axis=1, keepdims=True) for h in each]
            if own:
                own_probs = [lse_ref[rows, heads + h : heads + h + 1] for h in each]
                own_dprobs = [
                    jnp.sum(grad[h].astype(F32) * vn[rows, feat[h]].astype(F32), axis=1, keepdims=True) for h in each
                ]
                rowdots = [rowdots[h] + own_probs[h] * own_dprobs[h] for h in each]
                own_dscores = [
                    (own_probs[h] * (own_dprobs[h] - rowdots[h])).astype(BF).astype(F32) for h in each
                ]
            dscores = [(probs[h] * (dprobs[h] - rowdots[h])).astype(BF) for h in each]
            dqs_parts = [dot(dscores[h], ks[0:width, feat[h]]) for h in each]
            if own:
                dqs_parts = [dqs_parts[h] + own_dscores[h] * kn[rows, feat[h]].astype(F32) for h in each]
                dkn[rows, :] = jnp.concatenate([own_dscores[h] * query[h].astype(F32) for h in each], axis=1)
                dvn[rows, :] = jnp.concatenate([own_probs[h] * grad[h].astype(F32) for h in each], axis=1)
            dqs[rows, :] = jnp.concatenate(dqs_parts, axis=1) * HD**-0.5
            for h in each:
                dkt[feat[h], 0:width] += dot(qt[feat[h], rows], dscores[h])
                dvt[feat[h], 0:width] += dot(gt[feat[h], rows], probs[h].astype(BF))
            if causal:
                drel = jnp.zeros((TILE, TILE), F32)
                for h in each:
                    blocks = [
                        dot(dscores[h][:, TILE * b : TILE * (b + 1)], flip_ref[...])
                        for b in reversed(range(width // TILE))
                    ]
                    mirrored = jnp.concatenate(blocks, axis=1) if len(blocks) > 1 else blocks[0]
                    turned = pltpu.roll(mirrored, 0, 1, stride=1, stride_axis=0).astype(BF)
                    drel = drel + dot(turned, back_ref[table_slice(t, width), :]) * rel_mask(h)
                    if own:
                        drel = drel + own_dscores[h] * (hot_ref[...] * rel_mask(h))
                drs[rows, :] = drel
        store_rows(meta_ref, dq_ref, dqs, 0, width_all)
        dks[...] = dkt[...].T
        store_rows(meta_ref, dk_ref, dks, 0, width_all)
        dks[...] = dvt[...].T
        store_rows(meta_ref, dv_ref, dks, 0, width_all)
        if causal:
            store_rows(meta_ref, drel_ref, drs, 0, rel.shape[1])
        if own:
            store_rows(meta_ref, dkn_ref, dkn, 0, width_all)
            store_rows(meta_ref, dvn_ref, dvn, 0, width_all)

    args = [qkv, *attended, w_out, lse]
    shape = (total, width_all)
    turned = (width_all, total)
    outs = [(shape, BF), (shape, F32), (shape, F32), ((total, w_out.shape[1]), BF)]
    scratch = [pltpu.VMEM(shape, BF) for _ in range(4)] + [pltpu.VMEM(shape, F32) for _ in range(2)]
    scratch += [pltpu.VMEM(turned, BF) for _ in range(4)] + [pltpu.VMEM(turned, F32) for _ in range(2)]
    if own:
        args.append(main)
    if causal:
        args += [rel, *tables]
        outs.append(((total, rel.shape[1]), BF))
        scratch += [pltpu.VMEM((total, rel.shape[1]), F32) for _ in range(2)]
    if own:
        outs += [(shape, BF), (shape, BF)]
        scratch += [pltpu.VMEM(shape, BF) for _ in range(2)] + [pltpu.VMEM(shape, F32) for _ in range(2)]
    return chain(kernel, outs, args, scalars=[meta], scratch=scratch, after=after, room=12, cost=10 if causal else 6)


def rel_tables(rel_table, total):
    ahead, back = [], []
    for t in range(total // TILE):
        width = TILE * (t + 1)
        here = rel_table[:width]
        ahead += [jnp.flip(here[: TILE * t + 1]), jnp.flip(here[TILE * t + 1 :])]
        back += [here[width - TILE + 1 :], here[: width - TILE + 1]]
    ahead, back = jnp.concatenate(ahead), jnp.concatenate(back)
    rows = jnp.arange(2 * TILE, dtype=jnp.int32) % NB
    forward = (rows[:, None] == ahead[None, :]).astype(BF)
    backward = (back[:, None] == rows[None, :TILE]).astype(BF)
    hot = (rows[None, :TILE] == rel_table[0]).astype(F32)
    ids = jnp.arange(TILE, dtype=jnp.int32)
    flip = (ids[:, None] + ids[None, :] == TILE - 1).astype(BF)
    return forward, backward, hot, flip


def unit_of(values):
    center = values - jnp.mean(values, axis=-1, keepdims=True)
    spread = jnp.mean(center * center, axis=-1, keepdims=True)
    inverse = lax.rsqrt(spread + EPSILON)
    return center * inverse, inverse


def unit_back(grad, unit, inverse, gain):
    inner = grad * gain
    mean = jnp.mean(inner, axis=-1, keepdims=True)
    along = jnp.mean(inner * unit, axis=-1, keepdims=True)
    return inverse * (inner - mean - unit * along)


def column(values):
    return jnp.sum(values, axis=0, keepdims=True)


def tiny_sums(low, grad, unit):
    return jnp.concatenate([column(low.astype(F32)), column(grad * unit), column(grad)], axis=0)


def norm_first(chain, inputs, parts, w, after=()):
    rows, dim = inputs.shape

    def kernel(in_ref, own_ref, near_ref, far_ref, small_ref, unit_ref, inverse_ref, low_ref):
        values = in_ref[...].astype(F32) + scattered(own_ref, near_ref, far_ref) + small_ref[2:3, :]
        unit, inverse = unit_of(values)
        unit_ref[...] = unit
        inverse_ref[...] = inverse
        low_ref[...] = (unit * small_ref[4:5, :] + small_ref[6:7, :]).astype(BF)

    outs = [((rows, dim), F32), ((rows, 1), F32), ((rows, dim), BF)]
    return chain(kernel, outs, [inputs, *parts, w.small], after=after)


def norm_second(chain, unit0, parts, w, after=()):
    rows, dim = unit0.shape

    def kernel(unit_ref, own_ref, near_ref, far_ref, small_ref, unit1_ref, inverse_ref, out_ref, low_ref):
        hidden = unit_ref[...] * small_ref[4:5, :] + small_ref[6:7, :]
        unit, inverse = unit_of(hidden + scattered(own_ref, near_ref, far_ref) + small_ref[3:4, :])
        out = unit * small_ref[5:6, :] + small_ref[7:8, :]
        unit1_ref[...] = unit
        inverse_ref[...] = inverse
        out_ref[...] = out
        low_ref[...] = out.astype(BF)

    outs = [((rows, dim), F32), ((rows, 1), F32), ((rows, dim), F32), ((rows, dim), BF)]
    return chain(kernel, outs, [unit0, *parts, w.small], after=after)


def norm_second_back(chain, residual, parts, unit1, inverse, w, after=()):
    rows, dim = residual.shape

    def kernel(res_ref, own_ref, near_ref, far_ref, unit_ref, inverse_ref, small_ref, sum_ref, low_ref, tiny_ref):
        grad = res_ref[...] + scattered(own_ref, near_ref, far_ref)
        unit = unit_ref[...]
        back = unit_back(grad, unit, inverse_ref[...], small_ref[5:6, :])
        low = back.astype(BF)
        sum_ref[...] = back
        low_ref[...] = low
        tiny_ref[...] = tiny_sums(low, grad, unit)

    outs = [((rows, dim), F32), ((rows, dim), BF), ((3, dim), F32)]
    return chain(kernel, outs, [residual, *parts, unit1, inverse, w.small], after=after)


def norm_second_both(chain, unit0, parts, cotangent, w, after=()):
    rows, dim = unit0.shape

    def kernel(unit_ref, own_ref, near_ref, far_ref, cot_ref, small_ref, out_ref, sum_ref, low_ref, tiny_ref):
        hidden = unit_ref[...] * small_ref[4:5, :] + small_ref[6:7, :]
        unit, inverse = unit_of(hidden + scattered(own_ref, near_ref, far_ref) + small_ref[3:4, :])
        out_ref[...] = unit * small_ref[5:6, :] + small_ref[7:8, :]
        grad = cot_ref[...].astype(F32)
        back = unit_back(grad, unit, inverse, small_ref[5:6, :])
        low = back.astype(BF)
        sum_ref[...] = back
        low_ref[...] = low
        tiny_ref[...] = tiny_sums(low, grad, unit)

    outs = [((rows, dim), F32), ((rows, dim), F32), ((rows, dim), BF), ((3, dim), F32)]
    return chain(kernel, outs, [unit0, *parts, cotangent, w.small], after=after)


def norm_first_back(chain, sum_grad, parts, unit0, inverse, w, after=()):
    rows, dim = sum_grad.shape

    def kernel(sum_ref, own_ref, near_ref, far_ref, unit_ref, inverse_ref, small_ref, out_ref, low_ref, tiny_ref):
        grad = sum_ref[...] + scattered(own_ref, near_ref, far_ref)
        unit = unit_ref[...]
        back = unit_back(grad, unit, inverse_ref[...], small_ref[4:5, :])
        low = back.astype(BF)
        out_ref[...] = back
        low_ref[...] = low
        tiny_ref[...] = tiny_sums(low, grad, unit)

    outs = [((rows, dim), F32), ((rows, dim), BF), ((3, dim), F32)]
    return chain(kernel, outs, [sum_grad, *parts, unit0, inverse, w.small], after=after)


def input_gradient(chain, residual, parts, after=()):
    rows, dim = residual.shape

    def kernel(res_ref, own_ref, near_ref, far_ref, out_ref):
        out_ref[...] = res_ref[...] + scattered(own_ref, near_ref, far_ref)

    return chain(kernel, [((rows, dim), F32)], [residual, *parts], after=after)[0]


def project(chain, quads, w, with_rel, after=()):
    rows, dim = quads[0].shape
    width = w.qkv.shape[1]

    def kernel(*refs):
        refs = list(refs)
        quad_refs = [refs.pop(0) for _ in range(STREAMS)]
        qkv_ref, bias_ref = refs.pop(0), refs.pop(0)
        rel_ref, rel_bias_ref = (refs.pop(0), refs.pop(0)) if with_rel else (None, None)
        joined_ref, heads_ref = refs.pop(0), refs.pop(0)
        join(joined_ref, quad_refs)
        heads_ref[...] = (dot(joined_ref[...], qkv_ref[...]) + bias_ref[...]).astype(BF)
        if with_rel:
            refs[0][...] = dot(joined_ref[...], rel_ref[...]) + rel_bias_ref[...]

    args = [*quads, w.qkv, w.qkv_bias]
    outs = [((STREAMS * rows, dim), BF), ((STREAMS * rows, width), BF)]
    if with_rel:
        args += [w.rel, w.rel_bias]
        outs.append(((STREAMS * rows, w.rel.shape[1]), F32))
    return chain(kernel, outs, args, after=after)


def out_project(chain, context, w, after=()):
    total, _ = context.shape
    block = total // STREAMS

    def kernel(context_ref, out_ref, *parts_refs):
        for part in range(2):
            value = dot(context_ref[part * 2 * block : (part + 1) * 2 * block, :], out_ref[...])
            store_partials(part, value, *parts_refs)

    return chain(kernel, scatter_outs(block, w.out.shape[1]), [context, w.out], after=after)


def project_back(chain, dq, dk, dv, drel, w, after=()):
    total, width = dq.shape
    block = total // STREAMS
    dim = w.qkv.shape[0]
    with_rel = drel is not None
    keys, vals = len(dk), len(dv)

    def kernel(*refs):
        refs = list(refs)
        dq_ref = refs.pop(0)
        dk_refs = [refs.pop(0) for _ in range(keys)]
        dv_refs = [refs.pop(0) for _ in range(vals)]
        drel_ref = refs.pop(0) if with_rel else None
        qkv_ref = refs.pop(0)
        rel_ref = refs.pop(0) if with_rel else None
        parts_refs = [refs.pop(0) for _ in range(3)]
        heads_ref, sums_ref = refs.pop(0), refs.pop(0)
        heads_ref[:, :width] = dq_ref[...]
        heads_ref[:, width : 2 * width] = sum(r[...] for r in dk_refs).astype(BF)
        heads_ref[:, 2 * width :] = sum(r[...] for r in dv_refs).astype(BF)
        sums_ref[...] = column(heads_ref[...].astype(F32))
        if with_rel:
            refs[0][...] = column(drel_ref[...].astype(F32))
        for part in range(2):
            rows = slice(part * 2 * block, (part + 1) * 2 * block)
            value = dot_nt(heads_ref[rows, :], qkv_ref[...])
            if with_rel:
                value = value + dot_nt(drel_ref[rows, :], rel_ref[...])
            store_partials(part, value, *parts_refs)

    args = [dq, *dk, *dv]
    outs = scatter_outs(block, dim) + [((total, 3 * width), BF), ((1, 3 * width), F32)]
    if with_rel:
        args += [drel, w.qkv, w.rel]
        outs.append(((1, w.rel.shape[1]), F32))
    else:
        args.append(w.qkv)
    return chain(kernel, outs, args, after=after)


def gelu_and_slope(x):
    bell = jnp.exp(-0.5 * x * x)
    under = 1.0 + (0.3275911 * 0.5**0.5) * jnp.abs(x)
    t = pl.reciprocal(under, approx=True)
    t = t * (2.0 - under * t)
    series = ((((1.061405429 * t - 1.453152027) * t + 1.421413741) * t - 0.284496736) * t + 0.254829592) * t
    tail = (0.5 * series) * bell
    below = jnp.where(x >= 0.0, 1.0 - tail, tail)
    return x * below, below + x * bell * 0.3989422804014327


FFN_TILE = 256


def ffn_in_tile(ref, share, first):
    tile = ref[:, :share, first : first + FFN_TILE]
    return tile.reshape(tile.shape[0] * share, FFN_TILE)


def ffn_out_rows(ref, share, first, last):
    part = ref.shape[1] - share
    tile = ref[first // part : last // part, share:, :]
    return tile.reshape(last - first, ref.shape[2])


def ffn_forward(chain, quads, w, after=()):
    rows, dim = quads[0].shape
    n, both, units = w.ffn.shape
    share = dim // n
    half = 2 * rows

    def kernel(a_ref, b_ref, c_ref, d_ref, w_ref, bias_ref, own_ref, across_ref, near_ref, joined_ref, act_ref, slope_ref):
        join(joined_ref, (a_ref, b_ref, c_ref, d_ref))
        for part in range(2):
            block = slice(part * half, (part + 1) * half)
            for u in range(0, units, FFN_TILE):
                tile = slice(u, u + FFN_TILE)
                inner = dot(joined_ref[block, :], ffn_in_tile(w_ref, share, u)) + bias_ref[:, tile]
                active, slope = gelu_and_slope(inner)
                act_ref[block, tile] = active.astype(BF)
                slope_ref[block, tile] = slope.astype(BF)
            branch = dot(act_ref[block, :], ffn_out_rows(w_ref, share, 0, units))
            store_partials(part, branch, own_ref, across_ref, near_ref)

    wide = ((4 * rows, units), BF)
    outs = scatter_outs(rows, dim) + [((4 * rows, dim), BF), wide, wide]
    return chain(kernel, outs, [*quads, w.ffn, w.ffn_bias], after=after, cost=5)


def ffn_backward(chain, quads, slope, w, after=()):
    rows, dim = quads[0].shape
    n, both, units = w.ffn.shape
    share = dim // n
    half = 2 * rows

    def kernel(a_ref, b_ref, c_ref, d_ref, w_ref, slope_ref, own_ref, across_ref, near_ref, joined_ref, inner_ref, sums_ref):
        join(joined_ref, (a_ref, b_ref, c_ref, d_ref))
        for part in range(2):
            block = slice(part * half, (part + 1) * half)
            for u in range(0, units, FFN_TILE):
                tile = slice(u, u + FFN_TILE)
                back = dot_nt(joined_ref[block, :], ffn_out_rows(w_ref, share, u, u + FFN_TILE))
                inner = (back * slope_ref[block, tile].astype(F32)).astype(BF)
                inner_ref[block, tile] = inner
                if part == 0:
                    sums_ref[:, tile] = column(inner.astype(F32))
                else:
                    sums_ref[:, tile] += column(inner.astype(F32))
            hidden = sum(
                dot_nt(inner_ref[block, u : u + FFN_TILE], ffn_in_tile(w_ref, share, u))
                for u in range(0, units, FFN_TILE)
            )
            store_partials(part, hidden, own_ref, across_ref, near_ref)

    outs = scatter_outs(rows, dim) + [((4 * rows, dim), BF), ((4 * rows, units), BF), ((1, units), F32)]
    return chain(kernel, outs, [*quads, w.ffn, slope], after=after, cost=4)


def copy_all(moves, sems):
    copies = [pltpu.make_async_copy(source, target, sems.at[i]) for i, (source, target) in enumerate(moves)]
    for copy in copies:
        copy.start()
    for copy in copies:
        copy.wait()


def pack_attention(chain, devices, qkv, out, smalls=None, rel=None, after=()):
    share, dim = out.shape
    quarter = dim // STREAMS
    fixed = 4 * share
    half = share // 2
    more = 16 if rel is None else half
    extra = list(smalls) if rel is None else [rel]

    def kernel(devices_ref, qkv_ref, out_ref, *refs):
        sources, packed_ref, targets, sems = refs[: len(extra)], refs[len(extra)], refs[len(extra) + 1 : -1], refs[-1]
        columns = pl.ds(pl.multiple_of(devices_ref[0] * quarter, quarter), quarter)
        moves = [(qkv_ref.at[i, :, columns], packed_ref.at[i * share : (i + 1) * share, :]) for i in range(3)]
        moves.append((out_ref.at[:, columns], packed_ref.at[3 * share : fixed, :]))
        if rel is None:
            moves += list(zip(sources, targets))
        else:
            part = rel.shape[1] // STREAMS
            columns = pl.ds(pl.multiple_of(devices_ref[0] * part, part), part)
            for i in range(2):
                moves.append(
                    (
                        sources[0].at[i * half : (i + 1) * half, columns],
                        packed_ref.at[fixed:, i * part : (i + 1) * part],
                    )
                )
        copy_all(moves, sems)
        if rel is None:
            lines = []
            for layer in range(2):
                ffn_ref, bias_ref, gain_ref, shift_ref, last_ref = targets[5 * layer : 5 * layer + 5]
                left = jnp.concatenate([r[...].astype(F32) for r in (bias_ref, gain_ref, shift_ref)], axis=0)
                right = [ffn_ref[:, i * share : (i + 1) * share].astype(F32) for i in range(STREAMS)]
                last = last_ref[...].astype(F32)
                right.append(jnp.concatenate([last, jnp.zeros((1, share - last.shape[1]), F32)], axis=1))
                right.append(jnp.zeros((3, share), F32))
                lines.append(jnp.concatenate([left, jnp.concatenate(right, axis=0)], axis=1))
            lines = jnp.concatenate(lines, axis=0)
            packed_ref[fixed:, : 2 * share] = lines.astype(BF)
            if 2 * share < quarter:
                packed_ref[fixed:, 2 * share :] = jnp.zeros((more, quarter - 2 * share), BF)

    scratch = [pltpu.VMEM(a.shape, BF) for a in extra] if rel is None else []
    scratch.append(pltpu.SemaphoreType.DMA((4 + (len(extra) if rel is None else 2),)))
    outs = [((fixed + more, quarter), BF)]
    return chain(kernel, outs, [], scalars=[devices], stored=[qkv, out] + extra, scratch=scratch, after=after)[0]


def pack_ffn(chain, devices, here, matrix_in, matrix_out, n, after=()):
    share, ffn = matrix_in.shape
    ffn_share, dim = matrix_out.shape
    part = ffn_share // STREAMS
    if part % TILE:
        blocks = lax.dynamic_slice_in_dim(matrix_in.reshape(share, n, ffn_share), here * part, part, axis=2)
        rows = lax.dynamic_slice_in_dim(matrix_out, here * part, part, axis=0)
        return jnp.concatenate([blocks.reshape(share, n * part), rows], axis=0)

    def kernel(devices_ref, in_ref, out_ref, packed_ref, sems):
        first = devices_ref[0] * part
        moves = [(out_ref.at[pl.ds(pl.multiple_of(first, TILE), part), :], packed_ref.at[share:, :])]
        for g in range(n):
            columns = pl.ds(pl.multiple_of(g * ffn_share + first, TILE), part)
            moves.append((in_ref.at[:, columns], packed_ref.at[:share, g * part : (g + 1) * part]))
        copy_all(moves, sems)

    return chain(
        kernel,
        [((share + part, n * part), BF)],
        [],
        scalars=[devices],
        stored=[matrix_in, matrix_out],
        scratch=[pltpu.SemaphoreType.DMA((n + 1,))],
        after=after,
    )[0]


def place_ffn(chain, devices, here, blocks, share, n, after=()):
    rows, dim = blocks[0].shape
    part = rows - share
    ffn = n * part * STREAMS
    if part % TILE:
        stacked = jnp.stack([blocks[XOR.index(j)] for j in range(STREAMS)])
        ordered = [lax.dynamic_index_in_dim(stacked, here ^ a, 0, keepdims=False) for a in range(STREAMS)]
        grad_in = jnp.stack([b[:share].reshape(share, n, part) for b in ordered], axis=2)
        grad_out = jnp.concatenate([b[share:] for b in ordered], axis=0)
        return grad_in.reshape(share, ffn).astype(F32), grad_out.astype(F32)

    def kernel(devices_ref, *refs):
        in_ref, out_ref = refs[STREAMS:]
        for i in range(STREAMS):
            first = devices_ref[i] * part
            for g in range(n):
                columns = pl.ds(pl.multiple_of(g * part * STREAMS + first, TILE), part)
                in_ref[:, columns] = refs[i][:share, g * part : (g + 1) * part].astype(F32)
            out_ref[pl.ds(pl.multiple_of(first, TILE), part), :] = refs[i][share:, :].astype(F32)

    outs = [((share, ffn), F32), ((STREAMS * part, dim), F32)]
    return chain(kernel, outs, blocks, scalars=[devices], after=after, room=6)


def place_attention(chain, devices, blocks, share, ffn_part, rel_part, after=()):
    quarter = blocks[0].shape[1]
    dim = quarter * STREAMS
    fixed = 4 * share
    half = share // 2
    tiny = fixed + (half if rel_part else 0)
    tiny_rows = blocks[0].shape[0] - tiny

    def kernel(devices_ref, *refs):
        refs = list(refs)
        block_refs = [refs.pop(0) for _ in range(STREAMS)]
        qkv_ref, out_ref, tiny_ref, inner_ref = refs[:4]
        total = jnp.zeros((tiny_rows, quarter), F32)
        for i, ref in enumerate(block_refs):
            columns = pl.ds(pl.multiple_of(devices_ref[i] * quarter, quarter), quarter)
            for k in range(3):
                qkv_ref[k, :, columns] = ref[k * share : (k + 1) * share, :].astype(F32)
            out_ref[:, columns] = ref[3 * share : fixed, :].astype(F32)
            if rel_part:
                columns = pl.ds(pl.multiple_of(devices_ref[i] * rel_part, rel_part), rel_part)
                refs[4][:half, columns] = ref[fixed : fixed + half, :rel_part].astype(F32)
                refs[4][half:, columns] = ref[fixed : fixed + half, rel_part:].astype(F32)
            mine = ref[tiny:, :].astype(F32)
            total = total + mine
            inner_ref[pl.ds(devices_ref[i], 1), :] = mine[0:1, share : share + ffn_part]
        tiny_ref[...] = total

    outs = [
        ((3, share, dim), F32),
        ((share, dim), F32),
        ((tiny_rows, quarter), F32),
        ((STREAMS, ffn_part), F32),
    ]
    if rel_part:
        outs.append(((share, rel_part * STREAMS), F32))
    return chain(kernel, outs, blocks, scalars=[devices], after=after, room=6)


class Layer:
    pass


def own_columns(matrix, here):
    width = matrix.shape[-1] // STREAMS
    return lax.dynamic_slice_in_dim(matrix, here * width, width, axis=matrix.ndim - 1)


def per_device(
    enc_input, pred_input, cotangent, bucket_len, pad_len, rel_table,
    enc_qkv, enc_out, enc_ffn_in, enc_ffn_out, enc_ffn_bias, enc_bias, enc_gain, enc_shift,
    dec_qkv, dec_out, dec_rel, dec_rel_bias, dec_ffn_in, dec_ffn_out, dec_ffn_bias, dec_bias, dec_gain, dec_shift,
):
    chain = Chain()
    here = lax.axis_index("stream")
    n = lax.axis_size("dp")
    group = lax.axis_index("dp")
    place = ring_place(group, n)
    rows = enc_input.shape[0]
    total = STREAMS * rows
    dim = enc_input.shape[1]
    share = enc_out.shape[0]
    quarter = dim // STREAMS
    ffn_share = enc_ffn_out.shape[0]
    ffn_part = ffn_share // STREAMS
    rel_all = dec_rel.shape[1]
    rel_part = rel_all // STREAMS
    fixed = 4 * share
    half = share // 2

    bucket = bucket_len[0]
    starts = []
    for j in XOR:
        holder = here ^ j
        for chunk in range(2):
            starts.append(jnp.where(bucket == total, holder * rows + chunk * 64, chunk * bucket + holder * 64))
    meta = jnp.stack([v.astype(jnp.int32) for v in starts + [bucket, pad_len[0, 0], pad_len[0, 1]]])
    devices = jnp.stack([here ^ j for j in XOR]).astype(jnp.int32)
    ring_index = jnp.stack([ring_member(place - o, n) for o in range(n)]).astype(jnp.int32)
    tables = rel_tables(rel_table, total)

    smalls = (
        enc_ffn_bias[None], enc_bias, enc_gain, enc_shift, dec_rel_bias[None],
        dec_ffn_bias[None], dec_bias, dec_gain, dec_shift, dec_rel_bias[None],
    )
    small_rows = 16

    def pins(pieces, stage):
        k = stage * (n // 2) // 4
        return [piece for _, _, piece in pieces[2 * k - 1 : 2 * k + 1]]

    def attention_regions(extra):
        regions = [(i * share, (i + 1) * share, 0, quarter, 0, 0, i * quarter) for i in range(3)]
        regions.append((fixed - share, fixed, 0, quarter, 1, 0, 0))
        return regions + extra

    shapes = [(share, 3 * quarter), (share, quarter)]

    enc_pieces = ring_pieces(pack_attention(chain, devices, enc_qkv, enc_out, smalls=smalls), n)
    enc_quads = gather_rows(enc_input)
    pred_quads = [gather_rows(pred_input[i]) for i in range(2)]
    def ffn_gather(matrix_in, matrix_out, after=()):
        packed = pack_ffn(chain, devices, here, matrix_in, matrix_out, n, after)
        return lax.all_gather(packed, "dp", axis=0, tiled=False)

    enc_ffn = ffn_gather(enc_ffn_in, enc_ffn_out, pins(enc_pieces, 1))
    dec_pieces = ring_pieces(pack_attention(chain, devices, dec_qkv, dec_out, rel=dec_rel, after=pins(enc_pieces, 4)), n)
    dec_ffn = ffn_gather(dec_ffn_in, dec_ffn_out)

    def turn_out(columns):
        blocks = columns.reshape(dim, quarter)
        sent = [lax.dynamic_slice_in_dim(blocks, (here ^ j) * quarter, quarter, axis=0) for j in XOR]
        return jnp.concatenate(by_absolute(turn_blocks(sent), here), axis=1)

    def turn_out_back(grad):
        sent = [lax.dynamic_slice_in_dim(grad, (here ^ j) * quarter, quarter, axis=1) for j in XOR]
        return jnp.concatenate(by_absolute(turn_blocks(sent), here), axis=0).reshape(n, share, quarter)

    enc_wqkv, enc_wout, small_all = assemble(
        chain,
        enc_pieces,
        ring_index,
        attention_regions([(fixed, fixed + small_rows, 0, quarter, 2, 0, 0)]),
        shapes + [(small_rows, quarter)],
        n,
    )

    small_all = small_all.astype(F32)

    def attention_layer(number, wqkv, wout):
        w = Layer()
        w.qkv = wqkv.reshape(dim, 3 * quarter)
        w.out = turn_out(wout)
        block = small_all[:, 8 * number : 8 * number + 8]
        w.ffn_bias = lax.dynamic_slice_in_dim(block, here, 1, axis=1)[:, 0, share : 2 * share].reshape(1, -1)
        w.small = jnp.transpose(block[:, :, :share], (1, 0, 2)).reshape(8, dim)
        mine = own_columns(w.small, here)
        w.qkv_bias = jnp.concatenate([mine[0:1], jnp.zeros_like(mine[0:1]), mine[1:2]], axis=1)
        return w

    enc = attention_layer(0, enc_wqkv, enc_wout)
    enc_all, enc_heads = project(chain, enc_quads, enc, False)
    enc_context, enc_lse, _ = attention_forward(chain, meta, enc_heads)
    scatter = Scatter(out_project(chain, enc_context, enc))
    scatter.middle(chain, pins(dec_pieces, 1))
    enc_unit0, enc_inverse0, low = norm_first(chain, enc_input, scatter.parts(), enc, after=pins(dec_pieces, 2))
    quads = gather_rows(low)
    enc.ffn = enc_ffn
    *parts, enc_hidden, enc_active, enc_slope = ffn_forward(chain, quads, enc, after=pins(dec_pieces, 3))
    scatter = Scatter(parts)
    scatter.middle(chain, pins(dec_pieces, 4))
    dec_wqkv, dec_wout, dec_wrel = assemble(
        chain,
        dec_pieces,
        ring_index,
        attention_regions(
            [
                (fixed, fixed + half, 0, rel_part, 2, 0, 0),
                (fixed, fixed + half, rel_part, 2 * rel_part, 2, half, 0),
            ]
        ),
        shapes + [(share, rel_part)],
        n,
    )
    dec = attention_layer(1, dec_wqkv, dec_wout)
    dec.rel = dec_wrel.reshape(dim, rel_part)
    dec.rel_bias = own_columns(small_all[:, 12, share : share + rel_all // n].reshape(1, -1), here)
    alls, heads, rels = [None] * 3, [None] * 3, [None] * 3

    def project_stream(i, quads):
        alls[i], heads[i], rels[i] = project(chain, quads, dec, True)

    project_stream(1, pred_quads[0])
    project_stream(2, pred_quads[1])
    enc_unit1, enc_inverse1, main_rows, main_low = norm_second(chain, enc_unit0, scatter.parts(), enc)
    main_quads = gather_rows(main_low)

    stream_inputs = (main_rows, pred_input[0], pred_input[1])
    project_stream(0, main_quads)
    contexts, lses = [None] * 3, [None] * 3

    def attend(i, after=()):
        contexts[i], lses[i], parts = attention_forward(
            chain, meta, heads[i], None if i == 0 else heads[0], rels[i], tables, dec.out, after
        )
        return Scatter(parts)

    def staged(work, finish):
        scatters = []
        for i in range(3):
            scatters.append(work(i))
            if i:
                scatters[i - 1].middle(chain)
        results = [finish(0, scatters[0])]
        scatters[2].middle(chain)
        results += [finish(1, scatters[1]), finish(2, scatters[2])]
        return results

    firsts = staged(
        lambda i: attend(i),
        lambda i, scatter: norm_first(chain, stream_inputs[i], scatter.parts(), dec),
    )
    hidden_quads = [gather_rows(first[2]) for first in firsts]
    dec.ffn = dec_ffn
    kept = [None] * 3

    def feed(i):
        *parts, hidden, active, slope = ffn_forward(chain, hidden_quads[i], dec)
        kept[i] = (hidden, active, slope)
        return Scatter(parts)

    seconds = staged(
        feed, lambda i, scatter: norm_second_both(chain, firsts[i][0], scatter.parts(), cotangent[i], dec)
    )
    outputs = [second[0] for second in seconds]

    branch_quads = [gather_rows(second[2]) for second in seconds]
    branches = [None] * 3

    def feed_back(i):
        *parts, branch, inner, inner_sum = ffn_backward(chain, branch_quads[i], kept[i][2], dec)
        branches[i] = (branch, inner, inner_sum)
        return Scatter(parts)

    backs = staged(
        feed_back,
        lambda i, scatter: norm_first_back(
            chain, seconds[i][1], scatter.parts(), firsts[i][0], firsts[i][1], dec
        ),
    )
    attended_quads = [gather_rows(back[1]) for back in backs]

    def ffn_grads(pairs):
        grad_in = sum(dot_tn(hidden, inner) for hidden, _, inner, _ in pairs).astype(BF)
        grad_out = sum(dot_tn(active, branch) for _, active, _, branch in pairs).astype(BF)
        return grad_in.reshape(n, share, dim), grad_out.reshape(n, ffn_part, dim)

    def ffn_sum(pairs):
        regions = [(0, 0, 0, share), (1, 0, share, ffn_part)]
        return RingSum(chain, list(ffn_grads(pairs)), regions, dim, n, ring_index)

    def advance(ring, stage):
        result = None
        while ring.done < stage * (n // 2 + 1) // 5:
            result = ring.step()
            ring.done += 1
        return result

    dec_ffn_total = lax.psum_scatter(
        jnp.concatenate(
            ffn_grads([(kept[i][0], kept[i][1], branches[i][1], branches[i][0]) for i in range(3)]), axis=1
        ),
        "dp",
        scatter_dimension=0,
        tiled=False,
    )
    results = [None] * 3
    for i in (1, 2, 0):
        results[i] = attention_backward(
            chain, meta, heads[i], attended_quads[i], dec.out, lses[i], None if i == 0 else heads[0], rels[i], tables
        )
    dheads, head_sums, rel_sums = [None] * 3, [None] * 3, [None] * 3

    def back_project(i):
        dq, dk, dv, _, drel = results[i][:5]
        keys = [r[1] for r in results] if i == 0 else [results[i][5]]
        vals = [r[2] for r in results] if i == 0 else [results[i][6]]
        *parts, dheads[i], head_sums[i], rel_sums[i] = project_back(chain, dq, keys, vals, drel, dec)
        return Scatter(parts)

    main_scatter = back_project(0)
    pred_scatters = [back_project(1)]
    main_scatter.middle(chain)
    pred_scatters.append(back_project(2))
    pred_scatters[0].middle(chain)

    def widen(part, size):
        return lax.dynamic_update_slice(jnp.zeros((1, size), F32), part, (0, here * part.shape[1]))

    def small_pack(inner_sum, tiny0, tiny1, heads_sum, rel_sum=None):
        wide = jnp.concatenate(
            [
                widen(heads_sum[:, :quarter], dim),
                widen(heads_sum[:, 2 * quarter :], dim),
                tiny0[0:1],
                tiny1[0:1],
                tiny0[1:2],
                tiny1[1:2],
                tiny0[2:3],
                tiny1[2:3],
            ],
            axis=0,
        )
        left = jnp.transpose(wide.reshape(8, n, share), (1, 0, 2))
        spare = quarter - share
        lines = [jnp.pad(inner_sum.reshape(n, 1, ffn_part), ((0, 0), (0, 0), (0, spare - ffn_part)))]
        if rel_sum is not None:
            line = widen(rel_sum, rel_all).reshape(n, 1, rel_all // n)
            lines.append(jnp.pad(line, ((0, 0), (0, 0), (0, spare - rel_all // n))))
        lines.append(jnp.zeros((n, 8 - len(lines), spare), F32))
        packed = jnp.concatenate([left, jnp.concatenate(lines, axis=1)], axis=2)
        return jnp.pad(packed, ((0, 0), (0, 8), (0, 0))).astype(BF)

    def attention_grads(qkv_grad, out_grad, more):
        return [qkv_grad.astype(BF).reshape(n, share, 3 * quarter), turn_out_back(out_grad.astype(BF))] + more

    def attention_ring(*grads):
        arrays = attention_grads(*grads)
        regions = [(0, i * quarter, i * share, share) for i in range(3)] + [(1, 0, 3 * share, share)]
        at = fixed
        for which, array in enumerate(arrays[2:]):
            regions.append((2 + which, 0, at, array.shape[1]))
            at += array.shape[1]
        return RingSum(chain, arrays, regions, quarter, n, ring_index)

    dec_out_part = sum(dot_tn(contexts[i], results[i][3]) for i in range(3))
    dec_qkv_part = sum(dot_tn(alls[i], dheads[i]) for i in range(3))
    rel_blocks = sum(dot_tn(alls[i], results[i][4]) for i in range(3)).astype(BF).reshape(n, share, rel_part)
    dec_small = small_pack(
        sum(branches[i][2] for i in range(3)),
        sum(backs[i][2] for i in range(3)),
        sum(seconds[i][3] for i in range(3)),
        sum(head_sums),
        sum(rel_sums),
    )
    wide, *others = attention_grads(
        dec_qkv_part,
        dec_out_part,
        [jnp.concatenate([rel_blocks[:, :half], rel_blocks[:, half:]], axis=2), dec_small],
    )
    thirds = [wide[:, :, i * quarter : (i + 1) * quarter] for i in range(3)]
    dec_total = lax.psum_scatter(
        jnp.concatenate(thirds + others, axis=1), "dp", scatter_dimension=0, tiled=False
    )

    enc_sum_grad, low, enc_tiny1 = norm_second_back(
        chain, backs[0][0], main_scatter.parts(), enc_unit1, enc_inverse1, enc
    )
    quads = gather_rows(low)
    pred_scatters[1].middle(chain)
    *parts, enc_branch, enc_inner, enc_inner_sum = ffn_backward(chain, quads, enc_slope, enc)
    scatter = Scatter(parts)
    pred_grads = [input_gradient(chain, backs[1][0], pred_scatters[0].parts())]
    scatter.middle(chain)
    pred_grads.append(input_gradient(chain, backs[2][0], pred_scatters[1].parts()))
    enc_ffn_ring = ffn_sum([(enc_hidden, enc_active, enc_inner, enc_branch)])
    advance(enc_ffn_ring, 1)
    dec_ffn_blocks = gather_rows(dec_ffn_total)
    residual, attended_low, enc_tiny0 = norm_first_back(
        chain, enc_sum_grad, scatter.parts(), enc_unit0, enc_inverse0, enc
    )
    quads = gather_rows(attended_low)
    advance(enc_ffn_ring, 2)
    dq, dk, dv, attended = attention_backward(chain, meta, enc_heads, quads, enc.out, enc_lse)
    *parts, enc_dheads, enc_head_sum = project_back(chain, dq, [dk], [dv], None, enc)
    scatter = Scatter(parts)
    advance(enc_ffn_ring, 3)
    enc_ring = attention_ring(
        dot_tn(enc_all, enc_dheads),
        dot_tn(enc_context, attended),
        [small_pack(enc_inner_sum, enc_tiny0, enc_tiny1, enc_head_sum)],
    )
    advance(enc_ring, 1)
    scatter.middle(chain)
    advance(enc_ffn_ring, 4)
    advance(enc_ring, 2)
    dec_in_grad, dec_back_grad = place_ffn(chain, devices, here, dec_ffn_blocks, share, n)
    enc_input_grad = input_gradient(chain, residual, scatter.parts())
    advance(enc_ring, 3)
    enc_ffn_blocks = gather_rows(advance(enc_ffn_ring, 5))
    dec_blocks = gather_rows(dec_total)
    advance(enc_ring, 4)
    dec_results = place_attention(chain, devices, dec_blocks, share, ffn_part, rel_part)
    enc_blocks = gather_rows(advance(enc_ring, 5))
    enc_in_grad, enc_back_grad = place_ffn(chain, devices, here, enc_ffn_blocks, share, n)
    enc_results = place_attention(chain, devices, enc_blocks, share, ffn_part, 0)

    def tiny_out(results):
        tiny, inner = results[2], results[3]
        return inner.reshape(-1), tiny[0:4, :share], tiny[4:6, :share], tiny[6:8, :share]

    return (
        jnp.stack(outputs),
        enc_input_grad,
        jnp.stack(pred_grads),
        enc_results[0],
        enc_results[1],
        enc_in_grad,
        enc_back_grad,
        *tiny_out(enc_results),
        dec_results[0],
        dec_results[1],
        dec_results[4],
        dec_results[2][1, share : share + rel_all // n],
        dec_in_grad,
        dec_back_grad,
        *tiny_out(dec_results),
    )


def solution(mesh):
    tokens = P(("stream", "dp"), None)
    streams = P(None, ("stream", "dp"), None)
    first, second, cube = P("dp", None), P(None, "dp"), P(None, "dp", None)
    flat = P("dp")
    return jax.shard_map(
        per_device,
        mesh=mesh,
        in_specs=(
            tokens, streams, streams, flat, first, P(),
            cube, first, first, first, flat, second, second, second,
            cube, first, first, flat, first, first, flat, second, second, second,
        ),
        out_specs=(
            streams, tokens, streams,
            cube, first, first, first, flat, second, second, second,
            cube, first, first, flat, first, first, flat, second, second, second,
        ),
        check_vma=False,
    )
```

time: 648 us -> 575 us (0.89)
  Pallas kernels: 105 us -> 163 us
  other arithmetic: 47.7 us -> 8.62 us
  waiting for transfers between devices: 177 us -> 140 us
  matrix products: 49.8 us -> 19.3 us
  starting transfers between devices: 152 us -> 132 us
  local copies, waits for them, and re-layouts: 99.4 us -> 84.6 us
  between operations: 6.75 us -> 17.7 us
    pallas_call x33 -> x77, Pallas kernels: 105 us -> 163 us  [__call__(): pl.pallas_call(body, out_shape=[jax.ShapeDtypeStruct(shape, kind) for sha...]
    ppermute x64 -> x32, starting transfers between devices: 55.5 us -> 25.7 us  [ring_step(): return lax.ppermute(values, 'dp', pairs)]
    unnamed x701 -> x392, local copies, waits for them, and re-layouts: 40.2 us -> 66.3 us
    dot_general x22 -> x0, matrix products: 22.5 us -> none  [the longest x11 13.3 us: dot_nt(): lax.dot_general(a, b, (((1,), (1,)), ((), ())), preferred_element_type=F32)]
    ppermute x80 -> x100, waiting for transfers between devices: 97.4 us -> 77.2 us  [swap(): lax.ppermute(values, 'stream', [(i, i ^ bit) for i in range(STREAMS)])]
    convert_element_type x47 -> x1, other arithmetic: 18.5 us -> 0.01 us  [per_device(): small_all = small_all.astype(F32)]
    ppermute x64 -> x32, waiting for transfers between devices: 79.5 us -> 62.7 us  [ring_step(): return lax.ppermute(values, 'dp', pairs)]
    convert_element_type x4 -> x0, local copies, waits for them, and re-layouts: 11.5 us -> none  [ffn_out(): return (grad_in.reshape(share, ffn).astype(F32), grad_out.astype(F32))]
  transfers between devices with their start and end apart: 144 -> 136, of which waited for: 47 -> 40; matrix products, arithmetic and copies ran while one was open for 25% -> 8% of each run, Pallas kernels for 16% -> 28%
where the time goes in v3:
time: 575 us; the launch traced here: 566 us
  Pallas kernels  163 us (28%)
  waiting for transfers between devices  140 us (24%)
  starting transfers between devices  132 us (23%)
  local copies, waits for them, and re-layouts  84.6 us (15%)
  matrix products  19.3 us (3%)
  between operations  17.7 us (3%)
  other arithmetic  8.62 us (1%)
    pallas_call x77, Pallas kernels, __call__(): pl.pallas_call(body, out_shape=[jax.ShapeDtypeStruct(shape, kind) for sha...  163 us
    ppermute x100, starting transfers between devices, swap(): lax.ppermute(values, 'stream', [(i, i ^ bit) for i in range(STREAMS)])  107 us
    ppermute x100, waiting for transfers between devices, swap(): lax.ppermute(values, 'stream', [(i, i ^ bit) for i in range(STREAMS)])  77.2 us
    unnamed x392, local copies, waits for them, and re-layouts  66.3 us
    ppermute x32, waiting for transfers between devices, ring_step(): return lax.ppermute(values, 'dp', pairs)  62.7 us
    ppermute x32, starting transfers between devices, ring_step(): return lax.ppermute(values, 'dp', pairs)  25.7 us
    dot_general x19, matrix products, dot_tn(): lax.dot_general(a, b, (((0,), (0,)), ((), ())), preferred_element_type=F32)  19.3 us
  transfers between devices with their start and end apart: 136, of which 40 were waited for; matrix products, arithmetic and copies ran while one was open for 8% of the time, Pallas kernels for 28%

profile of v3, /device:TPU:1, one launch (start us, length us, event | category | flops | bytes accessed | tf_op | source)
XLA Modules:
  0.0 566.0 jit_solution(2095384589005707622)
XLA Ops:
  13.7 6.1 %collective-permute-done.4.refs_4_.refs_3_ = bf16[528,256]{1,0:T(8,128)(2,1)S(1)} collective-permute-done((bf16[528,256]{1,0:T(8,128)(2,1)S(1)}, bf16[528,256]{1,0:T(8,128)(2,1)S(1)}, u32[]{:S(2)}, u32[]{:S(2)}) %collective-permute-start.4) | collective-permute-done | bytes 270368 | tf_op jit(solution)/shard_map/ppermute | solution.py:145
  21.3 5.3 collective-permute-done.6.refs_5_
  28.9 3.3 collective-permute-start.1
  56.0 4.4 collective-permute-done.11
  62.4 4.7 shard_map.397
  74.7 3.9 collective-permute-done.14.refs_2_
  82.9 9.5 %collective-permute-done.17.refs_5_.refs_4_ = bf16[576,256]{1,0:T(8,128)(2,1)S(1)} collective-permute-done((bf16[576,256]{1,0:T(8,128)(2,1)S(1)}, bf16[576,256]{1,0:T(8,128)(2,1)S(1)}, u32[]{:S(2)}, u32[]{:S(2)}) %collective-permute-start.17) | collective-permute-done | bytes 294944 | tf_op jit(solution)/shard_map/ppermute | solution.py:145
  92.4 8.1 %collective-permute-done.18.refs_6_.refs_5_ = bf16[576,256]{1,0:T(8,128)(2,1)S(1)} collective-permute-done((bf16[576,256]{1,0:T(8,128)(2,1)S(1)}, bf16[576,256]{1,0:T(8,128)(2,1)S(1)}, u32[]{:S(2)}, u32[]{:S(2)}) %collective-permute-start.18) | collective-permute-done | bytes 294944 | tf_op jit(solution)/shard_map/ppermute | solution.py:145
  105.7 6.8 %collective-permute-start.20 = (bf16[128,1024]{1,0:T(8,128)(2,1)}, bf16[128,1024]{1,0:T(8,128)(2,1)S(1)}, u32[]{:S(2)}, u32[]{:S(2)}) collective-permute-start(bf16[128,1024]{1,0:T(8,128)(2,1)} %get-tuple-element.234.refs_0_), channel_id=1, source_target_pairs={{0,8},{8,0},{16,24},{24,16},{1,9},{9,1},{17,25},{25,17},{2,10},{10... | collective-permute-start | bytes 786440 | tf_op jit(solution)/shard_map/ppermute | solution.py:36
  112.4 2.8 collective-permute-start.21
  116.0 9.0 %collective-permute-done.23.refs_7_ = bf16[576,256]{1,0:T(8,128)(2,1)S(1)} collective-permute-done((bf16[576,256]{1,0:T(8,128)(2,1)}, bf16[576,256]{1,0:T(8,128)(2,1)S(1)}, u32[]{:S(2)}, u32[]{:S(2)}) %collective-permute-start.23) | collective-permute-done | bytes 294944 | tf_op jit(solution)/shard_map/ppermute | solution.py:145
  131.5 6.1 %shard_map.401 = (f32[128,1024]{1,0:T(8,128)S(1)}, f32[128,1024]{1,0:T(8,128)S(1)}, bf16[256,1024]{1,0:T(8,128)(2,1)}, bf16[512,1024]{1,0:T(8,128)(2,1)S(1)}, bf...) custom-call(bf16[128,1024]{1,0:T(8,128)(2,1)} %get-tuple-element.234.refs_0_, ...), custom_call_target="tpu_custom_call" | custom-call | flops 10000000000 | bytes 10000000 | tf_op jit(solution)/shard_map/pallas_call | solution.py:54
  158.0 2.8 shard_map.403
  164.3 2.5 shard_map.405
  166.9 3.5 collective-permute-done.37
  173.9 5.6 collective-permute-done.34.refs_1_
  182.9 6.0 %shard_map.408 = (bf16[512,256]{1,0:T(8,128)(2,1)S(1)}, f32[512,128]{1,0:T(8,128)S(1)}, f32[128,1024]{1,0:T(8,128)S(1)}, f32[128,1024]{1,0:T(8,128)S(1)}, bf16[256,1024]{1,0:T(8,128)(2,1)S(1)}) custom-call(s32[11]{0:T(128)S(1)} %stack.182.refs_0_, bf16[512,768]{1,0:T(8,128)(2,1)S(1)} %get-tuple-element.245.refs_1_.refs_2_.refs_8_, ...), custom_call_target="tpu_custom_call" | custom-call | flops 10000000000 | bytes 10000000 | tf_op jit(solution)/shard_map/pallas_call | solution.py:54
  189.4 15.9 %shard_map.409 = (bf16[512,256]{1,0:T(8,128)(2,1)S(1)}, f32[512,128]{1,0:T(8,128)S(1)}, f32[128,1024]{1,0:T(8,128)S(1)}, f32[128,1024]{1,0:T(8,128)S(1)}, bf16[256,1024]{1,0:T(8,128)(2,1)S(1)}) custom-call(s32[11]{0:T(128)S(1)} %stack.182.refs_0_, bf16[512,768]{1,0:T(8,128)(2,1)S(1)} %get-tuple-element.252.refs_1_, ...), custom_call_target="tpu_custom_call" | custom-call | flops 10000000000 | bytes 10000000 | tf_op jit(solution)/shard_map/pallas_call | solution.py:54
  207.2 7.1 %shard_map.411 = (bf16[512,256]{1,0:T(8,128)(2,1)S(1)}, f32[512,128]{1,0:T(8,128)S(1)}, f32[128,1024]{1,0:T(8,128)S(1)}, f32[128,1024]{1,0:T(8,128)S(1)}, bf16[256,1024]{1,0:T(8,128)(2,1)S(1)}) custom-call(s32[11]{0:T(128)S(1)} %stack.182.refs_0_, bf16[512,768]{1,0:T(8,128)(2,1)S(1)} %get-tuple-element.258.refs_1_, ...), custom_call_target="tpu_custom_call" | custom-call | flops 10000000000 | bytes 10000000 | tf_op jit(solution)/shard_map/pallas_call | solution.py:54
  218.7 4.1 collective-permute-done.47.refs_3_
  230.6 3.4 collective-permute-done.46.refs_3_
  247.6 5.6 shard_map.417
  253.4 5.4 shard_map.418
  261.5 5.3 shard_map.420
  271.0 4.1 collective-permute-done.57.refs_3_
  282.3 4.1 collective-permute-done.59.refs_3_
  305.1 3.3 shard_map.429
  313.2 2.8 pad_maximum_fusion
  323.2 2.9 collective-permute-done.77.refs_3_
  328.9 2.8 collective-permute-done.72.refs_3_
  333.3 4.1 collective-permute-done.76.refs_3_
  338.4 4.6 collective-permute-done.81.refs_3_
  345.7 10.6 %shard_map.435 = (bf16[512,256]{1,0:T(8,128)(2,1)S(1)}, f32[512,256]{1,0:T(8,128)S(1)}, f32[512,256]{1,0:T(8,128)S(1)}, bf16[512,1024]{1,0:T(8,128)(2,1)S(1)}, b...) custom-call(s32[11]{0:T(128)S(1)} %stack.182.refs_0_, ...), custom_call_target="tpu_custom_call" | custom-call | flops 10000000000 | bytes 10000000 | tf_op jit(solution)/shard_map/pallas_call | solution.py:54
  359.3 11.0 %shard_map.436 = (bf16[512,256]{1,0:T(8,128)(2,1)S(1)}, f32[512,256]{1,0:T(8,128)S(1)}, f32[512,256]{1,0:T(8,128)S(1)}, bf16[512,1024]{1,0:T(8,128)(2,1)S(1)}, b...) custom-call(s32[11]{0:T(128)S(1)} %stack.182.refs_0_, ...), custom_call_target="tpu_custom_call" | custom-call | flops 10000000000 | bytes 10000000 | tf_op jit(solution)/shard_map/pallas_call | solution.py:54
  370.3 8.7 %shard_map.437 = (bf16[512,256]{1,0:T(8,128)(2,1)S(1)}, f32[512,256]{1,0:T(8,128)S(1)}, f32[512,256]{1,0:T(8,128)S(1)}, bf16[512,1024]{1,0:T(8,128)(2,1)S(1)}, bf16[512,128]{1,0:T(8,128)(2,1)S(1)}) custom-call(s32[11]{0:T(128)S(1)} %stack.182.refs_0_, bf16[512,768]{1,0:T(8,128)(2,1)S(1)} %copy-done.86, bf16[128,1024]{1,0:T(8,128)(2,1)S(1)} %get-tuple-element.299.refs_2_, ...), custom_call_target="tpu_custom_call" | custom-call | flops 10000000000 | bytes 10000000 | tf_op jit(solution)/shard_map/pallas_call | solution.py:54
  407.7 5.2 collective-permute-done.87.refs_1_
  419.1 2.7 shard_map.445
  430.1 3.4 collective-permute-done.93.refs_3_
  437.0 3.7 collective-permute-done.95.refs_3_
  446.5 5.8 %shard_map.452 = (bf16[512,256]{1,0:T(8,128)(2,1)S(1)}, f32[512,256]{1,0:T(8,128)S(1)}, f32[512,256]{1,0:T(8,128)S(1)}, bf16[512,1024]{1,0:T(8,128)(2,1)S(1)}) custom-call(s32[11]{0:T(128)S(1)} %stack.182.refs_0_, bf16[512,768]{1,0:T(8,128)(2,1)S(1)} %copy-done.90, bf16[128,1024]{1,0:T(8,128)(2,1)S(1)} %get-tuple-element.352.refs_2_, ...), custom_call_target="tpu_custom_call" | custom-call | flops 10000000000 | bytes 10000000 | tf_op jit(solution)/shard_map/pallas_call | solution.py:54
  453.4 8.5 %collective-permute-done.103.refs_1_ = bf16[256,1024]{1,0:T(8,128)(2,1)S(1)} collective-permute-done((bf16[256,1024]{1,0:T(8,128)(2,1)S(1)}, bf16[256,1024]{1,0:T(8,128)(2,1)S(1)}, u32[]{:S(2)}, u32[]{:S(2)}) %collective-permute-start.103) | collective-permute-done | bytes 524320 | tf_op jit(solution)/shard_map/ppermute | solution.py:145
  470.1 3.3 collective-permute-done.101
  490.8 6.8 %collective-permute-start.107 = (bf16[256,1024]{1,0:T(8,128)(2,1)S(1)}, bf16[256,1024]{1,0:T(8,128)(2,1)S(1)}, u32[]{:S(2)}, u32[]{:S(2)}) collective-permute-start(bf16[256,1024]{1,0:T(8,128)(2,1)S(1)} %bitcast.219), channel_id=1, source_target_pairs={{0,8},{8,0},{16,24},{24,16},{1,9},{9,1},{17,25},{25,17},{2,10},{10... | collective-permute-start | bytes 1572872 | tf_op jit(solution)/shard_map/ppermute | solution.py:36
  497.5 3.3 collective-permute-done.106.refs_2_
  506.8 2.9 shard_map.459
  525.9 4.3 collective-permute-done.115.refs_1_
  546.8 2.7 collective-permute-done.126.refs_2_
  551.4 2.9 shard_map.466
  (829 shorter events, 296.5 us)
Async XLA Ops:
  7.2 119.2 %all-gather.5.cloned.1.call-start = ((), (), s32[]{:S(2)}) async-start(), calls=%async_computation.4 | async-start | bytes 4718592 | tf_op jit(solution)/shard_map/all_gather | solution.py:1041
  28.9 26.0 %collective-permute-start.1 = (bf16[128,1024]{1,0:T(8,128)(2,1)S(1)}, bf16[128,1024]{1,0:T(8,128)(2,1)S(1)}, u32[]{:S(2)}, u32[]{:S(2)}) collective-permute-start(bf16[128,1024]{1,0:T(8,128)(2,1)S(1)} %copy-done.38), channel_id=1, source_target_pairs={{0,8},{8,0},{16,24},{24,16},{1,9},{9,1},{17,25},{25,17},{2,10},{10... | collective-permute-start | bytes 786440 | tf_op jit(solution)/shard_map/ppermute | solution.py:36
  35.0 19.9 %collective-permute-start.2 = (bf16[128,1024]{1,0:T(8,128)(2,1)S(1)}, bf16[128,1024]{1,0:T(8,128)(2,1)S(1)}, u32[]{:S(2)}, u32[]{:S(2)}) collective-permute-start(bf16[128,1024]{1,0:T(8,128)(2,1)S(1)} %collective-permute-done.refs_1_), channel_id=1, source_target_pairs={{0,8},{8,0},{16,24},{24,16},{1,9},{9,1},{17,25},{25,17},{2,10},{10... | collective-permute-start | bytes 786440 | tf_op jit(solution)/shard_map/ppermute | solution.py:36
  41.8 200.0 %all-gather.7.cloned.1.call-start = ((), (), s32[]{:S(2)}) async-start(), calls=%async_computation.5 | async-start | bytes 4718592 | tf_op jit(solution)/shard_map/all_gather | solution.py:1041
  69.0 80.1 %collective-permute-start.31 = (bf16[128,1024]{1,0:T(8,128)(2,1)S(1)}, bf16[128,1024]{1,0:T(8,128)(2,1)}, u32[]{:S(2)}, u32[]{:S(2)}) collective-permute-start(bf16[128,1024]{1,0:T(8,128)(2,1)S(1)} %get-tuple-element.454.refs_0_), channel_id=1, source_target_pairs={{0,16},{8,24},{16,0},{24,8},{1,17},{9,25},{17,1},{25,9},{2,18},{10... | collective-permute-start | bytes 786440 | tf_op jit(solution)/shard_map/ppermute | solution.py:36
  78.8 21.7 %collective-permute-start.18 = (bf16[576,256]{1,0:T(8,128)(2,1)S(1)}, bf16[576,256]{1,0:T(8,128)(2,1)S(1)}, u32[]{:S(2)}, u32[]{:S(2)}) collective-permute-start(bf16[576,256]{1,0:T(8,128)(2,1)S(1)} %collective-permute-done.15.refs_3_), channel_id=1, source_target_pairs={{0,1},{2,0},{4,2},{6,4},{7,6},{5,7},{3,5},{1,3},{8,9},{10,8},{12,1... | collective-permute-start | bytes 884744 | tf_op jit(solution)/shard_map/ppermute | solution.py:145
  82.6 17.9 %collective-permute-start.16 = (bf16[128,1024]{1,0:T(8,128)(2,1)S(1)}, bf16[128,1024]{1,0:T(8,128)(2,1)S(1)}, u32[]{:S(2)}, u32[]{:S(2)}) collective-permute-start(bf16[128,1024]{1,0:T(8,128)(2,1)S(1)} %shard_map.399.refs_7_), channel_id=1, source_target_pairs={{0,16},{8,24},{16,0},{24,8},{1,17},{9,25},{17,1},{25,9},{2,18},{10... | collective-permute-start | bytes 786440 | tf_op jit(solution)/shard_map/ppermute | solution.py:36
  104.0 21.0 %collective-permute-start.23 = (bf16[576,256]{1,0:T(8,128)(2,1)}, bf16[576,256]{1,0:T(8,128)(2,1)S(1)}, u32[]{:S(2)}, u32[]{:S(2)}) collective-permute-start(bf16[576,256]{1,0:T(8,128)(2,1)} %copy-done.36), channel_id=1, source_target_pairs={{0,1},{2,0},{4,2},{6,4},{7,6},{5,7},{3,5},{1,3},{8,9},{10,8},{12,1... | collective-permute-start | bytes 884744 | tf_op jit(solution)/shard_map/ppermute | solution.py:145
  105.7 19.3 %collective-permute-start.20 = (bf16[128,1024]{1,0:T(8,128)(2,1)}, bf16[128,1024]{1,0:T(8,128)(2,1)S(1)}, u32[]{:S(2)}, u32[]{:S(2)}) collective-permute-start(bf16[128,1024]{1,0:T(8,128)(2,1)} %get-tuple-element.234.refs_0_), channel_id=1, source_target_pairs={{0,8},{8,0},{16,24},{24,16},{1,9},{9,1},{17,25},{25,17},{2,10},{10... | collective-permute-start | bytes 786440 | tf_op jit(solution)/shard_map/ppermute | solution.py:36
  115.9 33.6 %collective-permute-start.28 = (bf16[128,1024]{1,0:T(8,128)(2,1)S(1)}, bf16[128,1024]{1,0:T(8,128)(2,1)}, u32[]{:S(2)}, u32[]{:S(2)}) collective-permute-start(bf16[128,1024]{1,0:T(8,128)(2,1)S(1)} %get-tuple-element.455.refs_0_), channel_id=1, source_target_pairs={{0,16},{8,24},{16,0},{24,8},{1,17},{9,25},{17,1},{25,9},{2,18},{10... | collective-permute-start | bytes 786440 | tf_op jit(solution)/shard_map/ppermute | solution.py:36
  148.9 334.7 %reduce-scatter.3.cloned.1.call-start = ((), (), s32[]{:S(2)}) async-start(), calls=%async_computation.2 | async-start | bytes 4718592 | tf_op jit(solution)/shard_map/reduce_scatter | solution.py:1186
  149.5 14.8 %collective-permute-start.29 = (bf16[128,1024]{1,0:T(8,128)(2,1)S(1)}, bf16[128,1024]{1,0:T(8,128)(2,1)S(1)}, u32[]{:S(2)}, u32[]{:S(2)}) collective-permute-start(bf16[128,1024]{1,0:T(8,128)(2,1)S(1)} %get-tuple-element.455.refs_0_), channel_id=1, source_target_pairs={{0,8},{8,0},{16,24},{24,16},{1,9},{9,1},{17,25},{25,17},{2,10},{10... | collective-permute-start | bytes 786440 | tf_op jit(solution)/shard_map/ppermute | solution.py:36
  156.6 14.5 %collective-permute-start.27 = (bf16[128,1024]{1,0:T(8,128)(2,1)S(1)}, bf16[128,1024]{1,0:T(8,128)(2,1)S(1)}, u32[]{:S(2)}, u32[]{:S(2)}) collective-permute-start(bf16[128,1024]{1,0:T(8,128)(2,1)S(1)} %shard_map.402.refs_10_), channel_id=1, source_target_pairs={{0,16},{8,24},{16,0},{24,8},{1,17},{9,25},{17,1},{25,9},{2,18},{10... | collective-permute-start | bytes 786440 | tf_op jit(solution)/shard_map/ppermute | solution.py:36
  188.9 16.6 %collective-permute-start.39 = (bf16[256,1024]{1,0:T(8,128)(2,1)S(1)}, bf16[256,1024]{1,0:T(8,128)(2,1)S(1)}, u32[]{:S(2)}, u32[]{:S(2)}) collective-permute-start(bf16[256,1024]{1,0:T(8,128)(2,1)S(1)} %get-tuple-element.250), channel_id=1, source_target_pairs={{0,8},{8,0},{16,24},{24,16},{1,9},{9,1},{17,25},{25,17},{2,10},{10... | collective-permute-start | bytes 1572872 | tf_op jit(solution)/shard_map/ppermute | solution.py:36
  217.1 19.0 %collective-permute-start.43 = (bf16[128,1024]{1,0:T(8,128)(2,1)S(1)}, bf16[128,1024]{1,0:T(8,128)(2,1)S(1)}, u32[]{:S(2)}, u32[]{:S(2)}) collective-permute-start(bf16[128,1024]{1,0:T(8,128)(2,1)S(1)} %get-tuple-element.262.refs_0_), channel_id=1, source_target_pairs={{0,8},{8,0},{16,24},{24,16},{1,9},{9,1},{17,25},{25,17},{2,10},{10... | collective-permute-start | bytes 786440 | tf_op jit(solution)/shard_map/ppermute | solution.py:36
  218.2 15.7 %collective-permute-start.46 = (bf16[128,1024]{1,0:T(8,128)(2,1)S(1)}, bf16[128,1024]{1,0:T(8,128)(2,1)S(1)}, u32[]{:S(2)}, u32[]{:S(2)}) collective-permute-start(bf16[128,1024]{1,0:T(8,128)(2,1)S(1)} %shard_map.414.refs_5_), channel_id=1, source_target_pairs={{0,16},{8,24},{16,0},{24,8},{1,17},{9,25},{17,1},{25,9},{2,18},{10... | collective-permute-start | bytes 786440 | tf_op jit(solution)/shard_map/ppermute | solution.py:36
  224.5 15.2 %collective-permute-start.49 = (bf16[128,1024]{1,0:T(8,128)(2,1)}, bf16[128,1024]{1,0:T(8,128)(2,1)}, u32[]{:S(2)}, u32[]{:S(2)}) collective-permute-start(bf16[128,1024]{1,0:T(8,128)(2,1)} %get-tuple-element.272.refs_0_), channel_id=1, source_target_pairs={{0,16},{8,24},{16,0},{24,8},{1,17},{9,25},{17,1},{25,9},{2,18},{10... | collective-permute-start | bytes 786440 | tf_op jit(solution)/shard_map/ppermute | solution.py:36
  224.9 28.5 %collective-permute-start.50 = (bf16[128,1024]{1,0:T(8,128)(2,1)}, bf16[128,1024]{1,0:T(8,128)(2,1)}, u32[]{:S(2)}, u32[]{:S(2)}) collective-permute-start(bf16[128,1024]{1,0:T(8,128)(2,1)} %get-tuple-element.272.refs_0_), channel_id=1, source_target_pairs={{0,8},{8,0},{16,24},{24,16},{1,9},{9,1},{17,25},{25,17},{2,10},{10... | collective-permute-start | bytes 786440 | tf_op jit(solution)/shard_map/ppermute | solution.py:36
  235.7 23.7 %collective-permute-start.54 = (bf16[128,1024]{1,0:T(8,128)(2,1)S(1)}, bf16[128,1024]{1,0:T(8,128)(2,1)}, u32[]{:S(2)}, u32[]{:S(2)}) collective-permute-start(bf16[128,1024]{1,0:T(8,128)(2,1)S(1)} %get-tuple-element.276.refs_0_), channel_id=1, source_target_pairs={{0,16},{8,24},{16,0},{24,8},{1,17},{9,25},{17,1},{25,9},{2,18},{10... | collective-permute-start | bytes 786440 | tf_op jit(solution)/shard_map/ppermute | solution.py:36
  236.8 23.2 %collective-permute-start.55 = (bf16[128,1024]{1,0:T(8,128)(2,1)S(1)}, bf16[128,1024]{1,0:T(8,128)(2,1)}, u32[]{:S(2)}, u32[]{:S(2)}) collective-permute-start(bf16[128,1024]{1,0:T(8,128)(2,1)S(1)} %get-tuple-element.276.refs_0_), channel_id=1, source_target_pairs={{0,8},{8,0},{16,24},{24,16},{1,9},{9,1},{17,25},{25,17},{2,10},{10... | collective-permute-start | bytes 786440 | tf_op jit(solution)/shard_map/ppermute | solution.py:36
  269.5 18.4 %collective-permute-start.61 = (bf16[128,1024]{1,0:T(8,128)(2,1)S(1)}, bf16[128,1024]{1,0:T(8,128)(2,1)S(1)}, u32[]{:S(2)}, u32[]{:S(2)}) collective-permute-start(bf16[128,1024]{1,0:T(8,128)(2,1)S(1)} %get-tuple-element.284.refs_0_), channel_id=1, source_target_pairs={{0,8},{8,0},{16,24},{24,16},{1,9},{9,1},{17,25},{25,17},{2,10},{10... | collective-permute-start | bytes 786440 | tf_op jit(solution)/shard_map/ppermute | solution.py:36
  270.3 16.0 %collective-permute-start.59 = (bf16[128,1024]{1,0:T(8,128)(2,1)S(1)}, bf16[128,1024]{1,0:T(8,128)(2,1)S(1)}, u32[]{:S(2)}, u32[]{:S(2)}) collective-permute-start(bf16[128,1024]{1,0:T(8,128)(2,1)S(1)} %shard_map.423.refs_6_), channel_id=1, source_target_pairs={{0,16},{8,24},{16,0},{24,8},{1,17},{9,25},{17,1},{25,9},{2,18},{10... | collective-permute-start | bytes 786440 | tf_op jit(solution)/shard_map/ppermute | solution.py:36
  276.6 18.4 %collective-permute-start.64 = (bf16[128,1024]{1,0:T(8,128)(2,1)S(1)}, bf16[128,1024]{1,0:T(8,128)(2,1)S(1)}, u32[]{:S(2)}, u32[]{:S(2)}) collective-permute-start(bf16[128,1024]{1,0:T(8,128)(2,1)S(1)} %get-tuple-element.289.refs_0_), channel_id=1, source_target_pairs={{0,16},{8,24},{16,0},{24,8},{1,17},{9,25},{17,1},{25,9},{2,18},{10... | collective-permute-start | bytes 786440 | tf_op jit(solution)/shard_map/ppermute | solution.py:36
  277.0 20.5 %collective-permute-start.65 = (bf16[128,1024]{1,0:T(8,128)(2,1)S(1)}, bf16[128,1024]{1,0:T(8,128)(2,1)S(1)}, u32[]{:S(2)}, u32[]{:S(2)}) collective-permute-start(bf16[128,1024]{1,0:T(8,128)(2,1)S(1)} %get-tuple-element.289.refs_0_), channel_id=1, source_target_pairs={{0,8},{8,0},{16,24},{24,16},{1,9},{9,1},{17,25},{25,17},{2,10},{10... | collective-permute-start | bytes 786440 | tf_op jit(solution)/shard_map/ppermute | solution.py:36
  287.9 17.1 %collective-permute-start.70 = (bf16[128,1024]{1,0:T(8,128)(2,1)S(1)}, bf16[128,1024]{1,0:T(8,128)(2,1)S(1)}, u32[]{:S(2)}, u32[]{:S(2)}) collective-permute-start(bf16[128,1024]{1,0:T(8,128)(2,1)S(1)} %get-tuple-element.295.refs_0_), channel_id=1, source_target_pairs={{0,8},{8,0},{16,24},{24,16},{1,9},{9,1},{17,25},{25,17},{2,10},{10... | collective-permute-start | bytes 786440 | tf_op jit(solution)/shard_map/ppermute | solution.py:36
  299.9 16.2 %collective-permute-start.68 = (bf16[256,1024]{1,0:T(8,128)(2,1)S(1)}, bf16[256,1024]{1,0:T(8,128)(2,1)S(1)}, u32[]{:S(2)}, u32[]{:S(2)}) collective-permute-start(bf16[256,1024]{1,0:T(8,128)(2,1)S(1)} %get-tuple-element.294), channel_id=1, source_target_pairs={{0,8},{8,0},{16,24},{24,16},{1,9},{9,1},{17,25},{25,17},{2,10},{10... | collective-permute-start | bytes 1572872 | tf_op jit(solution)/shard_map/ppermute | solution.py:36
  304.0 14.8 %collective-permute-start.67 = (bf16[128,1024]{1,0:T(8,128)(2,1)}, bf16[128,1024]{1,0:T(8,128)(2,1)}, u32[]{:S(2)}, u32[]{:S(2)}) collective-permute-start(bf16[128,1024]{1,0:T(8,128)(2,1)} %shard_map.428.refs_6_), channel_id=1, source_target_pairs={{0,16},{8,24},{16,0},{24,8},{1,17},{9,25},{17,1},{25,9},{2,18},{10... | collective-permute-start | bytes 786440 | tf_op jit(solution)/shard_map/ppermute | solution.py:36
  316.0 193.7 %reduce-scatter.5.cloned.1.call-start = ((), (), s32[]{:S(2)}) async-start(), calls=%async_computation.3 | async-start | bytes 2727936 | tf_op jit(solution)/shard_map/reduce_scatter | solution.py:1269
  321.5 48.8 %collective-permute-start.73 = (bf16[128,1024]{1,0:T(8,128)(2,1)S(1)}, bf16[128,1024]{1,0:T(8,128)(2,1)S(1)}, u32[]{:S(2)}, u32[]{:S(2)}) collective-permute-start(bf16[128,1024]{1,0:T(8,128)(2,1)S(1)} %get-tuple-element.299.refs_2_), channel_id=1, source_target_pairs={{0,8},{8,0},{16,24},{24,16},{1,9},{9,1},{17,25},{25,17},{2,10},{10... | collective-permute-start | bytes 786440 | tf_op jit(solution)/shard_map/ppermute | solution.py:36
  322.2 15.1 %collective-permute-start.76 = (bf16[128,1024]{1,0:T(8,128)(2,1)S(1)}, bf16[128,1024]{1,0:T(8,128)(2,1)S(1)}, u32[]{:S(2)}, u32[]{:S(2)}) collective-permute-start(bf16[128,1024]{1,0:T(8,128)(2,1)S(1)} %shard_map.432.refs_7_), channel_id=1, source_target_pairs={{0,16},{8,24},{16,0},{24,8},{1,17},{9,25},{17,1},{25,9},{2,18},{10... | collective-permute-start | bytes 786440 | tf_op jit(solution)/shard_map/ppermute | solution.py:36
  326.6 16.3 %collective-permute-start.81 = (bf16[128,1024]{1,0:T(8,128)(2,1)S(1)}, bf16[128,1024]{1,0:T(8,128)(2,1)S(1)}, u32[]{:S(2)}, u32[]{:S(2)}) collective-permute-start(bf16[128,1024]{1,0:T(8,128)(2,1)S(1)} %get-tuple-element.310.refs_2_), channel_id=1, source_target_pairs={{0,16},{8,24},{16,0},{24,8},{1,17},{9,25},{17,1},{25,9},{2,18},{10... | collective-permute-start | bytes 786440 | tf_op jit(solution)/shard_map/ppermute | solution.py:36
  327.0 17.6 %collective-permute-start.82 = (bf16[128,1024]{1,0:T(8,128)(2,1)S(1)}, bf16[128,1024]{1,0:T(8,128)(2,1)S(1)}, u32[]{:S(2)}, u32[]{:S(2)}) collective-permute-start(bf16[128,1024]{1,0:T(8,128)(2,1)S(1)} %get-tuple-element.310.refs_2_), channel_id=1, source_target_pairs={{0,8},{8,0},{16,24},{24,16},{1,9},{9,1},{17,25},{25,17},{2,10},{10... | collective-permute-start | bytes 786440 | tf_op jit(solution)/shard_map/ppermute | solution.py:36
  331.7 38.5 %collective-permute-start.74 = (bf16[128,1024]{1,0:T(8,128)(2,1)S(1)}, bf16[128,1024]{1,0:T(8,128)(2,1)S(1)}, u32[]{:S(2)}, u32[]{:S(2)}) collective-permute-start(bf16[128,1024]{1,0:T(8,128)(2,1)S(1)} %collective-permute-done.72.refs_3_), channel_id=1, source_target_pairs={{0,8},{8,0},{16,24},{24,16},{1,9},{9,1},{17,25},{25,17},{2,10},{10... | collective-permute-start | bytes 786440 | tf_op jit(solution)/shard_map/ppermute | solution.py:36
  337.9 19.7 %collective-permute-start.78 = (bf16[128,1024]{1,0:T(8,128)(2,1)S(1)}, bf16[128,1024]{1,0:T(8,128)(2,1)S(1)}, u32[]{:S(2)}, u32[]{:S(2)}) collective-permute-start(bf16[128,1024]{1,0:T(8,128)(2,1)S(1)} %get-tuple-element.308.refs_2_), channel_id=1, source_target_pairs={{0,16},{8,24},{16,0},{24,8},{1,17},{9,25},{17,1},{25,9},{2,18},{10... | collective-permute-start | bytes 786440 | tf_op jit(solution)/shard_map/ppermute | solution.py:36
  393.6 20.8 %collective-permute-start.90 = (bf16[256,1024]{1,0:T(8,128)(2,1)S(1)}, bf16[256,1024]{1,0:T(8,128)(2,1)S(1)}, u32[]{:S(2)}, u32[]{:S(2)}) collective-permute-start(bf16[256,1024]{1,0:T(8,128)(2,1)S(1)} %get-tuple-element.341), channel_id=1, source_target_pairs={{0,8},{8,0},{16,24},{24,16},{1,9},{9,1},{17,25},{25,17},{2,10},{10... | collective-permute-start | bytes 1572872 | tf_op jit(solution)/shard_map/ppermute | solution.py:36
  394.4 27.5 %collective-permute-start.92 = (bf16[128,1024]{1,0:T(8,128)(2,1)S(1)}, bf16[128,1024]{1,0:T(8,128)(2,1)S(1)}, u32[]{:S(2)}, u32[]{:S(2)}) collective-permute-start(bf16[128,1024]{1,0:T(8,128)(2,1)S(1)} %shard_map.442.refs_7_), channel_id=1, source_target_pairs={{0,16},{8,24},{16,0},{24,8},{1,17},{9,25},{17,1},{25,9},{2,18},{10... | collective-permute-start | bytes 786440 | tf_op jit(solution)/shard_map/ppermute | solution.py:36
  444.9 17.0 %collective-permute-start.103 = (bf16[256,1024]{1,0:T(8,128)(2,1)S(1)}, bf16[256,1024]{1,0:T(8,128)(2,1)S(1)}, u32[]{:S(2)}, u32[]{:S(2)}) collective-permute-start(bf16[256,1024]{1,0:T(8,128)(2,1)S(1)} %get-tuple-element.355.refs_8_), channel_id=1, source_target_pairs={{0,2},{2,4},{4,6},{6,7},{7,5},{5,3},{3,1},{1,0},{8,10},{10,12},{12... | collective-permute-start | bytes 1572872 | tf_op jit(solution)/shard_map/ppermute | solution.py:145
  445.4 16.6 %collective-permute-start.104 = (bf16[256,1024]{1,0:T(8,128)(2,1)S(1)}, bf16[256,1024]{1,0:T(8,128)(2,1)S(1)}, u32[]{:S(2)}, u32[]{:S(2)}) collective-permute-start(bf16[256,1024]{1,0:T(8,128)(2,1)S(1)} %get-tuple-element.368), channel_id=1, source_target_pairs={{0,1},{2,0},{4,2},{6,4},{7,6},{5,7},{3,5},{1,3},{8,9},{10,8},{12,1... | collective-permute-start | bytes 1572872 | tf_op jit(solution)/shard_map/ppermute | solution.py:145
  463.6 20.0 %collective-permute-start.111 = (bf16[256,1024]{1,0:T(8,128)(2,1)}, bf16[256,1024]{1,0:T(8,128)(2,1)S(1)}, u32[]{:S(2)}, u32[]{:S(2)}) collective-permute-start(bf16[256,1024]{1,0:T(8,128)(2,1)} %get-tuple-element.369.refs_4_), channel_id=1, source_target_pairs={{0,2},{2,4},{4,6},{6,7},{7,5},{5,3},{3,1},{1,0},{8,10},{10,12},{12... | collective-permute-start | bytes 1572872 | tf_op jit(solution)/shard_map/ppermute | solution.py:145
  463.6 20.1 %collective-permute-start.112 = (bf16[256,1024]{1,0:T(8,128)(2,1)S(1)}, bf16[256,1024]{1,0:T(8,128)(2,1)S(1)}, u32[]{:S(2)}, u32[]{:S(2)}) collective-permute-start(bf16[256,1024]{1,0:T(8,128)(2,1)S(1)} %get-tuple-element.384), channel_id=1, source_target_pairs={{0,1},{2,0},{4,2},{6,4},{7,6},{5,7},{3,5},{1,3},{8,9},{10,8},{12,1... | collective-permute-start | bytes 1572872 | tf_op jit(solution)/shard_map/ppermute | solution.py:145
  482.1 27.6 %collective-permute-start.105 = (bf16[128,1024]{1,0:T(8,128)(2,1)}, bf16[128,1024]{1,0:T(8,128)(2,1)}, u32[]{:S(2)}, u32[]{:S(2)}) collective-permute-start(bf16[128,1024]{1,0:T(8,128)(2,1)} %shard_map.456.refs_5_), channel_id=1, source_target_pairs={{0,16},{8,24},{16,0},{24,8},{1,17},{9,25},{17,1},{25,9},{2,18},{10... | collective-permute-start | bytes 786440 | tf_op jit(solution)/shard_map/ppermute | solution.py:36
  483.6 17.2 %collective-permute-start.106 = (bf16[256,1024]{1,0:T(8,128)(2,1)}, bf16[256,1024]{1,0:T(8,128)(2,1)S(1)}, u32[]{:S(2)}, u32[]{:S(2)}) collective-permute-start(bf16[256,1024]{1,0:T(8,128)(2,1)} %bitcast.218), channel_id=1, source_target_pairs={{0,16},{8,24},{16,0},{24,8},{1,17},{9,25},{17,1},{25,9},{2,18},{10... | collective-permute-start | bytes 1572872 | tf_op jit(solution)/shard_map/ppermute | solution.py:36
  488.6 33.6 %collective-permute-start.117 = (bf16[256,1024]{1,0:T(8,128)(2,1)}, bf16[256,1024]{1,0:T(8,128)(2,1)S(1)}, u32[]{:S(2)}, u32[]{:S(2)}) collective-permute-start(bf16[256,1024]{1,0:T(8,128)(2,1)} %get-tuple-element.385.refs_6_), channel_id=1, source_target_pairs={{0,2},{2,4},{4,6},{6,7},{7,5},{5,3},{3,1},{1,0},{8,10},{10,12},{12... | collective-permute-start | bytes 1572872 | tf_op jit(solution)/shard_map/ppermute | solution.py:145
  488.7 34.9 %collective-permute-start.118 = (bf16[256,1024]{1,0:T(8,128)(2,1)S(1)}, bf16[256,1024]{1,0:T(8,128)(2,1)S(1)}, u32[]{:S(2)}, u32[]{:S(2)}) collective-permute-start(bf16[256,1024]{1,0:T(8,128)(2,1)S(1)} %get-tuple-element.391), channel_id=1, source_target_pairs={{0,1},{2,0},{4,2},{6,4},{7,6},{5,7},{3,5},{1,3},{8,9},{10,8},{12,1... | collective-permute-start | bytes 1572872 | tf_op jit(solution)/shard_map/ppermute | solution.py:145
  490.8 14.5 %collective-permute-start.107 = (bf16[256,1024]{1,0:T(8,128)(2,1)S(1)}, bf16[256,1024]{1,0:T(8,128)(2,1)S(1)}, u32[]{:S(2)}, u32[]{:S(2)}) collective-permute-start(bf16[256,1024]{1,0:T(8,128)(2,1)S(1)} %bitcast.219), channel_id=1, source_target_pairs={{0,8},{8,0},{16,24},{24,16},{1,9},{9,1},{17,25},{25,17},{2,10},{10... | collective-permute-start | bytes 1572872 | tf_op jit(solution)/shard_map/ppermute | solution.py:36
  516.8 15.4 %collective-permute-start.124 = (bf16[592,256]{1,0:T(8,128)(2,1)S(1)}, bf16[592,256]{1,0:T(8,128)(2,1)S(1)}, u32[]{:S(2)}, u32[]{:S(2)}) collective-permute-start(bf16[592,256]{1,0:T(8,128)(2,1)S(1)} %bitcast.222), channel_id=1, source_target_pairs={{0,8},{8,0},{16,24},{24,16},{1,9},{9,1},{17,25},{25,17},{2,10},{10... | collective-permute-start | bytes 909320 | tf_op jit(solution)/shard_map/ppermute | solution.py:36
  518.1 15.5 %collective-permute-start.125 = (bf16[592,256]{1,0:T(8,128)(2,1)S(1)}, bf16[592,256]{1,0:T(8,128)(2,1)S(1)}, u32[]{:S(2)}, u32[]{:S(2)}) collective-permute-start(bf16[592,256]{1,0:T(8,128)(2,1)S(1)} %collective-permute-done.123.refs_2_), channel_id=1, source_target_pairs={{0,8},{8,0},{16,24},{24,16},{1,9},{9,1},{17,25},{25,17},{2,10},{10... | collective-permute-start | bytes 909320 | tf_op jit(solution)/shard_map/ppermute | solution.py:36
  530.2 21.1 %collective-permute-start.130 = (bf16[256,1024]{1,0:T(8,128)(2,1)S(1)}, bf16[256,1024]{1,0:T(8,128)(2,1)S(1)}, u32[]{:S(2)}, u32[]{:S(2)}) collective-permute-start(bf16[256,1024]{1,0:T(8,128)(2,1)S(1)} %shard_map.462.refs_6_.refs_1_), channel_id=1, source_target_pairs={{0,8},{8,0},{16,24},{24,16},{1,9},{9,1},{17,25},{25,17},{2,10},{10... | collective-permute-start | bytes 1572872 | tf_op jit(solution)/shard_map/ppermute | solution.py:36
  (280 other events, 1920.4 us)
Sparse Core Ops, SparseCore 0:
  41.9 83.3 all-gather.4
  149.0 72.6 all-gather.6
  316.2 87.4 reduce-scatter.2
  407.5 81.9 reduce-scatter.4

commit v4 on v3

--- a/solution.py
+++ b/solution.py
@@ -126,6 +126,35 @@
     return [lax.dynamic_index_in_dim(stacked, here ^ a, 0, keepdims=False) for a in range(4)]
 
 
+class Turn:
+    def __init__(self, chain, devices, array, by_rows):
+        self.devices, self.by_rows = devices, by_rows
+        size = array.shape[0 if by_rows else 1] // STREAMS
+        self.size = size
+
+        def kernel(devices_ref, array_ref, *part_refs):
+            for i in range(STREAMS):
+                place = pl.ds(pl.multiple_of(devices_ref[i] * size, size), size)
+                part_refs[i][...] = (array_ref[place, :] if by_rows else array_ref[:, place]).astype(BF)
+
+        own, *others = chain(kernel, [((size, size), BF)] * STREAMS, [array], scalars=[devices])
+        self.parts = [own] + [swap(part, bit) for part, bit in zip(others, XOR[1:])]
+
+    def join(self, chain, after=()):
+        size, by_rows = self.size, self.by_rows
+
+        def kernel(devices_ref, *refs):
+            for i in range(STREAMS):
+                place = pl.ds(pl.multiple_of(devices_ref[i] * size, size), size)
+                if by_rows:
+                    refs[-1][:, place] = refs[i][...]
+                else:
+                    refs[-1][place, :] = refs[i][...]
+
+        shape = (size, STREAMS * size) if by_rows else (STREAMS * size, size)
+        return chain(kernel, [(shape, BF)], self.parts, scalars=[self.devices], after=after)[0]
+
+
 def ring_order(n):
     return list(range(0, n, 2)) + list(range(n - 1, 0, -2))
 
@@ -194,6 +223,31 @@
         scalars=[index],
         away=[piece for _, _, piece in pieces],
         scratch=[pltpu.SemaphoreType.DMA((len(moves),))],
+        after=after,
+    )
+
+
+def unpack(chain, packed, regions, shapes, after=()):
+    n = packed.shape[0]
+
+    def kernel(packed_ref, *refs):
+        copy_all(
+            [
+                (
+                    packed_ref.at[:, r0:r1, c0:c1],
+                    refs[which].at[:, row : row + r1 - r0, col : col + c1 - c0],
+                )
+                for r0, r1, c0, c1, which, row, col in regions
+            ],
+            refs[-1],
+        )
+
+    return chain(
+        kernel,
+        [((n,) + shape, BF) for shape in shapes],
+        [],
+        away=[packed],
+        scratch=[pltpu.SemaphoreType.DMA((len(regions),))],
         after=after,
     )
 
@@ -865,13 +919,17 @@
         copy_all(moves, sems)
         if rel is None:
             lines = []
+            ffn_share = STREAMS * share
+            last = targets[0][:, 2 * ffn_share :].astype(F32)
+            last = jnp.concatenate([last, jnp.zeros((1, share - last.shape[1]), F32)], axis=1)
             for layer in range(2):
-                ffn_ref, bias_ref, gain_ref, shift_ref, last_ref = targets[5 * layer : 5 * layer + 5]
+                bias_ref, gain_ref, shift_ref = targets[3 * layer + 1 : 3 * layer + 4]
                 left = jnp.concatenate([r[...].astype(F32) for r in (bias_ref, gain_ref, shift_ref)], axis=0)
-                right = [ffn_ref[:, i * share : (i + 1) * share].astype(F32) for i in range(STREAMS)]
-                last = last_ref[...].astype(F32)
-                right.append(jnp.concatenate([last, jnp.zeros((1, share - last.shape[1]), F32)], axis=1))
-                right.append(jnp.zeros((3, share), F32))
+                first = layer * ffn_share
+                right = [
+                    targets[0][:, first + i * share : first + (i + 1) * share].astype(F32) for i in range(STREAMS)
+                ]
+                right += [last, jnp.zeros((3, share), F32)]
                 lines.append(jnp.concatenate([left, jnp.concatenate(right, axis=0)], axis=1))
             lines = jnp.concatenate(lines, axis=0)
             packed_ref[fixed:, : 2 * share] = lines.astype(BF)
@@ -1016,15 +1074,9 @@
     ring_index = jnp.stack([ring_member(place - o, n) for o in range(n)]).astype(jnp.int32)
     tables = rel_tables(rel_table, total)
 
-    smalls = (
-        enc_ffn_bias[None], enc_bias, enc_gain, enc_shift, dec_rel_bias[None],
-        dec_ffn_bias[None], dec_bias, dec_gain, dec_shift, dec_rel_bias[None],
-    )
+    vectors = jnp.concatenate([enc_ffn_bias, dec_ffn_bias, dec_rel_bias])[None]
+    smalls = (vectors, enc_bias, enc_gain, enc_shift, dec_bias, dec_gain, dec_shift)
     small_rows = 16
-
-    def pins(pieces, stage):
-        k = stage * (n // 2) // 4
-        return [piece for _, _, piece in pieces[2 * k - 1 : 2 * k + 1]]
 
     def attention_regions(extra):
         regions = [(i * share, (i + 1) * share, 0, quarter, 0, 0, i * quarter) for i in range(3)]
@@ -1033,21 +1085,15 @@
 
     shapes = [(share, 3 * quarter), (share, quarter)]
 
+    def gather_shares(packed):
+        return lax.all_gather(packed, "dp", axis=0, tiled=False)
+
+    enc_ffn = gather_shares(pack_ffn(chain, devices, here, enc_ffn_in, enc_ffn_out, n))
     enc_pieces = ring_pieces(pack_attention(chain, devices, enc_qkv, enc_out, smalls=smalls), n)
     enc_quads = gather_rows(enc_input)
     pred_quads = [gather_rows(pred_input[i]) for i in range(2)]
-    def ffn_gather(matrix_in, matrix_out, after=()):
-        packed = pack_ffn(chain, devices, here, matrix_in, matrix_out, n, after)
-        return lax.all_gather(packed, "dp", axis=0, tiled=False)
-
-    enc_ffn = ffn_gather(enc_ffn_in, enc_ffn_out, pins(enc_pieces, 1))
-    dec_pieces = ring_pieces(pack_attention(chain, devices, dec_qkv, dec_out, rel=dec_rel, after=pins(enc_pieces, 4)), n)
-    dec_ffn = ffn_gather(dec_ffn_in, dec_ffn_out)
-
-    def turn_out(columns):
-        blocks = columns.reshape(dim, quarter)
-        sent = [lax.dynamic_slice_in_dim(blocks, (here ^ j) * quarter, quarter, axis=0) for j in XOR]
-        return jnp.concatenate(by_absolute(turn_blocks(sent), here), axis=1)
+    dec_packed = gather_shares(pack_attention(chain, devices, dec_qkv, dec_out, rel=dec_rel))
+    dec_ffn = gather_shares(pack_ffn(chain, devices, here, dec_ffn_in, dec_ffn_out, n))
 
     def turn_out_back(grad):
         sent = [lax.dynamic_slice_in_dim(grad, (here ^ j) * quarter, quarter, axis=1) for j in XOR]
@@ -1060,6 +1106,7 @@
         attention_regions([(fixed, fixed + small_rows, 0, quarter, 2, 0, 0)]),
         shapes + [(small_rows, quarter)],
         n,
+        after=[quads[1] for quads in pred_quads],
     )
 
     small_all = small_all.astype(F32)
@@ -1067,7 +1114,7 @@
     def attention_layer(number, wqkv, wout):
         w = Layer()
         w.qkv = wqkv.reshape(dim, 3 * quarter)
-        w.out = turn_out(wout)
+        w.turn = Turn(chain, devices, wout.reshape(dim, quarter), True)
         block = small_all[:, 8 * number : 8 * number + 8]
         w.ffn_bias = lax.dynamic_slice_in_dim(block, here, 1, axis=1)[:, 0, share : 2 * share].reshape(1, -1)
         w.small = jnp.transpose(block[:, :, :share], (1, 0, 2)).reshape(8, dim)
@@ -1078,18 +1125,21 @@
     enc = attention_layer(0, enc_wqkv, enc_wout)
     enc_all, enc_heads = project(chain, enc_quads, enc, False)
     enc_context, enc_lse, _ = attention_forward(chain, meta, enc_heads)
+    enc.out = enc.turn.join(chain)
     scatter = Scatter(out_project(chain, enc_context, enc))
-    scatter.middle(chain, pins(dec_pieces, 1))
-    enc_unit0, enc_inverse0, low = norm_first(chain, enc_input, scatter.parts(), enc, after=pins(dec_pieces, 2))
+    scatter.middle(chain)
+    enc_unit0, enc_inverse0, low = norm_first(chain, enc_input, scatter.parts(), enc)
     quads = gather_rows(low)
     enc.ffn = enc_ffn
-    *parts, enc_hidden, enc_active, enc_slope = ffn_forward(chain, quads, enc, after=pins(dec_pieces, 3))
+    *parts, enc_hidden, enc_active, enc_slope = ffn_forward(chain, quads, enc)
     scatter = Scatter(parts)
-    scatter.middle(chain, pins(dec_pieces, 4))
-    dec_wqkv, dec_wout, dec_wrel = assemble(
+    scatter.middle(chain)
+    enc_unit1, enc_inverse1, main_rows, main_low = norm_second(chain, enc_unit0, scatter.parts(), enc)
+    main_quads = gather_rows(main_low)
+
+    dec_wqkv, dec_wout, dec_wrel = unpack(
         chain,
-        dec_pieces,
-        ring_index,
+        dec_packed,
         attention_regions(
             [
                 (fixed, fixed + half, 0, rel_part, 2, 0, 0),
@@ -1097,29 +1147,23 @@
             ]
         ),
         shapes + [(share, rel_part)],
-        n,
     )
     dec = attention_layer(1, dec_wqkv, dec_wout)
     dec.rel = dec_wrel.reshape(dim, rel_part)
     dec.rel_bias = own_columns(small_all[:, 12, share : share + rel_all // n].reshape(1, -1), here)
     alls, heads, rels = [None] * 3, [None] * 3, [None] * 3
-
-    def project_stream(i, quads):
+    stream_inputs = (main_rows, pred_input[0], pred_input[1])
+    for i, quads in ((0, main_quads), (1, pred_quads[0]), (2, pred_quads[1])):
         alls[i], heads[i], rels[i] = project(chain, quads, dec, True)
-
-    project_stream(1, pred_quads[0])
-    project_stream(2, pred_quads[1])
-    enc_unit1, enc_inverse1, main_rows, main_low = norm_second(chain, enc_unit0, scatter.parts(), enc)
-    main_quads = gather_rows(main_low)
-
-    stream_inputs = (main_rows, pred_input[0], pred_input[1])
-    project_stream(0, main_quads)
     contexts, lses = [None] * 3, [None] * 3
 
     def attend(i, after=()):
         contexts[i], lses[i], parts = attention_forward(
-            chain, meta, heads[i], None if i == 0 else heads[0], rels[i], tables, dec.out, after
+            chain, meta, heads[i], heads[0] if i else None, rels[i], tables, dec.out if i else None, after
         )
+        if i == 0:
+            dec.out = dec.turn.join(chain)
+            parts = out_project(chain, contexts[i], dec)
         return Scatter(parts)
 
     def staged(work, finish):
@@ -1279,33 +1323,34 @@
     scatter = Scatter(parts)
     pred_grads = [input_gradient(chain, backs[1][0], pred_scatters[0].parts())]
     scatter.middle(chain)
-    pred_grads.append(input_gradient(chain, backs[2][0], pred_scatters[1].parts()))
     enc_ffn_ring = ffn_sum([(enc_hidden, enc_active, enc_inner, enc_branch)])
     advance(enc_ffn_ring, 1)
-    dec_ffn_blocks = gather_rows(dec_ffn_total)
+    pred_grads.append(input_gradient(chain, backs[2][0], pred_scatters[1].parts()))
     residual, attended_low, enc_tiny0 = norm_first_back(
         chain, enc_sum_grad, scatter.parts(), enc_unit0, enc_inverse0, enc
     )
     quads = gather_rows(attended_low)
+    dec_ffn_blocks = gather_rows(dec_ffn_total)
     advance(enc_ffn_ring, 2)
-    dq, dk, dv, attended = attention_backward(chain, meta, enc_heads, quads, enc.out, enc_lse)
+    enc_out_part = dot_tn(enc_context, jnp.concatenate(quads, axis=0))
+    dq, dk, dv, _ = attention_backward(chain, meta, enc_heads, quads, enc.out, enc_lse)
     *parts, enc_dheads, enc_head_sum = project_back(chain, dq, [dk], [dv], None, enc)
     scatter = Scatter(parts)
-    advance(enc_ffn_ring, 3)
     enc_ring = attention_ring(
         dot_tn(enc_all, enc_dheads),
-        dot_tn(enc_context, attended),
+        enc_out_part,
         [small_pack(enc_inner_sum, enc_tiny0, enc_tiny1, enc_head_sum)],
     )
     advance(enc_ring, 1)
     scatter.middle(chain)
-    advance(enc_ffn_ring, 4)
+    advance(enc_ffn_ring, 3)
     advance(enc_ring, 2)
     dec_in_grad, dec_back_grad = place_ffn(chain, devices, here, dec_ffn_blocks, share, n)
     enc_input_grad = input_gradient(chain, residual, scatter.parts())
+    advance(enc_ffn_ring, 4)
     advance(enc_ring, 3)
+    dec_blocks = gather_rows(dec_total)
     enc_ffn_blocks = gather_rows(advance(enc_ffn_ring, 5))
-    dec_blocks = gather_rows(dec_total)
     advance(enc_ring, 4)
     dec_results = place_attention(chain, devices, dec_blocks, share, ffn_part, rel_part)
     enc_blocks = gather_rows(advance(enc_ring, 5))

time: 575 us -> 552 us (0.960)
  starting transfers between devices: 132 us -> 122 us
  Pallas kernels: 163 us -> 156 us
    all_gather x2 -> x3, waiting for transfers between devices: 0.01 us -> 23.4 us  [gather_shares(): return lax.all_gather(packed, 'dp', axis=0, tiled=False)]
    ppermute x32 -> x24, waiting for transfers between devices: 62.7 us -> 40.8 us  [ring_step(): return lax.ppermute(values, 'dp', pairs)]
    pallas_call x77 -> x82, Pallas kernels: 163 us -> 156 us  [__call__(): pl.pallas_call(body, out_shape=[jax.ShapeDtypeStruct(shape, kind) for sha...]
    ppermute x32 -> x24, starting transfers between devices: 25.7 us -> 20.2 us  [ring_step(): return lax.ppermute(values, 'dp', pairs)]
    ppermute x100 -> x102, starting transfers between devices: 107 us -> 101 us  [swap(): lax.ppermute(values, 'stream', [(i, i ^ bit) for i in range(STREAMS)])]
    ppermute x100 -> x102, waiting for transfers between devices: 77.2 us -> 74.1 us  [swap(): lax.ppermute(values, 'stream', [(i, i ^ bit) for i in range(STREAMS)])]
    unnamed x392 -> x372, local copies, waits for them, and re-layouts: 66.3 us -> 67.3 us
  transfers between devices with their start and end apart: 136 -> 131, of which waited for: 40 -> 35; matrix products, arithmetic and copies ran while one was open for 8% -> 8% of each run, Pallas kernels for 28% -> 28%
where the time goes in v4:
time: 552 us; the launch traced here: 544 us
  Pallas kernels  156 us (28%)
  waiting for transfers between devices  138 us (25%)
  starting transfers between devices  122 us (22%)
  local copies, waits for them, and re-layouts  82.8 us (15%)
  matrix products  19.4 us (4%)
  between operations  17.5 us (3%)
  other arithmetic  7.58 us (1%)
    pallas_call x82, Pallas kernels, __call__(): pl.pallas_call(body, out_shape=[jax.ShapeDtypeStruct(shape, kind) for sha...  156 us
    ppermute x102, starting transfers between devices, swap(): lax.ppermute(values, 'stream', [(i, i ^ bit) for i in range(STREAMS)])  101 us
    ppermute x102, waiting for transfers between devices, swap(): lax.ppermute(values, 'stream', [(i, i ^ bit) for i in range(STREAMS)])  74.1 us
    unnamed x372, local copies, waits for them, and re-layouts  67.3 us
    ppermute x24, waiting for transfers between devices, ring_step(): return lax.ppermute(values, 'dp', pairs)  40.8 us
    all_gather x3, waiting for transfers between devices, gather_shares(): return lax.all_gather(packed, 'dp', axis=0, tiled=False)  23.4 us
    ppermute x24, starting transfers between devices, ring_step(): return lax.ppermute(values, 'dp', pairs)  20.2 us
    dot_general x19, matrix products, dot_tn(): lax.dot_general(a, b, (((0,), (0,)), ((), ())), preferred_element_type=F32)  19.4 us
  transfers between devices with their start and end apart: 131, of which 35 were waited for; matrix products, arithmetic and copies ran while one was open for 8% of the time, Pallas kernels for 28%

profile of v4, /device:TPU:1, one launch (start us, length us, event | category | flops | bytes accessed | tf_op | source)
XLA Modules:
  0.0 543.8 jit_solution(7351066835546824489)
XLA Ops:
  7.3 2.4 shard_map.391.refs_10_
  14.3 6.1 %collective-permute-done.4.refs_3_ = bf16[528,256]{1,0:T(8,128)(2,1)S(1)} collective-permute-done((bf16[528,256]{1,0:T(8,128)(2,1)S(1)}, bf16[528,256]{1,0:T(8,128)(2,1)S(1)}, u32[]{:S(2)}, u32[]{:S(2)}) %collective-permute-start.4) | collective-permute-done | bytes 270368 | tf_op jit(solution)/shard_map/ppermute | solution.py:174
  24.6 10.8 %collective-permute-done.6.refs_5_ = bf16[528,256]{1,0:T(8,128)(2,1)S(1)} collective-permute-done((bf16[528,256]{1,0:T(8,128)(2,1)S(1)}, bf16[528,256]{1,0:T(8,128)(2,1)S(1)}, u32[]{:S(2)}, u32[]{:S(2)}) %collective-permute-start.6) | collective-permute-done | bytes 270368 | tf_op jit(solution)/shard_map/ppermute | solution.py:174
  35.4 3.3 collective-permute-start.7
  41.0 9.3 %collective-permute-done.8.refs_7_ = bf16[528,256]{1,0:T(8,128)(2,1)S(1)} collective-permute-done((bf16[528,256]{1,0:T(8,128)(2,1)S(1)}, bf16[528,256]{1,0:T(8,128)(2,1)S(1)}, u32[]{:S(2)}, u32[]{:S(2)}) %collective-permute-start.8) | collective-permute-done | bytes 270368 | tf_op jit(solution)/shard_map/ppermute | solution.py:174
  53.1 2.4 shard_map.394.refs_12_
  60.9 2.7 shard_map.395
  68.9 4.7 shard_map.398
  81.8 6.3 %collective-permute-done.17.refs_3_ = bf16[128,1024]{1,0:T(8,128)(2,1)S(1)} collective-permute-done((bf16[128,1024]{1,0:T(8,128)(2,1)S(1)}, bf16[128,1024]{1,0:T(8,128)(2,1)S(1)}, u32[]{:S(2)}, u32[]{:S(2)}) %collective-permute-start.17) | collective-permute-done | bytes 262176 | tf_op jit(solution)/shard_map/ppermute | solution.py:36
  93.5 2.5 collective-permute-done.18.refs_1_
  102.4 4.3 shard_map.403
  119.1 4.8 collective-permute-done.22.refs_3_
  132.8 16.0 %all-gather.9.cloned.1.call-done = bf16[4608,256]{1,0:T(8,128)(2,1)} async-done(((bf16[576,256]{1,0:T(8,128)(2,1)}), bf16[4608,256]{1,0:T(8,128)(2,1)}) %all-gather.9.cloned.1.call-update) | async-done | bytes 2359312 | tf_op jit(solution)/shard_map/all_gather | solution.py:1089
  161.2 2.4 shard_map.410
  163.7 5.6 %shard_map.411 = (bf16[512,256]{1,0:T(8,128)(2,1)S(1)}, f32[512,128]{1,0:T(8,128)S(1)}) custom-call(s32[11]{0:T(128)S(1)} %stack.140.refs_0_, bf16[512,768]{1,0:T(8,128)(2,1)S(1)} %get-tuple-element.256.refs_1_.refs_2_.refs_8_, f32[512,128]{1,0:T(8,128)S(1)} %get-tuple-element.257.refs_2_.refs_8_, ...), custom_call_target="tpu_custom_call" | custom-call | flops 10000000000 | bytes 10000000 | tf_op jit(solution)/shard_map/pallas_call | solution.py:54
  171.7 7.3 %shard_map.414 = (bf16[512,256]{1,0:T(8,128)(2,1)S(1)}, f32[512,128]{1,0:T(8,128)S(1)}, f32[128,1024]{1,0:T(8,128)S(1)}, f32[128,1024]{1,0:T(8,128)S(1)}, bf16[256,1024]{1,0:T(8,128)(2,1)S(1)}) custom-call(s32[11]{0:T(128)S(1)} %stack.140.refs_0_, bf16[512,768]{1,0:T(8,128)(2,1)S(1)} %get-tuple-element.268.refs_1_, ...), custom_call_target="tpu_custom_call" | custom-call | flops 10000000000 | bytes 10000000 | tf_op jit(solution)/shard_map/pallas_call | solution.py:54
  181.6 7.2 %shard_map.416 = (bf16[512,256]{1,0:T(8,128)(2,1)S(1)}, f32[512,128]{1,0:T(8,128)S(1)}, f32[128,1024]{1,0:T(8,128)S(1)}, f32[128,1024]{1,0:T(8,128)S(1)}, bf16[256,1024]{1,0:T(8,128)(2,1)S(1)}) custom-call(s32[11]{0:T(128)S(1)} %stack.140.refs_0_, bf16[512,768]{1,0:T(8,128)(2,1)S(1)} %get-tuple-element.273.refs_1_, ...), custom_call_target="tpu_custom_call" | custom-call | flops 10000000000 | bytes 10000000 | tf_op jit(solution)/shard_map/pallas_call | solution.py:54
  192.8 4.4 collective-permute-done.41.refs_3_
  204.8 3.7 collective-permute-done.40.refs_3_
  216.1 7.4 %all-gather.11.cloned.1.call-done = bf16[2048,1024]{1,0:T(8,128)(2,1)} async-done(((bf16[256,1024]{1,0:T(8,128)(2,1)}), bf16[2048,1024]{1,0:T(8,128)(2,1)}) %all-gather.11.cloned.1.call-update) | async-done | bytes 4194320 | tf_op jit(solution)/shard_map/all_gather | solution.py:1089
  229.3 5.6 %shard_map.422 = (f32[128,1024]{1,0:T(8,128)S(1)}, f32[128,1024]{1,0:T(8,128)S(1)}, bf16[256,1024]{1,0:T(8,128)(2,1)S(1)}, bf16[512,1024]{1,0:T(8,128)(2,1)S(1)}...) custom-call(bf16[128,1024]{1,0:T(8,128)(2,1)S(1)} %get-tuple-element.277.refs_0_, ...), custom_call_target="tpu_custom_call" | custom-call | flops 10000000000 | bytes 10000000 | tf_op jit(solution)/shard_map/pallas_call | solution.py:54
  236.9 5.4 shard_map.423
  244.7 5.2 shard_map.425
  254.6 3.1 collective-permute-done.51.refs_3_
  265.4 3.6 collective-permute-done.53.refs_3_
  273.2 3.0 shard_map.431
  281.4 2.5 shard_map.432
  288.2 3.3 shard_map.434
  296.2 2.8 pad_maximum_fusion
  306.5 2.6 collective-permute-done.71.refs_3_
  316.3 4.1 collective-permute-done.70.refs_3_
  322.2 3.8 collective-permute-done.75.refs_3_
  328.8 10.6 %shard_map.440 = (bf16[512,256]{1,0:T(8,128)(2,1)S(1)}, f32[512,256]{1,0:T(8,128)S(1)}, f32[512,256]{1,0:T(8,128)S(1)}, bf16[512,1024]{1,0:T(8,128)(2,1)S(1)}, b...) custom-call(s32[11]{0:T(128)S(1)} %copy-done.19, ...), custom_call_target="tpu_custom_call" | custom-call | flops 10000000000 | bytes 10000000 | tf_op jit(solution)/shard_map/pallas_call | solution.py:54
  341.5 11.0 %shard_map.441 = (bf16[512,256]{1,0:T(8,128)(2,1)S(1)}, f32[512,256]{1,0:T(8,128)S(1)}, f32[512,256]{1,0:T(8,128)S(1)}, bf16[512,1024]{1,0:T(8,128)(2,1)S(1)}, b...) custom-call(s32[11]{0:T(128)S(1)} %copy-done.19, ...), custom_call_target="tpu_custom_call" | custom-call | flops 10000000000 | bytes 10000000 | tf_op jit(solution)/shard_map/pallas_call | solution.py:54
  352.6 8.7 %shard_map.442 = (bf16[512,256]{1,0:T(8,128)(2,1)S(1)}, f32[512,256]{1,0:T(8,128)S(1)}, f32[512,256]{1,0:T(8,128)S(1)}, bf16[512,1024]{1,0:T(8,128)(2,1)S(1)}, bf16[512,128]{1,0:T(8,128)(2,1)S(1)}) custom-call(s32[11]{0:T(128)S(1)} %copy-done.19, bf16[512,768]{1,0:T(8,128)(2,1)S(1)} %copy-done.70, bf16[128,1024]{1,0:T(8,128)(2,1)S(1)} %get-tuple-element.314.refs_2_, ...), custom_call_target="tpu_custom_call" | custom-call | flops 10000000000 | bytes 10000000 | tf_op jit(solution)/shard_map/pallas_call | solution.py:54
  392.0 4.7 collective-permute-done.81.refs_1_
  402.7 3.5 shard_map.450
  413.8 4.0 collective-permute-done.87.refs_3_
  422.1 2.9 collective-permute-done.89.refs_3_
  431.6 6.6 %shard_map.457 = (bf16[512,256]{1,0:T(8,128)(2,1)S(1)}, f32[512,256]{1,0:T(8,128)S(1)}, f32[512,256]{1,0:T(8,128)S(1)}, bf16[512,1024]{1,0:T(8,128)(2,1)}) custom-call(s32[11]{0:T(128)S(1)} %copy-done.19, bf16[512,768]{1,0:T(8,128)(2,1)S(1)} %copy-done.76, bf16[128,1024]{1,0:T(8,128)(2,1)S(1)} %get-tuple-element.367.refs_2_, ...), custom_call_target="tpu_custom_call" | custom-call | flops 10000000000 | bytes 10000000 | tf_op jit(solution)/shard_map/pallas_call | solution.py:54
  443.7 2.5 convolution_convert_fusion.2
  460.8 8.2 %collective-permute-done.98.refs_2_ = bf16[256,1024]{1,0:T(8,128)(2,1)S(1)} collective-permute-done((bf16[256,1024]{1,0:T(8,128)(2,1)}, bf16[256,1024]{1,0:T(8,128)(2,1)S(1)}, u32[]{:S(2)}, u32[]{:S(2)}) %collective-permute-start.98) | collective-permute-done | bytes 524320 | tf_op jit(solution)/shard_map/ppermute | solution.py:36
  474.2 2.9 shard_map.463
  492.5 10.0 %collective-permute-done.111.refs_1_ = bf16[256,1024]{1,0:T(8,128)(2,1)S(1)} collective-permute-done((bf16[256,1024]{1,0:T(8,128)(2,1)S(1)}, bf16[256,1024]{1,0:T(8,128)(2,1)S(1)}, u32[]{:S(2)}, u32[]{:S(2)}) %collective-permute-start.111) | collective-permute-done | bytes 524320 | tf_op jit(solution)/shard_map/ppermute | solution.py:174
  504.0 4.3 collective-permute-done.109.refs_1_
  515.6 2.4 collective-permute-start.125
  526.5 2.7 collective-permute-start.122
  529.2 2.9 shard_map.471
  (786 shorter events, 279.8 us)
Async XLA Ops:
  7.2 91.9 %all-gather.7.cloned.1.call-start = ((), (), s32[]{:S(2)}) async-start(), calls=%async_computation.4 | async-start | bytes 4718592 | tf_op jit(solution)/shard_map/all_gather | solution.py:1089
  9.7 139.0 %all-gather.9.cloned.1.call-start = ((), (), s32[]{:S(2)}) async-start(), calls=%async_computation.5 | async-start | bytes 2654208 | tf_op jit(solution)/shard_map/all_gather | solution.py:1089
  21.9 36.6 %collective-permute-start.11 = (bf16[128,1024]{1,0:T(8,128)(2,1)S(1)}, bf16[128,1024]{1,0:T(8,128)(2,1)S(1)}, u32[]{:S(2)}, u32[]{:S(2)}) collective-permute-start(bf16[128,1024]{1,0:T(8,128)(2,1)S(1)} %get-tuple-element.460.refs_0_), channel_id=1, source_target_pairs={{0,16},{8,24},{16,0},{24,8},{1,17},{9,25},{17,1},{25,9},{2,18},{10... | collective-permute-start | bytes 786440 | tf_op jit(solution)/shard_map/ppermute | solution.py:36
  23.1 37.8 %collective-permute-start.12 = (bf16[128,1024]{1,0:T(8,128)(2,1)S(1)}, bf16[128,1024]{1,0:T(8,128)(2,1)S(1)}, u32[]{:S(2)}, u32[]{:S(2)}) collective-permute-start(bf16[128,1024]{1,0:T(8,128)(2,1)S(1)} %get-tuple-element.461.refs_0_), channel_id=1, source_target_pairs={{0,16},{8,24},{16,0},{24,8},{1,17},{9,25},{17,1},{25,9},{2,18},{10... | collective-permute-start | bytes 786440 | tf_op jit(solution)/shard_map/ppermute | solution.py:36
  23.5 37.3 %collective-permute-start = (bf16[128,1024]{1,0:T(8,128)(2,1)S(1)}, bf16[128,1024]{1,0:T(8,128)(2,1)}, u32[]{:S(2)}, u32[]{:S(2)}) collective-permute-start(bf16[128,1024]{1,0:T(8,128)(2,1)S(1)} %copy-done.29), channel_id=1, source_target_pairs={{0,16},{8,24},{16,0},{24,8},{1,17},{9,25},{17,1},{25,9},{2,18},{10... | collective-permute-start | bytes 786440 | tf_op jit(solution)/shard_map/ppermute | solution.py:36
  35.4 15.7 %collective-permute-start.7 = (bf16[528,256]{1,0:T(8,128)(2,1)S(1)}, bf16[528,256]{1,0:T(8,128)(2,1)S(1)}, u32[]{:S(2)}, u32[]{:S(2)}) collective-permute-start(bf16[528,256]{1,0:T(8,128)(2,1)S(1)} %collective-permute-done.5.refs_4_), channel_id=1, source_target_pairs={{0,2},{2,4},{4,6},{6,7},{7,5},{5,3},{3,1},{1,0},{8,10},{10,12},{12... | collective-permute-start | bytes 811016 | tf_op jit(solution)/shard_map/ppermute | solution.py:174
  41.0 182.5 %all-gather.11.cloned.1.call-start = ((), (), s32[]{:S(2)}) async-start(), calls=%async_computation.6 | async-start | bytes 4718592 | tf_op jit(solution)/shard_map/all_gather | solution.py:1089
  77.1 80.7 %collective-permute-start.28 = (bf16[128,1024]{1,0:T(8,128)(2,1)S(1)}, bf16[128,1024]{1,0:T(8,128)(2,1)}, u32[]{:S(2)}, u32[]{:S(2)}) collective-permute-start(bf16[128,1024]{1,0:T(8,128)(2,1)S(1)} %get-tuple-element.460.refs_0_), channel_id=1, source_target_pairs={{0,8},{8,0},{16,24},{24,16},{1,9},{9,1},{17,25},{25,17},{2,10},{10... | collective-permute-start | bytes 786440 | tf_op jit(solution)/shard_map/ppermute | solution.py:36
  77.1 84.1 %collective-permute-start.26 = (bf16[128,1024]{1,0:T(8,128)(2,1)S(1)}, bf16[128,1024]{1,0:T(8,128)(2,1)}, u32[]{:S(2)}, u32[]{:S(2)}) collective-permute-start(bf16[128,1024]{1,0:T(8,128)(2,1)S(1)} %get-tuple-element.461.refs_0_), channel_id=1, source_target_pairs={{0,8},{8,0},{16,24},{24,16},{1,9},{9,1},{17,25},{25,17},{2,10},{10... | collective-permute-start | bytes 786440 | tf_op jit(solution)/shard_map/ppermute | solution.py:36
  77.6 373.5 %reduce-scatter.3.cloned.1.call-start = ((), (), s32[]{:S(2)}) async-start(), calls=%async_computation.2 | async-start | bytes 4718592 | tf_op jit(solution)/shard_map/reduce_scatter | solution.py:1230
  114.0 44.6 %collective-permute-start.29 = (bf16[128,1024]{1,0:T(8,128)(2,1)}, bf16[128,1024]{1,0:T(8,128)(2,1)}, u32[]{:S(2)}, u32[]{:S(2)}) collective-permute-start(bf16[128,1024]{1,0:T(8,128)(2,1)} %copy-done.32), channel_id=1, source_target_pairs={{0,8},{8,0},{16,24},{24,16},{1,9},{9,1},{17,25},{25,17},{2,10},{10... | collective-permute-start | bytes 786440 | tf_op jit(solution)/shard_map/ppermute | solution.py:36
  130.2 21.9 %collective-permute-start.23 = (bf16[128,1024]{1,0:T(8,128)(2,1)S(1)}, bf16[128,1024]{1,0:T(8,128)(2,1)S(1)}, u32[]{:S(2)}, u32[]{:S(2)}) collective-permute-start(bf16[128,1024]{1,0:T(8,128)(2,1)S(1)} %get-tuple-element.250.refs_0_), channel_id=1, source_target_pairs={{0,16},{8,24},{16,0},{24,8},{1,17},{9,25},{17,1},{25,9},{2,18},{10... | collective-permute-start | bytes 786440 | tf_op jit(solution)/shard_map/ppermute | solution.py:36
  131.4 23.3 %collective-permute-start.24 = (bf16[128,1024]{1,0:T(8,128)(2,1)S(1)}, bf16[128,1024]{1,0:T(8,128)(2,1)S(1)}, u32[]{:S(2)}, u32[]{:S(2)}) collective-permute-start(bf16[128,1024]{1,0:T(8,128)(2,1)S(1)} %get-tuple-element.250.refs_0_), channel_id=1, source_target_pairs={{0,8},{8,0},{16,24},{24,16},{1,9},{9,1},{17,25},{25,17},{2,10},{10... | collective-permute-start | bytes 786440 | tf_op jit(solution)/shard_map/ppermute | solution.py:36
  191.5 19.2 %collective-permute-start.37 = (bf16[128,1024]{1,0:T(8,128)(2,1)S(1)}, bf16[128,1024]{1,0:T(8,128)(2,1)S(1)}, u32[]{:S(2)}, u32[]{:S(2)}) collective-permute-start(bf16[128,1024]{1,0:T(8,128)(2,1)S(1)} %get-tuple-element.277.refs_0_), channel_id=1, source_target_pairs={{0,8},{8,0},{16,24},{24,16},{1,9},{9,1},{17,25},{25,17},{2,10},{10... | collective-permute-start | bytes 786440 | tf_op jit(solution)/shard_map/ppermute | solution.py:36
  192.5 16.0 %collective-permute-start.40 = (bf16[128,1024]{1,0:T(8,128)(2,1)S(1)}, bf16[128,1024]{1,0:T(8,128)(2,1)S(1)}, u32[]{:S(2)}, u32[]{:S(2)}) collective-permute-start(bf16[128,1024]{1,0:T(8,128)(2,1)S(1)} %shard_map.419.refs_5_), channel_id=1, source_target_pairs={{0,16},{8,24},{16,0},{24,8},{1,17},{9,25},{17,1},{25,9},{2,18},{10... | collective-permute-start | bytes 786440 | tf_op jit(solution)/shard_map/ppermute | solution.py:36
  198.2 15.9 %collective-permute-start.43 = (bf16[128,1024]{1,0:T(8,128)(2,1)S(1)}, bf16[128,1024]{1,0:T(8,128)(2,1)}, u32[]{:S(2)}, u32[]{:S(2)}) collective-permute-start(bf16[128,1024]{1,0:T(8,128)(2,1)S(1)} %get-tuple-element.287.refs_0_), channel_id=1, source_target_pairs={{0,16},{8,24},{16,0},{24,8},{1,17},{9,25},{17,1},{25,9},{2,18},{10... | collective-permute-start | bytes 786440 | tf_op jit(solution)/shard_map/ppermute | solution.py:36
  198.6 38.3 %collective-permute-start.44 = (bf16[128,1024]{1,0:T(8,128)(2,1)S(1)}, bf16[128,1024]{1,0:T(8,128)(2,1)}, u32[]{:S(2)}, u32[]{:S(2)}) collective-permute-start(bf16[128,1024]{1,0:T(8,128)(2,1)S(1)} %get-tuple-element.287.refs_0_), channel_id=1, source_target_pairs={{0,8},{8,0},{16,24},{24,16},{1,9},{9,1},{17,25},{25,17},{2,10},{10... | collective-permute-start | bytes 786440 | tf_op jit(solution)/shard_map/ppermute | solution.py:36
  202.9 20.6 %collective-permute-start.38 = (bf16[128,1024]{1,0:T(8,128)(2,1)}, bf16[128,1024]{1,0:T(8,128)(2,1)S(1)}, u32[]{:S(2)}, u32[]{:S(2)}) collective-permute-start(bf16[128,1024]{1,0:T(8,128)(2,1)} %collective-permute-done.36.refs_1_), channel_id=1, source_target_pairs={{0,8},{8,0},{16,24},{24,16},{1,9},{9,1},{17,25},{25,17},{2,10},{10... | collective-permute-start | bytes 786440 | tf_op jit(solution)/shard_map/ppermute | solution.py:36
  210.2 32.2 %collective-permute-start.48 = (bf16[128,1024]{1,0:T(8,128)(2,1)S(1)}, bf16[128,1024]{1,0:T(8,128)(2,1)S(1)}, u32[]{:S(2)}, u32[]{:S(2)}) collective-permute-start(bf16[128,1024]{1,0:T(8,128)(2,1)S(1)} %get-tuple-element.291.refs_0_), channel_id=1, source_target_pairs={{0,16},{8,24},{16,0},{24,8},{1,17},{9,25},{17,1},{25,9},{2,18},{10... | collective-permute-start | bytes 786440 | tf_op jit(solution)/shard_map/ppermute | solution.py:36
  211.4 32.9 %collective-permute-start.49 = (bf16[128,1024]{1,0:T(8,128)(2,1)S(1)}, bf16[128,1024]{1,0:T(8,128)(2,1)}, u32[]{:S(2)}, u32[]{:S(2)}) collective-permute-start(bf16[128,1024]{1,0:T(8,128)(2,1)S(1)} %get-tuple-element.291.refs_0_), channel_id=1, source_target_pairs={{0,8},{8,0},{16,24},{24,16},{1,9},{9,1},{17,25},{25,17},{2,10},{10... | collective-permute-start | bytes 786440 | tf_op jit(solution)/shard_map/ppermute | solution.py:36
  214.1 22.8 %collective-permute-start.45 = (bf16[128,1024]{1,0:T(8,128)(2,1)}, bf16[128,1024]{1,0:T(8,128)(2,1)}, u32[]{:S(2)}, u32[]{:S(2)}) collective-permute-start(bf16[128,1024]{1,0:T(8,128)(2,1)} %collective-permute-done.43.refs_1_), channel_id=1, source_target_pairs={{0,8},{8,0},{16,24},{24,16},{1,9},{9,1},{17,25},{25,17},{2,10},{10... | collective-permute-start | bytes 786440 | tf_op jit(solution)/shard_map/ppermute | solution.py:36
  253.0 17.9 %collective-permute-start.55 = (bf16[128,1024]{1,0:T(8,128)(2,1)S(1)}, bf16[128,1024]{1,0:T(8,128)(2,1)S(1)}, u32[]{:S(2)}, u32[]{:S(2)}) collective-permute-start(bf16[128,1024]{1,0:T(8,128)(2,1)S(1)} %get-tuple-element.299.refs_0_), channel_id=1, source_target_pairs={{0,8},{8,0},{16,24},{24,16},{1,9},{9,1},{17,25},{25,17},{2,10},{10... | collective-permute-start | bytes 786440 | tf_op jit(solution)/shard_map/ppermute | solution.py:36
  254.0 15.0 %collective-permute-start.53 = (bf16[128,1024]{1,0:T(8,128)(2,1)S(1)}, bf16[128,1024]{1,0:T(8,128)(2,1)S(1)}, u32[]{:S(2)}, u32[]{:S(2)}) collective-permute-start(bf16[128,1024]{1,0:T(8,128)(2,1)S(1)} %shard_map.428.refs_6_), channel_id=1, source_target_pairs={{0,16},{8,24},{16,0},{24,8},{1,17},{9,25},{17,1},{25,9},{2,18},{10... | collective-permute-start | bytes 786440 | tf_op jit(solution)/shard_map/ppermute | solution.py:36
  258.4 20.5 %collective-permute-start.58 = (bf16[128,1024]{1,0:T(8,128)(2,1)S(1)}, bf16[128,1024]{1,0:T(8,128)(2,1)S(1)}, u32[]{:S(2)}, u32[]{:S(2)}) collective-permute-start(bf16[128,1024]{1,0:T(8,128)(2,1)S(1)} %get-tuple-element.304.refs_0_), channel_id=1, source_target_pairs={{0,16},{8,24},{16,0},{24,8},{1,17},{9,25},{17,1},{25,9},{2,18},{10... | collective-permute-start | bytes 786440 | tf_op jit(solution)/shard_map/ppermute | solution.py:36
  259.6 21.7 %collective-permute-start.59 = (bf16[128,1024]{1,0:T(8,128)(2,1)S(1)}, bf16[128,1024]{1,0:T(8,128)(2,1)S(1)}, u32[]{:S(2)}, u32[]{:S(2)}) collective-permute-start(bf16[128,1024]{1,0:T(8,128)(2,1)S(1)} %get-tuple-element.304.refs_0_), channel_id=1, source_target_pairs={{0,8},{8,0},{16,24},{24,16},{1,9},{9,1},{17,25},{25,17},{2,10},{10... | collective-permute-start | bytes 786440 | tf_op jit(solution)/shard_map/ppermute | solution.py:36
  269.6 15.6 %collective-permute-start.63 = (bf16[128,1024]{1,0:T(8,128)(2,1)S(1)}, bf16[128,1024]{1,0:T(8,128)(2,1)S(1)}, u32[]{:S(2)}, u32[]{:S(2)}) collective-permute-start(bf16[128,1024]{1,0:T(8,128)(2,1)S(1)} %get-tuple-element.310.refs_0_), channel_id=1, source_target_pairs={{0,16},{8,24},{16,0},{24,8},{1,17},{9,25},{17,1},{25,9},{2,18},{10... | collective-permute-start | bytes 786440 | tf_op jit(solution)/shard_map/ppermute | solution.py:36
  270.9 17.3 %collective-permute-start.64 = (bf16[128,1024]{1,0:T(8,128)(2,1)S(1)}, bf16[128,1024]{1,0:T(8,128)(2,1)S(1)}, u32[]{:S(2)}, u32[]{:S(2)}) collective-permute-start(bf16[128,1024]{1,0:T(8,128)(2,1)S(1)} %get-tuple-element.310.refs_0_), channel_id=1, source_target_pairs={{0,8},{8,0},{16,24},{24,16},{1,9},{9,1},{17,25},{25,17},{2,10},{10... | collective-permute-start | bytes 786440 | tf_op jit(solution)/shard_map/ppermute | solution.py:36
  283.9 15.2 %collective-permute-start.62 = (bf16[256,1024]{1,0:T(8,128)(2,1)S(1)}, bf16[256,1024]{1,0:T(8,128)(2,1)S(1)}, u32[]{:S(2)}, u32[]{:S(2)}) collective-permute-start(bf16[256,1024]{1,0:T(8,128)(2,1)S(1)} %get-tuple-element.309), channel_id=1, source_target_pairs={{0,8},{8,0},{16,24},{24,16},{1,9},{9,1},{17,25},{25,17},{2,10},{10... | collective-permute-start | bytes 1572872 | tf_op jit(solution)/shard_map/ppermute | solution.py:36
  299.0 178.0 %reduce-scatter.5.cloned.1.call-start = ((), (), s32[]{:S(2)}) async-start(), calls=%async_computation.3 | async-start | bytes 2727936 | tf_op jit(solution)/shard_map/reduce_scatter | solution.py:1313
  305.3 47.2 %collective-permute-start.67 = (bf16[128,1024]{1,0:T(8,128)(2,1)S(1)}, bf16[128,1024]{1,0:T(8,128)(2,1)S(1)}, u32[]{:S(2)}, u32[]{:S(2)}) collective-permute-start(bf16[128,1024]{1,0:T(8,128)(2,1)S(1)} %get-tuple-element.314.refs_2_), channel_id=1, source_target_pairs={{0,8},{8,0},{16,24},{24,16},{1,9},{9,1},{17,25},{25,17},{2,10},{10... | collective-permute-start | bytes 786440 | tf_op jit(solution)/shard_map/ppermute | solution.py:36
  309.6 16.3 %collective-permute-start.75 = (bf16[128,1024]{1,0:T(8,128)(2,1)S(1)}, bf16[128,1024]{1,0:T(8,128)(2,1)S(1)}, u32[]{:S(2)}, u32[]{:S(2)}) collective-permute-start(bf16[128,1024]{1,0:T(8,128)(2,1)S(1)} %get-tuple-element.325.refs_2_), channel_id=1, source_target_pairs={{0,16},{8,24},{16,0},{24,8},{1,17},{9,25},{17,1},{25,9},{2,18},{10... | collective-permute-start | bytes 786440 | tf_op jit(solution)/shard_map/ppermute | solution.py:36
  310.9 16.7 %collective-permute-start.76 = (bf16[128,1024]{1,0:T(8,128)(2,1)S(1)}, bf16[128,1024]{1,0:T(8,128)(2,1)S(1)}, u32[]{:S(2)}, u32[]{:S(2)}) collective-permute-start(bf16[128,1024]{1,0:T(8,128)(2,1)S(1)} %get-tuple-element.325.refs_2_), channel_id=1, source_target_pairs={{0,8},{8,0},{16,24},{24,16},{1,9},{9,1},{17,25},{25,17},{2,10},{10... | collective-permute-start | bytes 786440 | tf_op jit(solution)/shard_map/ppermute | solution.py:36
  314.8 37.8 %collective-permute-start.68 = (bf16[128,1024]{1,0:T(8,128)(2,1)S(1)}, bf16[128,1024]{1,0:T(8,128)(2,1)S(1)}, u32[]{:S(2)}, u32[]{:S(2)}) collective-permute-start(bf16[128,1024]{1,0:T(8,128)(2,1)S(1)} %collective-permute-done.66.refs_3_), channel_id=1, source_target_pairs={{0,8},{8,0},{16,24},{24,16},{1,9},{9,1},{17,25},{25,17},{2,10},{10... | collective-permute-start | bytes 786440 | tf_op jit(solution)/shard_map/ppermute | solution.py:36
  320.9 18.9 %collective-permute-start.72 = (bf16[128,1024]{1,0:T(8,128)(2,1)S(1)}, bf16[128,1024]{1,0:T(8,128)(2,1)S(1)}, u32[]{:S(2)}, u32[]{:S(2)}) collective-permute-start(bf16[128,1024]{1,0:T(8,128)(2,1)S(1)} %get-tuple-element.323.refs_2_), channel_id=1, source_target_pairs={{0,16},{8,24},{16,0},{24,8},{1,17},{9,25},{17,1},{25,9},{2,18},{10... | collective-permute-start | bytes 786440 | tf_op jit(solution)/shard_map/ppermute | solution.py:36
  377.3 20.8 %collective-permute-start.84 = (bf16[256,1024]{1,0:T(8,128)(2,1)S(1)}, bf16[256,1024]{1,0:T(8,128)(2,1)S(1)}, u32[]{:S(2)}, u32[]{:S(2)}) collective-permute-start(bf16[256,1024]{1,0:T(8,128)(2,1)S(1)} %get-tuple-element.356), channel_id=1, source_target_pairs={{0,8},{8,0},{16,24},{24,16},{1,9},{9,1},{17,25},{25,17},{2,10},{10... | collective-permute-start | bytes 1572872 | tf_op jit(solution)/shard_map/ppermute | solution.py:36
  378.1 28.2 %collective-permute-start.86 = (bf16[128,1024]{1,0:T(8,128)(2,1)S(1)}, bf16[128,1024]{1,0:T(8,128)(2,1)S(1)}, u32[]{:S(2)}, u32[]{:S(2)}) collective-permute-start(bf16[128,1024]{1,0:T(8,128)(2,1)S(1)} %shard_map.447.refs_7_), channel_id=1, source_target_pairs={{0,16},{8,24},{16,0},{24,8},{1,17},{9,25},{17,1},{25,9},{2,18},{10... | collective-permute-start | bytes 786440 | tf_op jit(solution)/shard_map/ppermute | solution.py:36
  428.0 23.1 %collective-permute-start.103 = (bf16[256,1024]{1,0:T(8,128)(2,1)S(1)}, bf16[256,1024]{1,0:T(8,128)(2,1)S(1)}, u32[]{:S(2)}, u32[]{:S(2)}) collective-permute-start(bf16[256,1024]{1,0:T(8,128)(2,1)S(1)} %get-tuple-element.370.refs_8_), channel_id=1, source_target_pairs={{0,2},{2,4},{4,6},{6,7},{7,5},{5,3},{3,1},{1,0},{8,10},{10,12},{12... | collective-permute-start | bytes 1572872 | tf_op jit(solution)/shard_map/ppermute | solution.py:174
  428.6 23.7 %collective-permute-start.104 = (bf16[256,1024]{1,0:T(8,128)(2,1)S(1)}, bf16[256,1024]{1,0:T(8,128)(2,1)S(1)}, u32[]{:S(2)}, u32[]{:S(2)}) collective-permute-start(bf16[256,1024]{1,0:T(8,128)(2,1)S(1)} %get-tuple-element.396), channel_id=1, source_target_pairs={{0,1},{2,0},{4,2},{6,4},{7,6},{5,7},{3,5},{1,3},{8,9},{10,8},{12,1... | collective-permute-start | bytes 1572872 | tf_op jit(solution)/shard_map/ppermute | solution.py:174
  450.8 26.3 %collective-permute-start.97 = (bf16[128,1024]{1,0:T(8,128)(2,1)}, bf16[128,1024]{1,0:T(8,128)(2,1)}, u32[]{:S(2)}, u32[]{:S(2)}) collective-permute-start(bf16[128,1024]{1,0:T(8,128)(2,1)} %shard_map.460.refs_5_), channel_id=1, source_target_pairs={{0,16},{8,24},{16,0},{24,8},{1,17},{9,25},{17,1},{25,9},{2,18},{10... | collective-permute-start | bytes 786440 | tf_op jit(solution)/shard_map/ppermute | solution.py:36
  451.1 17.9 %collective-permute-start.98 = (bf16[256,1024]{1,0:T(8,128)(2,1)}, bf16[256,1024]{1,0:T(8,128)(2,1)S(1)}, u32[]{:S(2)}, u32[]{:S(2)}) collective-permute-start(bf16[256,1024]{1,0:T(8,128)(2,1)} %bitcast.184), channel_id=1, source_target_pairs={{0,16},{8,24},{16,0},{24,8},{1,17},{9,25},{17,1},{25,9},{2,18},{10... | collective-permute-start | bytes 1572872 | tf_op jit(solution)/shard_map/ppermute | solution.py:36
  457.1 26.1 %collective-permute-start.107 = (bf16[256,1024]{1,0:T(8,128)(2,1)}, bf16[256,1024]{1,0:T(8,128)(2,1)S(1)}, u32[]{:S(2)}, u32[]{:S(2)}) collective-permute-start(bf16[256,1024]{1,0:T(8,128)(2,1)} %get-tuple-element.397.refs_6_), channel_id=1, source_target_pairs={{0,2},{2,4},{4,6},{6,7},{7,5},{5,3},{3,1},{1,0},{8,10},{10,12},{12... | collective-permute-start | bytes 1572872 | tf_op jit(solution)/shard_map/ppermute | solution.py:174
  457.7 29.3 %collective-permute-start.108 = (bf16[256,1024]{1,0:T(8,128)(2,1)S(1)}, bf16[256,1024]{1,0:T(8,128)(2,1)S(1)}, u32[]{:S(2)}, u32[]{:S(2)}) collective-permute-start(bf16[256,1024]{1,0:T(8,128)(2,1)S(1)} %get-tuple-element.401), channel_id=1, source_target_pairs={{0,1},{2,0},{4,2},{6,4},{7,6},{5,7},{3,5},{1,3},{8,9},{10,8},{12,1... | collective-permute-start | bytes 1572872 | tf_op jit(solution)/shard_map/ppermute | solution.py:174
  472.6 16.8 %collective-permute-start.105 = (bf16[528,256]{1,0:T(8,128)(2,1)}, bf16[528,256]{1,0:T(8,128)(2,1)}, u32[]{:S(2)}, u32[]{:S(2)}) collective-permute-start(bf16[528,256]{1,0:T(8,128)(2,1)} %get-tuple-element.398.refs_5_), channel_id=1, source_target_pairs={{0,2},{2,4},{4,6},{6,7},{7,5},{5,3},{3,1},{1,0},{8,10},{10,12},{12... | collective-permute-start | bytes 811016 | tf_op jit(solution)/shard_map/ppermute | solution.py:174
  473.2 17.2 %collective-permute-start.106 = (bf16[528,256]{1,0:T(8,128)(2,1)S(1)}, bf16[528,256]{1,0:T(8,128)(2,1)}, u32[]{:S(2)}, u32[]{:S(2)}) collective-permute-start(bf16[528,256]{1,0:T(8,128)(2,1)S(1)} %get-tuple-element.400), channel_id=1, source_target_pairs={{0,1},{2,0},{4,2},{6,4},{7,6},{5,7},{3,5},{1,3},{8,9},{10,8},{12,1... | collective-permute-start | bytes 811016 | tf_op jit(solution)/shard_map/ppermute | solution.py:174
  483.1 27.8 %collective-permute-start.118 = (bf16[592,256]{1,0:T(8,128)(2,1)S(1)}, bf16[592,256]{1,0:T(8,128)(2,1)S(1)}, u32[]{:S(2)}, u32[]{:S(2)}) collective-permute-start(bf16[592,256]{1,0:T(8,128)(2,1)S(1)} %bitcast.188), channel_id=1, source_target_pairs={{0,8},{8,0},{16,24},{24,16},{1,9},{9,1},{17,25},{25,17},{2,10},{10... | collective-permute-start | bytes 909320 | tf_op jit(solution)/shard_map/ppermute | solution.py:36
  485.5 26.3 %collective-permute-start.119 = (bf16[592,256]{1,0:T(8,128)(2,1)S(1)}, bf16[592,256]{1,0:T(8,128)(2,1)S(1)}, u32[]{:S(2)}, u32[]{:S(2)}) collective-permute-start(bf16[592,256]{1,0:T(8,128)(2,1)S(1)} %collective-permute-done.117.refs_2_), channel_id=1, source_target_pairs={{0,8},{8,0},{16,24},{24,16},{1,9},{9,1},{17,25},{25,17},{2,10},{10... | collective-permute-start | bytes 909320 | tf_op jit(solution)/shard_map/ppermute | solution.py:36
  491.9 16.3 %collective-permute-start.109 = (bf16[528,256]{1,0:T(8,128)(2,1)S(1)}, bf16[528,256]{1,0:T(8,128)(2,1)S(1)}, u32[]{:S(2)}, u32[]{:S(2)}) collective-permute-start(bf16[528,256]{1,0:T(8,128)(2,1)S(1)} %get-tuple-element.403.refs_5_), channel_id=1, source_target_pairs={{0,2},{2,4},{4,6},{6,7},{7,5},{5,3},{3,1},{1,0},{8,10},{10,12},{12... | collective-permute-start | bytes 811016 | tf_op jit(solution)/shard_map/ppermute | solution.py:174
  508.3 20.9 %collective-permute-start.124 = (bf16[256,1024]{1,0:T(8,128)(2,1)S(1)}, bf16[256,1024]{1,0:T(8,128)(2,1)S(1)}, u32[]{:S(2)}, u32[]{:S(2)}) collective-permute-start(bf16[256,1024]{1,0:T(8,128)(2,1)S(1)} %shard_map.467.refs_6_.refs_1_), channel_id=1, source_target_pairs={{0,8},{8,0},{16,24},{24,16},{1,9},{9,1},{17,25},{25,17},{2,10},{10... | collective-permute-start | bytes 1572872 | tf_op jit(solution)/shard_map/ppermute | solution.py:36
  (264 other events, 1737.8 us)
Sparse Core Ops, SparseCore 0:
  10.7 84.8 all-gather.6
  98.4 50.3 all-gather.8
  151.5 71.9 all-gather.10
  299.2 85.7 reduce-scatter.2
  391.1 75.4 reduce-scatter.4

commit v5 on v4

--- a/solution.py
+++ b/solution.py
@@ -1005,7 +1005,7 @@
     def kernel(devices_ref, *refs):
         refs = list(refs)
         block_refs = [refs.pop(0) for _ in range(STREAMS)]
-        qkv_ref, out_ref, tiny_ref, inner_ref = refs[:4]
+        qkv_ref, out_ref, bias_ref, gain_ref, shift_ref, inner_ref = refs[:6]
         total = jnp.zeros((tiny_rows, quarter), F32)
         for i, ref in enumerate(block_refs):
             columns = pl.ds(pl.multiple_of(devices_ref[i] * quarter, quarter), quarter)
@@ -1014,21 +1014,27 @@
             out_ref[:, columns] = ref[3 * share : fixed, :].astype(F32)
             if rel_part:
                 columns = pl.ds(pl.multiple_of(devices_ref[i] * rel_part, rel_part), rel_part)
-                refs[4][:half, columns] = ref[fixed : fixed + half, :rel_part].astype(F32)
-                refs[4][half:, columns] = ref[fixed : fixed + half, rel_part:].astype(F32)
+                refs[6][:half, columns] = ref[fixed : fixed + half, :rel_part].astype(F32)
+                refs[6][half:, columns] = ref[fixed : fixed + half, rel_part:].astype(F32)
             mine = ref[tiny:, :].astype(F32)
             total = total + mine
             inner_ref[pl.ds(devices_ref[i], 1), :] = mine[0:1, share : share + ffn_part]
-        tiny_ref[...] = total
+        bias_ref[...] = total[0:4, :share]
+        gain_ref[...] = total[4:6, :share]
+        shift_ref[...] = total[6:8, :share]
+        if rel_part:
+            refs[7][...] = total[1:2, share : 2 * share]
 
     outs = [
         ((3, share, dim), F32),
         ((share, dim), F32),
-        ((tiny_rows, quarter), F32),
+        ((4, share), F32),
+        ((2, share), F32),
+        ((2, share), F32),
         ((STREAMS, ffn_part), F32),
     ]
     if rel_part:
-        outs.append(((share, rel_part * STREAMS), F32))
+        outs += [((share, rel_part * STREAMS), F32), ((1, share), F32)]
     return chain(kernel, outs, blocks, scalars=[devices], after=after, room=6)
 
 
@@ -1358,8 +1364,7 @@
     enc_results = place_attention(chain, devices, enc_blocks, share, ffn_part, 0)
 
     def tiny_out(results):
-        tiny, inner = results[2], results[3]
-        return inner.reshape(-1), tiny[0:4, :share], tiny[4:6, :share], tiny[6:8, :share]
+        return results[5].reshape(-1), *results[2:5]
 
     return (
         jnp.stack(outputs),
@@ -1372,8 +1377,8 @@
         *tiny_out(enc_results),
         dec_results[0],
         dec_results[1],
-        dec_results[4],
-        dec_results[2][1, share : share + rel_all // n],
+        dec_results[6],
+        dec_results[7][0, : rel_all // n],
         dec_in_grad,
         dec_back_grad,
         *tiny_out(dec_results),

time: 552 us -> 562 us (1.018)
  matrix products: 19.4 us -> 25.5 us
    dot_general x19, matrix products: 19.4 us -> 25.5 us  [dot_tn(): lax.dot_general(a, b, (((0,), (0,)), ((), ())), preferred_element_type=F32)]
    unnamed x372 -> x396, local copies, waits for them, and re-layouts: 67.3 us -> 69.1 us
  transfers between devices with their start and end apart: 131 -> 131, of which waited for: 35 -> 35; matrix products, arithmetic and copies ran while one was open for 8% -> 10% of each run, Pallas kernels for 28% -> 28%
where the time goes in v5:
time: 562 us; the launch traced here: 554 us
  Pallas kernels  158 us (28%)
  waiting for transfers between devices  140 us (25%)
  starting transfers between devices  118 us (21%)
  local copies, waits for them, and re-layouts  85.2 us (15%)
  matrix products  25.5 us (5%)
  between operations  17.5 us (3%)
  other arithmetic  9.95 us (2%)
    pallas_call x82, Pallas kernels, __call__(): pl.pallas_call(body, out_shape=[jax.ShapeDtypeStruct(shape, kind) for sha...  158 us
    ppermute x102, starting transfers between devices, swap(): lax.ppermute(values, 'stream', [(i, i ^ bit) for i in range(STREAMS)])  97.1 us
    ppermute x102, waiting for transfers between devices, swap(): lax.ppermute(values, 'stream', [(i, i ^ bit) for i in range(STREAMS)])  74.6 us
    unnamed x396, local copies, waits for them, and re-layouts  69.1 us
    ppermute x24, waiting for transfers between devices, ring_step(): return lax.ppermute(values, 'dp', pairs)  41.6 us
    dot_general x19, matrix products, dot_tn(): lax.dot_general(a, b, (((0,), (0,)), ((), ())), preferred_element_type=F32)  25.5 us
    all_gather x3, waiting for transfers between devices, gather_shares(): return lax.all_gather(packed, 'dp', axis=0, tiled=False)  23.3 us
    ppermute x24, starting transfers between devices, ring_step(): return lax.ppermute(values, 'dp', pairs)  20.2 us
  transfers between devices with their start and end apart: 131, of which 35 were waited for; matrix products, arithmetic and copies ran while one was open for 10% of the time, Pallas kernels for 28%

profile of v5, /device:TPU:1, one launch (start us, length us, event | category | flops | bytes accessed | tf_op | source)
XLA Modules:
  0.0 553.6 jit_solution(1701468069274896673)
XLA Ops:
  14.3 6.1 %collective-permute-done.4.refs_3_ = bf16[528,256]{1,0:T(8,128)(2,1)S(1)} collective-permute-done((bf16[528,256]{1,0:T(8,128)(2,1)S(1)}, bf16[528,256]{1,0:T(8,128)(2,1)S(1)}, u32[]{:S(2)}, u32[]{:S(2)}) %collective-permute-start.4) | collective-permute-done | bytes 270368 | tf_op jit(solution)/shard_map/ppermute | solution.py:174
  24.6 10.8 %collective-permute-done.6.refs_5_ = bf16[528,256]{1,0:T(8,128)(2,1)S(1)} collective-permute-done((bf16[528,256]{1,0:T(8,128)(2,1)S(1)}, bf16[528,256]{1,0:T(8,128)(2,1)S(1)}, u32[]{:S(2)}, u32[]{:S(2)}) %collective-permute-start.6) | collective-permute-done | bytes 270368 | tf_op jit(solution)/shard_map/ppermute | solution.py:174
  35.4 3.3 collective-permute-start.7
  41.0 9.3 %collective-permute-done.8.refs_7_ = bf16[528,256]{1,0:T(8,128)(2,1)S(1)} collective-permute-done((bf16[528,256]{1,0:T(8,128)(2,1)S(1)}, bf16[528,256]{1,0:T(8,128)(2,1)S(1)}, u32[]{:S(2)}, u32[]{:S(2)}) %collective-permute-start.8) | collective-permute-done | bytes 270368 | tf_op jit(solution)/shard_map/ppermute | solution.py:174
  60.9 2.7 shard_map.395
  68.9 4.7 shard_map.398
  81.8 6.3 %collective-permute-done.17.refs_3_ = bf16[128,1024]{1,0:T(8,128)(2,1)S(1)} collective-permute-done((bf16[128,1024]{1,0:T(8,128)(2,1)S(1)}, bf16[128,1024]{1,0:T(8,128)(2,1)S(1)}, u32[]{:S(2)}, u32[]{:S(2)}) %collective-permute-start.17) | collective-permute-done | bytes 262176 | tf_op jit(solution)/shard_map/ppermute | solution.py:36
  93.6 2.5 collective-permute-done.18.refs_1_
  102.4 4.3 shard_map.403
  119.2 4.7 collective-permute-done.22.refs_3_
  132.9 15.8 %all-gather.9.cloned.1.call-done = bf16[4608,256]{1,0:T(8,128)(2,1)} async-done(((bf16[576,256]{1,0:T(8,128)(2,1)}), bf16[4608,256]{1,0:T(8,128)(2,1)}) %all-gather.9.cloned.1.call-update) | async-done | bytes 2359312 | tf_op jit(solution)/shard_map/all_gather | solution.py:1095
  161.1 2.4 shard_map.410
  163.6 5.6 %shard_map.411 = (bf16[512,256]{1,0:T(8,128)(2,1)S(1)}, f32[512,128]{1,0:T(8,128)S(1)}) custom-call(s32[11]{0:T(128)S(1)} %stack.140.refs_0_, bf16[512,768]{1,0:T(8,128)(2,1)S(1)} %get-tuple-element.261.refs_1_.refs_2_.refs_8_, f32[512,128]{1,0:T(8,128)S(1)} %get-tuple-element.262.refs_2_.refs_8_, ...), custom_call_target="tpu_custom_call" | custom-call | flops 10000000000 | bytes 10000000 | tf_op jit(solution)/shard_map/pallas_call | solution.py:54
  171.6 7.3 %shard_map.414 = (bf16[512,256]{1,0:T(8,128)(2,1)S(1)}, f32[512,128]{1,0:T(8,128)S(1)}, f32[128,1024]{1,0:T(8,128)S(1)}, f32[128,1024]{1,0:T(8,128)S(1)}, bf16[256,1024]{1,0:T(8,128)(2,1)S(1)}) custom-call(s32[11]{0:T(128)S(1)} %stack.140.refs_0_, bf16[512,768]{1,0:T(8,128)(2,1)S(1)} %get-tuple-element.273.refs_1_, ...), custom_call_target="tpu_custom_call" | custom-call | flops 10000000000 | bytes 10000000 | tf_op jit(solution)/shard_map/pallas_call | solution.py:54
  181.5 7.2 %shard_map.416 = (bf16[512,256]{1,0:T(8,128)(2,1)S(1)}, f32[512,128]{1,0:T(8,128)S(1)}, f32[128,1024]{1,0:T(8,128)S(1)}, f32[128,1024]{1,0:T(8,128)S(1)}, bf16[256,1024]{1,0:T(8,128)(2,1)S(1)}) custom-call(s32[11]{0:T(128)S(1)} %stack.140.refs_0_, bf16[512,768]{1,0:T(8,128)(2,1)S(1)} %get-tuple-element.278.refs_1_, ...), custom_call_target="tpu_custom_call" | custom-call | flops 10000000000 | bytes 10000000 | tf_op jit(solution)/shard_map/pallas_call | solution.py:54
  192.8 4.4 collective-permute-done.41.refs_3_
  204.7 3.7 collective-permute-done.40.refs_3_
  215.9 7.4 %all-gather.11.cloned.1.call-done = bf16[2048,1024]{1,0:T(8,128)(2,1)} async-done(((bf16[256,1024]{1,0:T(8,128)(2,1)}), bf16[2048,1024]{1,0:T(8,128)(2,1)}) %all-gather.11.cloned.1.call-update) | async-done | bytes 4194320 | tf_op jit(solution)/shard_map/all_gather | solution.py:1095
  229.2 5.6 %shard_map.422 = (f32[128,1024]{1,0:T(8,128)S(1)}, f32[128,1024]{1,0:T(8,128)S(1)}, bf16[256,1024]{1,0:T(8,128)(2,1)S(1)}, bf16[512,1024]{1,0:T(8,128)(2,1)S(1)}...) custom-call(bf16[128,1024]{1,0:T(8,128)(2,1)S(1)} %get-tuple-element.282.refs_0_, ...), custom_call_target="tpu_custom_call" | custom-call | flops 10000000000 | bytes 10000000 | tf_op jit(solution)/shard_map/pallas_call | solution.py:54
  236.8 5.4 shard_map.423
  244.6 5.2 shard_map.425
  254.5 3.1 collective-permute-done.51.refs_3_
  265.3 3.6 collective-permute-done.53.refs_3_
  273.1 3.0 shard_map.431
  281.3 2.5 shard_map.432
  288.1 3.3 shard_map.434
  296.1 2.8 pad_maximum_fusion
  306.4 2.6 collective-permute-done.71.refs_3_
  316.2 4.1 collective-permute-done.70.refs_3_
  322.1 3.8 collective-permute-done.75.refs_3_
  328.7 10.6 %shard_map.440 = (bf16[512,256]{1,0:T(8,128)(2,1)S(1)}, f32[512,256]{1,0:T(8,128)S(1)}, f32[512,256]{1,0:T(8,128)S(1)}, bf16[512,1024]{1,0:T(8,128)(2,1)S(1)}, b...) custom-call(s32[11]{0:T(128)S(1)} %copy-done.23, ...), custom_call_target="tpu_custom_call" | custom-call | flops 10000000000 | bytes 10000000 | tf_op jit(solution)/shard_map/pallas_call | solution.py:54
  341.4 11.0 %shard_map.441 = (bf16[512,256]{1,0:T(8,128)(2,1)S(1)}, f32[512,256]{1,0:T(8,128)S(1)}, f32[512,256]{1,0:T(8,128)S(1)}, bf16[512,1024]{1,0:T(8,128)(2,1)S(1)}, b...) custom-call(s32[11]{0:T(128)S(1)} %copy-done.23, ...), custom_call_target="tpu_custom_call" | custom-call | flops 10000000000 | bytes 10000000 | tf_op jit(solution)/shard_map/pallas_call | solution.py:54
  352.5 8.7 %shard_map.442 = (bf16[512,256]{1,0:T(8,128)(2,1)S(1)}, f32[512,256]{1,0:T(8,128)S(1)}, f32[512,256]{1,0:T(8,128)S(1)}, bf16[512,1024]{1,0:T(8,128)(2,1)S(1)}, bf16[512,128]{1,0:T(8,128)(2,1)S(1)}) custom-call(s32[11]{0:T(128)S(1)} %copy-done.23, bf16[512,768]{1,0:T(8,128)(2,1)S(1)} %copy-done.78, bf16[128,1024]{1,0:T(8,128)(2,1)S(1)} %get-tuple-element.319.refs_2_, ...), custom_call_target="tpu_custom_call" | custom-call | flops 10000000000 | bytes 10000000 | tf_op jit(solution)/shard_map/pallas_call | solution.py:54
  368.3 2.7 fusion.40
  370.9 2.7 fusion.39
  389.5 3.9 add_convert_fusion.2
  401.5 4.5 collective-permute-done.81.refs_1_
  410.6 2.5 shard_map.450
  420.2 4.7 collective-permute-done.87.refs_3_
  427.4 4.7 collective-permute-done.89.refs_3_
  440.1 6.6 %shard_map.457 = (bf16[512,256]{1,0:T(8,128)(2,1)S(1)}, f32[512,256]{1,0:T(8,128)S(1)}, f32[512,256]{1,0:T(8,128)S(1)}, bf16[512,1024]{1,0:T(8,128)(2,1)}) custom-call(s32[11]{0:T(128)S(1)} %copy-done.24, bf16[512,768]{1,0:T(8,128)(2,1)S(1)} %copy-done.84, bf16[128,1024]{1,0:T(8,128)(2,1)S(1)} %get-tuple-element.372.refs_2_, ...), custom_call_target="tpu_custom_call" | custom-call | flops 10000000000 | bytes 10000000 | tf_op jit(solution)/shard_map/pallas_call | solution.py:54
  452.9 2.5 convolution_convert_fusion.2
  471.1 7.6 %collective-permute-done.98.refs_2_ = bf16[256,1024]{1,0:T(8,128)(2,1)S(1)} collective-permute-done((bf16[256,1024]{1,0:T(8,128)(2,1)}, bf16[256,1024]{1,0:T(8,128)(2,1)S(1)}, u32[]{:S(2)}, u32[]{:S(2)}) %collective-permute-start.98) | collective-permute-done | bytes 524320 | tf_op jit(solution)/shard_map/ppermute | solution.py:36
  485.1 2.9 shard_map.463
  503.5 9.9 %collective-permute-done.111.refs_1_ = bf16[256,1024]{1,0:T(8,128)(2,1)S(1)} collective-permute-done((bf16[256,1024]{1,0:T(8,128)(2,1)S(1)}, bf16[256,1024]{1,0:T(8,128)(2,1)S(1)}, u32[]{:S(2)}, u32[]{:S(2)}) %collective-permute-start.111) | collective-permute-done | bytes 524320 | tf_op jit(solution)/shard_map/ppermute | solution.py:174
  515.0 4.3 collective-permute-done.109.refs_1_
  537.3 2.8 collective-permute-start.122
  540.1 2.9 shard_map.471
  (806 shorter events, 287.0 us)
Async XLA Ops:
  7.2 92.0 %all-gather.7.cloned.1.call-start = ((), (), s32[]{:S(2)}) async-start(), calls=%async_computation.4 | async-start | bytes 4718592 | tf_op jit(solution)/shard_map/all_gather | solution.py:1095
  9.7 139.0 %all-gather.9.cloned.1.call-start = ((), (), s32[]{:S(2)}) async-start(), calls=%async_computation.5 | async-start | bytes 2654208 | tf_op jit(solution)/shard_map/all_gather | solution.py:1095
  21.9 36.6 %collective-permute-start.11 = (bf16[128,1024]{1,0:T(8,128)(2,1)S(1)}, bf16[128,1024]{1,0:T(8,128)(2,1)S(1)}, u32[]{:S(2)}, u32[]{:S(2)}) collective-permute-start(bf16[128,1024]{1,0:T(8,128)(2,1)S(1)} %get-tuple-element.470.refs_0_), channel_id=1, source_target_pairs={{0,16},{8,24},{16,0},{24,8},{1,17},{9,25},{17,1},{25,9},{2,18},{10... | collective-permute-start | bytes 786440 | tf_op jit(solution)/shard_map/ppermute | solution.py:36
  23.1 37.8 %collective-permute-start.12 = (bf16[128,1024]{1,0:T(8,128)(2,1)S(1)}, bf16[128,1024]{1,0:T(8,128)(2,1)S(1)}, u32[]{:S(2)}, u32[]{:S(2)}) collective-permute-start(bf16[128,1024]{1,0:T(8,128)(2,1)S(1)} %get-tuple-element.471.refs_0_), channel_id=1, source_target_pairs={{0,16},{8,24},{16,0},{24,8},{1,17},{9,25},{17,1},{25,9},{2,18},{10... | collective-permute-start | bytes 786440 | tf_op jit(solution)/shard_map/ppermute | solution.py:36
  23.5 37.3 %collective-permute-start = (bf16[128,1024]{1,0:T(8,128)(2,1)S(1)}, bf16[128,1024]{1,0:T(8,128)(2,1)}, u32[]{:S(2)}, u32[]{:S(2)}) collective-permute-start(bf16[128,1024]{1,0:T(8,128)(2,1)S(1)} %copy-done.35), channel_id=1, source_target_pairs={{0,16},{8,24},{16,0},{24,8},{1,17},{9,25},{17,1},{25,9},{2,18},{10... | collective-permute-start | bytes 786440 | tf_op jit(solution)/shard_map/ppermute | solution.py:36
  35.4 15.7 %collective-permute-start.7 = (bf16[528,256]{1,0:T(8,128)(2,1)S(1)}, bf16[528,256]{1,0:T(8,128)(2,1)S(1)}, u32[]{:S(2)}, u32[]{:S(2)}) collective-permute-start(bf16[528,256]{1,0:T(8,128)(2,1)S(1)} %collective-permute-done.5.refs_4_), channel_id=1, source_target_pairs={{0,2},{2,4},{4,6},{6,7},{7,5},{5,3},{3,1},{1,0},{8,10},{10,12},{12... | collective-permute-start | bytes 811016 | tf_op jit(solution)/shard_map/ppermute | solution.py:174
  41.0 182.4 %all-gather.11.cloned.1.call-start = ((), (), s32[]{:S(2)}) async-start(), calls=%async_computation.6 | async-start | bytes 4718592 | tf_op jit(solution)/shard_map/all_gather | solution.py:1095
  77.1 80.6 %collective-permute-start.28 = (bf16[128,1024]{1,0:T(8,128)(2,1)S(1)}, bf16[128,1024]{1,0:T(8,128)(2,1)}, u32[]{:S(2)}, u32[]{:S(2)}) collective-permute-start(bf16[128,1024]{1,0:T(8,128)(2,1)S(1)} %get-tuple-element.470.refs_0_), channel_id=1, source_target_pairs={{0,8},{8,0},{16,24},{24,16},{1,9},{9,1},{17,25},{25,17},{2,10},{10... | collective-permute-start | bytes 786440 | tf_op jit(solution)/shard_map/ppermute | solution.py:36
  77.1 83.9 %collective-permute-start.26 = (bf16[128,1024]{1,0:T(8,128)(2,1)S(1)}, bf16[128,1024]{1,0:T(8,128)(2,1)}, u32[]{:S(2)}, u32[]{:S(2)}) collective-permute-start(bf16[128,1024]{1,0:T(8,128)(2,1)S(1)} %get-tuple-element.471.refs_0_), channel_id=1, source_target_pairs={{0,8},{8,0},{16,24},{24,16},{1,9},{9,1},{17,25},{25,17},{2,10},{10... | collective-permute-start | bytes 786440 | tf_op jit(solution)/shard_map/ppermute | solution.py:36
  77.7 383.1 %reduce-scatter.3.cloned.1.call-start = ((), (), s32[]{:S(2)}) async-start(), calls=%async_computation.2 | async-start | bytes 4718592 | tf_op jit(solution)/shard_map/reduce_scatter | solution.py:1236
  114.0 44.4 %collective-permute-start.29 = (bf16[128,1024]{1,0:T(8,128)(2,1)}, bf16[128,1024]{1,0:T(8,128)(2,1)}, u32[]{:S(2)}, u32[]{:S(2)}) collective-permute-start(bf16[128,1024]{1,0:T(8,128)(2,1)} %copy-done.38), channel_id=1, source_target_pairs={{0,8},{8,0},{16,24},{24,16},{1,9},{9,1},{17,25},{25,17},{2,10},{10... | collective-permute-start | bytes 786440 | tf_op jit(solution)/shard_map/ppermute | solution.py:36
  130.3 21.8 %collective-permute-start.23 = (bf16[128,1024]{1,0:T(8,128)(2,1)S(1)}, bf16[128,1024]{1,0:T(8,128)(2,1)S(1)}, u32[]{:S(2)}, u32[]{:S(2)}) collective-permute-start(bf16[128,1024]{1,0:T(8,128)(2,1)S(1)} %get-tuple-element.255.refs_0_), channel_id=1, source_target_pairs={{0,16},{8,24},{16,0},{24,8},{1,17},{9,25},{17,1},{25,9},{2,18},{10... | collective-permute-start | bytes 786440 | tf_op jit(solution)/shard_map/ppermute | solution.py:36
  131.4 23.2 %collective-permute-start.24 = (bf16[128,1024]{1,0:T(8,128)(2,1)S(1)}, bf16[128,1024]{1,0:T(8,128)(2,1)S(1)}, u32[]{:S(2)}, u32[]{:S(2)}) collective-permute-start(bf16[128,1024]{1,0:T(8,128)(2,1)S(1)} %get-tuple-element.255.refs_0_), channel_id=1, source_target_pairs={{0,8},{8,0},{16,24},{24,16},{1,9},{9,1},{17,25},{25,17},{2,10},{10... | collective-permute-start | bytes 786440 | tf_op jit(solution)/shard_map/ppermute | solution.py:36
  191.4 19.1 %collective-permute-start.37 = (bf16[128,1024]{1,0:T(8,128)(2,1)S(1)}, bf16[128,1024]{1,0:T(8,128)(2,1)S(1)}, u32[]{:S(2)}, u32[]{:S(2)}) collective-permute-start(bf16[128,1024]{1,0:T(8,128)(2,1)S(1)} %get-tuple-element.282.refs_0_), channel_id=1, source_target_pairs={{0,8},{8,0},{16,24},{24,16},{1,9},{9,1},{17,25},{25,17},{2,10},{10... | collective-permute-start | bytes 786440 | tf_op jit(solution)/shard_map/ppermute | solution.py:36
  192.4 16.1 %collective-permute-start.40 = (bf16[128,1024]{1,0:T(8,128)(2,1)S(1)}, bf16[128,1024]{1,0:T(8,128)(2,1)S(1)}, u32[]{:S(2)}, u32[]{:S(2)}) collective-permute-start(bf16[128,1024]{1,0:T(8,128)(2,1)S(1)} %shard_map.419.refs_5_), channel_id=1, source_target_pairs={{0,16},{8,24},{16,0},{24,8},{1,17},{9,25},{17,1},{25,9},{2,18},{10... | collective-permute-start | bytes 786440 | tf_op jit(solution)/shard_map/ppermute | solution.py:36
  198.2 15.9 %collective-permute-start.43 = (bf16[128,1024]{1,0:T(8,128)(2,1)S(1)}, bf16[128,1024]{1,0:T(8,128)(2,1)}, u32[]{:S(2)}, u32[]{:S(2)}) collective-permute-start(bf16[128,1024]{1,0:T(8,128)(2,1)S(1)} %get-tuple-element.292.refs_0_), channel_id=1, source_target_pairs={{0,16},{8,24},{16,0},{24,8},{1,17},{9,25},{17,1},{25,9},{2,18},{10... | collective-permute-start | bytes 786440 | tf_op jit(solution)/shard_map/ppermute | solution.py:36
  198.5 38.3 %collective-permute-start.44 = (bf16[128,1024]{1,0:T(8,128)(2,1)S(1)}, bf16[128,1024]{1,0:T(8,128)(2,1)}, u32[]{:S(2)}, u32[]{:S(2)}) collective-permute-start(bf16[128,1024]{1,0:T(8,128)(2,1)S(1)} %get-tuple-element.292.refs_0_), channel_id=1, source_target_pairs={{0,8},{8,0},{16,24},{24,16},{1,9},{9,1},{17,25},{25,17},{2,10},{10... | collective-permute-start | bytes 786440 | tf_op jit(solution)/shard_map/ppermute | solution.py:36
  202.8 20.6 %collective-permute-start.38 = (bf16[128,1024]{1,0:T(8,128)(2,1)}, bf16[128,1024]{1,0:T(8,128)(2,1)S(1)}, u32[]{:S(2)}, u32[]{:S(2)}) collective-permute-start(bf16[128,1024]{1,0:T(8,128)(2,1)} %collective-permute-done.36.refs_1_), channel_id=1, source_target_pairs={{0,8},{8,0},{16,24},{24,16},{1,9},{9,1},{17,25},{25,17},{2,10},{10... | collective-permute-start | bytes 786440 | tf_op jit(solution)/shard_map/ppermute | solution.py:36
  210.2 32.1 %collective-permute-start.48 = (bf16[128,1024]{1,0:T(8,128)(2,1)S(1)}, bf16[128,1024]{1,0:T(8,128)(2,1)S(1)}, u32[]{:S(2)}, u32[]{:S(2)}) collective-permute-start(bf16[128,1024]{1,0:T(8,128)(2,1)S(1)} %get-tuple-element.296.refs_0_), channel_id=1, source_target_pairs={{0,16},{8,24},{16,0},{24,8},{1,17},{9,25},{17,1},{25,9},{2,18},{10... | collective-permute-start | bytes 786440 | tf_op jit(solution)/shard_map/ppermute | solution.py:36
  211.2 32.9 %collective-permute-start.49 = (bf16[128,1024]{1,0:T(8,128)(2,1)S(1)}, bf16[128,1024]{1,0:T(8,128)(2,1)}, u32[]{:S(2)}, u32[]{:S(2)}) collective-permute-start(bf16[128,1024]{1,0:T(8,128)(2,1)S(1)} %get-tuple-element.296.refs_0_), channel_id=1, source_target_pairs={{0,8},{8,0},{16,24},{24,16},{1,9},{9,1},{17,25},{25,17},{2,10},{10... | collective-permute-start | bytes 786440 | tf_op jit(solution)/shard_map/ppermute | solution.py:36
  214.0 22.7 %collective-permute-start.45 = (bf16[128,1024]{1,0:T(8,128)(2,1)}, bf16[128,1024]{1,0:T(8,128)(2,1)}, u32[]{:S(2)}, u32[]{:S(2)}) collective-permute-start(bf16[128,1024]{1,0:T(8,128)(2,1)} %collective-permute-done.43.refs_1_), channel_id=1, source_target_pairs={{0,8},{8,0},{16,24},{24,16},{1,9},{9,1},{17,25},{25,17},{2,10},{10... | collective-permute-start | bytes 786440 | tf_op jit(solution)/shard_map/ppermute | solution.py:36
  252.9 17.9 %collective-permute-start.55 = (bf16[128,1024]{1,0:T(8,128)(2,1)S(1)}, bf16[128,1024]{1,0:T(8,128)(2,1)S(1)}, u32[]{:S(2)}, u32[]{:S(2)}) collective-permute-start(bf16[128,1024]{1,0:T(8,128)(2,1)S(1)} %get-tuple-element.304.refs_0_), channel_id=1, source_target_pairs={{0,8},{8,0},{16,24},{24,16},{1,9},{9,1},{17,25},{25,17},{2,10},{10... | collective-permute-start | bytes 786440 | tf_op jit(solution)/shard_map/ppermute | solution.py:36
  258.3 20.5 %collective-permute-start.58 = (bf16[128,1024]{1,0:T(8,128)(2,1)S(1)}, bf16[128,1024]{1,0:T(8,128)(2,1)S(1)}, u32[]{:S(2)}, u32[]{:S(2)}) collective-permute-start(bf16[128,1024]{1,0:T(8,128)(2,1)S(1)} %get-tuple-element.309.refs_0_), channel_id=1, source_target_pairs={{0,16},{8,24},{16,0},{24,8},{1,17},{9,25},{17,1},{25,9},{2,18},{10... | collective-permute-start | bytes 786440 | tf_op jit(solution)/shard_map/ppermute | solution.py:36
  259.5 21.7 %collective-permute-start.59 = (bf16[128,1024]{1,0:T(8,128)(2,1)S(1)}, bf16[128,1024]{1,0:T(8,128)(2,1)S(1)}, u32[]{:S(2)}, u32[]{:S(2)}) collective-permute-start(bf16[128,1024]{1,0:T(8,128)(2,1)S(1)} %get-tuple-element.309.refs_0_), channel_id=1, source_target_pairs={{0,8},{8,0},{16,24},{24,16},{1,9},{9,1},{17,25},{25,17},{2,10},{10... | collective-permute-start | bytes 786440 | tf_op jit(solution)/shard_map/ppermute | solution.py:36
  269.5 15.6 %collective-permute-start.63 = (bf16[128,1024]{1,0:T(8,128)(2,1)S(1)}, bf16[128,1024]{1,0:T(8,128)(2,1)S(1)}, u32[]{:S(2)}, u32[]{:S(2)}) collective-permute-start(bf16[128,1024]{1,0:T(8,128)(2,1)S(1)} %get-tuple-element.315.refs_0_), channel_id=1, source_target_pairs={{0,16},{8,24},{16,0},{24,8},{1,17},{9,25},{17,1},{25,9},{2,18},{10... | collective-permute-start | bytes 786440 | tf_op jit(solution)/shard_map/ppermute | solution.py:36
  270.8 17.3 %collective-permute-start.64 = (bf16[128,1024]{1,0:T(8,128)(2,1)S(1)}, bf16[128,1024]{1,0:T(8,128)(2,1)S(1)}, u32[]{:S(2)}, u32[]{:S(2)}) collective-permute-start(bf16[128,1024]{1,0:T(8,128)(2,1)S(1)} %get-tuple-element.315.refs_0_), channel_id=1, source_target_pairs={{0,8},{8,0},{16,24},{24,16},{1,9},{9,1},{17,25},{25,17},{2,10},{10... | collective-permute-start | bytes 786440 | tf_op jit(solution)/shard_map/ppermute | solution.py:36
  299.0 189.1 %reduce-scatter.5.cloned.1.call-start = ((), (), s32[]{:S(2)}) async-start(), calls=%async_computation.3 | async-start | bytes 2727936 | tf_op jit(solution)/shard_map/reduce_scatter | solution.py:1319
  305.2 47.2 %collective-permute-start.67 = (bf16[128,1024]{1,0:T(8,128)(2,1)S(1)}, bf16[128,1024]{1,0:T(8,128)(2,1)S(1)}, u32[]{:S(2)}, u32[]{:S(2)}) collective-permute-start(bf16[128,1024]{1,0:T(8,128)(2,1)S(1)} %get-tuple-element.319.refs_2_), channel_id=1, source_target_pairs={{0,8},{8,0},{16,24},{24,16},{1,9},{9,1},{17,25},{25,17},{2,10},{10... | collective-permute-start | bytes 786440 | tf_op jit(solution)/shard_map/ppermute | solution.py:36
  309.6 16.3 %collective-permute-start.75 = (bf16[128,1024]{1,0:T(8,128)(2,1)S(1)}, bf16[128,1024]{1,0:T(8,128)(2,1)S(1)}, u32[]{:S(2)}, u32[]{:S(2)}) collective-permute-start(bf16[128,1024]{1,0:T(8,128)(2,1)S(1)} %get-tuple-element.330.refs_2_), channel_id=1, source_target_pairs={{0,16},{8,24},{16,0},{24,8},{1,17},{9,25},{17,1},{25,9},{2,18},{10... | collective-permute-start | bytes 786440 | tf_op jit(solution)/shard_map/ppermute | solution.py:36
  310.8 16.7 %collective-permute-start.76 = (bf16[128,1024]{1,0:T(8,128)(2,1)S(1)}, bf16[128,1024]{1,0:T(8,128)(2,1)S(1)}, u32[]{:S(2)}, u32[]{:S(2)}) collective-permute-start(bf16[128,1024]{1,0:T(8,128)(2,1)S(1)} %get-tuple-element.330.refs_2_), channel_id=1, source_target_pairs={{0,8},{8,0},{16,24},{24,16},{1,9},{9,1},{17,25},{25,17},{2,10},{10... | collective-permute-start | bytes 786440 | tf_op jit(solution)/shard_map/ppermute | solution.py:36
  314.7 37.8 %collective-permute-start.68 = (bf16[128,1024]{1,0:T(8,128)(2,1)S(1)}, bf16[128,1024]{1,0:T(8,128)(2,1)S(1)}, u32[]{:S(2)}, u32[]{:S(2)}) collective-permute-start(bf16[128,1024]{1,0:T(8,128)(2,1)S(1)} %collective-permute-done.66.refs_3_), channel_id=1, source_target_pairs={{0,8},{8,0},{16,24},{24,16},{1,9},{9,1},{17,25},{25,17},{2,10},{10... | collective-permute-start | bytes 786440 | tf_op jit(solution)/shard_map/ppermute | solution.py:36
  320.9 18.9 %collective-permute-start.72 = (bf16[128,1024]{1,0:T(8,128)(2,1)S(1)}, bf16[128,1024]{1,0:T(8,128)(2,1)S(1)}, u32[]{:S(2)}, u32[]{:S(2)}) collective-permute-start(bf16[128,1024]{1,0:T(8,128)(2,1)S(1)} %get-tuple-element.328.refs_2_), channel_id=1, source_target_pairs={{0,16},{8,24},{16,0},{24,8},{1,17},{9,25},{17,1},{25,9},{2,18},{10... | collective-permute-start | bytes 786440 | tf_op jit(solution)/shard_map/ppermute | solution.py:36
  378.2 17.8 %collective-permute-start.79 = (bf16[128,1024]{1,0:T(8,128)(2,1)}, bf16[128,1024]{1,0:T(8,128)(2,1)}, u32[]{:S(2)}, u32[]{:S(2)}) collective-permute-start(bf16[128,1024]{1,0:T(8,128)(2,1)} %shard_map.445.refs_6_), channel_id=1, source_target_pairs={{0,16},{8,24},{16,0},{24,8},{1,17},{9,25},{17,1},{25,9},{2,18},{10... | collective-permute-start | bytes 786440 | tf_op jit(solution)/shard_map/ppermute | solution.py:36
  382.4 24.7 %collective-permute-start.84 = (bf16[256,1024]{1,0:T(8,128)(2,1)}, bf16[256,1024]{1,0:T(8,128)(2,1)S(1)}, u32[]{:S(2)}, u32[]{:S(2)}) collective-permute-start(bf16[256,1024]{1,0:T(8,128)(2,1)} %copy-done.33), channel_id=1, source_target_pairs={{0,8},{8,0},{16,24},{24,16},{1,9},{9,1},{17,25},{25,17},{2,10},{10... | collective-permute-start | bytes 1572872 | tf_op jit(solution)/shard_map/ppermute | solution.py:36
  386.0 27.1 %collective-permute-start.86 = (bf16[128,1024]{1,0:T(8,128)(2,1)}, bf16[128,1024]{1,0:T(8,128)(2,1)S(1)}, u32[]{:S(2)}, u32[]{:S(2)}) collective-permute-start(bf16[128,1024]{1,0:T(8,128)(2,1)} %shard_map.447.refs_7_), channel_id=1, source_target_pairs={{0,16},{8,24},{16,0},{24,8},{1,17},{9,25},{17,1},{25,9},{2,18},{10... | collective-permute-start | bytes 786440 | tf_op jit(solution)/shard_map/ppermute | solution.py:36
  419.3 15.8 %collective-permute-start.93 = (bf16[128,1024]{1,0:T(8,128)(2,1)S(1)}, bf16[128,1024]{1,0:T(8,128)(2,1)S(1)}, u32[]{:S(2)}, u32[]{:S(2)}) collective-permute-start(bf16[128,1024]{1,0:T(8,128)(2,1)S(1)} %get-tuple-element.374), channel_id=1, source_target_pairs={{0,1},{2,0},{4,2},{6,4},{7,6},{5,7},{3,5},{1,3},{8,9},{10,8},{12,1... | collective-permute-start | bytes 786440 | tf_op jit(solution)/shard_map/ppermute | solution.py:174
  435.9 24.8 %collective-permute-start.103 = (bf16[256,1024]{1,0:T(8,128)(2,1)S(1)}, bf16[256,1024]{1,0:T(8,128)(2,1)S(1)}, u32[]{:S(2)}, u32[]{:S(2)}) collective-permute-start(bf16[256,1024]{1,0:T(8,128)(2,1)S(1)} %get-tuple-element.375.refs_8_), channel_id=1, source_target_pairs={{0,2},{2,4},{4,6},{6,7},{7,5},{5,3},{3,1},{1,0},{8,10},{10,12},{12... | collective-permute-start | bytes 1572872 | tf_op jit(solution)/shard_map/ppermute | solution.py:174
  436.1 25.8 %collective-permute-start.104 = (bf16[256,1024]{1,0:T(8,128)(2,1)S(1)}, bf16[256,1024]{1,0:T(8,128)(2,1)S(1)}, u32[]{:S(2)}, u32[]{:S(2)}) collective-permute-start(bf16[256,1024]{1,0:T(8,128)(2,1)S(1)} %get-tuple-element.401), channel_id=1, source_target_pairs={{0,1},{2,0},{4,2},{6,4},{7,6},{5,7},{3,5},{1,3},{8,9},{10,8},{12,1... | collective-permute-start | bytes 1572872 | tf_op jit(solution)/shard_map/ppermute | solution.py:174
  460.5 27.6 %collective-permute-start.97 = (bf16[128,1024]{1,0:T(8,128)(2,1)}, bf16[128,1024]{1,0:T(8,128)(2,1)}, u32[]{:S(2)}, u32[]{:S(2)}) collective-permute-start(bf16[128,1024]{1,0:T(8,128)(2,1)} %shard_map.460.refs_5_), channel_id=1, source_target_pairs={{0,16},{8,24},{16,0},{24,8},{1,17},{9,25},{17,1},{25,9},{2,18},{10... | collective-permute-start | bytes 786440 | tf_op jit(solution)/shard_map/ppermute | solution.py:36
  460.8 17.9 %collective-permute-start.98 = (bf16[256,1024]{1,0:T(8,128)(2,1)}, bf16[256,1024]{1,0:T(8,128)(2,1)S(1)}, u32[]{:S(2)}, u32[]{:S(2)}) collective-permute-start(bf16[256,1024]{1,0:T(8,128)(2,1)} %bitcast.184), channel_id=1, source_target_pairs={{0,16},{8,24},{16,0},{24,8},{1,17},{9,25},{17,1},{25,9},{2,18},{10... | collective-permute-start | bytes 1572872 | tf_op jit(solution)/shard_map/ppermute | solution.py:36
  466.7 27.3 %collective-permute-start.107 = (bf16[256,1024]{1,0:T(8,128)(2,1)}, bf16[256,1024]{1,0:T(8,128)(2,1)S(1)}, u32[]{:S(2)}, u32[]{:S(2)}) collective-permute-start(bf16[256,1024]{1,0:T(8,128)(2,1)} %get-tuple-element.402.refs_6_), channel_id=1, source_target_pairs={{0,2},{2,4},{4,6},{6,7},{7,5},{5,3},{3,1},{1,0},{8,10},{10,12},{12... | collective-permute-start | bytes 1572872 | tf_op jit(solution)/shard_map/ppermute | solution.py:174
  467.4 30.4 %collective-permute-start.108 = (bf16[256,1024]{1,0:T(8,128)(2,1)S(1)}, bf16[256,1024]{1,0:T(8,128)(2,1)S(1)}, u32[]{:S(2)}, u32[]{:S(2)}) collective-permute-start(bf16[256,1024]{1,0:T(8,128)(2,1)S(1)} %get-tuple-element.406), channel_id=1, source_target_pairs={{0,1},{2,0},{4,2},{6,4},{7,6},{5,7},{3,5},{1,3},{8,9},{10,8},{12,1... | collective-permute-start | bytes 1572872 | tf_op jit(solution)/shard_map/ppermute | solution.py:174
  483.6 16.9 %collective-permute-start.105 = (bf16[528,256]{1,0:T(8,128)(2,1)}, bf16[528,256]{1,0:T(8,128)(2,1)}, u32[]{:S(2)}, u32[]{:S(2)}) collective-permute-start(bf16[528,256]{1,0:T(8,128)(2,1)} %get-tuple-element.403.refs_5_), channel_id=1, source_target_pairs={{0,2},{2,4},{4,6},{6,7},{7,5},{5,3},{3,1},{1,0},{8,10},{10,12},{12... | collective-permute-start | bytes 811016 | tf_op jit(solution)/shard_map/ppermute | solution.py:174
  484.2 17.1 %collective-permute-start.106 = (bf16[528,256]{1,0:T(8,128)(2,1)S(1)}, bf16[528,256]{1,0:T(8,128)(2,1)}, u32[]{:S(2)}, u32[]{:S(2)}) collective-permute-start(bf16[528,256]{1,0:T(8,128)(2,1)S(1)} %get-tuple-element.405), channel_id=1, source_target_pairs={{0,1},{2,0},{4,2},{6,4},{7,6},{5,7},{3,5},{1,3},{8,9},{10,8},{12,1... | collective-permute-start | bytes 811016 | tf_op jit(solution)/shard_map/ppermute | solution.py:174
  494.0 27.9 %collective-permute-start.118 = (bf16[592,256]{1,0:T(8,128)(2,1)S(1)}, bf16[592,256]{1,0:T(8,128)(2,1)S(1)}, u32[]{:S(2)}, u32[]{:S(2)}) collective-permute-start(bf16[592,256]{1,0:T(8,128)(2,1)S(1)} %bitcast.188), channel_id=1, source_target_pairs={{0,8},{8,0},{16,24},{24,16},{1,9},{9,1},{17,25},{25,17},{2,10},{10... | collective-permute-start | bytes 909320 | tf_op jit(solution)/shard_map/ppermute | solution.py:36
  496.4 26.4 %collective-permute-start.119 = (bf16[592,256]{1,0:T(8,128)(2,1)S(1)}, bf16[592,256]{1,0:T(8,128)(2,1)S(1)}, u32[]{:S(2)}, u32[]{:S(2)}) collective-permute-start(bf16[592,256]{1,0:T(8,128)(2,1)S(1)} %collective-permute-done.117.refs_2_), channel_id=1, source_target_pairs={{0,8},{8,0},{16,24},{24,16},{1,9},{9,1},{17,25},{25,17},{2,10},{10... | collective-permute-start | bytes 909320 | tf_op jit(solution)/shard_map/ppermute | solution.py:36
  502.9 16.3 %collective-permute-start.109 = (bf16[528,256]{1,0:T(8,128)(2,1)S(1)}, bf16[528,256]{1,0:T(8,128)(2,1)S(1)}, u32[]{:S(2)}, u32[]{:S(2)}) collective-permute-start(bf16[528,256]{1,0:T(8,128)(2,1)S(1)} %get-tuple-element.408.refs_5_), channel_id=1, source_target_pairs={{0,2},{2,4},{4,6},{6,7},{7,5},{5,3},{3,1},{1,0},{8,10},{10,12},{12... | collective-permute-start | bytes 811016 | tf_op jit(solution)/shard_map/ppermute | solution.py:174
  519.2 20.9 %collective-permute-start.124 = (bf16[256,1024]{1,0:T(8,128)(2,1)S(1)}, bf16[256,1024]{1,0:T(8,128)(2,1)S(1)}, u32[]{:S(2)}, u32[]{:S(2)}) collective-permute-start(bf16[256,1024]{1,0:T(8,128)(2,1)S(1)} %shard_map.467.refs_6_.refs_1_), channel_id=1, source_target_pairs={{0,8},{8,0},{16,24},{24,16},{1,9},{9,1},{17,25},{25,17},{2,10},{10... | collective-permute-start | bytes 1572872 | tf_op jit(solution)/shard_map/ppermute | solution.py:36
  (276 other events, 1796.0 us)
Sparse Core Ops, SparseCore 0:
  10.7 84.8 all-gather.6
  98.4 50.2 all-gather.8
  151.4 71.9 all-gather.10
  299.1 85.7 reduce-scatter.2
  401.0 77.2 reduce-scatter.4
